TPU v7x, 512 devices: a whole 4x8x8 slice. The times are simulated.
512 devices in a mesh: aln: 4 (over x), rows: 128 (over z, y, core).
Axes of the slice: x: 4, y: 8, z: 8, core: 2. Of those that a mesh axis runs over, the one named last changes fastest.
Arguments:
- sequence_stack: bfloat16 [512, 128, 768], P(('aln', 'rows')), parts along dimension 0, may hold values from -6 to 6
- protein_spans: int32 [4], P('aln'), parts along dimension 0, may hold values from 1 to 128
- twofold_contacts: bfloat16 [512, 128, 128], P(('aln', 'rows')), parts along dimension 0, may hold values from -6 to 6
- horizontal_projection_triple: bfloat16 [768, 2304], P(None, 'rows'), may hold values from -0.21875 to 0.21875
- horizontal_projection_out: bfloat16 [768, 768], P(None, 'rows'), may hold values from -0.21875 to 0.21875
- vertical_projection_triple: bfloat16 [768, 2304], P(None, 'rows'), may hold values from -0.21875 to 0.21875
- vertical_projection_out: bfloat16 [768, 768], P(None, 'rows'), may hold values from -0.21875 to 0.21875
- contact_logit_offsets: bfloat16 [128, 12], replicated, may hold values from -0.5 to 0.5
- contact_projection_weights: bfloat16 [12, 128], replicated, may hold values from -1.75 to 1.75
Outputs:
- alignment_output: bfloat16 [512, 128, 768], P('aln', 'rows'), parts along dimension 0
- pair_feature_output: bfloat16 [512, 128, 128], P(('aln', 'rows')), parts along dimension 0
There are 4 independent parts, one for each index of `aln`. A program takes and returns all parts, laid end to end along the dimension named above; an argument that names none is the same for every part. Nothing has to cross between parts.
All inputs are finite; a program needn't handle non-finite values.
Results may differ from a plain program's by a relative error of at most 0.0075.
Values may be sent and summed in bfloat16 or wider, within the bound.
No kernel may reach another device: no remote copies, remote signals or barrier semaphores. Data moves between devices by JAX's collectives and lax.ppermute only.
A program may use at most 64 MiB of HBM per device.

v0:
```python
import jax
import jax.numpy as jnp
from jax import lax
from jax.sharding import Mesh
from jax.sharding import PartitionSpec as P

ROWS = ("rows_0", "rows_1", "rows_2")
ALN_ROWS = ("aln", "rows_0", "rows_1", "rows_2")


def in_blocks(x, dim, peers):
    dims = x.shape
    tiles = x.reshape(*dims[:dim], peers, dims[dim] // peers, *dims[dim + 1 :])
    return jnp.moveaxis(tiles, dim, 0)


def sent_and_summed(x, axis, dim):
    tiles = in_blocks(x, dim, lax.axis_size(axis))
    arrived = lax.all_to_all(tiles, axis, split_axis=0, concat_axis=0, tiled=True)
    return arrived.sum(axis=0)


def summed_rows(x, axes, dim):
    far, near = axes
    own = sent_and_summed(in_blocks(x, dim, lax.axis_size(far)), near, dim + 1)
    return jnp.sum(lax.all_to_all(own, far, 0, 0, tiled=True), axis=0)


def sent_to_all(x, axis):
    copies = jnp.broadcast_to(x, (lax.axis_size(axis), *x.shape))
    return lax.all_to_all(copies, axis, split_axis=0, concat_axis=0, tiled=True)


def joined_along(tiles, dim):
    dims = list(tiles.shape[1:])
    dims[dim] *= tiles.shape[0]
    return jnp.moveaxis(tiles, 0, dim).reshape(dims)


def gather_axes(x, axes, dim):
    far, near = axes
    tiles = sent_to_all(sent_to_all(x, far), near)
    return joined_along(tiles.swapaxes(0, 1).reshape(-1, *x.shape), dim)


def normalize(incoming_sequence_stack):
    center = jnp.mean(incoming_sequence_stack, axis=-1, keepdims=True)
    spread = jnp.mean(jnp.square(incoming_sequence_stack - center), axis=-1, keepdims=True)
    return (incoming_sequence_stack - center) * lax.rsqrt(spread + 1e-05)


def split_three(packed, hidden_channel_size, head_count, shape_rows, shape_res):
    head_dim = hidden_channel_size // head_count
    queries = (packed[:, :hidden_channel_size] * head_dim ** (-0.5)).astype(jnp.bfloat16)
    key_rows = packed[:, hidden_channel_size : 2 * hidden_channel_size].astype(jnp.bfloat16)
    value_rows = packed[:, 2 * hidden_channel_size :].astype(jnp.bfloat16)
    input_dimensions = (shape_rows, shape_res, head_count, head_dim)
    return (
        queries.reshape(input_dimensions),
        key_rows.reshape(input_dimensions),
        value_rows.reshape(input_dimensions),
    )


def masked_softmax(scores, protein_spans):
    key_valid = lax.broadcasted_iota(jnp.int32, (1, 1, scores.shape[2]), 2) < protein_spans[0]
    return jax.nn.softmax(jnp.where(key_valid, scores, -1e30), axis=-1).astype(jnp.bfloat16)


def per_device(
    sequence_stack,
    protein_spans,
    twofold_contacts,
    horizontal_projection_triple,
    horizontal_projection_out,
    vertical_projection_triple,
    vertical_projection_out,
    contact_logit_offsets,
    contact_projection_weights,
):
    sequences_per_shard, sequence_positions, hidden_channel_size = sequence_stack.shape
    parties = lax.axis_size(ROWS)
    overall_sequence_number = sequences_per_shard * parties
    residue_portion = sequence_positions // parties
    head_count = contact_logit_offsets.shape[1]
    channels = contact_logit_offsets.shape[0]
    scale_rows = float(overall_sequence_number) ** (-0.5)
    incoming_sequence_stack = sequence_stack.astype(jnp.float32)
    normed = (
        normalize(incoming_sequence_stack).astype(jnp.bfloat16).reshape(-1, hidden_channel_size)
    )
    row_whole = lax.all_gather(horizontal_projection_triple, ROWS, axis=1, tiled=True)
    packed = jnp.dot(normed, row_whole, preferred_element_type=jnp.float32)
    queries, key_rows, value_rows = split_three(
        packed, hidden_channel_size, head_count, sequences_per_shard, sequence_positions
    )
    partial_value = jnp.einsum(
        "rihe,rjhe->hij", queries, key_rows, preferred_element_type=jnp.float32
    )
    bias_own = jnp.dot(
        twofold_contacts.reshape(-1, channels),
        contact_logit_offsets,
        preferred_element_type=jnp.float32,
    )
    bias_own = bias_own.reshape(residue_portion, sequence_positions, head_count).transpose(2, 0, 1)
    owned = summed_rows(partial_value, (("rows_0", "rows_1"), "rows_2"), 1)
    scores = owned * scale_rows + bias_own
    probs_own = masked_softmax(scores, protein_spans)
    row_probs = gather_axes(probs_own, (("rows_0", "rows_1"), "rows_2"), 1)
    flat_scores = scores.astype(jnp.bfloat16).transpose(1, 2, 0).reshape(-1, head_count)
    pair_feature_output = (
        twofold_contacts.astype(jnp.float32)
        + jnp.dot(
            flat_scores, contact_projection_weights, preferred_element_type=jnp.float32
        ).reshape(residue_portion, sequence_positions, channels)
    ).astype(jnp.bfloat16)
    blended = jnp.einsum(
        "hij,rjhe->rihe", row_probs, value_rows, preferred_element_type=jnp.float32
    )
    blended = blended.astype(jnp.bfloat16).reshape(-1, hidden_channel_size)
    out_whole = gather_axes(horizontal_projection_out, (("rows_0", "rows_1"), "rows_2"), 1)
    attended = jnp.dot(blended, out_whole, preferred_element_type=jnp.float32)
    updated_alignment = (
        incoming_sequence_stack
        + attended.reshape(sequences_per_shard, sequence_positions, hidden_channel_size)
    ).astype(jnp.bfloat16)
    columns = lax.all_to_all(updated_alignment, ROWS, split_axis=1, concat_axis=0, tiled=True)
    column_input_rows = columns.astype(jnp.float32)
    col_normed = normalize(column_input_rows).astype(jnp.bfloat16).reshape(-1, hidden_channel_size)
    col_whole = lax.all_gather(vertical_projection_triple, ROWS, axis=1, tiled=True)
    col_packed = jnp.dot(col_normed, col_whole, preferred_element_type=jnp.float32)
    col_queries, col_keys, col_values = split_three(
        col_packed, hidden_channel_size, head_count, overall_sequence_number, residue_portion
    )
    logits = jnp.einsum(
        "alhe,blhe->lhab", col_queries, col_keys, preferred_element_type=jnp.float32
    )
    col_probs = jax.nn.softmax(logits, axis=-1).astype(jnp.bfloat16)
    column_mixed_output = jnp.einsum(
        "lhab,blhe->alhe", col_probs, col_values, preferred_element_type=jnp.float32
    )
    column_mixed_output = column_mixed_output.astype(jnp.bfloat16).reshape(-1, hidden_channel_size)
    col_out_whole = gather_axes(vertical_projection_out, (("rows_0", "rows_1"), "rows_2"), 1)
    column_attention_result = jnp.dot(
        column_mixed_output, col_out_whole, preferred_element_type=jnp.float32
    )
    alignment_output = (
        column_input_rows
        + column_attention_result.reshape(
            overall_sequence_number, residue_portion, hidden_channel_size
        )
    ).astype(jnp.bfloat16)
    return (alignment_output, pair_feature_output)


def solution(mesh):
    torus = Mesh(
        mesh.devices.reshape(mesh.shape["aln"], 8, 8, 2), ("aln", "rows_0", "rows_1", "rows_2")
    )
    in_specs = (
        P(ALN_ROWS, None, None),
        P("aln"),
        P(ALN_ROWS, None, None),
        P(None, ROWS),
        P(None, ROWS),
        P(None, ROWS),
        P(None, ROWS),
        P(),
        P(),
    )
    out_specs = (P("aln", ROWS, None), P(ALN_ROWS, None, None))
    return jax.shard_map(
        per_device, mesh=torus, in_specs=in_specs, out_specs=out_specs, check_vma=False
    )
```

profile of v0, /device:TPU:1, one launch (start us, length us, event | category | flops | bytes accessed | tf_op | source)
XLA Modules:
  0.0 264.8 jit_solution(3789819001439043487)
XLA Ops:
  7.2 0.7 all-gather.5.cloned.1.call-update
  8.0 0.7 all-gather.7.cloned.1.call-update
  8.7 1.7 broadcast_in_dim.42
  10.4 17.1 %all-to-all-start.4 = ((bf16[64,768,6]{1,2,0:T(8,128)(2,1)}), bf16[64,768,6]{1,2,0:T(8,128)(2,1)S(1)}, u32[]{:S(2)}, u32[]{:S(2)}) async-start(bf16[64,768,6]{1,2,0:T(8,128)(2,1)} %broadcast_in_dim.42), calls=%async_computation.4 | async-start | bytes 1572864 | tf_op jit(solution)/shard_map/all_to_all | solution.py:31
  27.6 0.2 fusion.13
  27.8 22.1 %all-to-all-done.4 = bf16[64,768,6]{1,2,0:T(8,128)(2,1)S(1)} async-done(((bf16[64,768,6]{1,2,0:T(8,128)(2,1)}), bf16[64,768,6]{1,2,0:T(8,128)(2,1)S(1)}, u32[]{:S(2)}, u32[]{:S(2)}) %all-to-all-start.4) | async-done | bytes 589856 | tf_op jit(solution)/shard_map/all_to_all | solution.py:31
  50.0 0.9 copy.37
  50.9 57.5 %all-gather.5.cloned.1.call-done = bf16[128,18,768]{2,1,0:T(8,128)(2,1)} async-done(((bf16[1,18,768]{2,1,0:T(8,128)(2,1)}), bf16[128,18,768]{2,1,0:T(8,128)(2,1)}) %all-gather.5.cloned.1.call-update) | async-done | bytes 3538960 | tf_op jit(solution)/shard_map/all_gather | solution.py:92
  108.4 5.0 %reshape.274 = bf16[2304,768]{1,0:T(8,128)(2,1)S(1)} reshape(bf16[128,18,768]{2,1,0:T(8,128)(2,1)} %all-gather.5.cloned.1.call-done) | data formatting | bytes 7077888
  113.4 3.3 %fusion.41 = (bf16[128,2304]{1,0:T(8,128)(2,1)S(1)}, f32[128,2304]{1,0:T(8,128)}) fusion(bf16[2304,768]{1,0:T(8,128)(2,1)S(1)} %reshape.274, bf16[1,128,768]{2,1,0:T(8,128)(2,1)} %param.9, f32[128]{0:T(128)S(1)} %add_rsqrt_fusion.1, f32[128]{0:T(128)S(1)} %broadcast_multiply_fusion.1), kind=kOutput, calls=%fused_computation.61 | convolution fusion | flops 453672960 | bytes 5506048 | tf_op jit(solution)/shard_map/dot_general | solution.py:93
  116.7 0.7 fusion.40
  117.6 1.0 fusion.21
  118.6 0.2 copy.30
  118.8 0.3 fusion.44
  119.2 4.4 %all_to_all.52 = f32[2,64,12,1,128]{4,1,2,3,0:T(8,128)S(1)} all-to-all(f32[2,64,12,1,128]{4,1,2,3,0:T(8,128)S(1)} %bitcast.139), channel_id=1, replica_groups=mesh['aln'=4,'rows_0'=8,'rows_1'=8,'rows_2'=2] {'rows_2'}, dimensions={0} | all-to-all | bytes 1572864 | tf_op jit(solution)/shard_map/all_to_all | solution.py:19
  123.6 1.2 broadcast_in_dim.43
  124.7 4.0 %all-to-all-start.5 = ((bf16[2,64,768,6]{2,1,3,0:T(8,128)(2,1)}), bf16[2,64,768,6]{2,1,3,0:T(8,128)(2,1)S(1)}, u32[]{:S(2)}, u32[]{:S(2)}) async-start(bf16[2,64,768,6]{2,1,3,0:T(8,128)(2,1)} %broadcast_in_dim.43), calls=%async_computation.5 | async-start | bytes 2359296 | tf_op jit(solution)/shard_map/all_to_all | solution.py:31
  128.8 0.4 copy.34
  129.2 1.4 all-to-all-done.5
  130.5 23.4 %all_to_all.53 = f32[64,12,1,128]{3,2,1,0:T(1,128)S(1)} all-to-all(f32[64,12,1,128]{3,2,1,0:T(1,128)S(1)} %copy.34), channel_id=1, replica_groups=mesh['aln'=4,'rows_0'=8,'rows_1'=8,'rows_2'=2] {'rows_0','rows_1'}, dimensions={0} | all-to-all | bytes 786432 | tf_op jit(solution)/shard_map/all_to_all | solution.py:26
  154.0 0.9 broadcast_in_dim.44
  154.9 6.7 %all-to-all-start.7 = ((bf16[64,768,6]{1,2,0:T(8,128)(2,1)}), bf16[64,768,6]{1,2,0:T(8,128)(2,1)S(1)}, u32[]{:S(2)}, u32[]{:S(2)}) async-start(bf16[64,768,6]{1,2,0:T(8,128)(2,1)} %broadcast_in_dim.44), calls=%async_computation.7 | async-start | bytes 1572864 | tf_op jit(solution)/shard_map/all_to_all | solution.py:31
  162.2 0.3 reduce_sum.78
  162.5 0.2 select_reduce_fusion
  162.8 0.2 fusion.34
  163.0 22.6 %all-to-all-done.7 = bf16[64,768,6]{1,2,0:T(8,128)(2,1)S(1)} async-done(((bf16[64,768,6]{1,2,0:T(8,128)(2,1)}), bf16[64,768,6]{1,2,0:T(8,128)(2,1)S(1)}, u32[]{:S(2)}, u32[]{:S(2)}) %all-to-all-start.7) | async-done | bytes 589856 | tf_op jit(solution)/shard_map/all_to_all | solution.py:31
  185.7 0.8 broadcast_in_dim.40
  186.4 9.3 %all-to-all-start.2 = ((bf16[64,12,1,128]{3,1,2,0:T(8,128)(2,1)}), bf16[64,12,1,128]{3,1,2,0:T(8,128)(2,1)}, u32[]{:S(2)}, u32[]{:S(2)}) async-start(bf16[64,12,1,128]{3,1,2,0:T(8,128)(2,1)} %broadcast_in_dim.40), calls=%async_computation.2 | async-start | bytes 524288 | tf_op jit(solution)/shard_map/all_to_all | solution.py:31
  195.8 1.2 copy.38
  197.0 0.5 reshape.261
  197.5 0.7 copy.39
  198.2 0.4 reshape.262
  198.7 0.8 copy-done.7
  199.7 8.4 %all-to-all-done.2 = bf16[64,12,1,128]{3,1,2,0:T(8,128)(2,1)} async-done(((bf16[64,12,1,128]{3,1,2,0:T(8,128)(2,1)}), bf16[64,12,1,128]{3,1,2,0:T(8,128)(2,1)}, u32[]{:S(2)}, u32[]{:S(2)}) %all-to-all-start.2) | async-done | bytes 196640 | tf_op jit(solution)/shard_map/all_to_all | solution.py:31
  208.1 1.0 copy.35
  209.2 8.0 %all_to_all.54 = bf16[2,64,12,1,128]{4,1,2,3,0:T(8,128)(2,1)S(1)} all-to-all(bf16[2,64,12,1,128]{4,1,2,3,0:T(8,128)(2,1)S(1)} %broadcast_in_dim.41), channel_id=1, replica_groups=mesh['aln'=4,'rows_0'=8,'rows_1'=8,'rows_2'=2] {'rows_2'}, dimensions={0} | all-to-all | bytes 786432 | tf_op jit(solution)/shard_map/all_to_all | solution.py:31
  217.2 1.2 broadcast_in_dim.45
  218.3 4.0 %all-to-all-start.8 = ((bf16[2,64,768,6]{2,1,3,0:T(8,128)(2,1)}), bf16[2,64,768,6]{2,1,3,0:T(8,128)(2,1)S(1)}, u32[]{:S(2)}, u32[]{:S(2)}) async-start(bf16[2,64,768,6]{2,1,3,0:T(8,128)(2,1)} %broadcast_in_dim.45), calls=%async_computation.8 | async-start | bytes 2359296 | tf_op jit(solution)/shard_map/all_to_all | solution.py:31
  222.3 0.4 copy.36
  222.7 0.4 convolution_convert_fusion.1
  223.2 0.5 fusion.4
  223.7 0.3 copy.55
  224.1 0.5 broadcast.103
  224.6 1.8 reduce.13
  226.4 0.7 reshape.277
  227.1 6.4 %all-to-all-start.6 = ((bf16[128,2,384]{2,1,0:T(2,128)(2,1)}), bf16[128,2,384]{2,1,0:T(2,128)(2,1)}, u32[]{:S(2)}, u32[]{:S(2)}) async-start(bf16[128,2,384]{2,1,0:T(2,128)(2,1)} %reshape.277), calls=%async_computation.6 | async-start | bytes 393216 | tf_op jit(solution)/shard_map/all_to_all | solution.py:127
  233.5 1.2 copy.47
  234.7 0.5 reshape.268
  235.2 0.7 copy.48
  235.9 1.3 reshape.269
  237.2 5.0 %reshape.276 = bf16[2304,768]{1,0:T(8,128)(2,1)S(1)} reshape(bf16[128,18,768]{2,1,0:T(8,128)(2,1)} %all-gather.7.cloned.1.call-done) | data formatting | bytes 7077888
  242.2 1.6 fusion.8
  243.8 3.5 %all-to-all-done.6 = bf16[128,2,384]{2,1,0:T(2,128)(2,1)} async-done(((bf16[128,2,384]{2,1,0:T(2,128)(2,1)}), bf16[128,2,384]{2,1,0:T(2,128)(2,1)}, u32[]{:S(2)}, u32[]{:S(2)}) %all-to-all-start.6) | async-done | bytes 196640 | tf_op jit(solution)/shard_map/all_to_all | solution.py:127
  247.3 2.2 reshape.278
  249.5 1.1 convert_reduce_fusion
  250.6 0.2 fusion.19
  250.8 2.3 fusion.42
  253.2 0.2 copy.44
  253.4 1.0 fusion.20
  254.6 0.3 fusion.45
  254.9 0.4 fusion.43
  255.5 0.3 convolution_convert_fusion
  255.8 0.9 copy-done.1
  256.8 1.2 fusion.6
  (40 shorter events, 1.5 us)
Async XLA Ops:
  7.2 235.0 %copy-start = (bf16[12,128]{1,0:T(8,128)(2,1)S(1)}, bf16[12,128]{1,0:T(8,128)(2,1)}, u32[]{:S(2)}) copy-start(bf16[12,128]{1,0:T(8,128)(2,1)} %param.17) | copy-start | bytes 9220
  7.2 101.2 %all-gather.5.cloned.1.call-start = ((), (), s32[]{:S(2)}) async-start(), calls=%async_computation.9 | async-start | bytes 4755456 | tf_op jit(solution)/shard_map/all_gather | solution.py:92
  7.9 229.3 %all-gather.7.cloned.1.call-start = ((), (), s32[]{:S(2)}) async-start(), calls=%async_computation.10 | async-start | bytes 4755456 | tf_op jit(solution)/shard_map/all_gather | solution.py:130
  8.7 18.8 %copy-start.2 = (bf16[1,128,768]{2,1,0:T(8,128)(2,1)S(1)}, bf16[1,128,768]{2,1,0:T(8,128)(2,1)}, u32[]{:S(2)}) copy-start(bf16[1,128,768]{2,1,0:T(8,128)(2,1)} %param.9) | copy-start | bytes 589828
  10.4 39.6 %all-to-all-start.4 = ((bf16[64,768,6]{1,2,0:T(8,128)(2,1)}), bf16[64,768,6]{1,2,0:T(8,128)(2,1)S(1)}, u32[]{:S(2)}, u32[]{:S(2)}) async-start(bf16[64,768,6]{1,2,0:T(8,128)(2,1)} %broadcast_in_dim.42), calls=%async_computation.4 | async-start | bytes 1572864 | tf_op jit(solution)/shard_map/all_to_all | solution.py:31
  119.2 4.4 %copy-start.6 = (bf16[64,768,6]{1,0,2:T(8,128)(2,1)S(1)}, bf16[64,768,6]{1,0,2:T(8,128)(2,1)}, u32[]{:S(2)}) copy-start(bf16[64,768,6]{1,0,2:T(8,128)(2,1)} %copy.37) | copy-start | bytes 1769476
  124.7 5.8 %all-to-all-start.5 = ((bf16[2,64,768,6]{2,1,3,0:T(8,128)(2,1)}), bf16[2,64,768,6]{2,1,3,0:T(8,128)(2,1)S(1)}, u32[]{:S(2)}, u32[]{:S(2)}) async-start(bf16[2,64,768,6]{2,1,3,0:T(8,128)(2,1)} %broadcast_in_dim.43), calls=%async_computation.5 | async-start | bytes 2359296 | tf_op jit(solution)/shard_map/all_to_all | solution.py:31
  128.7 25.3 %copy-start.9 = (bf16[768,6]{0,1:T(8,128)(2,1)S(1)}, bf16[768,6]{0,1:T(8,128)(2,1)}, u32[]{:S(2)}) copy-start(bf16[768,6]{0,1:T(8,128)(2,1)} %param.15) | copy-start | bytes 27652
  154.9 7.6 %copy-start.8 = (bf16[1,128,128]{2,1,0:T(8,128)(2,1)S(1)}, bf16[1,128,128]{2,1,0:T(8,128)(2,1)}, u32[]{:S(2)}) copy-start(bf16[1,128,128]{2,1,0:T(8,128)(2,1)} %param.11) | copy-start | bytes 98308
  154.9 7.6 %copy-start.10 = (bf16[128,12]{0,1:T(8,128)(2,1)S(1)}, bf16[128,12]{0,1:T(8,128)(2,1)}, u32[]{:S(2)}) copy-start(bf16[128,12]{0,1:T(8,128)(2,1)} %param.16) | copy-start | bytes 9220
  154.9 30.8 %all-to-all-start.7 = ((bf16[64,768,6]{1,2,0:T(8,128)(2,1)}), bf16[64,768,6]{1,2,0:T(8,128)(2,1)S(1)}, u32[]{:S(2)}, u32[]{:S(2)}) async-start(bf16[64,768,6]{1,2,0:T(8,128)(2,1)} %broadcast_in_dim.44), calls=%async_computation.7 | async-start | bytes 1572864 | tf_op jit(solution)/shard_map/all_to_all | solution.py:31
  186.4 21.7 %all-to-all-start.2 = ((bf16[64,12,1,128]{3,1,2,0:T(8,128)(2,1)}), bf16[64,12,1,128]{3,1,2,0:T(8,128)(2,1)}, u32[]{:S(2)}, u32[]{:S(2)}) async-start(bf16[64,12,1,128]{3,1,2,0:T(8,128)(2,1)} %broadcast_in_dim.40), calls=%async_computation.2 | async-start | bytes 524288 | tf_op jit(solution)/shard_map/all_to_all | solution.py:31
  198.6 0.9 copy-start.7
  218.3 8.8 %all-to-all-start.8 = ((bf16[2,64,768,6]{2,1,3,0:T(8,128)(2,1)}), bf16[2,64,768,6]{2,1,3,0:T(8,128)(2,1)S(1)}, u32[]{:S(2)}, u32[]{:S(2)}) async-start(bf16[2,64,768,6]{2,1,3,0:T(8,128)(2,1)} %broadcast_in_dim.45), calls=%async_computation.8 | async-start | bytes 2359296 | tf_op jit(solution)/shard_map/all_to_all | solution.py:31
  222.3 0.9 copy-start.3
  227.1 20.2 %all-to-all-start.6 = ((bf16[128,2,384]{2,1,0:T(2,128)(2,1)}), bf16[128,2,384]{2,1,0:T(2,128)(2,1)}, u32[]{:S(2)}, u32[]{:S(2)}) async-start(bf16[128,2,384]{2,1,0:T(2,128)(2,1)} %reshape.277), calls=%async_computation.6 | async-start | bytes 393216 | tf_op jit(solution)/shard_map/all_to_all | solution.py:127
  250.6 2.6 copy-start.4
  255.5 1.3 copy-start.1
  255.5 1.3 copy-start.5
Sparse Core Ops, SparseCore 0:
  11.2 97.1 all-gather.4
  111.6 95.3 all-gather.6
where the time goes:
time: 266 us; the launch traced here: 265 us
  waiting for transfers between devices  117 us (44%)
  starting transfers between devices  47.5 us (18%)
  blocking collectives  35.7 us (13%)
  local copies, waits for them, and re-layouts  32.6 us (12%)
  between operations  15 us (6%)
  matrix products  10.9 us (4%)
  other arithmetic  6.12 us (2%)
    all_gather x1, waiting for transfers between devices, per_device(): lax.all_gather(horizontal_projection_triple, ROWS, axis=1, tiled=True)  57.5 us
    all_to_all x5, waiting for transfers between devices, sent_to_all(): return lax.all_to_all(copies, axis, split_axis=0, concat_axis=0, tiled=True)  54.5 us
    all_to_all x5, starting transfers between devices, sent_to_all(): return lax.all_to_all(copies, axis, split_axis=0, concat_axis=0, tiled=True)  41.1 us
    all_to_all x1, blocking collectives, summed_rows(): return jnp.sum(lax.all_to_all(own, far, 0, 0, tiled=True), axis=0)  23.4 us
    unnamed x27, local copies, waits for them, and re-layouts  15.4 us
    all_to_all x1, blocking collectives, sent_to_all(): return lax.all_to_all(copies, axis, split_axis=0, concat_axis=0, tiled=True)  7.96 us
    all_to_all x1, starting transfers between devices, per_device(): lax.all_to_all(updated_alignment, ROWS, split_axis=1, concat_axis=0, tile...  6.37 us
    broadcast_in_dim x6, local copies, waits for them, and re-layouts, sent_to_all(): copies = jnp.broadcast_to(x, (lax.axis_size(axis), *x.shape))  5.8 us
  transfers between devices with their start and end apart: 8, of which 6 were waited for; matrix products, arithmetic and copies ran while one was open for 14% of the time, Pallas kernels for 0%

commit v1 on v0

v1 whole, which is shorter than its diff:
```python
import functools

import jax
import jax.numpy as jnp
from jax import lax
from jax.experimental import pallas as pl
from jax.experimental.pallas import tpu as pltpu
from jax.sharding import Mesh
from jax.sharding import PartitionSpec as P

ALL = ("a", "z", "y", "c")
ROWS = ("z", "y", "c")
CHIPS = ("z", "y")
D, H, E, L, R = 768, 12, 64, 128, 128
BF, F32 = jnp.bfloat16, jnp.float32
VMEM = pl.BlockSpec(memory_space=pltpu.VMEM)
SMEM = pl.BlockSpec(memory_space=pltpu.SMEM)


def params():
    return pltpu.CompilerParams(vmem_limit_bytes=48 << 20)


def dot_nt(a, b):
    return lax.dot_general(a, b, (((1,), (1,)), ((), ())), preferred_element_type=F32)


def dot_tn(a, b):
    return lax.dot_general(a, b, (((0,), (0,)), ((), ())), preferred_element_type=F32)


def first_head(y):
    return 3 * (y // 2) + y % 2


def normalize(x):
    center = jnp.mean(x, axis=-1, keepdims=True)
    spread = jnp.mean(jnp.square(x - center), axis=-1, keepdims=True)
    return (x - center) * lax.rsqrt(spread + 1e-05)


def project_and_tie(y_ref, w_ref, *refs):
    row_refs, (tied_ref, v_ref) = refs[:9], refs[9:]
    w = w_ref[...]
    lane = lax.broadcasted_iota(jnp.int32, (L, 2 * E), 1)
    offsets = (0, -1, 1, -2, 2, -3, 3, 4)
    tied = [jnp.zeros((L, L), F32), jnp.zeros((L, L), F32)]
    for n, offset in enumerate(offsets):
        if n < 7:
            x = row_refs[n][...]
        else:
            x = jnp.concatenate([row_refs[7][...], row_refs[8][...]], axis=0)
        packed = jnp.dot(x, w, preferred_element_type=F32)
        q = packed[:, : 2 * E] * E**-0.5
        k = packed[:, 2 * E : 4 * E].astype(BF)
        v_ref[lax.rem(y_ref[0] + (8 + offset), 8)] = packed[:, 4 * E :].astype(BF)
        tied[0] += dot_nt(jnp.where(lane < E, q, 0.0).astype(BF), k)
        tied[1] += dot_nt(jnp.where(lane < E, 0.0, q).astype(BF), k)
    for h in range(2):
        tied_ref[h] = tied[h] * R**-0.5


def attend(span_ref, part_ref, bias_ref, out_ref):
    scores = bias_ref[...].astype(F32)
    for n in range(8):
        scores += part_ref[n].astype(F32)
    j = lax.broadcasted_iota(jnp.int32, (L, L), 1)
    masked = jnp.where(j < span_ref[0], scores, -1e30)
    e = jnp.exp(masked - jnp.max(masked, axis=1, keepdims=True))
    out_ref[0] = (e / jnp.sum(e, axis=1, keepdims=True)).astype(BF)
    out_ref[1] = scores.astype(BF)


def blend(y_ref, probs_ref, v_ref, out_ref, held):
    lane = lax.broadcasted_iota(jnp.int32, (L, 2 * E), 1)
    low = lane < E
    odd = lax.rem(y_ref[0], 2) == 1
    plain = [probs_ref[h, 1].astype(F32) for h in range(2)]
    moved = [pltpu.roll(s, E, 1) for s in plain]
    for n in range(8):
        v = v_ref[n]
        o = jnp.where(
            low,
            jnp.dot(probs_ref[0, 0], v, preferred_element_type=F32),
            jnp.dot(probs_ref[1, 0], v, preferred_element_type=F32),
        )
        h, half = (n % 4) // 2, n % 2
        if n < 4:
            extra = moved[h] if half else plain[h]
            o = jnp.where(jnp.logical_and(low, odd), extra, o)
        else:
            extra = plain[h] if half else moved[h]
            o = jnp.where(jnp.logical_or(low, odd), o, extra)
        held[:, n, :] = o
    out_ref[...] = held[...].astype(BF)


def column_block(
    c_ref, bl_ref, stack_ref, g_ref, pair_ref, cw_ref, out_ref, pair_out_ref, tall, feat, packed, mixed
):
    mine = c_ref[0]
    lane = lax.broadcasted_iota(jnp.int32, (L, L), 1)
    row = lax.broadcasted_iota(jnp.int32, (L, L), 0)
    low = lane < E
    early = lax.rem(row, 8) < 4

    def tile(c, z, y):
        both = bl_ref[c, z * 8 + y].astype(F32)
        return jnp.where(mine == 0, both[:8], both[8:])

    tiles = [[tile(c, z, y) for c in range(2) for z in range(8)] for y in range(8)]
    blocks = [jnp.concatenate(t, axis=0) for t in tiles]
    parts = []
    for n in range(2):
        e0, o0, e1, o1 = blocks[4 * n : 4 * n + 4]
        ro0, re1 = pltpu.roll(o0, E, 1), pltpu.roll(e1, E, 1)
        parts.append(jnp.where(jnp.logical_or(low, early), e0, ro0))
        parts.append(jnp.where(low, ro0, re1))
        parts.append(jnp.where(jnp.logical_and(low, early), re1, o1))
    blended = jnp.concatenate(parts, axis=1).astype(BF)

    tail = g_ref[:, 16:32, :].reshape(2048, D)
    tall[...] = dot_nt(tail, blended)
    for d in range(128):
        feat[6 * d : 6 * d + 6, :] = tall[16 * d + 8 : 16 * d + 14, :]
    for n in range(6):
        own = jnp.concatenate([stack_ref[:, 128 * n : 128 * n + 128]], axis=1).astype(F32).T
        feat[128 * n : 128 * n + 128, :] += own
    updated = feat[...].astype(BF).astype(F32)
    feat[...] = updated
    center = jnp.mean(updated, axis=0, keepdims=True)
    spread = jnp.mean(jnp.square(updated - center), axis=0, keepdims=True)
    normed = ((updated - center) * lax.rsqrt(spread + 1e-05)).astype(BF)

    tall[...] = jnp.dot(g_ref[:, 0:16, :].reshape(2048, D), normed, preferred_element_type=F32)
    for d in range(128):
        packed[18 * d : 18 * d + 16, :] = tall[16 * d : 16 * d + 16, :]
    tall[...] = jnp.dot(tail, normed, preferred_element_type=F32)
    for d in range(128):
        packed[18 * d + 16 : 18 * d + 18, :] = tall[16 * d : 16 * d + 2, :]

    for h in range(H):
        q = (packed[E * h : E * h + E, :] * E**-0.5).astype(BF)
        k = packed[D + E * h : D + E * h + E, :].astype(BF)
        v = packed[2 * D + E * h : 2 * D + E * h + E, :].astype(BF)
        logits = dot_tn(k, q)
        e = jnp.exp(logits - jnp.max(logits, axis=0, keepdims=True))
        probs = (e / jnp.sum(e, axis=0, keepdims=True)).astype(BF)
        mixed[E * h : E * h + E, :] = jnp.dot(v, probs, preferred_element_type=F32).astype(BF)

    tall[...] = jnp.dot(tail, mixed[...], preferred_element_type=F32)
    for d in range(128):
        feat[6 * d : 6 * d + 6, :] += tall[16 * d + 2 : 16 * d + 8, :]
    place = (lax.rem(row, 2) * E + row // 2 == lane).astype(BF)
    out_ref[...] = dot_nt(place, feat[...].astype(BF)).astype(BF)

    one = lax.broadcasted_iota(jnp.int32, (1, L), 1) < E
    lines = []
    for n in range(4):
        e, o = tiles[2 * n][0], tiles[2 * n + 1][0]
        re, ro = pltpu.roll(e, E, 1), pltpu.roll(o, E, 1)
        lines.append(jnp.where(one, re[4:5], e[5:6]))
        lines.append(jnp.where(one, re[6:7], e[7:8]))
        lines.append(jnp.where(one, o[2:3], ro[3:4]))
    scores = jnp.concatenate(lines + [jnp.zeros((L - H, L), F32)], axis=0).T
    weights = jnp.concatenate([cw_ref[...].astype(F32), jnp.zeros((L - H, L), F32)], axis=0)
    pair = pair_ref[...].astype(F32) + jnp.dot(
        scores.astype(BF), weights.astype(BF), preferred_element_type=F32
    )
    pair_out_ref[...] = pair.astype(BF)


def ring_rows(x):
    right = [(i, (i + 1) % 8) for i in range(8)]
    left = [(i, (i + 7) % 8) for i in range(8)]
    from_left, from_right = [x], [x]
    for step in range(3):
        from_left.append(lax.ppermute(from_left[-1], "y", right))
        from_right.append(lax.ppermute(from_right[-1], "y", left))
    far = [
        lax.ppermute(from_left[-1][: L // 2], "y", right),
        lax.ppermute(from_right[-1][L // 2 :], "y", left),
    ]
    return [x] + [t[n] for n in (1, 2, 3) for t in (from_left, from_right)] + far


def per_device(stack, spans, pair, w_triple, w_out, v_triple, v_out, offsets, contact_w):
    y, c = lax.axis_index("y"), lax.axis_index("c")
    y1, c1 = y[None].astype(jnp.int32), c[None].astype(jnp.int32)
    pair_own = pair.reshape(L, 128)
    own_row = stack.reshape(L, D)

    column_weights = jnp.concatenate([v_triple.T, v_out.T, w_out.T, jnp.zeros((2, D), BF)], axis=0)
    gathered = lax.all_gather(column_weights, ROWS, axis=0, tiled=False)

    normed = normalize(own_row.astype(F32)).astype(BF)
    rows = ring_rows(normed)

    bias = lax.dot_general(offsets, pair_own, (((0,), (1,)), ((), ())), preferred_element_type=F32).astype(BF)
    bias_pairs = jnp.stack([bias[first_head(n) : first_head(n) + 2] for n in range(8)])
    slices = w_triple.T.reshape(18, 2, 8, 48).transpose(2, 0, 1, 3).reshape(8, 1, 18, 96)
    slices = jnp.pad(slices, ((0, 0), (0, 0), (0, 0), (0, 32)))
    message = jnp.concatenate(
        [
            jnp.broadcast_to(slices, (8, 8, 18, 128)).reshape(64, 18, 128),
            own_row.reshape(64, 12, 128),
            jnp.broadcast_to(bias_pairs[None], (8, 8, 2, 128)).reshape(64, 2, 128),
        ],
        axis=1,
    )
    came = lax.all_to_all(message, CHIPS, 0, 0, tiled=True)

    source = lax.broadcasted_iota(jnp.int32, (2048, 384), 0)
    target = lax.broadcasted_iota(jnp.int32, (2048, 384), 1)
    column = (source // 32 * 2 + c) * 18 + source % 32
    wanted = target // 128 * D + first_head(y) * E + target % 128
    pick = jnp.logical_and(column == wanted, source % 32 < 18).astype(BF)
    picked = dot_tn(came.reshape(2048, 128), pick)[:96].astype(BF)
    picked = lax.all_gather(picked, "c", axis=0, tiled=False)
    half = lax.dynamic_slice_in_dim(picked, c * 48, 48, axis=1)
    half = half[0] + half[1]
    over_z = lax.all_to_all(jnp.broadcast_to(half, (8, 48, 384)), "z", 0, 0, tiled=True)
    w_heads = lax.all_gather(over_z, "c", axis=0, tiled=False).reshape(D, 384)

    rest = lax.all_gather(came[:, 18:, :], "c", axis=0, tiled=False)
    stack_own = rest[:, :, :12].reshape(2, 64, 2, D)
    stack_own = lax.dynamic_index_in_dim(stack_own, c, 2, keepdims=False).reshape(R, D)
    bias_own = lax.dynamic_index_in_dim(rest[:, :, 12:], c, 2, keepdims=False)
    bias_own = bias_own.transpose(1, 0, 2).reshape(L, L)

    tied, values = pl.pallas_call(
        project_and_tie,
        out_shape=(
            jax.ShapeDtypeStruct((2, L, L), F32),
            jax.ShapeDtypeStruct((8, L, 2 * E), BF),
        ),
        in_specs=[SMEM] + [VMEM] * 10,
        out_specs=(VMEM, VMEM),
        compiler_params=params(),
    )(y1, w_heads, *rows)

    tied = lax.all_gather(tied, "c", axis=0, tiled=False)
    tied = lax.dynamic_index_in_dim(tied, c, 1, keepdims=False)
    tied = (tied[0] + tied[1]).astype(BF)
    parts = lax.all_to_all(jnp.broadcast_to(tied, (8, L, L)), "z", 0, 0, tiled=True)
    head = pl.pallas_call(
        attend,
        out_shape=jax.ShapeDtypeStruct((2, L, L), BF),
        in_specs=[SMEM, VMEM, VMEM],
        out_specs=VMEM,
        compiler_params=params(),
    )(spans, parts, bias_own)
    heads = lax.all_gather(head, "c", axis=0, tiled=False)
    message = pl.pallas_call(
        blend,
        out_shape=jax.ShapeDtypeStruct((L, 8, 2 * E), BF),
        in_specs=[SMEM, VMEM, VMEM],
        out_specs=VMEM,
        scratch_shapes=[pltpu.VMEM((L, 8, 2 * E), F32)],
        compiler_params=params(),
    )(y1, heads, values)
    came = lax.all_to_all(message.reshape(64, 16, 128), CHIPS, 0, 0, tiled=True)
    blended = lax.all_gather(came, "c", axis=0, tiled=False)

    alignment, pair_out = pl.pallas_call(
        column_block,
        out_shape=(jax.ShapeDtypeStruct((R, D), BF), jax.ShapeDtypeStruct((L, 128), BF)),
        in_specs=[SMEM] + [VMEM] * 5,
        out_specs=(VMEM, VMEM),
        scratch_shapes=[
            pltpu.VMEM((2048, L), F32),
            pltpu.VMEM((D, L), F32),
            pltpu.VMEM((3 * D, L), F32),
            pltpu.VMEM((D, L), BF),
        ],
        compiler_params=params(),
    )(c1, blended, stack_own, gathered, pair_own, contact_w)
    return alignment.reshape(R, 1, D), pair_out.reshape(1, L, 128)


def solution(mesh):
    torus = Mesh(mesh.devices.reshape(mesh.shape["aln"], 8, 8, 2), ALL)
    in_specs = (
        P(ALL, None, None),
        P("a"),
        P(ALL, None, None),
        P(None, ROWS),
        P(None, ROWS),
        P(None, ROWS),
        P(None, ROWS),
        P(),
        P(),
    )
    out_specs = (P("a", ROWS, None), P(ALL, None, None))
    return jax.shard_map(
        per_device, mesh=torus, in_specs=in_specs, out_specs=out_specs, check_vma=False
    )
```

time: 266 us -> 162 us (0.61)
  waiting for transfers between devices: 117 us -> 36.7 us
  local copies, waits for them, and re-layouts: 32.6 us -> 5.16 us
  Pallas kernels: 0 us -> 15.7 us
  blocking collectives: 35.7 us -> 22.7 us
  starting transfers between devices: 47.5 us -> 59.6 us
  matrix products: 10.9 us -> 3 us
  other arithmetic: 6.12 us -> 3.02 us
    all_gather x2 -> x1, waiting for transfers between devices: 57.5 us -> 0.01 us  [per_device(): gathered = lax.all_gather(column_weights, ROWS, axis=0, tiled=False)]
    all_to_all x3 -> x0, blocking collectives: 35.7 us -> none  [the longest x1 23.4 us: summed_rows(): return jnp.sum(lax.all_to_all(own, far, 0, 0, tiled=True), axis=0)]
    all_to_all x6 -> x4, waiting for transfers between devices: 58 us -> 30.6 us  [the longest x1 12.1 us: per_device(): came = lax.all_to_all(message.reshape(64, 16, 128), CHIPS, 0, 0, tiled=True)]
    ppermute x0 -> x8, starting transfers between devices: none -> 26.8 us  [the longest x3 12 us: ring_rows(): from_right.append(lax.ppermute(from_right[-1], 'y', left))]
    all_gather x0 -> x6, blocking collectives: none -> 22.7 us  [the longest x1 6.01 us: per_device(): picked = lax.all_gather(picked, 'c', axis=0, tiled=False)]
    pallas_call x0 -> x4, Pallas kernels: none -> 15.7 us  [the longest x1 12.1 us: per_device(): pl.pallas_call(column_block, out_shape=(jax.ShapeDtypeStruct((R, D), BF),...]
    unnamed x27 -> x16, local copies, waits for them, and re-layouts: 15.4 us -> 0.15 us
    all_to_all x6 -> x4, starting transfers between devices: 47.4 us -> 32.8 us  [the longest x1 17.1 us: per_device(): came = lax.all_to_all(message, CHIPS, 0, 0, tiled=True)]
  transfers between devices with their start and end apart: 8 -> 13, of which waited for: 6 -> 6; matrix products, arithmetic and copies ran while one was open for 14% -> 6% of each run, Pallas kernels for 0% -> 2%
where the time goes in v1:
time: 162 us; the launch traced here: 161 us
  starting transfers between devices  59.6 us (37%)
  waiting for transfers between devices  36.7 us (23%)
  blocking collectives  22.7 us (14%)
  Pallas kernels  15.7 us (10%)
  between operations  15.1 us (9%)
  local copies, waits for them, and re-layouts  5.16 us (3%)
  other arithmetic  3.02 us (2%)
  matrix products  3 us (2%)
    all_to_all x1, starting transfers between devices, per_device(): came = lax.all_to_all(message, CHIPS, 0, 0, tiled=True)  17.1 us
    pallas_call x1, Pallas kernels, per_device(): pl.pallas_call(column_block, out_shape=(jax.ShapeDtypeStruct((R, D), BF),...  12.1 us
    all_to_all x1, waiting for transfers between devices, per_device(): came = lax.all_to_all(message.reshape(64, 16, 128), CHIPS, 0, 0, tiled=True)  12.1 us
    ppermute x3, starting transfers between devices, ring_rows(): from_right.append(lax.ppermute(from_right[-1], 'y', left))  12 us
    all_to_all x1, waiting for transfers between devices, per_device(): came = lax.all_to_all(message, CHIPS, 0, 0, tiled=True)  10.2 us
    all_to_all x1, waiting for transfers between devices, per_device(): lax.all_to_all(jnp.broadcast_to(tied, (8, L, L)), 'z', 0, 0, tiled=True)  8.28 us
    ppermute x3, starting transfers between devices, ring_rows(): from_left.append(lax.ppermute(from_left[-1], 'y', right))  7.45 us
    all_to_all x1, starting transfers between devices, per_device(): came = lax.all_to_all(message.reshape(64, 16, 128), CHIPS, 0, 0, tiled=True)  6.32 us
  transfers between devices with their start and end apart: 13, of which 6 were waited for; matrix products, arithmetic and copies ran while one was open for 6% of the time, Pallas kernels for 2%

profile of v1, /device:TPU:1, one launch (start us, length us, event | category | flops | bytes accessed | tf_op | source)
XLA Modules:
  0.0 161.0 jit_solution(6732928596836701570)
XLA Ops:
  7.2 0.0 copy-start
  7.2 0.0 copy-start.3
  7.2 0.0 all-gather.9.cloned.1.call-start
  7.2 0.1 pad.8.clone
  7.3 1.5 maximum_maximum_fusion
  8.8 0.0 all-gather.9.cloned.1.call-update
  8.8 0.9 reshape.66
  9.7 0.1 copy.27
  9.8 0.1 reshape.67
  10.0 1.1 reshape_reshape.3
  11.1 0.0 copy-done
  11.1 0.9 convolution_convert_fusion
  12.1 0.1 broadcast_in_dim.33
  12.2 1.0 pad_maximum_fusion
  13.2 17.1 %all-to-all-start = ((bf16[64,32,128]{2,1,0:T(8,128)(2,1)}), bf16[64,32,128]{2,1,0:T(8,128)(2,1)S(1)}, u32[]{:S(2)}, u32[]{:S(2)}) async-start(bf16[64,32,128]{2,1,0:T(8,128)(2,1)} %pad_maximum_fusion), calls=%async_computation | async-start | bytes 1048576 | tf_op jit(solution)/shard_map/all_to_all | solution.py:211
  30.3 0.0 copy-done.3
  30.3 0.1 convert_reduce_fusion
  30.5 0.2 fusion.24
  30.7 0.1 fusion.25.refs_0_
  30.8 2.9 %collective-permute-start = (bf16[128,768]{1,0:T(8,128)(2,1)S(1)}, bf16[128,768]{1,0:T(8,128)(2,1)S(1)}, u32[]{:S(2)}, u32[]{:S(2)}) collective-permute-start(bf16[128,768]{1,0:T(8,128)(2,1)S(1)} %fusion.25.refs_0_), channel_id=1, source_target_pairs={{0,2},{2,4},{4,6},{6,8},{8,10},{10,12},{12,14},{14,0},{1,3},{3,5},... | collective-permute-start | bytes 589832 | tf_op jit(solution)/shard_map/ppermute | solution.py:178
  33.8 3.6 %collective-permute-start.1 = (bf16[128,768]{1,0:T(8,128)(2,1)S(1)}, bf16[128,768]{1,0:T(8,128)(2,1)S(1)}, u32[]{:S(2)}, u32[]{:S(2)}) collective-permute-start(bf16[128,768]{1,0:T(8,128)(2,1)S(1)} %fusion.25.refs_0_), channel_id=1, source_target_pairs={{0,14},{2,0},{4,2},{6,4},{8,6},{10,8},{12,10},{14,12},{1,15},{3,1}... | collective-permute-start | bytes 589832 | tf_op jit(solution)/shard_map/ppermute | solution.py:179
  37.4 10.2 %all-to-all-done = bf16[64,32,128]{2,1,0:T(8,128)(2,1)S(1)} async-done(((bf16[64,32,128]{2,1,0:T(8,128)(2,1)}), bf16[64,32,128]{2,1,0:T(8,128)(2,1)S(1)}, u32[]{:S(2)}, u32[]{:S(2)}) %all-to-all-start) | async-done | bytes 524320 | tf_op jit(solution)/shard_map/all_to_all | solution.py:211
  47.7 2.1 %fusion.2 = bf16[128,384]{1,0:T(8,128)(2,1)S(1)} fusion(bf16[2048,128]{1,0:T(8,128)(2,1)S(1)} %bitcast.95, s32[384]{0:T(512)S(1)} %get-tuple-element.19, s32[384]{0:T(512)S(1)} %get-tuple-element.20, s32[]{:T(128)S(6)} %mul.34, s32[384]{0:T(512)S(1)} %get-tuple-element.18, s32[384]{0:T(512)S(1)} %get-tuple-element.21, s32[2048]{0:T(1024)S(1)} %get-tuple-element.13, ...), kind=kOutput, calls=%fused_computation.4 | convolution fusion | flops 212336640 | bytes 666376 | tf_op jit(solution)/shard_map/dot_general | solution.py:29
  49.8 6.0 %all-gather = bf16[192,384]{1,0:T(8,128)(2,1)S(1)} all-gather(bf16[96,384]{1,0:T(8,128)(2,1)S(1)} %slice.114), channel_id=2, replica_groups=mesh['a'=4,'z'=8,'y'=8,'c'=2] {'c'}, dimensions={0}, use_global_device_ids=true | all-gather | bytes 221184 | tf_op jit(solution)/shard_map/all_gather | solution.py:219
  55.8 0.7 broadcast_in_dim.35
  56.6 3.6 %all-to-all-start.1 = ((bf16[8,48,384]{2,1,0:T(8,128)(2,1)}), bf16[8,48,384]{2,1,0:T(8,128)(2,1)S(1)}, u32[]{:S(2)}, u32[]{:S(2)}) async-start(bf16[8,48,384]{2,1,0:T(8,128)(2,1)} %broadcast_in_dim.35), calls=%async_computation.1 | async-start | bytes 589824 | tf_op jit(solution)/shard_map/all_to_all | solution.py:222
  60.1 0.0 collective-permute-done.refs_1_
  60.1 2.6 %collective-permute-start.2 = (bf16[128,768]{1,0:T(8,128)(2,1)S(1)}, bf16[128,768]{1,0:T(8,128)(2,1)S(1)}, u32[]{:S(2)}, u32[]{:S(2)}) collective-permute-start(bf16[128,768]{1,0:T(8,128)(2,1)S(1)} %collective-permute-done.refs_1_), channel_id=1, source_target_pairs={{0,2},{2,4},{4,6},{6,8},{8,10},{10,12},{12,14},{14,0},{1,3},{3,5},... | collective-permute-start | bytes 589832 | tf_op jit(solution)/shard_map/ppermute | solution.py:178
  62.8 0.0 collective-permute-done.1.refs_2_
  62.8 3.9 %collective-permute-start.3 = (bf16[128,768]{1,0:T(8,128)(2,1)S(1)}, bf16[128,768]{1,0:T(8,128)(2,1)S(1)}, u32[]{:S(2)}, u32[]{:S(2)}) collective-permute-start(bf16[128,768]{1,0:T(8,128)(2,1)S(1)} %collective-permute-done.1.refs_2_), channel_id=1, source_target_pairs={{0,14},{2,0},{4,2},{6,4},{8,6},{10,8},{12,10},{14,12},{1,15},{3,1}... | collective-permute-start | bytes 589832 | tf_op jit(solution)/shard_map/ppermute | solution.py:179
  66.7 2.4 %collective-permute-done.2.refs_3_ = bf16[128,768]{1,0:T(8,128)(2,1)S(1)} collective-permute-done((bf16[128,768]{1,0:T(8,128)(2,1)S(1)}, bf16[128,768]{1,0:T(8,128)(2,1)S(1)}, u32[]{:S(2)}, u32[]{:S(2)}) %collective-permute-start.2) | collective-permute-done | bytes 196640 | tf_op jit(solution)/shard_map/ppermute | solution.py:178
  69.1 1.9 %collective-permute-start.4 = (bf16[128,768]{1,0:T(8,128)(2,1)S(1)}, bf16[128,768]{1,0:T(8,128)(2,1)S(1)}, u32[]{:S(2)}, u32[]{:S(2)}) collective-permute-start(bf16[128,768]{1,0:T(8,128)(2,1)S(1)} %collective-permute-done.2.refs_3_), channel_id=1, source_target_pairs={{0,2},{2,4},{4,6},{6,8},{8,10},{10,12},{12,14},{14,0},{1,3},{3,5},... | collective-permute-start | bytes 589832 | tf_op jit(solution)/shard_map/ppermute | solution.py:178
  71.0 0.0 collective-permute-done.3.refs_4_
  71.0 4.6 %collective-permute-start.5 = (bf16[128,768]{1,0:T(8,128)(2,1)S(1)}, bf16[128,768]{1,0:T(8,128)(2,1)S(1)}, u32[]{:S(2)}, u32[]{:S(2)}) collective-permute-start(bf16[128,768]{1,0:T(8,128)(2,1)S(1)} %collective-permute-done.3.refs_4_), channel_id=1, source_target_pairs={{0,14},{2,0},{4,2},{6,4},{8,6},{10,8},{12,10},{14,12},{1,15},{3,1}... | collective-permute-start | bytes 589832 | tf_op jit(solution)/shard_map/ppermute | solution.py:179
  75.6 1.5 collective-permute-done.4.refs_5_
  77.1 1.9 %collective-permute-start.6 = (bf16[64,768]{1,0:T(8,128)(2,1)S(1)}, bf16[64,768]{1,0:T(8,128)(2,1)S(1)}, u32[]{:S(2)}, u32[]{:S(2)}) collective-permute-start(bf16[64,768]{1,0:T(8,128)(2,1)S(1)} %slice.84), channel_id=1, source_target_pairs={{0,2},{2,4},{4,6},{6,8},{8,10},{10,12},{12,14},{14,0},{1,3},{3,5},... | collective-permute-start | bytes 294920 | tf_op jit(solution)/shard_map/ppermute | solution.py:181
  79.0 2.2 %collective-permute-done.5.refs_6_ = bf16[128,768]{1,0:T(8,128)(2,1)S(1)} collective-permute-done((bf16[128,768]{1,0:T(8,128)(2,1)S(1)}, bf16[128,768]{1,0:T(8,128)(2,1)S(1)}, u32[]{:S(2)}, u32[]{:S(2)}) %collective-permute-start.5) | collective-permute-done | bytes 196640 | tf_op jit(solution)/shard_map/ppermute | solution.py:179
  81.2 5.4 %collective-permute-start.7 = (bf16[64,768]{1,0:T(8,128)(2,1)S(1)}, bf16[64,768]{1,0:T(8,128)(2,1)S(1)}, u32[]{:S(2)}, u32[]{:S(2)}) collective-permute-start(bf16[64,768]{1,0:T(8,128)(2,1)S(1)} %slice.85), channel_id=1, source_target_pairs={{0,14},{2,0},{4,2},{6,4},{8,6},{10,8},{12,10},{14,12},{1,15},{3,1}... | collective-permute-start | bytes 294920 | tf_op jit(solution)/shard_map/ppermute | solution.py:182
  86.7 0.0 all-to-all-done.1
  86.7 4.0 %all-gather.1 = bf16[16,48,384]{2,1,0:T(8,128)(2,1)S(1)} all-gather(bf16[8,48,384]{2,1,0:T(8,128)(2,1)S(1)} %all-to-all-done.1), channel_id=3, replica_groups=mesh['a'=4,'z'=8,'y'=8,'c'=2] {'c'}, dimensions={0}, use_global_device_ids=true | all-gather | bytes 884736 | tf_op jit(solution)/shard_map/all_gather | solution.py:223
  90.7 0.0 collective-permute-done.6.refs_7_
  90.7 0.0 collective-permute-done.7.refs_8_
  90.7 2.1 %shard_map.104 = (f32[2,128,128]{2,1,0:T(8,128)S(1)}, bf16[8,128,128]{2,1,0:T(8,128)(2,1)S(1)}) custom-call(s32[1]{0:T(128)} %bitcast.1.y_ref, bf16[768,384]{1,0:T(8,128)(2,1)S(1)} %bitcast.85, bf16[128,768]{1,0:T(8,128)(2,1)S(1)} %fusion.25.refs_0_, bf16[128,768]{1,0:T(8,128)(2,1)S(1)} %collective-permute-done.refs_1_, ...), custom_call_target="tpu_custom_call" | custom-call | tf_op jit(solution)/shard_map/pallas_call | solution.py:231
  92.8 3.2 %all-gather.2 = f32[4,128,128]{2,1,0:T(8,128)S(1)} all-gather(f32[2,128,128]{2,1,0:T(8,128)S(1)} %get-tuple-element.6), channel_id=4, replica_groups=mesh['a'=4,'z'=8,'y'=8,'c'=2] {'c'}, dimensions={0}, use_global_device_ids=true | all-gather | bytes 393216 | tf_op jit(solution)/shard_map/all_gather | solution.py:242
  96.1 0.7 broadcast_in_dim.36
  96.8 5.7 %all-to-all-start.2 = ((bf16[8,128,128]{2,1,0:T(8,128)(2,1)}), bf16[8,128,128]{2,1,0:T(8,128)(2,1)S(1)}, u32[]{:S(2)}, u32[]{:S(2)}) async-start(bf16[8,128,128]{2,1,0:T(8,128)(2,1)} %broadcast_in_dim.36), calls=%async_computation.2 | async-start | bytes 524288 | tf_op jit(solution)/shard_map/all_to_all | solution.py:245
  103.2 0.1 slice.86
  103.3 0.1 copy.22
  103.4 2.4 %all-gather.3 = bf16[128,14,128]{2,0,1:T(8,128)(2,1)S(1)} all-gather(bf16[64,14,128]{2,0,1:T(8,128)(2,1)S(1)} %copy.22), channel_id=5, replica_groups=mesh['a'=4,'z'=8,'y'=8,'c'=2] {'c'}, dimensions={0}, use_global_device_ids=true | all-gather | bytes 688128 | tf_op jit(solution)/shard_map/all_gather | solution.py:225
  105.9 8.3 %all-to-all-done.2.part_ref = bf16[8,128,128]{2,1,0:T(8,128)(2,1)S(1)} async-done(((bf16[8,128,128]{2,1,0:T(8,128)(2,1)}), bf16[8,128,128]{2,1,0:T(8,128)(2,1)S(1)}, u32[]{:S(2)}, u32[]{:S(2)}) %all-to-all-start.2) | async-done | bytes 262176 | tf_op jit(solution)/shard_map/all_to_all | solution.py:245
  114.2 0.2 shard_map.105
  114.4 0.0 copy-start.1
  114.4 0.0 copy-start.2
  114.4 2.2 %all-gather.4 = bf16[4,128,128]{2,1,0:T(8,128)(2,1)S(1)} all-gather(bf16[2,128,128]{2,1,0:T(8,128)(2,1)S(1)} %shard_map.105), channel_id=6, replica_groups=mesh['a'=4,'z'=8,'y'=8,'c'=2] {'c'}, dimensions={0}, use_global_device_ids=true | all-gather | bytes 196608 | tf_op jit(solution)/shard_map/all_gather | solution.py:253
  116.6 1.2 shard_map.106
  117.9 6.3 %all-to-all-start.3 = ((bf16[64,16,128]{2,1,0:T(8,128)(2,1)}), bf16[64,16,128]{2,1,0:T(8,128)(2,1)S(1)}, u32[]{:S(2)}, u32[]{:S(2)}) async-start(bf16[64,16,128]{2,1,0:T(8,128)(2,1)} %bitcast.28), calls=%async_computation.3 | async-start | bytes 524288 | tf_op jit(solution)/shard_map/all_to_all | solution.py:262
  124.2 0.3 copy.24
  124.5 0.2 reshape.75
  124.7 0.4 constant_dynamic-slice_fusion
  125.2 12.1 %all-to-all-done.3 = bf16[64,16,128]{2,1,0:T(8,128)(2,1)S(1)} async-done(((bf16[64,16,128]{2,1,0:T(8,128)(2,1)}), bf16[64,16,128]{2,1,0:T(8,128)(2,1)S(1)}, u32[]{:S(2)}, u32[]{:S(2)}) %all-to-all-start.3) | async-done | bytes 262176 | tf_op jit(solution)/shard_map/all_to_all | solution.py:262
  137.3 4.7 %all-gather.5 = bf16[128,16,128]{2,1,0:T(8,128)(2,1)S(1)} all-gather(bf16[64,16,128]{2,1,0:T(8,128)(2,1)S(1)} %all-to-all-done.3), channel_id=7, replica_groups=mesh['a'=4,'z'=8,'y'=8,'c'=2] {'c'}, dimensions={0}, use_global_device_ids=true | all-gather | bytes 786432 | tf_op jit(solution)/shard_map/all_gather | solution.py:263
  142.1 0.0 copy-done.1
  142.1 0.0 copy-done.2
  142.1 12.1 %shard_map.107 = (bf16[128,768]{1,0:T(8,128)(2,1)}, bf16[128,128]{1,0:T(8,128)(2,1)}) custom-call(s32[1]{0:T(128)} %bitcast.c_ref, bf16[2,64,16,128]{3,2,1,0:T(8,128)(2,1)S(1)} %bitcast.86, bf16[128,768]{1,0:T(8,128)(2,1)S(1)} %bitcast.87, bf16[128,32,768]{2,1,0:T(8,128)(2,1)} %bitcast.91, bf16[128,128]{1,0:T(8,128)(2,1)S(1)} %bitcast.89, ...), custom_call_target="tpu_custom_call" | custom-call | tf_op jit(solution)/shard_map/pallas_call | solution.py:265
  (31 shorter events, 0.3 us)
Async XLA Ops:
  7.2 3.9 %copy-start = (bf16[128,12]{0,1:T(8,128)(2,1)S(1)}, bf16[128,12]{0,1:T(8,128)(2,1)}, u32[]{:S(2)}) copy-start(bf16[128,12]{0,1:T(8,128)(2,1)} %param.16) | copy-start | bytes 9220
  7.2 23.2 %copy-start.3 = (bf16[1,128,768]{2,1,0:T(8,128)(2,1)S(1)}, bf16[1,128,768]{2,1,0:T(8,128)(2,1)}, u32[]{:S(2)}) copy-start(bf16[1,128,768]{2,1,0:T(8,128)(2,1)} %param.9) | copy-start | bytes 589828
  7.2 134.9 %all-gather.9.cloned.1.call-start = ((), (), s32[]{:S(2)}) async-start(), calls=%async_computation.4 | async-start | bytes 6340608 | tf_op jit(solution)/shard_map/all_gather | solution.py:194
  13.2 34.5 %all-to-all-start = ((bf16[64,32,128]{2,1,0:T(8,128)(2,1)}), bf16[64,32,128]{2,1,0:T(8,128)(2,1)S(1)}, u32[]{:S(2)}, u32[]{:S(2)}) async-start(bf16[64,32,128]{2,1,0:T(8,128)(2,1)} %pad_maximum_fusion), calls=%async_computation | async-start | bytes 1048576 | tf_op jit(solution)/shard_map/all_to_all | solution.py:211
  30.8 29.3 %collective-permute-start = (bf16[128,768]{1,0:T(8,128)(2,1)S(1)}, bf16[128,768]{1,0:T(8,128)(2,1)S(1)}, u32[]{:S(2)}, u32[]{:S(2)}) collective-permute-start(bf16[128,768]{1,0:T(8,128)(2,1)S(1)} %fusion.25.refs_0_), channel_id=1, source_target_pairs={{0,2},{2,4},{4,6},{6,8},{8,10},{10,12},{12,14},{14,0},{1,3},{3,5},... | collective-permute-start | bytes 589832 | tf_op jit(solution)/shard_map/ppermute | solution.py:178
  33.8 29.0 %collective-permute-start.1 = (bf16[128,768]{1,0:T(8,128)(2,1)S(1)}, bf16[128,768]{1,0:T(8,128)(2,1)S(1)}, u32[]{:S(2)}, u32[]{:S(2)}) collective-permute-start(bf16[128,768]{1,0:T(8,128)(2,1)S(1)} %fusion.25.refs_0_), channel_id=1, source_target_pairs={{0,14},{2,0},{4,2},{6,4},{8,6},{10,8},{12,10},{14,12},{1,15},{3,1}... | collective-permute-start | bytes 589832 | tf_op jit(solution)/shard_map/ppermute | solution.py:179
  56.6 30.1 %all-to-all-start.1 = ((bf16[8,48,384]{2,1,0:T(8,128)(2,1)}), bf16[8,48,384]{2,1,0:T(8,128)(2,1)S(1)}, u32[]{:S(2)}, u32[]{:S(2)}) async-start(bf16[8,48,384]{2,1,0:T(8,128)(2,1)} %broadcast_in_dim.35), calls=%async_computation.1 | async-start | bytes 589824 | tf_op jit(solution)/shard_map/all_to_all | solution.py:222
  60.1 8.9 %collective-permute-start.2 = (bf16[128,768]{1,0:T(8,128)(2,1)S(1)}, bf16[128,768]{1,0:T(8,128)(2,1)S(1)}, u32[]{:S(2)}, u32[]{:S(2)}) collective-permute-start(bf16[128,768]{1,0:T(8,128)(2,1)S(1)} %collective-permute-done.refs_1_), channel_id=1, source_target_pairs={{0,2},{2,4},{4,6},{6,8},{8,10},{10,12},{12,14},{14,0},{1,3},{3,5},... | collective-permute-start | bytes 589832 | tf_op jit(solution)/shard_map/ppermute | solution.py:178
  62.8 8.2 %collective-permute-start.3 = (bf16[128,768]{1,0:T(8,128)(2,1)S(1)}, bf16[128,768]{1,0:T(8,128)(2,1)S(1)}, u32[]{:S(2)}, u32[]{:S(2)}) collective-permute-start(bf16[128,768]{1,0:T(8,128)(2,1)S(1)} %collective-permute-done.1.refs_2_), channel_id=1, source_target_pairs={{0,14},{2,0},{4,2},{6,4},{8,6},{10,8},{12,10},{14,12},{1,15},{3,1}... | collective-permute-start | bytes 589832 | tf_op jit(solution)/shard_map/ppermute | solution.py:179
  69.1 8.0 %collective-permute-start.4 = (bf16[128,768]{1,0:T(8,128)(2,1)S(1)}, bf16[128,768]{1,0:T(8,128)(2,1)S(1)}, u32[]{:S(2)}, u32[]{:S(2)}) collective-permute-start(bf16[128,768]{1,0:T(8,128)(2,1)S(1)} %collective-permute-done.2.refs_3_), channel_id=1, source_target_pairs={{0,2},{2,4},{4,6},{6,8},{8,10},{10,12},{12,14},{14,0},{1,3},{3,5},... | collective-permute-start | bytes 589832 | tf_op jit(solution)/shard_map/ppermute | solution.py:178
  71.0 10.2 %collective-permute-start.5 = (bf16[128,768]{1,0:T(8,128)(2,1)S(1)}, bf16[128,768]{1,0:T(8,128)(2,1)S(1)}, u32[]{:S(2)}, u32[]{:S(2)}) collective-permute-start(bf16[128,768]{1,0:T(8,128)(2,1)S(1)} %collective-permute-done.3.refs_4_), channel_id=1, source_target_pairs={{0,14},{2,0},{4,2},{6,4},{8,6},{10,8},{12,10},{14,12},{1,15},{3,1}... | collective-permute-start | bytes 589832 | tf_op jit(solution)/shard_map/ppermute | solution.py:179
  77.1 13.6 %collective-permute-start.6 = (bf16[64,768]{1,0:T(8,128)(2,1)S(1)}, bf16[64,768]{1,0:T(8,128)(2,1)S(1)}, u32[]{:S(2)}, u32[]{:S(2)}) collective-permute-start(bf16[64,768]{1,0:T(8,128)(2,1)S(1)} %slice.84), channel_id=1, source_target_pairs={{0,2},{2,4},{4,6},{6,8},{8,10},{10,12},{12,14},{14,0},{1,3},{3,5},... | collective-permute-start | bytes 294920 | tf_op jit(solution)/shard_map/ppermute | solution.py:181
  81.2 9.5 %collective-permute-start.7 = (bf16[64,768]{1,0:T(8,128)(2,1)S(1)}, bf16[64,768]{1,0:T(8,128)(2,1)S(1)}, u32[]{:S(2)}, u32[]{:S(2)}) collective-permute-start(bf16[64,768]{1,0:T(8,128)(2,1)S(1)} %slice.85), channel_id=1, source_target_pairs={{0,14},{2,0},{4,2},{6,4},{8,6},{10,8},{12,10},{14,12},{1,15},{3,1}... | collective-permute-start | bytes 294920 | tf_op jit(solution)/shard_map/ppermute | solution.py:182
  96.8 17.3 %all-to-all-start.2 = ((bf16[8,128,128]{2,1,0:T(8,128)(2,1)}), bf16[8,128,128]{2,1,0:T(8,128)(2,1)S(1)}, u32[]{:S(2)}, u32[]{:S(2)}) async-start(bf16[8,128,128]{2,1,0:T(8,128)(2,1)} %broadcast_in_dim.36), calls=%async_computation.2 | async-start | bytes 524288 | tf_op jit(solution)/shard_map/all_to_all | solution.py:245
  114.4 27.7 %copy-start.1 = (bf16[1,128,128]{2,1,0:T(8,128)(2,1)S(1)}, bf16[1,128,128]{2,1,0:T(8,128)(2,1)}, u32[]{:S(2)}) copy-start(bf16[1,128,128]{2,1,0:T(8,128)(2,1)} %param.11) | copy-start | bytes 98308
  114.4 27.7 %copy-start.2 = (bf16[12,128]{1,0:T(8,128)(2,1)S(1)}, bf16[12,128]{1,0:T(8,128)(2,1)}, u32[]{:S(2)}) copy-start(bf16[12,128]{1,0:T(8,128)(2,1)} %cw_ref.1) | copy-start | bytes 9220
  117.9 19.4 %all-to-all-start.3 = ((bf16[64,16,128]{2,1,0:T(8,128)(2,1)}), bf16[64,16,128]{2,1,0:T(8,128)(2,1)S(1)}, u32[]{:S(2)}, u32[]{:S(2)}) async-start(bf16[64,16,128]{2,1,0:T(8,128)(2,1)} %bitcast.28), calls=%async_computation.3 | async-start | bytes 524288 | tf_op jit(solution)/shard_map/all_to_all | solution.py:262
Sparse Core Ops, SparseCore 0:
  11.7 98.2 all-gather.8

commit v2 on v1

--- a/solution.py
+++ b/solution.py
@@ -40,16 +40,18 @@
 
 
 def project_and_tie(y_ref, w_ref, *refs):
-    row_refs, (tied_ref, v_ref) = refs[:9], refs[9:]
+    row_refs, (left_ref, right_ref, tied_ref, v_ref) = refs[:5], refs[5:]
     w = w_ref[...]
     lane = lax.broadcasted_iota(jnp.int32, (L, 2 * E), 1)
     offsets = (0, -1, 1, -2, 2, -3, 3, 4)
     tied = [jnp.zeros((L, L), F32), jnp.zeros((L, L), F32)]
     for n, offset in enumerate(offsets):
-        if n < 7:
+        if n < 5:
             x = row_refs[n][...]
+        elif n < 7:
+            x = refs[n][:L]
         else:
-            x = jnp.concatenate([row_refs[7][...], row_refs[8][...]], axis=0)
+            x = jnp.concatenate([left_ref[L:], right_ref[L:]], axis=0)
         packed = jnp.dot(x, w, preferred_element_type=F32)
         q = packed[:, : 2 * E] * E**-0.5
         k = packed[:, 2 * E : 4 * E].astype(BF)
@@ -95,9 +97,7 @@
     out_ref[...] = held[...].astype(BF)
 
 
-def column_block(
-    c_ref, bl_ref, stack_ref, g_ref, pair_ref, cw_ref, out_ref, pair_out_ref, tall, feat, packed, mixed
-):
+def column_block(c_ref, bl_ref, stack_ref, who_ref, wv_ref, wvo_ref, pair_ref, cw_ref, out_ref, pair_out_ref):
     mine = c_ref[0]
     lane = lax.broadcasted_iota(jnp.int32, (L, L), 1)
     row = lax.broadcasted_iota(jnp.int32, (L, L), 0)
@@ -119,40 +119,26 @@
         parts.append(jnp.where(jnp.logical_and(low, early), re1, o1))
     blended = jnp.concatenate(parts, axis=1).astype(BF)
 
-    tail = g_ref[:, 16:32, :].reshape(2048, D)
-    tall[...] = dot_nt(tail, blended)
-    for d in range(128):
-        feat[6 * d : 6 * d + 6, :] = tall[16 * d + 8 : 16 * d + 14, :]
-    for n in range(6):
-        own = jnp.concatenate([stack_ref[:, 128 * n : 128 * n + 128]], axis=1).astype(F32).T
-        feat[128 * n : 128 * n + 128, :] += own
-    updated = feat[...].astype(BF).astype(F32)
-    feat[...] = updated
+    updated = (dot_nt(who_ref[...], blended) + stack_ref[...].astype(F32)).astype(BF).astype(F32)
     center = jnp.mean(updated, axis=0, keepdims=True)
     spread = jnp.mean(jnp.square(updated - center), axis=0, keepdims=True)
     normed = ((updated - center) * lax.rsqrt(spread + 1e-05)).astype(BF)
-
-    tall[...] = jnp.dot(g_ref[:, 0:16, :].reshape(2048, D), normed, preferred_element_type=F32)
-    for d in range(128):
-        packed[18 * d : 18 * d + 16, :] = tall[16 * d : 16 * d + 16, :]
-    tall[...] = jnp.dot(tail, normed, preferred_element_type=F32)
-    for d in range(128):
-        packed[18 * d + 16 : 18 * d + 18, :] = tall[16 * d : 16 * d + 2, :]
-
+    packed = jnp.dot(wv_ref[...], normed, preferred_element_type=F32)
+
+    mixed = []
     for h in range(H):
-        q = (packed[E * h : E * h + E, :] * E**-0.5).astype(BF)
-        k = packed[D + E * h : D + E * h + E, :].astype(BF)
-        v = packed[2 * D + E * h : 2 * D + E * h + E, :].astype(BF)
+        q = (packed[E * h : E * h + E] * E**-0.5).astype(BF)
+        k = packed[D + E * h : D + E * h + E].astype(BF)
+        v = packed[2 * D + E * h : 2 * D + E * h + E].astype(BF)
         logits = dot_tn(k, q)
         e = jnp.exp(logits - jnp.max(logits, axis=0, keepdims=True))
         probs = (e / jnp.sum(e, axis=0, keepdims=True)).astype(BF)
-        mixed[E * h : E * h + E, :] = jnp.dot(v, probs, preferred_element_type=F32).astype(BF)
-
-    tall[...] = jnp.dot(tail, mixed[...], preferred_element_type=F32)
-    for d in range(128):
-        feat[6 * d : 6 * d + 6, :] += tall[16 * d + 2 : 16 * d + 8, :]
+        mixed.append(jnp.dot(v, probs, preferred_element_type=F32).astype(BF))
+    mixed = jnp.concatenate(mixed, axis=0)
+
+    result = (updated + jnp.dot(wvo_ref[...], mixed, preferred_element_type=F32)).astype(BF)
     place = (lax.rem(row, 2) * E + row // 2 == lane).astype(BF)
-    out_ref[...] = dot_nt(place, feat[...].astype(BF)).astype(BF)
+    out_ref[...] = dot_nt(place, result).astype(BF)
 
     one = lax.broadcasted_iota(jnp.int32, (1, L), 1) < E
     lines = []
@@ -170,18 +156,8 @@
     pair_out_ref[...] = pair.astype(BF)
 
 
-def ring_rows(x):
-    right = [(i, (i + 1) % 8) for i in range(8)]
-    left = [(i, (i + 7) % 8) for i in range(8)]
-    from_left, from_right = [x], [x]
-    for step in range(3):
-        from_left.append(lax.ppermute(from_left[-1], "y", right))
-        from_right.append(lax.ppermute(from_right[-1], "y", left))
-    far = [
-        lax.ppermute(from_left[-1][: L // 2], "y", right),
-        lax.ppermute(from_right[-1][L // 2 :], "y", left),
-    ]
-    return [x] + [t[n] for n in (1, 2, 3) for t in (from_left, from_right)] + far
+def moved(x, step):
+    return lax.ppermute(x, "y", [(i, (i + step) % 8) for i in range(8)])
 
 
 def per_device(stack, spans, pair, w_triple, w_out, v_triple, v_out, offsets, contact_w):
@@ -194,7 +170,7 @@
     gathered = lax.all_gather(column_weights, ROWS, axis=0, tiled=False)
 
     normed = normalize(own_row.astype(F32)).astype(BF)
-    rows = ring_rows(normed)
+    near = [moved(normed, step) for step in (1, -1, 2, -2)]
 
     bias = lax.dot_general(offsets, pair_own, (((0,), (1,)), ((), ())), preferred_element_type=F32).astype(BF)
     bias_pairs = jnp.stack([bias[first_head(n) : first_head(n) + 2] for n in range(8)])
@@ -209,6 +185,11 @@
         axis=1,
     )
     came = lax.all_to_all(message, CHIPS, 0, 0, tiled=True)
+    far = [
+        moved(jnp.concatenate([near[0], near[2][: L // 2]]), 2),
+        moved(jnp.concatenate([near[1], near[3][L // 2 :]]), -2),
+    ]
+    came, *near = lax.optimization_barrier((came, *near))
 
     source = lax.broadcasted_iota(jnp.int32, (2048, 384), 0)
     target = lax.broadcasted_iota(jnp.int32, (2048, 384), 1)
@@ -234,10 +215,10 @@
             jax.ShapeDtypeStruct((2, L, L), F32),
             jax.ShapeDtypeStruct((8, L, 2 * E), BF),
         ),
-        in_specs=[SMEM] + [VMEM] * 10,
+        in_specs=[SMEM] + [VMEM] * 8,
         out_specs=(VMEM, VMEM),
         compiler_params=params(),
-    )(y1, w_heads, *rows)
+    )(y1, w_heads, normed, *near, *far)
 
     tied = lax.all_gather(tied, "c", axis=0, tiled=False)
     tied = lax.dynamic_index_in_dim(tied, c, 1, keepdims=False)
@@ -260,21 +241,21 @@
         compiler_params=params(),
     )(y1, heads, values)
     came = lax.all_to_all(message.reshape(64, 16, 128), CHIPS, 0, 0, tiled=True)
+    column_triple = gathered[:, :18].reshape(3 * D, D)
+    column_out = gathered[:, 18:24].reshape(D, D)
+    row_out = gathered[:, 24:30].reshape(D, D)
+    came, column_triple, column_out, row_out = lax.optimization_barrier(
+        (came, column_triple, column_out, row_out)
+    )
     blended = lax.all_gather(came, "c", axis=0, tiled=False)
 
     alignment, pair_out = pl.pallas_call(
         column_block,
         out_shape=(jax.ShapeDtypeStruct((R, D), BF), jax.ShapeDtypeStruct((L, 128), BF)),
-        in_specs=[SMEM] + [VMEM] * 5,
+        in_specs=[SMEM] + [VMEM] * 7,
         out_specs=(VMEM, VMEM),
-        scratch_shapes=[
-            pltpu.VMEM((2048, L), F32),
-            pltpu.VMEM((D, L), F32),
-            pltpu.VMEM((3 * D, L), F32),
-            pltpu.VMEM((D, L), BF),
-        ],
-        compiler_params=params(),
-    )(c1, blended, stack_own, gathered, pair_own, contact_w)
+        compiler_params=params(),
+    )(c1, blended, stack_own.T, row_out, column_triple, column_out, pair_own, contact_w)
     return alignment.reshape(R, 1, D), pair_out.reshape(1, L, 128)
 
 

time: 162 us -> 169 us (1.043)
  local copies, waits for them, and re-layouts: 5.16 us -> 22.8 us
  blocking collectives: 22.7 us -> 17 us
  Pallas kernels: 15.7 us -> 12.1 us
  starting transfers between devices: 59.6 us -> 57.6 us
    ppermute x8 -> x6, waiting for transfers between devices: 6.12 us -> 25.5 us  [moved(): return lax.ppermute(x, 'y', [(i, (i + step) % 8) for i in range(8)])]
    all_to_all x1, waiting for transfers between devices: 12.1 us -> 0.01 us  [per_device(): came = lax.all_to_all(message.reshape(64, 16, 128), CHIPS, 0, 0, tiled=True)]
    all_to_all x1, waiting for transfers between devices: 10.2 us -> 0.01 us  [per_device(): came = lax.all_to_all(message, CHIPS, 0, 0, tiled=True)]
    reshape x0 -> x6, local copies, waits for them, and re-layouts: none -> 9.52 us  [the longest x1 6.56 us: per_device(): column_triple = gathered[:, :18].reshape(3 * D, D)]
    slice x2 -> x4, local copies, waits for them, and re-layouts: 0.01 us -> 6.71 us  [the longest x1 5.05 us: per_device(): column_triple = gathered[:, :18].reshape(3 * D, D)]
    ppermute x8 -> x6, starting transfers between devices: 26.8 us -> 21.3 us  [moved(): return lax.ppermute(x, 'y', [(i, (i + step) % 8) for i in range(8)])]
    all_to_all x1, waiting for transfers between devices: 0.01 us -> 4.98 us  [per_device(): lax.all_to_all(jnp.broadcast_to(half, (8, 48, 384)), 'z', 0, 0, tiled=True)]
    pallas_call x1, Pallas kernels: 12.1 us -> 8.57 us  [per_device(): pl.pallas_call(column_block, out_shape=(jax.ShapeDtypeStruct((R, D), BF),...]
  transfers between devices with their start and end apart: 13 -> 11, of which waited for: 6 -> 7; matrix products, arithmetic and copies ran while one was open for 6% -> 16% of each run, Pallas kernels for 2% -> 2%
where the time goes in v2:
time: 169 us; the launch traced here: 168 us
  starting transfers between devices  57.6 us (34%)
  waiting for transfers between devices  38.3 us (23%)
  local copies, waits for them, and re-layouts  22.8 us (13%)
  blocking collectives  17 us (10%)
  between operations  15.1 us (9%)
  Pallas kernels  12.1 us (7%)
  matrix products  3 us (2%)
  other arithmetic  2.14 us (1%)
    ppermute x6, waiting for transfers between devices, moved(): return lax.ppermute(x, 'y', [(i, (i + step) % 8) for i in range(8)])  25.5 us
    ppermute x6, starting transfers between devices, moved(): return lax.ppermute(x, 'y', [(i, (i + step) % 8) for i in range(8)])  21.3 us
    all_to_all x1, starting transfers between devices, per_device(): came = lax.all_to_all(message, CHIPS, 0, 0, tiled=True)  17.1 us
    pallas_call x1, Pallas kernels, per_device(): pl.pallas_call(column_block, out_shape=(jax.ShapeDtypeStruct((R, D), BF),...  8.57 us
    all_to_all x1, waiting for transfers between devices, per_device(): lax.all_to_all(jnp.broadcast_to(tied, (8, L, L)), 'z', 0, 0, tiled=True)  7.79 us
    all_to_all x1, starting transfers between devices, per_device(): lax.all_to_all(jnp.broadcast_to(tied, (8, L, L)), 'z', 0, 0, tiled=True)  7.28 us
    all_to_all x1, starting transfers between devices, per_device(): lax.all_to_all(jnp.broadcast_to(half, (8, 48, 384)), 'z', 0, 0, tiled=True)  6.74 us
    reshape x1, local copies, waits for them, and re-layouts, per_device(): column_triple = gathered[:, :18].reshape(3 * D, D)  6.56 us
  transfers between devices with their start and end apart: 11, of which 7 were waited for; matrix products, arithmetic and copies ran while one was open for 16% of the time, Pallas kernels for 2%

profile of v2, /device:TPU:1, one launch (start us, length us, event | category | flops | bytes accessed | tf_op | source)
XLA Modules:
  0.0 168.0 jit_solution(8801598399059928732)
XLA Ops:
  7.2 0.0 copy-start
  7.2 0.0 copy-start.4
  7.2 0.0 all-gather.9.cloned.1.call-start
  7.2 0.1 pad.8.clone
  7.3 1.5 maximum_maximum_fusion
  8.8 0.0 all-gather.9.cloned.1.call-update
  8.9 0.9 convolution_convert_fusion
  9.9 0.9 reshape.75
  10.8 0.1 copy.36
  10.8 0.1 reshape.76
  10.9 1.1 reshape_reshape.3
  12.1 0.1 copy.28
  12.2 0.1 broadcast_bitcast_fusion
  12.2 0.1 pad_maximum_fusion
  12.3 1.1 copy.29
  13.5 17.1 %all-to-all-start = ((bf16[64,32,128]{2,1,0:T(8,128)(2,1)}), bf16[64,32,128]{2,1,0:T(8,128)(2,1)S(1)}, u32[]{:S(2)}, u32[]{:S(2)}) async-start(bf16[64,32,128]{2,1,0:T(8,128)(2,1)} %copy.29), calls=%async_computation | async-start | bytes 1048576 | tf_op jit(solution)/shard_map/all_to_all | solution.py:187
  30.6 0.1 convert_reduce_fusion
  30.7 0.2 fusion.24
  31.0 0.1 fusion.25.refs_0_
  31.1 2.9 %collective-permute-start = (bf16[128,768]{1,0:T(8,128)(2,1)S(1)}, bf16[128,768]{1,0:T(8,128)(2,1)S(1)}, u32[]{:S(2)}, u32[]{:S(2)}) collective-permute-start(bf16[128,768]{1,0:T(8,128)(2,1)S(1)} %fusion.25.refs_0_), channel_id=1, source_target_pairs={{0,2},{2,4},{4,6},{6,8},{8,10},{10,12},{12,14},{14,0},{1,3},{3,5},... | collective-permute-start | bytes 589832 | tf_op jit(solution)/shard_map/ppermute | solution.py:160
  34.0 3.6 %collective-permute-start.1 = (bf16[128,768]{1,0:T(8,128)(2,1)S(1)}, bf16[128,768]{1,0:T(8,128)(2,1)S(1)}, u32[]{:S(2)}, u32[]{:S(2)}) collective-permute-start(bf16[128,768]{1,0:T(8,128)(2,1)S(1)} %fusion.25.refs_0_), channel_id=1, source_target_pairs={{0,14},{2,0},{4,2},{6,4},{8,6},{10,8},{12,10},{14,12},{1,15},{3,1}... | collective-permute-start | bytes 589832 | tf_op jit(solution)/shard_map/ppermute | solution.py:160
  37.6 2.6 %collective-permute-start.2 = (bf16[128,768]{1,0:T(8,128)(2,1)S(1)}, bf16[128,768]{1,0:T(8,128)(2,1)S(1)}, u32[]{:S(2)}, u32[]{:S(2)}) collective-permute-start(bf16[128,768]{1,0:T(8,128)(2,1)S(1)} %fusion.25.refs_0_), channel_id=1, source_target_pairs={{0,4},{2,6},{4,8},{6,10},{8,12},{10,14},{12,0},{14,2},{1,5},{3,7},... | collective-permute-start | bytes 589832 | tf_op jit(solution)/shard_map/ppermute | solution.py:160
  40.2 4.8 %collective-permute-start.3 = (bf16[128,768]{1,0:T(8,128)(2,1)S(1)}, bf16[128,768]{1,0:T(8,128)(2,1)S(1)}, u32[]{:S(2)}, u32[]{:S(2)}) collective-permute-start(bf16[128,768]{1,0:T(8,128)(2,1)S(1)} %fusion.25.refs_0_), channel_id=1, source_target_pairs={{0,12},{2,14},{4,0},{6,2},{8,4},{10,6},{12,8},{14,10},{1,13},{3,15... | collective-permute-start | bytes 589832 | tf_op jit(solution)/shard_map/ppermute | solution.py:160
  45.1 4.0 %collective-permute-done.refs_1_ = bf16[128,768]{1,0:T(8,128)(2,1)S(1)} collective-permute-done((bf16[128,768]{1,0:T(8,128)(2,1)S(1)}, bf16[128,768]{1,0:T(8,128)(2,1)S(1)}, u32[]{:S(2)}, u32[]{:S(2)}) %collective-permute-start) | collective-permute-done | bytes 196640 | tf_op jit(solution)/shard_map/ppermute | solution.py:160
  49.1 0.0 collective-permute-done.1.refs_2_
  49.1 7.4 %collective-permute-done.2.refs_3_ = bf16[128,768]{1,0:T(8,128)(2,1)S(1)} collective-permute-done((bf16[128,768]{1,0:T(8,128)(2,1)S(1)}, bf16[128,768]{1,0:T(8,128)(2,1)S(1)}, u32[]{:S(2)}, u32[]{:S(2)}) %collective-permute-start.2) | collective-permute-done | bytes 196640 | tf_op jit(solution)/shard_map/ppermute | solution.py:160
  56.5 1.2 collective-permute-done.3.refs_4_
  57.8 2.1 %fusion.2 = bf16[128,384]{1,0:T(8,128)(2,1)S(1)} fusion(bf16[2048,128]{1,0:T(8,128)(2,1)S(1)} %bitcast.96, s32[384]{0:T(512)S(1)} %get-tuple-element.39, s32[384]{0:T(512)S(1)} %get-tuple-element.40, s32[]{:T(128)S(6)} %mul.36, s32[384]{0:T(512)S(1)} %get-tuple-element.38, s32[384]{0:T(512)S(1)} %get-tuple-element.41, s32[2048]{0:T(1024)S(1)} %get-tuple-element.33, ...), kind=kOutput, calls=%fused_computation.4 | convolution fusion | flops 212336640 | bytes 666376 | tf_op jit(solution)/shard_map/dot_general | solution.py:29
  59.9 3.1 %all-gather = bf16[192,384]{1,0:T(8,128)(2,1)S(1)} all-gather(bf16[96,384]{1,0:T(8,128)(2,1)S(1)} %slice.129), channel_id=2, replica_groups=mesh['a'=4,'z'=8,'y'=8,'c'=2] {'c'}, dimensions={0}, use_global_device_ids=true | all-gather | bytes 221184 | tf_op jit(solution)/shard_map/all_gather | solution.py:200
  63.0 0.7 broadcast_in_dim.35
  63.8 6.7 %all-to-all-start.1 = ((bf16[8,48,384]{2,1,0:T(8,128)(2,1)}), bf16[8,48,384]{2,1,0:T(8,128)(2,1)S(1)}, u32[]{:S(2)}, u32[]{:S(2)}) async-start(bf16[8,48,384]{2,1,0:T(8,128)(2,1)} %broadcast_in_dim.35), calls=%async_computation.1 | async-start | bytes 589824 | tf_op jit(solution)/shard_map/all_to_all | solution.py:203
  70.6 5.2 %collective-permute-start.4 = (bf16[192,768]{1,0:T(8,128)(2,1)S(1)}, bf16[192,768]{1,0:T(8,128)(2,1)S(1)}, u32[]{:S(2)}, u32[]{:S(2)}) collective-permute-start(bf16[192,768]{1,0:T(8,128)(2,1)S(1)} %pad_maximum_fusion.1), channel_id=1, source_target_pairs={{0,4},{2,6},{4,8},{6,10},{8,12},{10,14},{12,0},{14,2},{1,5},{3,7},... | collective-permute-start | bytes 884744 | tf_op jit(solution)/shard_map/ppermute | solution.py:160
  75.8 2.2 %collective-permute-start.5 = (bf16[192,768]{1,0:T(8,128)(2,1)S(1)}, bf16[192,768]{1,0:T(8,128)(2,1)S(1)}, u32[]{:S(2)}, u32[]{:S(2)}) collective-permute-start(bf16[192,768]{1,0:T(8,128)(2,1)S(1)} %pad_maximum_fusion.2), channel_id=1, source_target_pairs={{0,12},{2,14},{4,0},{6,2},{8,4},{10,6},{12,8},{14,10},{1,13},{3,15... | collective-permute-start | bytes 884744 | tf_op jit(solution)/shard_map/ppermute | solution.py:160
  78.0 5.0 %all-to-all-done.1 = bf16[8,48,384]{2,1,0:T(8,128)(2,1)S(1)} async-done(((bf16[8,48,384]{2,1,0:T(8,128)(2,1)}), bf16[8,48,384]{2,1,0:T(8,128)(2,1)S(1)}, u32[]{:S(2)}, u32[]{:S(2)}) %all-to-all-start.1) | async-done | bytes 294944 | tf_op jit(solution)/shard_map/all_to_all | solution.py:203
  83.0 3.4 %all-gather.1 = bf16[16,48,384]{2,1,0:T(8,128)(2,1)S(1)} all-gather(bf16[8,48,384]{2,1,0:T(8,128)(2,1)S(1)} %all-to-all-done.1), channel_id=3, replica_groups=mesh['a'=4,'z'=8,'y'=8,'c'=2] {'c'}, dimensions={0}, use_global_device_ids=true | all-gather | bytes 884736 | tf_op jit(solution)/shard_map/all_gather | solution.py:204
  86.4 3.9 %collective-permute-done.4.refs_5_ = bf16[192,768]{1,0:T(8,128)(2,1)S(1)} collective-permute-done((bf16[192,768]{1,0:T(8,128)(2,1)S(1)}, bf16[192,768]{1,0:T(8,128)(2,1)S(1)}, u32[]{:S(2)}, u32[]{:S(2)}) %collective-permute-start.4) | collective-permute-done | bytes 294944 | tf_op jit(solution)/shard_map/ppermute | solution.py:160
  90.2 8.9 %collective-permute-done.5.refs_6_ = bf16[192,768]{1,0:T(8,128)(2,1)S(1)} collective-permute-done((bf16[192,768]{1,0:T(8,128)(2,1)S(1)}, bf16[192,768]{1,0:T(8,128)(2,1)S(1)}, u32[]{:S(2)}, u32[]{:S(2)}) %collective-permute-start.5) | collective-permute-done | bytes 294944 | tf_op jit(solution)/shard_map/ppermute | solution.py:160
  99.2 2.1 %shard_map.104 = (f32[2,128,128]{2,1,0:T(8,128)S(1)}, bf16[8,128,128]{2,1,0:T(8,128)(2,1)S(1)}) custom-call(s32[1]{0:T(128)} %bitcast.1.y_ref, bf16[768,384]{1,0:T(8,128)(2,1)S(1)} %bitcast.88, bf16[128,768]{1,0:T(8,128)(2,1)S(1)} %fusion.25.refs_0_, bf16[128,768]{1,0:T(8,128)(2,1)S(1)} %collective-permute-done.refs_1_, ...), custom_call_target="tpu_custom_call" | custom-call | tf_op jit(solution)/shard_map/pallas_call | solution.py:212
  101.3 2.4 %all-gather.2 = f32[4,128,128]{2,1,0:T(8,128)S(1)} all-gather(f32[2,128,128]{2,1,0:T(8,128)S(1)} %get-tuple-element.20), channel_id=4, replica_groups=mesh['a'=4,'z'=8,'y'=8,'c'=2] {'c'}, dimensions={0}, use_global_device_ids=true | all-gather | bytes 393216 | tf_op jit(solution)/shard_map/all_gather | solution.py:223
  103.7 0.7 broadcast_in_dim.36
  104.5 7.3 %all-to-all-start.2 = ((bf16[8,128,128]{2,1,0:T(8,128)(2,1)}), bf16[8,128,128]{2,1,0:T(8,128)(2,1)S(1)}, u32[]{:S(2)}, u32[]{:S(2)}) async-start(bf16[8,128,128]{2,1,0:T(8,128)(2,1)} %broadcast_in_dim.36), calls=%async_computation.2 | async-start | bytes 524288 | tf_op jit(solution)/shard_map/all_to_all | solution.py:226
  112.4 0.2 copy.30
  112.7 2.4 %all-gather.3 = bf16[128,14,128]{2,0,1:T(8,128)(2,1)S(1)} all-gather(bf16[64,14,128]{2,0,1:T(8,128)(2,1)S(1)} %slice.98), channel_id=5, replica_groups=mesh['a'=4,'z'=8,'y'=8,'c'=2] {'c'}, dimensions={0}, use_global_device_ids=true | all-gather | bytes 688128 | tf_op jit(solution)/shard_map/all_gather | solution.py:206
  115.1 7.8 %all-to-all-done.2.part_ref = bf16[8,128,128]{2,1,0:T(8,128)(2,1)S(1)} async-done(((bf16[8,128,128]{2,1,0:T(8,128)(2,1)}), bf16[8,128,128]{2,1,0:T(8,128)(2,1)S(1)}, u32[]{:S(2)}, u32[]{:S(2)}) %all-to-all-start.2) | async-done | bytes 262176 | tf_op jit(solution)/shard_map/all_to_all | solution.py:226
  122.9 0.2 shard_map.105
  123.1 3.2 %all-gather.4 = bf16[4,128,128]{2,1,0:T(8,128)(2,1)S(1)} all-gather(bf16[2,128,128]{2,1,0:T(8,128)(2,1)S(1)} %shard_map.105), channel_id=6, replica_groups=mesh['a'=4,'z'=8,'y'=8,'c'=2] {'c'}, dimensions={0}, use_global_device_ids=true | all-gather | bytes 196608 | tf_op jit(solution)/shard_map/all_gather | solution.py:234
  126.4 1.2 shard_map.106
  127.6 5.2 %all-to-all-start.3 = ((bf16[64,16,128]{2,1,0:T(8,128)(2,1)}), bf16[64,16,128]{2,1,0:T(8,128)(2,1)S(1)}, u32[]{:S(2)}, u32[]{:S(2)}) async-start(bf16[64,16,128]{2,1,0:T(8,128)(2,1)} %bitcast.28), calls=%async_computation.3 | async-start | bytes 524288 | tf_op jit(solution)/shard_map/all_to_all | solution.py:243
  132.8 0.3 copy.32
  133.1 0.2 reshape.87
  133.3 0.4 constant_dynamic-slice_fusion
  133.7 0.2 copy.33
  133.9 0.0 all-gather.9.cloned.1.call-done
  133.9 5.0 %slice.100 = bf16[128,18,768]{2,1,0:T(8,128)(2,1)} slice(bf16[128,32,768]{2,1,0:T(8,128)(2,1)} %bitcast.94), slice={[0:128], [0:18], [0:768]} | slice | bytes 7077888 | tf_op jit(solution)/shard_map/slice | solution.py:244
  139.0 0.2 copy-done.3
  139.2 1.6 fusion.45
  140.8 0.4 reshape.85.wvo_ref
  141.2 2.3 %reshape.86.who_ref = bf16[768,768]{1,0:T(8,128)(2,1)S(1)} reshape(bf16[128,6,768]{2,1,0:T(8,128)(2,1)} %get-tuple-element.28) | data formatting | bytes 2359296 | tf_op jit(solution)/shard_map/reshape | solution.py:246
  143.6 0.0 copy-start.1
  143.6 0.0 copy-start.2
  143.6 6.6 %reshape.84.wv_ref = bf16[2304,768]{1,0:T(8,128)(2,1)} reshape(bf16[128,18,768]{2,1,0:T(8,128)(2,1)} %slice.100) | data formatting | bytes 7077888 | tf_op jit(solution)/shard_map/reshape | solution.py:244
  150.2 0.0 all-to-all-done.3
  150.2 2.4 %all-gather.6 = bf16[128,16,128]{2,1,0:T(8,128)(2,1)S(1)} all-gather(bf16[64,16,128]{2,1,0:T(8,128)(2,1)S(1)} %all-to-all-done.3), channel_id=8, replica_groups=mesh['a'=4,'z'=8,'y'=8,'c'=2] {'c'}, dimensions={0}, use_global_device_ids=true | all-gather | bytes 786432 | tf_op jit(solution)/shard_map/all_gather | solution.py:250
  152.6 8.6 %shard_map.107 = (bf16[128,768]{1,0:T(8,128)(2,1)}, bf16[128,128]{1,0:T(8,128)(2,1)}) custom-call(s32[1]{0:T(128)} %bitcast.c_ref, bf16[2,64,16,128]{3,2,1,0:T(8,128)(2,1)S(1)} %bitcast.89, bf16[768,128]{1,0:T(8,128)(2,1)S(1)} %bitcast.90, bf16[768,768]{1,0:T(8,128)(2,1)S(1)} %reshape.86.who_ref, bf16[2304,768]{1,0:T(8,128)(2,1)} %reshape.84.wv_ref, ...), custom_call_target="tpu_custom_call" | custom-call | tf_op jit(solution)/shard_map/pallas_call | solution.py:252
  (39 shorter events, 0.4 us)
Async XLA Ops:
  7.2 1.7 %copy-start = (bf16[128,12]{0,1:T(8,128)(2,1)S(1)}, bf16[128,12]{0,1:T(8,128)(2,1)}, u32[]{:S(2)}) copy-start(bf16[128,12]{0,1:T(8,128)(2,1)} %param.16) | copy-start | bytes 9220
  7.2 23.4 %copy-start.4 = (bf16[1,128,768]{2,1,0:T(8,128)(2,1)S(1)}, bf16[1,128,768]{2,1,0:T(8,128)(2,1)}, u32[]{:S(2)}) copy-start(bf16[1,128,768]{2,1,0:T(8,128)(2,1)} %param.9) | copy-start | bytes 589828
  7.2 126.7 %all-gather.9.cloned.1.call-start = ((), (), s32[]{:S(2)}) async-start(), calls=%async_computation.4 | async-start | bytes 6340608 | tf_op jit(solution)/shard_map/all_gather | solution.py:170
  13.5 44.3 %all-to-all-start = ((bf16[64,32,128]{2,1,0:T(8,128)(2,1)}), bf16[64,32,128]{2,1,0:T(8,128)(2,1)S(1)}, u32[]{:S(2)}, u32[]{:S(2)}) async-start(bf16[64,32,128]{2,1,0:T(8,128)(2,1)} %copy.29), calls=%async_computation | async-start | bytes 1048576 | tf_op jit(solution)/shard_map/all_to_all | solution.py:187
  31.1 18.0 %collective-permute-start = (bf16[128,768]{1,0:T(8,128)(2,1)S(1)}, bf16[128,768]{1,0:T(8,128)(2,1)S(1)}, u32[]{:S(2)}, u32[]{:S(2)}) collective-permute-start(bf16[128,768]{1,0:T(8,128)(2,1)S(1)} %fusion.25.refs_0_), channel_id=1, source_target_pairs={{0,2},{2,4},{4,6},{6,8},{8,10},{10,12},{12,14},{14,0},{1,3},{3,5},... | collective-permute-start | bytes 589832 | tf_op jit(solution)/shard_map/ppermute | solution.py:160
  34.0 15.1 %collective-permute-start.1 = (bf16[128,768]{1,0:T(8,128)(2,1)S(1)}, bf16[128,768]{1,0:T(8,128)(2,1)S(1)}, u32[]{:S(2)}, u32[]{:S(2)}) collective-permute-start(bf16[128,768]{1,0:T(8,128)(2,1)S(1)} %fusion.25.refs_0_), channel_id=1, source_target_pairs={{0,14},{2,0},{4,2},{6,4},{8,6},{10,8},{12,10},{14,12},{1,15},{3,1}... | collective-permute-start | bytes 589832 | tf_op jit(solution)/shard_map/ppermute | solution.py:160
  37.6 18.9 %collective-permute-start.2 = (bf16[128,768]{1,0:T(8,128)(2,1)S(1)}, bf16[128,768]{1,0:T(8,128)(2,1)S(1)}, u32[]{:S(2)}, u32[]{:S(2)}) collective-permute-start(bf16[128,768]{1,0:T(8,128)(2,1)S(1)} %fusion.25.refs_0_), channel_id=1, source_target_pairs={{0,4},{2,6},{4,8},{6,10},{8,12},{10,14},{12,0},{14,2},{1,5},{3,7},... | collective-permute-start | bytes 589832 | tf_op jit(solution)/shard_map/ppermute | solution.py:160
  40.2 17.6 %collective-permute-start.3 = (bf16[128,768]{1,0:T(8,128)(2,1)S(1)}, bf16[128,768]{1,0:T(8,128)(2,1)S(1)}, u32[]{:S(2)}, u32[]{:S(2)}) collective-permute-start(bf16[128,768]{1,0:T(8,128)(2,1)S(1)} %fusion.25.refs_0_), channel_id=1, source_target_pairs={{0,12},{2,14},{4,0},{6,2},{8,4},{10,6},{12,8},{14,10},{1,13},{3,15... | collective-permute-start | bytes 589832 | tf_op jit(solution)/shard_map/ppermute | solution.py:160
  63.8 19.2 %all-to-all-start.1 = ((bf16[8,48,384]{2,1,0:T(8,128)(2,1)}), bf16[8,48,384]{2,1,0:T(8,128)(2,1)S(1)}, u32[]{:S(2)}, u32[]{:S(2)}) async-start(bf16[8,48,384]{2,1,0:T(8,128)(2,1)} %broadcast_in_dim.35), calls=%async_computation.1 | async-start | bytes 589824 | tf_op jit(solution)/shard_map/all_to_all | solution.py:203
  70.6 19.7 %collective-permute-start.4 = (bf16[192,768]{1,0:T(8,128)(2,1)S(1)}, bf16[192,768]{1,0:T(8,128)(2,1)S(1)}, u32[]{:S(2)}, u32[]{:S(2)}) collective-permute-start(bf16[192,768]{1,0:T(8,128)(2,1)S(1)} %pad_maximum_fusion.1), channel_id=1, source_target_pairs={{0,4},{2,6},{4,8},{6,10},{8,12},{10,14},{12,0},{14,2},{1,5},{3,7},... | collective-permute-start | bytes 884744 | tf_op jit(solution)/shard_map/ppermute | solution.py:160
  75.8 23.4 %collective-permute-start.5 = (bf16[192,768]{1,0:T(8,128)(2,1)S(1)}, bf16[192,768]{1,0:T(8,128)(2,1)S(1)}, u32[]{:S(2)}, u32[]{:S(2)}) collective-permute-start(bf16[192,768]{1,0:T(8,128)(2,1)S(1)} %pad_maximum_fusion.2), channel_id=1, source_target_pairs={{0,12},{2,14},{4,0},{6,2},{8,4},{10,6},{12,8},{14,10},{1,13},{3,15... | collective-permute-start | bytes 884744 | tf_op jit(solution)/shard_map/ppermute | solution.py:160
  104.5 18.4 %all-to-all-start.2 = ((bf16[8,128,128]{2,1,0:T(8,128)(2,1)}), bf16[8,128,128]{2,1,0:T(8,128)(2,1)S(1)}, u32[]{:S(2)}, u32[]{:S(2)}) async-start(bf16[8,128,128]{2,1,0:T(8,128)(2,1)} %broadcast_in_dim.36), calls=%async_computation.2 | async-start | bytes 524288 | tf_op jit(solution)/shard_map/all_to_all | solution.py:226
  127.6 22.6 %all-to-all-start.3 = ((bf16[64,16,128]{2,1,0:T(8,128)(2,1)}), bf16[64,16,128]{2,1,0:T(8,128)(2,1)S(1)}, u32[]{:S(2)}, u32[]{:S(2)}) async-start(bf16[64,16,128]{2,1,0:T(8,128)(2,1)} %bitcast.28), calls=%async_computation.3 | async-start | bytes 524288 | tf_op jit(solution)/shard_map/all_to_all | solution.py:243
  133.9 5.2 %copy-start.3 = (bf16[4096,768]{1,0:T(8,128)(2,1)S(1)}, bf16[4096,768]{1,0:T(8,128)(2,1)}, u32[]{:S(2)}) copy-start(bf16[4096,768]{1,0:T(8,128)(2,1)} %all-gather.9.cloned.1.call-done) | copy-start | bytes 18874372
  143.6 9.0 %copy-start.1 = (bf16[1,128,128]{2,1,0:T(8,128)(2,1)S(1)}, bf16[1,128,128]{2,1,0:T(8,128)(2,1)}, u32[]{:S(2)}) copy-start(bf16[1,128,128]{2,1,0:T(8,128)(2,1)} %param.11) | copy-start | bytes 98308
  143.6 9.0 %copy-start.2 = (bf16[12,128]{1,0:T(8,128)(2,1)S(1)}, bf16[12,128]{1,0:T(8,128)(2,1)}, u32[]{:S(2)}) copy-start(bf16[12,128]{1,0:T(8,128)(2,1)} %cw_ref.1) | copy-start | bytes 9220
Sparse Core Ops, SparseCore 0:
  11.7 102.8 all-gather.8

commit v3 on v2

v3 whole, which is shorter than its diff:
```python
import jax
import jax.numpy as jnp
from jax import lax
from jax.experimental import pallas as pl
from jax.experimental.pallas import tpu as pltpu
from jax.sharding import Mesh
from jax.sharding import PartitionSpec as P

ROWS = ("zh", "zl", "yh", "yl", "c")
ALL = ("a",) + ROWS
CHIPS = ROWS[:4]
FAR = ("zh", "yh")
D, H, E, L, R = 768, 12, 64, 128, 128
BF, F32 = jnp.bfloat16, jnp.float32
VMEM = pl.BlockSpec(memory_space=pltpu.VMEM)
SMEM = pl.BlockSpec(memory_space=pltpu.SMEM)


def params():
    return pltpu.CompilerParams(vmem_limit_bytes=48 << 20)


def dot_nt(a, b):
    return lax.dot_general(a, b, (((1,), (1,)), ((), ())), preferred_element_type=F32)


def dot_tn(a, b):
    return lax.dot_general(a, b, (((0,), (0,)), ((), ())), preferred_element_type=F32)


def normalize(x):
    center = jnp.mean(x, axis=-1, keepdims=True)
    spread = jnp.mean(jnp.square(x - center), axis=-1, keepdims=True)
    return (x - center) * lax.rsqrt(spread + 1e-05)


def spread_columns(c_ref, picked_ref, out_ref):
    both = picked_ref[0].astype(F32) + picked_ref[1].astype(F32)
    second = c_ref[0] == 1
    parts = []
    for n in range(3):
        three = both[:, 192 * n : 192 * n + 192]
        parts.append(jnp.where(second, three[:, 64:], three[:, :128]))
    mine = jnp.concatenate(parts, axis=1).astype(BF)
    for n in range(16):
        out_ref[n] = mine


def project_and_tie(at_ref, w_ref, near_ref, far_ref, tied_ref, v_ref):
    w = w_ref[...]
    lane = lax.broadcasted_iota(jnp.int32, (L, 2 * E), 1)
    zl, yl = at_ref[0], at_ref[1]
    tied = [jnp.zeros((L, L), F32), jnp.zeros((L, L), F32)]
    for n, ref in enumerate((near_ref, far_ref)):
        for core in range(2):
            for m in range(2):
                packed = jnp.dot(ref[core, m], w, preferred_element_type=F32)
                q = packed[:, : 2 * E] * E**-0.5
                k = packed[:, 2 * E : 4 * E].astype(BF)
                slot = 4 * lax.rem(zl + n, 2) + 2 * lax.rem(yl + m, 2) + core
                v_ref[slot] = packed[:, 4 * E :].astype(BF)
                tied[0] += dot_nt(jnp.where(lane < E, q, 0.0).astype(BF), k)
                tied[1] += dot_nt(jnp.where(lane < E, 0.0, q).astype(BF), k)
    for h in range(2):
        part = (tied[h] * R**-0.5).astype(BF)
        for n in range(4):
            tied_ref[n, h] = part


def add_four(part_ref, out_ref):
    total = part_ref[0].astype(F32)
    for n in range(1, 4):
        total += part_ref[n].astype(F32)
    total = total.astype(BF)
    for n in range(4):
        out_ref[n] = total


def attend(c_ref, span_ref, part_ref, bias_ref, v_ref, out_ref, held):
    lane = lax.broadcasted_iota(jnp.int32, (L, 2 * E), 1)
    low = lane < E
    odd = c_ref[0] == 1
    probs, plain, turned = [], [], []
    for h in range(2):
        scores = bias_ref[h].astype(F32)
        for n in range(4):
            scores += part_ref[n, h].astype(F32)
        masked = jnp.where(lane < span_ref[0], scores, -1e30)
        e = jnp.exp(masked - jnp.max(masked, axis=1, keepdims=True))
        probs.append((e / jnp.sum(e, axis=1, keepdims=True)).astype(BF))
        plain.append(scores)
        turned.append(pltpu.roll(scores, E, 1))
    for n in range(8):
        v = v_ref[n]
        o = jnp.where(
            low,
            jnp.dot(probs[0], v, preferred_element_type=F32),
            jnp.dot(probs[1], v, preferred_element_type=F32),
        )
        h, half = (n % 4) // 2, n % 2
        if n < 4:
            extra = turned[h] if half else plain[h]
            o = jnp.where(jnp.logical_and(low, odd), extra, o)
        else:
            extra = plain[h] if half else turned[h]
            o = jnp.where(jnp.logical_or(low, odd), o, extra)
        held[:, n, :] = o
    out_ref[...] = held[...].astype(BF)


def column_block(c_ref, bl_ref, stack_ref, who_ref, wv_ref, wvo_ref, pair_ref, cw_ref, out_ref, pair_out_ref):
    mine = c_ref[0]
    lane = lax.broadcasted_iota(jnp.int32, (L, L), 1)
    row = lax.broadcasted_iota(jnp.int32, (L, L), 0)
    low = lane < E
    early = lax.rem(row, 8) < 4

    def tile(pair, far):
        zl, yl, c = pair // 4, pair // 2 % 2, pair % 2
        both = bl_ref[c, far // 4 * 16 + zl * 8 + far % 4 * 2 + yl].astype(F32)
        return jnp.where(mine == 0, both[:8], both[8:])

    tiles = [[tile(pair, far) for far in range(16)] for pair in range(8)]
    blocks = [jnp.concatenate(t, axis=0) for t in tiles]
    parts = []
    for n in range(2):
        e0, o0, e1, o1 = blocks[4 * n : 4 * n + 4]
        ro0, re1 = pltpu.roll(o0, E, 1), pltpu.roll(e1, E, 1)
        parts.append(jnp.where(jnp.logical_or(low, early), e0, ro0))
        parts.append(jnp.where(low, ro0, re1))
        parts.append(jnp.where(jnp.logical_and(low, early), re1, o1))
    blended = jnp.concatenate(parts, axis=1).astype(BF)

    updated = (dot_nt(who_ref[...], blended) + stack_ref[...].astype(F32)).astype(BF).astype(F32)
    center = jnp.mean(updated, axis=0, keepdims=True)
    spread = jnp.mean(jnp.square(updated - center), axis=0, keepdims=True)
    normed = ((updated - center) * lax.rsqrt(spread + 1e-05)).astype(BF)
    packed = jnp.dot(wv_ref[...], normed, preferred_element_type=F32)

    mixed = []
    for h in range(H):
        q = (packed[E * h : E * h + E] * E**-0.5).astype(BF)
        k = packed[D + E * h : D + E * h + E].astype(BF)
        v = packed[2 * D + E * h : 2 * D + E * h + E].astype(BF)
        logits = dot_tn(k, q)
        e = jnp.exp(logits - jnp.max(logits, axis=0, keepdims=True))
        probs = (e / jnp.sum(e, axis=0, keepdims=True)).astype(BF)
        mixed.append(jnp.dot(v, probs, preferred_element_type=F32).astype(BF))
    mixed = jnp.concatenate(mixed, axis=0)

    result = (updated + jnp.dot(wvo_ref[...], mixed, preferred_element_type=F32)).astype(BF)
    place = (row // 32 * 32 + row // 4 % 4 * 8 + row // 16 % 2 * 4 + row % 4 == lane).astype(BF)
    out_ref[...] = dot_nt(place, result).astype(BF)

    one = lax.broadcasted_iota(jnp.int32, (1, L), 1) < E
    lines = []
    for n in range(4):
        e, o = tiles[2 * n][0], tiles[2 * n + 1][0]
        re, ro = pltpu.roll(e, E, 1), pltpu.roll(o, E, 1)
        lines.append(jnp.where(one, re[4:5], e[5:6]))
        lines.append(jnp.where(one, re[6:7], e[7:8]))
        lines.append(jnp.where(one, o[2:3], ro[3:4]))
    scores = jnp.concatenate(lines + [jnp.zeros((L - H, L), F32)], axis=0).T
    weights = jnp.concatenate([cw_ref[...].astype(F32), jnp.zeros((L - H, L), F32)], axis=0)
    pair = pair_ref[...].astype(F32) + jnp.dot(
        scores.astype(BF), weights.astype(BF), preferred_element_type=F32
    )
    pair_out_ref[...] = pair.astype(BF)


def swapped(x, axis):
    return lax.ppermute(x, axis, [(0, 1), (1, 0)])


def call(kernel, out_shape, *args, scalars=0, scratch=()):
    return pl.pallas_call(
        kernel,
        out_shape=out_shape,
        in_specs=[SMEM] * scalars + [VMEM] * (len(args) - scalars),
        out_specs=jax.tree.map(lambda _: VMEM, out_shape),
        scratch_shapes=scratch,
        compiler_params=params(),
    )(*args)


def like(*dims, dtype=BF):
    return jax.ShapeDtypeStruct(dims, dtype)


def per_device(stack, spans, pair, w_triple, w_out, v_triple, v_out, offsets, contact_w):
    zl, yl, c = (lax.axis_index(n).astype(jnp.int32) for n in ("zl", "yl", "c"))
    c1 = c[None]
    pair_own = pair.reshape(L, 128)
    own_row = stack.reshape(L, D)

    column_weights = jnp.concatenate([v_triple.T, v_out.T, w_out.T, jnp.zeros((2, D), BF)], axis=0)
    gathered = lax.all_gather(column_weights, ROWS, axis=0, tiled=False)

    normed = normalize(own_row.astype(F32)).astype(BF)
    near = jnp.concatenate([normed, swapped(normed, "yl")])
    far = swapped(near, "zl")

    bias = lax.dot_general(offsets, pair_own, (((0,), (1,)), ((), ())), preferred_element_type=F32).astype(BF)
    bias = jnp.pad(bias.reshape(4, 6, E), ((0, 0), (0, 12), (0, 0)))
    slices = jnp.pad(w_triple.T.reshape(18, 16, 48).transpose(1, 0, 2), ((0, 0), (0, 0), (0, 16)))
    front = jnp.concatenate(
        [
            jnp.broadcast_to(slices.reshape(4, 1, 4, 1, 18, E), (4, 2, 4, 2, 18, E)),
            jnp.broadcast_to(bias.reshape(1, 2, 1, 2, 18, E), (4, 2, 4, 2, 18, E)),
        ],
        axis=-1,
    ).reshape(64, 18, 128)
    message = jnp.concatenate([front, own_row.reshape(64, 12, 128), jnp.zeros((64, 2, 128), BF)], axis=1)
    came = lax.all_to_all(message, CHIPS, 0, 0, tiled=True)

    source = lax.broadcasted_iota(jnp.int32, (2048, 576), 0)
    target = lax.broadcasted_iota(jnp.int32, (2048, 576), 1)
    column = (source // 32 * 2 + c) * 18 + source % 32
    wanted = target // 192 * D + (2 * zl + yl) * 192 + target % 192
    pick = jnp.logical_and(column == wanted, source % 32 < 18).astype(BF)
    came, near, pick = lax.optimization_barrier((came, near, pick))
    picked = dot_tn(came.reshape(2048, 128), pick)[:48].astype(BF)
    picked = lax.all_gather(picked, "c", axis=0, tiled=False)
    copies = call(spread_columns, like(16, 48, 384), c1, picked, scalars=1)
    w_heads = lax.all_to_all(copies, FAR, 0, 0, tiled=True).reshape(D, 384)
    near = lax.all_gather(near.reshape(2, L, D), "c", axis=0, tiled=False)
    far = lax.all_gather(far.reshape(2, L, D), "c", axis=0, tiled=False)

    rest = lax.all_gather(came[:, :30], "c", axis=0, tiled=False)
    stack_own = rest[:, :, 18:].reshape(2, 64, 2, D)
    stack_own = lax.dynamic_index_in_dim(stack_own, c, 2, keepdims=False).reshape(2, 4, 2, 4, 2, D)
    stack_own = stack_own.transpose(1, 3, 2, 4, 0, 5).reshape(R, D).T
    bias_own = rest[:, :, :6, E:].reshape(2, 64, 3, L)
    bias_own = lax.dynamic_slice_in_dim(bias_own, c, 2, axis=2).transpose(2, 1, 0, 3).reshape(2, L, L)

    at = jnp.stack([zl, yl])
    tied, values = call(
        project_and_tie, (like(4, 2, L, L), like(8, L, 2 * E)), at, w_heads, near, far, scalars=1
    )
    parts = lax.all_to_all(tied, "zh", 0, 0, tiled=True)
    parts = call(add_four, like(4, 2, L, L), parts)
    parts = lax.all_to_all(parts, "yh", 0, 0, tiled=True)
    message = call(
        attend,
        like(L, 8, 2 * E),
        c1,
        spans,
        parts,
        bias_own,
        values,
        scalars=2,
        scratch=[pltpu.VMEM((L, 8, 2 * E), F32)],
    )
    came = lax.all_to_all(message.reshape(64, 16, 128), CHIPS, 0, 0, tiled=True)

    column_triple = gathered[:, :18].reshape(3 * D, D)
    column_out = gathered[:, 18:24].reshape(D, D)
    row_out = gathered[:, 24:30].reshape(D, D)
    came, column_triple, column_out, row_out = lax.optimization_barrier(
        (came, column_triple, column_out, row_out)
    )
    blended = lax.all_gather(came, "c", axis=0, tiled=False)

    alignment, pair_out = call(
        column_block,
        (like(R, D), like(L, 128)),
        c1,
        blended,
        stack_own,
        row_out,
        column_triple,
        column_out,
        pair_own,
        contact_w,
        scalars=1,
    )
    return alignment.reshape(R, 1, D), pair_out.reshape(1, L, 128)


def solution(mesh):
    torus = Mesh(mesh.devices.reshape(mesh.shape["aln"], 4, 2, 4, 2, 2), ALL)
    in_specs = (
        P(ALL, None, None),
        P("a"),
        P(ALL, None, None),
        P(None, ROWS),
        P(None, ROWS),
        P(None, ROWS),
        P(None, ROWS),
        P(),
        P(),
    )
    out_specs = (P("a", ROWS, None), P(ALL, None, None))
    return jax.shard_map(
        per_device, mesh=torus, in_specs=in_specs, out_specs=out_specs, check_vma=False
    )
```

time: 169 us -> 183 us (1.083)
  blocking collectives: 17 us -> 35.6 us
  starting transfers between devices: 57.6 us -> 41.5 us
  other arithmetic: 2.14 us -> 9.89 us
  waiting for transfers between devices: 38.3 us -> 41.4 us
  Pallas kernels: 12.1 us -> 14.4 us
    all_to_all x0 -> x1, blocking collectives: none -> 16.3 us  [per_device(): parts = lax.all_to_all(tied, 'zh', 0, 0, tiled=True)]
    ppermute x6 -> x2, starting transfers between devices: 21.3 us -> 6.96 us  [swapped(): return lax.ppermute(x, axis, [(0, 1), (1, 0)])]
    all_to_all x1, waiting for transfers between devices: 0.01 us -> 13 us  [per_device(): came = lax.all_to_all(message, CHIPS, 0, 0, tiled=True)]
    all_to_all x2, waiting for transfers between devices: 12.8 us -> 1.4 us  [the longest x1 1.39 us: per_device(): parts = lax.all_to_all(parts, 'yh', 0, 0, tiled=True)]
    all_to_all x2, starting transfers between devices: 14 us -> 10.8 us  [the longest x1 6.91 us: per_device(): parts = lax.all_to_all(parts, 'yh', 0, 0, tiled=True)]
    all_to_all x1, starting transfers between devices: 5.15 us -> 8.34 us  [per_device(): came = lax.all_to_all(message.reshape(64, 16, 128), CHIPS, 0, 0, tiled=True)]
    all_gather x1, blocking collectives: 3.08 us -> 5.99 us  [per_device(): picked = lax.all_gather(picked, 'c', axis=0, tiled=False)]
    convert_element_type x1, other arithmetic: 0.01 us -> 2.71 us  [per_device(): pick = jnp.logical_and(column == wanted, source % 32 < 18).astype(BF)]
  transfers between devices with their start and end apart: 11 -> 7, of which waited for: 7 -> 3; matrix products, arithmetic and copies ran while one was open for 16% -> 18% of each run, Pallas kernels for 2% -> 3%
where the time goes in v3:
time: 183 us; the launch traced here: 182 us
  starting transfers between devices  41.5 us (23%)
  waiting for transfers between devices  41.4 us (23%)
  blocking collectives  35.6 us (19%)
  local copies, waits for them, and re-layouts  22.2 us (12%)
  between operations  15 us (8%)
  Pallas kernels  14.4 us (8%)
  other arithmetic  9.89 us (5%)
    ppermute x2, waiting for transfers between devices, swapped(): return lax.ppermute(x, axis, [(0, 1), (1, 0)])  27 us
    all_to_all x1, blocking collectives, per_device(): parts = lax.all_to_all(tied, 'zh', 0, 0, tiled=True)  16.3 us
    all_to_all x1, starting transfers between devices, per_device(): came = lax.all_to_all(message, CHIPS, 0, 0, tiled=True)  15.4 us
    pallas_call x5, Pallas kernels, call(): pl.pallas_call(kernel, out_shape=out_shape, in_specs=[SMEM] * scalars + [...  14.4 us
    all_to_all x1, waiting for transfers between devices, per_device(): came = lax.all_to_all(message, CHIPS, 0, 0, tiled=True)  13 us
    all_to_all x1, starting transfers between devices, per_device(): came = lax.all_to_all(message.reshape(64, 16, 128), CHIPS, 0, 0, tiled=True)  8.34 us
    ppermute x2, starting transfers between devices, swapped(): return lax.ppermute(x, axis, [(0, 1), (1, 0)])  6.96 us
    all_to_all x1, starting transfers between devices, per_device(): parts = lax.all_to_all(parts, 'yh', 0, 0, tiled=True)  6.91 us
  transfers between devices with their start and end apart: 7, of which 3 were waited for; matrix products, arithmetic and copies ran while one was open for 18% of the time, Pallas kernels for 3%

profile of v3, /device:TPU:1, one launch (start us, length us, event | category | flops | bytes accessed | tf_op | source)
XLA Modules:
  0.0 181.6 jit_solution(17290327370522439506)
XLA Ops:
  7.2 0.0 copy-start
  7.2 0.0 all-gather.6.cloned.1.call-start
  7.2 0.1 pad.18.clone
  7.3 1.5 maximum_maximum_fusion.1
  8.8 0.0 all-gather.6.cloned.1.call-update
  8.8 1.0 convert_reduce_fusion
  9.9 1.1 fusion.6
  11.0 1.1 fusion.7
  12.1 0.0 copy-start.3
  12.1 4.0 %collective-permute-start = (bf16[128,768]{1,0:T(8,128)(2,1)S(1)}, bf16[128,768]{1,0:T(8,128)(2,1)}, u32[]{:S(2)}, u32[]{:S(2)}) collective-permute-start(bf16[128,768]{1,0:T(8,128)(2,1)S(1)} %fusion.7), channel_id=1, source_target_pairs={{0,2},{2,0},{1,3},{3,1},{4,6},{6,4},{5,7},{7,5},{8,10},{10,8},{9,1... | collective-permute-start | bytes 589832 | tf_op jit(solution)/shard_map/ppermute | solution.py:172
  16.2 1.1 reshape_reshape.3
  17.3 0.0 copy-done
  17.3 0.9 convolution_convert_fusion
  18.2 0.1 reshape.76
  18.3 0.9 reshape.74
  19.3 0.1 broadcast_in_dim.27
  19.3 0.1 broadcast_in_dim.29
  19.4 0.2 pad_maximum_fusion
  19.7 1.0 maximum_maximum_fusion
  20.7 15.4 %all-to-all-start = ((bf16[64,32,128]{2,1,0:T(8,128)(2,1)}), bf16[64,32,128]{2,1,0:T(8,128)(2,1)S(1)}, u32[]{:S(2)}, u32[]{:S(2)}) async-start(bf16[64,32,128]{2,1,0:T(8,128)(2,1)} %maximum_maximum_fusion), calls=%async_computation | async-start | bytes 1048576 | tf_op jit(solution)/shard_map/all_to_all | solution.py:214
  36.2 2.7 %fusion.2 = bf16[2048,576]{1,0:T(8,128)(2,1)S(1)} fusion(s32[576]{0:T(1024)S(1)} %get-tuple-element.33, s32[576]{0:T(1024)S(1)} %get-tuple-element.34, s32[]{:T(128)S(6)} %mul.37, s32[576]{0:T(1024)S(1)} %get-tuple-element.32, s32[576]{0:T(1024)S(1)} %get-tuple-element.35, s32[2048]{0:T(1024)S(1)} %get-tuple-element.27, s32[2048]{0:T(1024)S(1)} %get-tuple-element.28, ...), kind=kLoop, calls=%fused_computation.4 | loop fusion | flops 17694720 | bytes 2406536 | tf_op jit(solution)/shard_map/convert_element_type | solution.py:220
  38.9 0.0 copy-done.3
  38.9 0.0 collective-permute-done
  38.9 1.0 pad_maximum_fusion.1
  40.0 13.0 %all-to-all-done = bf16[64,32,128]{2,1,0:T(8,128)(2,1)S(1)} async-done(((bf16[64,32,128]{2,1,0:T(8,128)(2,1)}), bf16[64,32,128]{2,1,0:T(8,128)(2,1)S(1)}, u32[]{:S(2)}, u32[]{:S(2)}) %all-to-all-start) | async-done | bytes 524320 | tf_op jit(solution)/shard_map/all_to_all | solution.py:214
  53.0 0.6 fusion.22
  53.6 6.0 %all-gather = bf16[96,576]{1,0:T(8,128)(2,1)S(1)} all-gather(bf16[48,576]{1,0:T(8,128)(2,1)S(1)} %slice.36), channel_id=2, replica_groups=mesh['a'=4,'zh'=4,'zl'=2,'yh'=4,'yl'=2,'c'=2] {'c'}, dimensions={0}, use_global_device_ids=true | all-gather | bytes 165888 | tf_op jit(solution)/shard_map/all_gather | solution.py:223
  59.6 1.0 shard_map.104
  60.6 3.8 %all-to-all-start.1 = ((bf16[16,48,384]{2,1,0:T(8,128)(2,1)}), bf16[16,48,384]{2,1,0:T(8,128)(2,1)S(1)}, u32[]{:S(2)}, u32[]{:S(2)}) async-start(bf16[16,48,384]{2,1,0:T(8,128)(2,1)} %shard_map.104), calls=%async_computation.1 | async-start | bytes 1179648 | tf_op jit(solution)/shard_map/all_to_all | solution.py:225
  64.4 2.9 %collective-permute-start.1 = (bf16[256,768]{1,0:T(8,128)(2,1)S(1)}, bf16[256,768]{1,0:T(8,128)(2,1)S(1)}, u32[]{:S(2)}, u32[]{:S(2)}) collective-permute-start(bf16[256,768]{1,0:T(8,128)(2,1)S(1)} %pad_maximum_fusion.1), channel_id=1, source_target_pairs={{0,16},{16,0},{1,17},{17,1},{2,18},{18,2},{3,19},{19,3},{4,20},{20... | collective-permute-start | bytes 1179656 | tf_op jit(solution)/shard_map/ppermute | solution.py:172
  67.4 0.1 pad_add_fusion.at_ref
  67.5 27.0 %collective-permute-done.1 = bf16[256,768]{1,0:T(8,128)(2,1)S(1)} collective-permute-done((bf16[256,768]{1,0:T(8,128)(2,1)S(1)}, bf16[256,768]{1,0:T(8,128)(2,1)S(1)}, u32[]{:S(2)}, u32[]{:S(2)}) %collective-permute-start.1) | collective-permute-done | bytes 393248 | tf_op jit(solution)/shard_map/ppermute | solution.py:172
  94.4 2.6 %all_gather.33.far_ref = bf16[2,2,128,768]{3,2,1,0:T(8,128)(2,1)S(1)} all-gather(bf16[1,2,128,768]{3,2,1,0:T(8,128)(2,1)S(1)} %bitcast.65), channel_id=1, replica_groups=mesh['a'=4,'zh'=4,'zl'=2,'yh'=4,'yl'=2,'c'=2] {'c'}, dimensions={0}, use_global_device_ids=true | all-gather | bytes 1179648 | tf_op jit(solution)/shard_map/all_gather | solution.py:227
  97.0 2.4 %all_gather.32.near_ref = bf16[2,2,128,768]{3,2,1,0:T(8,128)(2,1)S(1)} all-gather(bf16[1,2,128,768]{3,2,1,0:T(8,128)(2,1)S(1)} %bitcast.61), channel_id=1, replica_groups=mesh['a'=4,'zh'=4,'zl'=2,'yh'=4,'yl'=2,'c'=2] {'c'}, dimensions={0}, use_global_device_ids=true | all-gather | bytes 1179648 | tf_op jit(solution)/shard_map/all_gather | solution.py:226
  99.4 0.0 all-to-all-done.1
  99.4 2.7 %shard_map.105 = (bf16[4,2,128,128]{3,2,1,0:T(8,128)(2,1)S(1)}, bf16[8,128,128]{2,1,0:T(8,128)(2,1)S(1)}) custom-call(s32[2]{0:T(128)S(1)} %pad_add_fusion.at_ref, bf16[768,384]{1,0:T(8,128)(2,1)S(1)} %bitcast.49, bf16[2,2,128,768]{3,2,1,0:T(8,128)(2,1)S(1)} %all_gather.32.near_ref, bf16[2,2,128,768]{3,2,1,0:T(8,128)(2,1)S(1)} %all_gather.33.far_ref), custom_call_target="tpu_custom_call" | custom-call | tf_op jit(solution)/shard_map/pallas_call | solution.py:176
  102.1 16.3 %all_to_all.25.part_ref = bf16[4,2,128,128]{3,2,1,0:T(8,128)(2,1)S(1)} all-to-all(bf16[4,2,128,128]{3,2,1,0:T(8,128)(2,1)S(1)} %get-tuple-element.16), channel_id=1, replica_groups=mesh['a'=4,'zh'=4,'zl'=2,'yh'=4,'yl'=2,'c'=2] {'zh'}, dimensions={0} | all-to-all | bytes 524288 | tf_op jit(solution)/shard_map/all_to_all | solution.py:240
  118.4 0.8 shard_map.106
  119.1 6.9 %all-to-all-start.3 = ((bf16[4,2,128,128]{3,2,1,0:T(8,128)(2,1)}), bf16[4,2,128,128]{3,2,1,0:T(8,128)(2,1)S(1)}, u32[]{:S(2)}, u32[]{:S(2)}) async-start(bf16[4,2,128,128]{3,2,1,0:T(8,128)(2,1)} %shard_map.106), calls=%async_computation.3 | async-start | bytes 524288 | tf_op jit(solution)/shard_map/all_to_all | solution.py:242
  126.7 0.2 copy.27
  126.9 5.4 %all-gather.1 = bf16[128,30,128]{2,0,1:T(8,128)(2,1)S(1)} all-gather(bf16[64,30,128]{2,0,1:T(8,128)(2,1)S(1)} %copy.27), channel_id=3, replica_groups=mesh['a'=4,'zh'=4,'zl'=2,'yh'=4,'yl'=2,'c'=2] {'c'}, dimensions={0}, use_global_device_ids=true | all-gather | bytes 1474560 | tf_op jit(solution)/shard_map/all_gather | solution.py:229
  132.3 0.1 slice.30
  132.4 0.2 copy.34
  132.6 0.1 copy.29
  132.7 1.4 all-to-all-done.3.part_ref
  134.1 1.4 shard_map.107
  135.5 8.3 %all-to-all-start.4 = ((bf16[64,16,128]{2,1,0:T(8,128)(2,1)}), bf16[64,16,128]{2,1,0:T(8,128)(2,1)S(1)}, u32[]{:S(2)}, u32[]{:S(2)}) async-start(bf16[64,16,128]{2,1,0:T(8,128)(2,1)} %bitcast.19), calls=%async_computation.4 | async-start | bytes 524288 | tf_op jit(solution)/shard_map/all_to_all | solution.py:254
  143.9 0.3 copy.35
  144.1 0.2 reshape.86
  144.4 0.4 constant_dynamic-slice_fusion
  144.8 0.3 copy.31
  145.1 0.1 copy.32
  145.3 0.1 reshape.88
  145.3 0.2 copy.33
  145.5 0.0 all-gather.6.cloned.1.call-done
  145.5 4.9 %slice.31 = bf16[128,18,768]{2,1,0:T(8,128)(2,1)} slice(bf16[128,32,768]{2,1,0:T(8,128)(2,1)} %bitcast.55), slice={[0:128], [0:18], [0:768]} | slice | bytes 7077888 | tf_op jit(solution)/shard_map/slice | solution.py:256
  150.4 6.6 %reshape.83.wv_ref = bf16[2304,768]{1,0:T(8,128)(2,1)} reshape(bf16[128,18,768]{2,1,0:T(8,128)(2,1)} %slice.31) | data formatting | bytes 7077888 | tf_op jit(solution)/shard_map/reshape | solution.py:256
  157.0 3.4 %fusion.21 = (bf16[128,6,768]{2,1,0:T(8,128)(2,1)S(1)}, bf16[128,6,768]{2,1,0:T(8,128)(2,1)}) fusion(bf16[128,32,768]{2,1,0:T(8,128)(2,1)} %bitcast.56), kind=kLoop, calls=%fused_computation.44 | loop fusion | bytes 4718592 | tf_op jit(solution)/shard_map/slice | solution.py:258
  160.4 0.4 reshape.85.who_ref
  160.8 2.3 %reshape.84.wvo_ref = bf16[768,768]{1,0:T(8,128)(2,1)S(1)} reshape(bf16[128,6,768]{2,1,0:T(8,128)(2,1)} %get-tuple-element.25) | data formatting | bytes 2359296 | tf_op jit(solution)/shard_map/reshape | solution.py:257
  163.2 0.0 all-to-all-done.4
  163.2 3.0 %all-gather.3 = bf16[128,16,128]{2,1,0:T(8,128)(2,1)S(1)} all-gather(bf16[64,16,128]{2,1,0:T(8,128)(2,1)S(1)} %all-to-all-done.4), channel_id=5, replica_groups=mesh['a'=4,'zh'=4,'zl'=2,'yh'=4,'yl'=2,'c'=2] {'c'}, dimensions={0}, use_global_device_ids=true | all-gather | bytes 786432 | tf_op jit(solution)/shard_map/all_gather | solution.py:262
  166.2 0.0 copy-done.1
  166.2 8.6 %shard_map.108 = (bf16[128,768]{1,0:T(8,128)(2,1)}, bf16[128,128]{1,0:T(8,128)(2,1)}) custom-call(s32[1]{0:T(128)} %bitcast.c_ref, bf16[2,64,16,128]{3,2,1,0:T(8,128)(2,1)S(1)} %bitcast.50, bf16[768,128]{1,0:T(8,128)(2,1)S(1)} %bitcast.51, bf16[768,768]{1,0:T(8,128)(2,1)S(1)} %reshape.85.who_ref, bf16[2304,768]{1,0:T(8,128)(2,1)} %reshape.83.wv_ref, ...), custom_call_target="tpu_custom_call" | custom-call | tf_op jit(solution)/shard_map/pallas_call | solution.py:176
  (18 shorter events, 0.2 us)
Async XLA Ops:
  7.2 10.1 %copy-start = (bf16[128,12]{0,1:T(8,128)(2,1)S(1)}, bf16[128,12]{0,1:T(8,128)(2,1)}, u32[]{:S(2)}) copy-start(bf16[128,12]{0,1:T(8,128)(2,1)} %param.16) | copy-start | bytes 9220
  7.2 138.3 %all-gather.6.cloned.1.call-start = ((), (), s32[]{:S(2)}) async-start(), calls=%async_computation.5 | async-start | bytes 6340608 | tf_op jit(solution)/shard_map/all_gather | solution.py:197
  12.1 26.8 %copy-start.3 = (bf16[128,768]{1,0:T(8,128)(2,1)}, bf16[128,768]{1,0:T(8,128)(2,1)S(1)}, u32[]{:S(2)}) copy-start(bf16[128,768]{1,0:T(8,128)(2,1)S(1)} %fusion.7) | copy-start | bytes 589828
  12.1 26.8 %collective-permute-start = (bf16[128,768]{1,0:T(8,128)(2,1)S(1)}, bf16[128,768]{1,0:T(8,128)(2,1)}, u32[]{:S(2)}, u32[]{:S(2)}) collective-permute-start(bf16[128,768]{1,0:T(8,128)(2,1)S(1)} %fusion.7), channel_id=1, source_target_pairs={{0,2},{2,0},{1,3},{3,1},{4,6},{6,4},{5,7},{7,5},{8,10},{10,8},{9,1... | collective-permute-start | bytes 589832 | tf_op jit(solution)/shard_map/ppermute | solution.py:172
  20.7 32.3 %all-to-all-start = ((bf16[64,32,128]{2,1,0:T(8,128)(2,1)}), bf16[64,32,128]{2,1,0:T(8,128)(2,1)S(1)}, u32[]{:S(2)}, u32[]{:S(2)}) async-start(bf16[64,32,128]{2,1,0:T(8,128)(2,1)} %maximum_maximum_fusion), calls=%async_computation | async-start | bytes 1048576 | tf_op jit(solution)/shard_map/all_to_all | solution.py:214
  60.6 38.8 %all-to-all-start.1 = ((bf16[16,48,384]{2,1,0:T(8,128)(2,1)}), bf16[16,48,384]{2,1,0:T(8,128)(2,1)S(1)}, u32[]{:S(2)}, u32[]{:S(2)}) async-start(bf16[16,48,384]{2,1,0:T(8,128)(2,1)} %shard_map.104), calls=%async_computation.1 | async-start | bytes 1179648 | tf_op jit(solution)/shard_map/all_to_all | solution.py:225
  64.4 30.0 %collective-permute-start.1 = (bf16[256,768]{1,0:T(8,128)(2,1)S(1)}, bf16[256,768]{1,0:T(8,128)(2,1)S(1)}, u32[]{:S(2)}, u32[]{:S(2)}) collective-permute-start(bf16[256,768]{1,0:T(8,128)(2,1)S(1)} %pad_maximum_fusion.1), channel_id=1, source_target_pairs={{0,16},{16,0},{1,17},{17,1},{2,18},{18,2},{3,19},{19,3},{4,20},{20... | collective-permute-start | bytes 1179656 | tf_op jit(solution)/shard_map/ppermute | solution.py:172
  119.1 14.9 %all-to-all-start.3 = ((bf16[4,2,128,128]{3,2,1,0:T(8,128)(2,1)}), bf16[4,2,128,128]{3,2,1,0:T(8,128)(2,1)S(1)}, u32[]{:S(2)}, u32[]{:S(2)}) async-start(bf16[4,2,128,128]{3,2,1,0:T(8,128)(2,1)} %shard_map.106), calls=%async_computation.3 | async-start | bytes 524288 | tf_op jit(solution)/shard_map/all_to_all | solution.py:242
  135.5 27.7 %all-to-all-start.4 = ((bf16[64,16,128]{2,1,0:T(8,128)(2,1)}), bf16[64,16,128]{2,1,0:T(8,128)(2,1)S(1)}, u32[]{:S(2)}, u32[]{:S(2)}) async-start(bf16[64,16,128]{2,1,0:T(8,128)(2,1)} %bitcast.19), calls=%async_computation.4 | async-start | bytes 524288 | tf_op jit(solution)/shard_map/all_to_all | solution.py:254
  157.0 9.2 %copy-start.1 = (bf16[1,128,128]{2,1,0:T(8,128)(2,1)S(1)}, bf16[1,128,128]{2,1,0:T(8,128)(2,1)}, u32[]{:S(2)}) copy-start(bf16[1,128,128]{2,1,0:T(8,128)(2,1)} %param.11) | copy-start | bytes 98308
  157.0 9.2 %copy-start.2 = (bf16[12,128]{1,0:T(8,128)(2,1)S(1)}, bf16[12,128]{1,0:T(8,128)(2,1)}, u32[]{:S(2)}) copy-start(bf16[12,128]{1,0:T(8,128)(2,1)} %cw_ref.1) | copy-start | bytes 9220
Sparse Core Ops, SparseCore 0:
  11.1 102.8 all-gather.5

commit v4 on v3

v4 whole, which is shorter than its diff:
```python
import jax
import jax.numpy as jnp
from jax import lax
from jax.experimental import pallas as pl
from jax.experimental.pallas import tpu as pltpu
from jax.sharding import Mesh
from jax.sharding import PartitionSpec as P

ROWS = ("z", "y", "c")
ALL = ("a",) + ROWS
CHIPS = ("z", "y")
D, H, E, L, R = 768, 12, 64, 128, 128
BF, F32 = jnp.bfloat16, jnp.float32
VMEM = pl.BlockSpec(memory_space=pltpu.VMEM)
SMEM = pl.BlockSpec(memory_space=pltpu.SMEM)


def params():
    return pltpu.CompilerParams(vmem_limit_bytes=48 << 20)


def dot_nt(a, b):
    return lax.dot_general(a, b, (((1,), (1,)), ((), ())), preferred_element_type=F32)


def dot_tn(a, b):
    return lax.dot_general(a, b, (((0,), (0,)), ((), ())), preferred_element_type=F32)


def normalize(x):
    center = jnp.mean(x, axis=-1, keepdims=True)
    spread = jnp.mean(jnp.square(x - center), axis=-1, keepdims=True)
    return (x - center) * lax.rsqrt(spread + 1e-05)


def first_head(y):
    return 3 * (y // 2) + y % 2


def spread_columns(at_ref, picked_ref, out_ref):
    both = picked_ref[0].astype(F32) + picked_ref[1].astype(F32)
    second = at_ref[1] == 1
    parts = [
        jnp.where(second, both[:, 128 * n + E : 128 * n + 128], both[:, 128 * n : 128 * n + E]) for n in range(3)
    ]
    mine = jnp.concatenate(parts, axis=1).astype(BF)
    for n in range(8):
        out_ref[n] = mine


def project_and_tie(at_ref, w_ref, own_ref, *refs):
    near_refs, far_ref, tied_ref, v_ref = refs[:3], refs[3], refs[4], refs[5]
    w = w_ref[...]
    low = lax.broadcasted_iota(jnp.int32, (L, 2 * E), 1) < E
    total = jnp.zeros((L, L), F32)

    def rows_of(offset):
        if offset == 0:
            return [own_ref[core] for core in range(2)]
        if abs(offset) < 4:
            return [near_refs[abs(offset) - 1][int(offset > 0), core] for core in range(2)]
        return [jnp.concatenate([far_ref[0, core], far_ref[1, core]], axis=0) for core in range(2)]

    for offset in (0, -1, 1, -2, 2, -3, 3, 4):
        values = []
        for x in rows_of(offset):
            packed = jnp.dot(x, w, preferred_element_type=F32)
            both = packed[:, : 2 * E]
            q = jnp.where(low, both * E**-0.5, 0.0).astype(BF)
            k = pltpu.roll(both, E, 1).astype(BF)
            total += dot_nt(q, k)
            values.append(packed[:, 2 * E :])
        v_ref[lax.rem(at_ref[0] + (8 + offset), 8)] = jnp.concatenate(values, axis=1).astype(BF)
    part = (total * R**-0.5).astype(BF)
    for n in range(8):
        tied_ref[n] = part


def attend(span_ref, part_ref, bias_ref, probs_ref, scores_ref):
    scores = bias_ref[...].astype(F32)
    for n in range(8):
        scores += part_ref[n].astype(F32)
    j = lax.broadcasted_iota(jnp.int32, (L, L), 1)
    masked = jnp.where(j < span_ref[0], scores, -1e30)
    e = jnp.exp(masked - jnp.max(masked, axis=1, keepdims=True))
    probs_ref[...] = (e / jnp.sum(e, axis=1, keepdims=True)).astype(BF)
    scores_ref[...] = scores.astype(BF)


def blend(at_ref, probs_ref, scores_ref, v_ref, out_ref, held):
    parity = lax.rem(at_ref[0], 2)
    even = jnp.logical_and(parity == 0, at_ref[1] == 1)
    odd = jnp.logical_and(parity == 1, at_ref[1] == 0)
    for n in range(8):
        o = jnp.dot(probs_ref[...], v_ref[n], preferred_element_type=F32)
        if n in (0, 1):
            o = jnp.where(odd, scores_ref[n].astype(F32), o)
        if n in (4, 5):
            o = jnp.where(even, scores_ref[n - 4].astype(F32), o)
        held[:, n, :] = o
    out_ref[...] = held[...].astype(BF)


def column_block(c_ref, bl_ref, stack_ref, who_ref, wv_ref, wvo_ref, pair_ref, cw_ref, out_ref, pair_out_ref):
    mine = c_ref[0]
    lane = lax.broadcasted_iota(jnp.int32, (L, L), 1)
    row = lax.broadcasted_iota(jnp.int32, (L, L), 0)
    low = lax.broadcasted_iota(jnp.int32, (E, L), 1) < E
    early = lax.rem(lax.broadcasted_iota(jnp.int32, (E, L), 0), 8) < 4

    def tile(y, c, z):
        both = bl_ref[c, z * 8 + y].astype(F32)
        return jnp.where(mine == 0, both[:8], both[8:])

    def block(y, c):
        return jnp.concatenate([tile(y, c, z) for z in range(8)], axis=0)

    heads = []
    for n in range(4):
        shared = jnp.where(early, block(2 * n, 1), block(2 * n + 1, 0))
        heads += [block(2 * n, 0), shared, block(2 * n + 1, 1)]
    parts = []
    for n in range(6):
        first, second = heads[2 * n], heads[2 * n + 1]
        top = jnp.where(low, first, pltpu.roll(second, E, 1))
        bottom = jnp.where(low, pltpu.roll(first, E, 1), second)
        parts.append(jnp.concatenate([top, bottom], axis=0))
    blended = jnp.concatenate(parts, axis=1).astype(BF)

    updated = (dot_nt(who_ref[...], blended) + stack_ref[...].astype(F32)).astype(BF).astype(F32)
    center = jnp.mean(updated, axis=0, keepdims=True)
    spread = jnp.mean(jnp.square(updated - center), axis=0, keepdims=True)
    normed = ((updated - center) * lax.rsqrt(spread + 1e-05)).astype(BF)
    packed = jnp.dot(wv_ref[...], normed, preferred_element_type=F32)

    mixed = []
    for h in range(H):
        q = (packed[E * h : E * h + E] * E**-0.5).astype(BF)
        k = packed[D + E * h : D + E * h + E].astype(BF)
        v = packed[2 * D + E * h : 2 * D + E * h + E].astype(BF)
        logits = dot_tn(k, q)
        e = jnp.exp(logits - jnp.max(logits, axis=0, keepdims=True))
        probs = (e / jnp.sum(e, axis=0, keepdims=True)).astype(BF)
        mixed.append(jnp.dot(v, probs, preferred_element_type=F32).astype(BF))
    mixed = jnp.concatenate(mixed, axis=0)

    result = (updated + jnp.dot(wvo_ref[...], mixed, preferred_element_type=F32)).astype(BF)
    place = (row % 2 * E + row // 2 == lane).astype(BF)
    out_ref[...] = dot_nt(place, result).astype(BF)

    lines = []
    for n in range(4):
        even, odd = tile(2 * n, 1, 0), tile(2 * n + 1, 0, 0)
        lines += [even[4:5], even[5:6], odd[1:2]]
    scores = jnp.concatenate(lines + [jnp.zeros((L - H, L), F32)], axis=0).T
    weights = jnp.concatenate([cw_ref[...].astype(F32), jnp.zeros((L - H, L), F32)], axis=0)
    pair = pair_ref[...].astype(F32) + jnp.dot(
        scores.astype(BF), weights.astype(BF), preferred_element_type=F32
    )
    pair_out_ref[...] = pair.astype(BF)


def around(x):
    pairs = [(2 * y + c, (y + 1 - 2 * c) % 8 * 2 + c) for y in range(8) for c in range(2)]
    return lax.ppermute(x, ("y", "c"), pairs)


def both_cores(x):
    return lax.all_gather(x, "c", axis=0, tiled=False)


def call(kernel, out_shape, *args, scalars=0, scratch=()):
    return pl.pallas_call(
        kernel,
        out_shape=out_shape,
        in_specs=[SMEM] * scalars + [VMEM] * (len(args) - scalars),
        out_specs=jax.tree.map(lambda _: VMEM, out_shape),
        scratch_shapes=scratch,
        compiler_params=params(),
    )(*args)


def like(*dims, dtype=BF):
    return jax.ShapeDtypeStruct(dims, dtype)


def per_device(stack, spans, pair, w_triple, w_out, v_triple, v_out, offsets, contact_w):
    y, c = lax.axis_index("y").astype(jnp.int32), lax.axis_index("c").astype(jnp.int32)
    at, c1 = jnp.stack([y, c]), c[None]
    pair_own = pair.reshape(L, 128)
    own_row = stack.reshape(L, D)

    column_weights = jnp.concatenate([v_triple.T, v_out.T, w_out.T, jnp.zeros((2, D), BF)], axis=0)
    gathered = lax.all_gather(column_weights, ROWS, axis=0, tiled=False)

    bias = lax.dot_general(offsets, pair_own, (((0,), (1,)), ((), ())), preferred_element_type=F32).astype(BF)
    bias_pairs = jnp.stack([bias[first_head(n) : first_head(n) + 2] for n in range(8)])
    slices = w_triple.T.reshape(18, 8, 96).transpose(1, 0, 2).reshape(8, 1, 18, 96)
    slices = jnp.pad(slices, ((0, 0), (0, 0), (0, 0), (0, 32)))
    message = jnp.concatenate(
        [
            jnp.broadcast_to(slices, (8, 8, 18, 128)).reshape(64, 18, 128),
            own_row.reshape(64, 12, 128),
            jnp.broadcast_to(bias_pairs[None], (8, 8, 2, 128)).reshape(64, 2, 128),
        ],
        axis=1,
    )
    came = lax.all_to_all(message, CHIPS, 0, 0, tiled=True)

    normed = normalize(own_row.astype(F32)).astype(BF)
    own = both_cores(normed)
    first = around(own)
    second = around(first)
    third = around(second)
    fourth = around(jnp.where(c == 0, third[:, : L // 2], third[:, L // 2 :]))

    source = lax.broadcasted_iota(jnp.int32, (2048, 384), 0)
    target = lax.broadcasted_iota(jnp.int32, (2048, 384), 1)
    column = (source // 32 * 2 + c) * 18 + source % 32
    wanted = target // 128 * D + first_head(y) * E + target % 128
    pick = jnp.logical_and(column == wanted, source % 32 < 18).astype(BF)
    came, second, pick = lax.optimization_barrier((came, second, pick))
    picked = both_cores(dot_tn(came.reshape(2048, 128), pick)[:96].astype(BF))
    copies = call(spread_columns, like(8, 96, 192), at, picked, scalars=1)
    w_head = lax.all_to_all(copies, "z", 0, 0, tiled=True).reshape(D, 192)

    rest = both_cores(came[:, 18:])
    stack_own = rest[:, :, :12].reshape(2, 64, 2, D)
    stack_own = lax.dynamic_index_in_dim(stack_own, c, 2, keepdims=False).reshape(R, D).T
    bias_own = lax.dynamic_index_in_dim(rest[:, :, 12:], c, 2, keepdims=False)
    bias_own = bias_own.transpose(1, 0, 2).reshape(L, L)

    tied, values = call(
        project_and_tie,
        (like(8, L, L), like(8, L, 2 * E)),
        at,
        w_head,
        own,
        both_cores(first),
        both_cores(second),
        both_cores(third),
        both_cores(fourth),
        scalars=1,
    )
    parts = lax.all_to_all(tied, "z", 0, 0, tiled=True)
    probs, scores = call(attend, (like(L, L), like(L, L)), spans, parts, bias_own, scalars=1)
    message = call(
        blend,
        like(L, 8, 2 * E),
        at,
        probs,
        both_cores(scores),
        values,
        scalars=1,
        scratch=[pltpu.VMEM((L, 8, 2 * E), F32)],
    )
    came = lax.all_to_all(message.reshape(64, 16, 128), CHIPS, 0, 0, tiled=True)

    column_triple = gathered[:, :18].reshape(3 * D, D)
    column_out = gathered[:, 18:24].reshape(D, D)
    row_out = gathered[:, 24:30].reshape(D, D)
    came, column_triple, column_out, row_out = lax.optimization_barrier(
        (came, column_triple, column_out, row_out)
    )
    blended = lax.all_gather(came, "c", axis=0, tiled=False)

    alignment, pair_out = call(
        column_block,
        (like(R, D), like(L, 128)),
        c1,
        blended,
        stack_own,
        row_out,
        column_triple,
        column_out,
        pair_own,
        contact_w,
        scalars=1,
    )
    return alignment.reshape(R, 1, D), pair_out.reshape(1, L, 128)


def solution(mesh):
    torus = Mesh(mesh.devices.reshape(mesh.shape["aln"], 8, 8, 2), ALL)
    in_specs = (
        P(ALL, None, None),
        P("a"),
        P(ALL, None, None),
        P(None, ROWS),
        P(None, ROWS),
        P(None, ROWS),
        P(None, ROWS),
        P(),
        P(),
    )
    out_specs = (P("a", ROWS, None), P(ALL, None, None))
    return jax.shard_map(
        per_device, mesh=torus, in_specs=in_specs, out_specs=out_specs, check_vma=False
    )
```

time: 183 us -> 163 us (0.89)
  waiting for transfers between devices: 41.4 us -> 26 us
  blocking collectives: 35.6 us -> 23.2 us
  starting transfers between devices: 41.5 us -> 51.5 us
  other arithmetic: 9.89 us -> 5.79 us
    all_to_all x1 -> x0, blocking collectives: 16.3 us -> none  [per_device(): parts = lax.all_to_all(tied, 'zh', 0, 0, tiled=True)]
    ppermute x2 -> x4, waiting for transfers between devices: 27 us -> 13.3 us  [around(): return lax.ppermute(x, ('y', 'c'), pairs)]
    all_to_all x1, waiting for transfers between devices: 13 us -> 0.01 us  [per_device(): came = lax.all_to_all(message, CHIPS, 0, 0, tiled=True)]
    all_to_all x2, waiting for transfers between devices: 1.4 us -> 12.7 us  [the longest x1 9.24 us: per_device(): parts = lax.all_to_all(tied, 'z', 0, 0, tiled=True)]
    ppermute x2 -> x4, starting transfers between devices: 6.96 us -> 16.8 us  [around(): return lax.ppermute(x, ('y', 'c'), pairs)]
    all_gather x4 -> x8, blocking collectives: 16.3 us -> 20.6 us  [both_cores(): return lax.all_gather(x, 'c', axis=0, tiled=False)]
    concatenate x3 -> x1, other arithmetic: 2.3 us -> 0.07 us  [per_device(): jnp.concatenate([jnp.broadcast_to(slices, (8, 8, 18, 128)).reshape(64, 18...]
    reshape x1, local copies, waits for them, and re-layouts: 0.41 us -> 2.32 us  [per_device(): row_out = gathered[:, 24:30].reshape(D, D)]
  transfers between devices with their start and end apart: 7 -> 9, of which waited for: 3 -> 5; matrix products, arithmetic and copies ran while one was open for 18% -> 17% of each run, Pallas kernels for 3% -> 4%
where the time goes in v4:
time: 163 us; the launch traced here: 162 us
  starting transfers between devices  51.5 us (32%)
  waiting for transfers between devices  26 us (16%)
  local copies, waits for them, and re-layouts  23.5 us (14%)
  blocking collectives  23.2 us (14%)
  Pallas kernels  15.1 us (9%)
  between operations  15.1 us (9%)
  other arithmetic  5.79 us (4%)
    all_gather x8, blocking collectives, both_cores(): return lax.all_gather(x, 'c', axis=0, tiled=False)  20.6 us
    all_to_all x1, starting transfers between devices, per_device(): came = lax.all_to_all(message, CHIPS, 0, 0, tiled=True)  17.1 us
    ppermute x4, starting transfers between devices, around(): return lax.ppermute(x, ('y', 'c'), pairs)  16.8 us
    pallas_call x5, Pallas kernels, call(): pl.pallas_call(kernel, out_shape=out_shape, in_specs=[SMEM] * scalars + [...  15.1 us
    ppermute x4, waiting for transfers between devices, around(): return lax.ppermute(x, ('y', 'c'), pairs)  13.3 us
    all_to_all x1, waiting for transfers between devices, per_device(): parts = lax.all_to_all(tied, 'z', 0, 0, tiled=True)  9.24 us
    all_to_all x1, starting transfers between devices, per_device(): came = lax.all_to_all(message.reshape(64, 16, 128), CHIPS, 0, 0, tiled=True)  6.96 us
    all_to_all x1, starting transfers between devices, per_device(): w_head = lax.all_to_all(copies, 'z', 0, 0, tiled=True).reshape(D, 192)  6.57 us
  transfers between devices with their start and end apart: 9, of which 5 were waited for; matrix products, arithmetic and copies ran while one was open for 17% of the time, Pallas kernels for 4%

profile of v4, /device:TPU:1, one launch (start us, length us, event | category | flops | bytes accessed | tf_op | source)
XLA Modules:
  0.0 161.6 jit_solution(6819532214967526007)
XLA Ops:
  7.2 0.0 copy-start
  7.2 0.0 copy-start.8
  7.2 0.0 all-gather.11.cloned.1.call-start
  7.2 0.1 pad.8.clone
  7.3 1.5 maximum_maximum_fusion
  8.8 0.0 all-gather.11.cloned.1.call-update
  8.9 0.9 convolution_convert_fusion
  9.9 1.1 reshape_reshape.3
  11.0 0.1 copy.26
  11.1 0.9 reshape.82
  12.0 0.1 broadcast_bitcast_fusion
  12.0 0.1 pad_maximum_fusion
  12.1 1.2 copy.27
  13.3 17.1 %all-to-all-start = ((bf16[64,32,128]{2,1,0:T(8,128)(2,1)}), bf16[64,32,128]{2,1,0:T(8,128)(2,1)S(1)}, u32[]{:S(2)}, u32[]{:S(2)}) async-start(bf16[64,32,128]{2,1,0:T(8,128)(2,1)} %copy.27), calls=%async_computation | async-start | bytes 1048576 | tf_op jit(solution)/shard_map/all_to_all | solution.py:208
  30.4 0.1 convert_reduce_fusion
  30.6 0.2 fusion.7
  30.8 0.1 fusion.4
  30.9 2.7 %all_gather.58.own_ref = bf16[2,128,768]{2,1,0:T(8,128)(2,1)S(1)} all-gather(bf16[1,128,768]{2,1,0:T(8,128)(2,1)S(1)} %fusion.4), channel_id=1, replica_groups=mesh['a'=4,'z'=8,'y'=8,'c'=2] {'c'}, dimensions={0}, use_global_device_ids=true | all-gather | bytes 589824 | tf_op jit(solution)/shard_map/all_gather | solution.py:169
  33.6 4.4 %collective-permute-start = (bf16[2,128,768]{2,1,0:T(8,128)(2,1)S(1)}, bf16[2,128,768]{2,1,0:T(8,128)(2,1)}, u32[]{:S(2)}, u32[]{:S(2)}) collective-permute-start(bf16[2,128,768]{2,1,0:T(8,128)(2,1)S(1)} %all_gather.58.own_ref), channel_id=1, source_target_pairs={{0,2},{1,15},{2,4},{3,1},{4,6},{5,3},{6,8},{7,5},{8,10},{9,7},{10,... | collective-permute-start | bytes 1179656 | tf_op jit(solution)/shard_map/ppermute | solution.py:165
  38.1 10.8 %collective-permute-done = bf16[2,128,768]{2,1,0:T(8,128)(2,1)} collective-permute-done((bf16[2,128,768]{2,1,0:T(8,128)(2,1)S(1)}, bf16[2,128,768]{2,1,0:T(8,128)(2,1)}, u32[]{:S(2)}, u32[]{:S(2)}) %collective-permute-start) | collective-permute-done | bytes 393248 | tf_op jit(solution)/shard_map/ppermute | solution.py:165
  48.9 3.2 %collective-permute-start.1 = (bf16[2,128,768]{2,1,0:T(8,128)(2,1)}, bf16[2,128,768]{2,1,0:T(8,128)(2,1)}, u32[]{:S(2)}, u32[]{:S(2)}) collective-permute-start(bf16[2,128,768]{2,1,0:T(8,128)(2,1)} %collective-permute-done), channel_id=1, source_target_pairs={{0,2},{1,15},{2,4},{3,1},{4,6},{5,3},{6,8},{7,5},{8,10},{9,7},{10,... | collective-permute-start | bytes 1179656 | tf_op jit(solution)/shard_map/ppermute | solution.py:165
  52.1 2.6 %fusion.2 = bf16[2048,384]{1,0:T(8,128)(2,1)S(1)} fusion(s32[384]{0:T(512)S(1)} %get-tuple-element.37, s32[384]{0:T(512)S(1)} %get-tuple-element.38, s32[]{:T(128)S(6)} %mul.34, s32[384]{0:T(512)S(1)} %get-tuple-element.36, s32[384]{0:T(512)S(1)} %get-tuple-element.39, s32[2048]{0:T(1024)S(1)} %get-tuple-element.31, s32[2048]{0:T(1024)S(1)} %get-tuple-element.32, ...), kind=kLoop, calls=%fused_computation.4 | loop fusion | flops 11796480 | bytes 1616648 | tf_op jit(solution)/shard_map/convert_element_type | solution.py:221
  54.7 0.1 pad_add_fusion.at_ref
  54.8 2.6 %all-gather.1 = bf16[4,128,768]{2,1,0:T(8,128)(2,1)S(1)} all-gather(bf16[2,128,768]{2,1,0:T(8,128)(2,1)} %collective-permute-done), channel_id=3, replica_groups=mesh['a'=4,'z'=8,'y'=8,'c'=2] {'c'}, dimensions={0}, use_global_device_ids=true | all-gather | bytes 1179648 | tf_op jit(solution)/shard_map/all_gather | solution.py:169
  57.3 1.0 collective-permute-done.1
  58.4 4.4 %collective-permute-start.2 = (bf16[2,128,768]{2,1,0:T(8,128)(2,1)}, bf16[2,128,768]{2,1,0:T(8,128)(2,1)}, u32[]{:S(2)}, u32[]{:S(2)}) collective-permute-start(bf16[2,128,768]{2,1,0:T(8,128)(2,1)} %collective-permute-done.1), channel_id=1, source_target_pairs={{0,2},{1,15},{2,4},{3,1},{4,6},{5,3},{6,8},{7,5},{8,10},{9,7},{10,... | collective-permute-start | bytes 1179656 | tf_op jit(solution)/shard_map/ppermute | solution.py:165
  62.8 0.0 all-to-all-done
  62.8 0.5 fusion.22
  63.3 2.7 %all-gather = bf16[192,384]{1,0:T(8,128)(2,1)S(1)} all-gather(bf16[96,384]{1,0:T(8,128)(2,1)S(1)} %slice.113), channel_id=2, replica_groups=mesh['a'=4,'z'=8,'y'=8,'c'=2] {'c'}, dimensions={0}, use_global_device_ids=true | all-gather | bytes 221184 | tf_op jit(solution)/shard_map/all_gather | solution.py:169
  66.0 1.5 shard_map.104
  67.5 6.6 %all-to-all-start.1 = ((bf16[8,96,192]{2,1,0:T(8,128)(2,1)}), bf16[8,96,192]{2,1,0:T(8,128)(2,1)S(1)}, u32[]{:S(2)}, u32[]{:S(2)}) async-start(bf16[8,96,192]{2,1,0:T(8,128)(2,1)} %shard_map.104), calls=%async_computation.1 | async-start | bytes 786432 | tf_op jit(solution)/shard_map/all_to_all | solution.py:225
  74.1 2.8 %all-gather.2 = bf16[4,128,768]{2,1,0:T(8,128)(2,1)S(1)} all-gather(bf16[2,128,768]{2,1,0:T(8,128)(2,1)} %collective-permute-done.1), channel_id=4, replica_groups=mesh['a'=4,'z'=8,'y'=8,'c'=2] {'c'}, dimensions={0}, use_global_device_ids=true | all-gather | bytes 1179648 | tf_op jit(solution)/shard_map/all_gather | solution.py:169
  76.9 1.0 slice_select_fusion
  78.0 4.8 %collective-permute-start.3 = (bf16[2,64,768]{2,1,0:T(8,128)(2,1)S(1)}, bf16[2,64,768]{2,1,0:T(8,128)(2,1)S(1)}, u32[]{:S(2)}, u32[]{:S(2)}) collective-permute-start(bf16[2,64,768]{2,1,0:T(8,128)(2,1)S(1)} %slice_select_fusion), channel_id=1, source_target_pairs={{0,2},{1,15},{2,4},{3,1},{4,6},{5,3},{6,8},{7,5},{8,10},{9,7},{10,... | collective-permute-start | bytes 589832 | tf_op jit(solution)/shard_map/ppermute | solution.py:165
  82.8 2.7 %all-gather.3 = bf16[4,128,768]{2,1,0:T(8,128)(2,1)S(1)} all-gather(bf16[2,128,768]{2,1,0:T(8,128)(2,1)} %collective-permute-done.2), channel_id=5, replica_groups=mesh['a'=4,'z'=8,'y'=8,'c'=2] {'c'}, dimensions={0}, use_global_device_ids=true | all-gather | bytes 1179648 | tf_op jit(solution)/shard_map/all_gather | solution.py:169
  85.5 1.4 collective-permute-done.3
  86.9 2.5 %all-gather.4 = bf16[4,64,768]{2,1,0:T(8,128)(2,1)S(1)} all-gather(bf16[2,64,768]{2,1,0:T(8,128)(2,1)S(1)} %collective-permute-done.3), channel_id=6, replica_groups=mesh['a'=4,'z'=8,'y'=8,'c'=2] {'c'}, dimensions={0}, use_global_device_ids=true | all-gather | bytes 589824 | tf_op jit(solution)/shard_map/all_gather | solution.py:169
  89.4 3.5 %all-to-all-done.1 = bf16[8,96,192]{2,1,0:T(8,128)(2,1)S(1)} async-done(((bf16[8,96,192]{2,1,0:T(8,128)(2,1)}), bf16[8,96,192]{2,1,0:T(8,128)(2,1)S(1)}, u32[]{:S(2)}, u32[]{:S(2)}) %all-to-all-start.1) | async-done | bytes 294944 | tf_op jit(solution)/shard_map/all_to_all | solution.py:225
  92.8 3.1 %shard_map.105 = (bf16[8,128,128]{2,1,0:T(8,128)(2,1)S(1)}, bf16[8,128,128]{2,1,0:T(8,128)(2,1)S(1)}) custom-call(s32[2]{0:T(128)S(1)} %pad_add_fusion.at_ref, bf16[768,192]{1,0:T(8,128)(2,1)S(1)} %bitcast.86, bf16[2,128,768]{2,1,0:T(8,128)(2,1)S(1)} %all_gather.58.own_ref, bf16[2,2,128,768]{3,2,1,0:T(8,128)(2,1)S(1)} %bitcast.82, ...), custom_call_target="tpu_custom_call" | custom-call | tf_op jit(solution)/shard_map/pallas_call | solution.py:173
  96.0 0.7 copy-done.1
  96.7 0.7 copy-done.3
  97.3 4.0 %all-to-all-start.2 = ((bf16[8,128,128]{2,1,0:T(8,128)(2,1)}), bf16[8,128,128]{2,1,0:T(8,128)(2,1)S(1)}, u32[]{:S(2)}, u32[]{:S(2)}) async-start(bf16[8,128,128]{2,1,0:T(8,128)(2,1)} %copy-done.3), calls=%async_computation.2 | async-start | bytes 524288 | tf_op jit(solution)/shard_map/all_to_all | solution.py:245
  102.0 1.3 copy.28
  103.3 2.4 %all-gather.5 = bf16[128,14,128]{2,0,1:T(8,128)(2,1)S(1)} all-gather(bf16[64,14,128]{2,0,1:T(8,128)(2,1)S(1)} %slice.80), channel_id=7, replica_groups=mesh['a'=4,'z'=8,'y'=8,'c'=2] {'c'}, dimensions={0}, use_global_device_ids=true | all-gather | bytes 688128 | tf_op jit(solution)/shard_map/all_gather | solution.py:169
  105.8 9.2 %all-to-all-done.2.part_ref = bf16[8,128,128]{2,1,0:T(8,128)(2,1)S(1)} async-done(((bf16[8,128,128]{2,1,0:T(8,128)(2,1)}), bf16[8,128,128]{2,1,0:T(8,128)(2,1)S(1)}, u32[]{:S(2)}, u32[]{:S(2)}) %all-to-all-start.2) | async-done | bytes 262176 | tf_op jit(solution)/shard_map/all_to_all | solution.py:245
  115.0 0.2 shard_map.106
  115.2 2.2 %all-gather.6 = bf16[256,128]{1,0:T(8,128)(2,1)S(1)} all-gather(bf16[128,128]{1,0:T(8,128)(2,1)S(1)} %get-tuple-element.20), channel_id=8, replica_groups=mesh['a'=4,'z'=8,'y'=8,'c'=2] {'c'}, dimensions={0}, use_global_device_ids=true | all-gather | bytes 98304 | tf_op jit(solution)/shard_map/all_gather | solution.py:169
  117.4 1.7 %shard_map.107 = bf16[128,8,128]{2,1,0:T(8,128)(2,1)} custom-call(s32[2]{0:T(128)S(1)} %pad_add_fusion.at_ref, bf16[128,128]{1,0:T(8,128)(2,1)S(1)} %get-tuple-element.19.probs_ref, bf16[2,128,128]{2,1,0:T(8,128)(2,1)S(1)} %bitcast.90, bf16[8,128,128]{2,1,0:T(8,128)(2,1)S(1)} %copy-done.2), custom_call_target="tpu_custom_call" | custom-call | tf_op jit(solution)/shard_map/pallas_call | solution.py:173
  119.1 7.0 %all-to-all-start.3 = ((bf16[64,16,128]{2,1,0:T(8,128)(2,1)}), bf16[64,16,128]{2,1,0:T(8,128)(2,1)S(1)}, u32[]{:S(2)}, u32[]{:S(2)}) async-start(bf16[64,16,128]{2,1,0:T(8,128)(2,1)} %bitcast.30), calls=%async_computation.3 | async-start | bytes 524288 | tf_op jit(solution)/shard_map/all_to_all | solution.py:257
  126.1 0.3 copy.30
  126.4 0.2 reshape.94
  126.7 0.4 constant_dynamic-slice_fusion
  127.1 0.2 copy.31
  127.3 0.0 all-gather.11.cloned.1.call-done
  127.3 5.1 %slice.82 = bf16[128,18,768]{2,1,0:T(8,128)(2,1)} slice(bf16[128,32,768]{2,1,0:T(8,128)(2,1)} %bitcast.93), slice={[0:128], [0:18], [0:768]} | slice | bytes 7077888 | tf_op jit(solution)/shard_map/slice | solution.py:259
  132.4 0.2 copy-done.6
  132.5 1.7 %fusion.21 = (bf16[128,6,768]{2,1,0:T(8,128)(2,1)}, bf16[128,6,768]{2,1,0:T(8,128)(2,1)S(1)}) fusion(bf16[128,32,768]{2,1,0:T(8,128)(2,1)S(1)} %bitcast.94), kind=kLoop, calls=%fused_computation.63 | loop fusion | bytes 4718592 | tf_op jit(solution)/shard_map/slice | solution.py:261
  134.2 0.4 reshape.92.wvo_ref
  134.6 2.3 %reshape.93.who_ref = bf16[768,768]{1,0:T(8,128)(2,1)S(1)} reshape(bf16[128,6,768]{2,1,0:T(8,128)(2,1)} %get-tuple-element.28) | data formatting | bytes 2359296 | tf_op jit(solution)/shard_map/reshape | solution.py:261
  136.9 0.0 copy-start.4
  137.0 0.0 copy-start.5
  137.0 6.6 %reshape.91.wv_ref = bf16[2304,768]{1,0:T(8,128)(2,1)} reshape(bf16[128,18,768]{2,1,0:T(8,128)(2,1)} %slice.82) | data formatting | bytes 7077888 | tf_op jit(solution)/shard_map/reshape | solution.py:259
  143.5 2.6 %all-gather.8 = bf16[128,16,128]{2,1,0:T(8,128)(2,1)S(1)} all-gather(bf16[64,16,128]{2,1,0:T(8,128)(2,1)S(1)} %all-to-all-done.3), channel_id=10, replica_groups=mesh['a'=4,'z'=8,'y'=8,'c'=2] {'c'}, dimensions={0}, use_global_device_ids=true | all-gather | bytes 786432 | tf_op jit(solution)/shard_map/all_gather | solution.py:265
  146.1 8.6 %shard_map.108 = (bf16[128,768]{1,0:T(8,128)(2,1)}, bf16[128,128]{1,0:T(8,128)(2,1)}) custom-call(s32[1]{0:T(128)} %bitcast.c_ref, bf16[2,64,16,128]{3,2,1,0:T(8,128)(2,1)S(1)} %bitcast.85, bf16[768,128]{1,0:T(8,128)(2,1)S(1)} %bitcast.88, bf16[768,768]{1,0:T(8,128)(2,1)S(1)} %reshape.93.who_ref, bf16[2304,768]{1,0:T(8,128)(2,1)} %reshape.91.wv_ref, ...), custom_call_target="tpu_custom_call" | custom-call | tf_op jit(solution)/shard_map/pallas_call | solution.py:173
  (40 shorter events, 0.3 us)
Async XLA Ops:
  7.2 1.7 %copy-start = (bf16[128,12]{0,1:T(8,128)(2,1)S(1)}, bf16[128,12]{0,1:T(8,128)(2,1)}, u32[]{:S(2)}) copy-start(bf16[128,12]{0,1:T(8,128)(2,1)} %param.16) | copy-start | bytes 9220
  7.2 23.2 %copy-start.8 = (bf16[1,128,768]{2,1,0:T(8,128)(2,1)S(1)}, bf16[1,128,768]{2,1,0:T(8,128)(2,1)}, u32[]{:S(2)}) copy-start(bf16[1,128,768]{2,1,0:T(8,128)(2,1)} %param.9) | copy-start | bytes 589828
  7.2 120.1 %all-gather.11.cloned.1.call-start = ((), (), s32[]{:S(2)}) async-start(), calls=%async_computation.4 | async-start | bytes 6340608 | tf_op jit(solution)/shard_map/all_gather | solution.py:194
  13.3 49.5 %all-to-all-start = ((bf16[64,32,128]{2,1,0:T(8,128)(2,1)}), bf16[64,32,128]{2,1,0:T(8,128)(2,1)S(1)}, u32[]{:S(2)}, u32[]{:S(2)}) async-start(bf16[64,32,128]{2,1,0:T(8,128)(2,1)} %copy.27), calls=%async_computation | async-start | bytes 1048576 | tf_op jit(solution)/shard_map/all_to_all | solution.py:208
  33.6 15.3 %collective-permute-start = (bf16[2,128,768]{2,1,0:T(8,128)(2,1)S(1)}, bf16[2,128,768]{2,1,0:T(8,128)(2,1)}, u32[]{:S(2)}, u32[]{:S(2)}) collective-permute-start(bf16[2,128,768]{2,1,0:T(8,128)(2,1)S(1)} %all_gather.58.own_ref), channel_id=1, source_target_pairs={{0,2},{1,15},{2,4},{3,1},{4,6},{5,3},{6,8},{7,5},{8,10},{9,7},{10,... | collective-permute-start | bytes 1179656 | tf_op jit(solution)/shard_map/ppermute | solution.py:165
  48.9 9.4 %collective-permute-start.1 = (bf16[2,128,768]{2,1,0:T(8,128)(2,1)}, bf16[2,128,768]{2,1,0:T(8,128)(2,1)}, u32[]{:S(2)}, u32[]{:S(2)}) collective-permute-start(bf16[2,128,768]{2,1,0:T(8,128)(2,1)} %collective-permute-done), channel_id=1, source_target_pairs={{0,2},{1,15},{2,4},{3,1},{4,6},{5,3},{6,8},{7,5},{8,10},{9,7},{10,... | collective-permute-start | bytes 1179656 | tf_op jit(solution)/shard_map/ppermute | solution.py:165
  58.4 18.6 %collective-permute-start.2 = (bf16[2,128,768]{2,1,0:T(8,128)(2,1)}, bf16[2,128,768]{2,1,0:T(8,128)(2,1)}, u32[]{:S(2)}, u32[]{:S(2)}) collective-permute-start(bf16[2,128,768]{2,1,0:T(8,128)(2,1)} %collective-permute-done.1), channel_id=1, source_target_pairs={{0,2},{1,15},{2,4},{3,1},{4,6},{5,3},{6,8},{7,5},{8,10},{9,7},{10,... | collective-permute-start | bytes 1179656 | tf_op jit(solution)/shard_map/ppermute | solution.py:165
  62.8 15.2 %copy-start.7 = (bf16[64,32,128]{2,1,0:T(8,128)(2,1)}, bf16[64,32,128]{2,1,0:T(8,128)(2,1)S(1)}, u32[]{:S(2)}) copy-start(bf16[64,32,128]{2,1,0:T(8,128)(2,1)S(1)} %all-to-all-done) | copy-start | bytes 1572868
  67.5 25.3 %all-to-all-start.1 = ((bf16[8,96,192]{2,1,0:T(8,128)(2,1)}), bf16[8,96,192]{2,1,0:T(8,128)(2,1)S(1)}, u32[]{:S(2)}, u32[]{:S(2)}) async-start(bf16[8,96,192]{2,1,0:T(8,128)(2,1)} %shard_map.104), calls=%async_computation.1 | async-start | bytes 786432 | tf_op jit(solution)/shard_map/all_to_all | solution.py:225
  78.0 8.9 %collective-permute-start.3 = (bf16[2,64,768]{2,1,0:T(8,128)(2,1)S(1)}, bf16[2,64,768]{2,1,0:T(8,128)(2,1)S(1)}, u32[]{:S(2)}, u32[]{:S(2)}) collective-permute-start(bf16[2,64,768]{2,1,0:T(8,128)(2,1)S(1)} %slice_select_fusion), channel_id=1, source_target_pairs={{0,2},{1,15},{2,4},{3,1},{4,6},{5,3},{6,8},{7,5},{8,10},{9,7},{10,... | collective-permute-start | bytes 589832 | tf_op jit(solution)/shard_map/ppermute | solution.py:165
  95.9 0.7 copy-start.1
  96.7 0.7 copy-start.3
  97.3 20.1 %copy-start.2 = (bf16[8,128,128]{2,1,0:T(8,128)(2,1)S(1)}, bf16[8,128,128]{2,1,0:T(8,128)(2,1)}, u32[]{:S(2)}) copy-start(bf16[8,128,128]{2,1,0:T(8,128)(2,1)} %copy-done.1) | copy-start | bytes 786436
  97.3 17.7 %all-to-all-start.2 = ((bf16[8,128,128]{2,1,0:T(8,128)(2,1)}), bf16[8,128,128]{2,1,0:T(8,128)(2,1)S(1)}, u32[]{:S(2)}, u32[]{:S(2)}) async-start(bf16[8,128,128]{2,1,0:T(8,128)(2,1)} %copy-done.3), calls=%async_computation.2 | async-start | bytes 524288 | tf_op jit(solution)/shard_map/all_to_all | solution.py:245
  119.1 24.4 %all-to-all-start.3 = ((bf16[64,16,128]{2,1,0:T(8,128)(2,1)}), bf16[64,16,128]{2,1,0:T(8,128)(2,1)S(1)}, u32[]{:S(2)}, u32[]{:S(2)}) async-start(bf16[64,16,128]{2,1,0:T(8,128)(2,1)} %bitcast.30), calls=%async_computation.3 | async-start | bytes 524288 | tf_op jit(solution)/shard_map/all_to_all | solution.py:257
  127.3 5.2 %copy-start.6 = (bf16[4096,768]{1,0:T(8,128)(2,1)S(1)}, bf16[4096,768]{1,0:T(8,128)(2,1)}, u32[]{:S(2)}) copy-start(bf16[4096,768]{1,0:T(8,128)(2,1)} %all-gather.11.cloned.1.call-done) | copy-start | bytes 18874372
  136.9 9.2 %copy-start.4 = (bf16[1,128,128]{2,1,0:T(8,128)(2,1)S(1)}, bf16[1,128,128]{2,1,0:T(8,128)(2,1)}, u32[]{:S(2)}) copy-start(bf16[1,128,128]{2,1,0:T(8,128)(2,1)} %param.11) | copy-start | bytes 98308
  137.0 9.2 %copy-start.5 = (bf16[12,128]{1,0:T(8,128)(2,1)S(1)}, bf16[12,128]{1,0:T(8,128)(2,1)}, u32[]{:S(2)}) copy-start(bf16[12,128]{1,0:T(8,128)(2,1)} %cw_ref.1) | copy-start | bytes 9220
Sparse Core Ops, SparseCore 0:
  11.7 102.6 all-gather.10

commit v5 on v4

--- a/solution.py
+++ b/solution.py
@@ -37,15 +37,13 @@
     return 3 * (y // 2) + y % 2
 
 
-def spread_columns(at_ref, picked_ref, out_ref):
+def own_columns(at_ref, picked_ref, out_ref):
     both = picked_ref[0].astype(F32) + picked_ref[1].astype(F32)
     second = at_ref[1] == 1
     parts = [
         jnp.where(second, both[:, 128 * n + E : 128 * n + 128], both[:, 128 * n : 128 * n + E]) for n in range(3)
     ]
-    mine = jnp.concatenate(parts, axis=1).astype(BF)
-    for n in range(8):
-        out_ref[n] = mine
+    out_ref[...] = jnp.concatenate(parts, axis=1).astype(BF)
 
 
 def project_and_tie(at_ref, w_ref, own_ref, *refs):
@@ -193,38 +191,52 @@
     column_weights = jnp.concatenate([v_triple.T, v_out.T, w_out.T, jnp.zeros((2, D), BF)], axis=0)
     gathered = lax.all_gather(column_weights, ROWS, axis=0, tiled=False)
 
-    bias = lax.dot_general(offsets, pair_own, (((0,), (1,)), ((), ())), preferred_element_type=F32).astype(BF)
-    bias_pairs = jnp.stack([bias[first_head(n) : first_head(n) + 2] for n in range(8)])
-    slices = w_triple.T.reshape(18, 8, 96).transpose(1, 0, 2).reshape(8, 1, 18, 96)
-    slices = jnp.pad(slices, ((0, 0), (0, 0), (0, 0), (0, 32)))
-    message = jnp.concatenate(
-        [
-            jnp.broadcast_to(slices, (8, 8, 18, 128)).reshape(64, 18, 128),
-            own_row.reshape(64, 12, 128),
-            jnp.broadcast_to(bias_pairs[None], (8, 8, 2, 128)).reshape(64, 2, 128),
-        ],
-        axis=1,
-    )
-    came = lax.all_to_all(message, CHIPS, 0, 0, tiled=True)
-
     normed = normalize(own_row.astype(F32)).astype(BF)
     own = both_cores(normed)
     first = around(own)
     second = around(first)
     third = around(second)
-    fourth = around(jnp.where(c == 0, third[:, : L // 2], third[:, L // 2 :]))
-
-    source = lax.broadcasted_iota(jnp.int32, (2048, 384), 0)
-    target = lax.broadcasted_iota(jnp.int32, (2048, 384), 1)
-    column = (source // 32 * 2 + c) * 18 + source % 32
-    wanted = target // 128 * D + first_head(y) * E + target % 128
-    pick = jnp.logical_and(column == wanted, source % 32 < 18).astype(BF)
-    came, second, pick = lax.optimization_barrier((came, second, pick))
-    picked = both_cores(dot_tn(came.reshape(2048, 128), pick)[:96].astype(BF))
-    copies = call(spread_columns, like(8, 96, 192), at, picked, scalars=1)
-    w_head = lax.all_to_all(copies, "z", 0, 0, tiled=True).reshape(D, 192)
-
-    rest = both_cores(came[:, 18:])
+    last = jnp.where(c == 0, third[:, : L // 2], third[:, L // 2 :])
+
+    bias = lax.dot_general(offsets, pair_own, (((0,), (1,)), ((), ())), preferred_element_type=F32).astype(BF)
+    bias_pairs = jnp.stack([bias[first_head(n) : first_head(n) + 2] for n in range(8)])
+    quarter = lax.dynamic_slice_in_dim(w_triple, lax.axis_index("a") * 192, 192, axis=0).T
+    tail = jnp.concatenate([quarter[:9, 128:], quarter[9:, 128:]], axis=1)
+    quarter = jnp.concatenate([quarter[:, :128], tail], axis=0)
+    message = jnp.concatenate(
+        [
+            jnp.broadcast_to(quarter, (64, 27, 128)),
+            jnp.zeros((64, 5, 128), BF),
+            own_row.reshape(64, 12, 128),
+            jnp.broadcast_to(bias_pairs[None], (8, 8, 2, 128)).reshape(64, 2, 128),
+            jnp.zeros((64, 2, 128), BF),
+        ],
+        axis=1,
+    )
+    message, own = lax.optimization_barrier((message, own))
+    came = lax.all_to_all(message, CHIPS, 0, 0, tiled=True)
+
+    def wanted_at(source_rows, columns):
+        source = lax.broadcasted_iota(jnp.int32, (64 * source_rows, 384), 0)
+        target = lax.broadcasted_iota(jnp.int32, (64 * source_rows, 384), 1)
+        wanted = target // 128 * D + first_head(y) * E + target % 128
+        low, high, start = columns
+        inside = source % source_rows + start
+        found = (source // source_rows * 2 + c) * 18 + inside == wanted
+        return jnp.logical_and(found, jnp.logical_and(inside >= low, inside < high)).astype(BF)
+
+    pick = [wanted_at(24, (0, 18, 0)), wanted_at(16, (0, 9, -2)), wanted_at(16, (9, 18, 7))]
+    came, second, *pick = lax.optimization_barrier((came, second, *pick))
+    front = dot_tn(came[:, :24].reshape(1536, 128), pick[0])
+    back = came[:, 16:32].reshape(1024, 128)
+    back = dot_tn(back, pick[1])[:E] + dot_tn(back, pick[2])[E:]
+    picked = both_cores(jnp.concatenate([front, back], axis=0).astype(BF))
+    picked, last = lax.optimization_barrier((picked, last))
+    fourth = around(last)
+    mine = call(own_columns, like(192, 192), at, picked, scalars=1)
+    w_head = lax.all_gather(mine, "a", axis=0, tiled=True)
+
+    rest = both_cores(came[:, 32:46])
     stack_own = rest[:, :, :12].reshape(2, 64, 2, D)
     stack_own = lax.dynamic_index_in_dim(stack_own, c, 2, keepdims=False).reshape(R, D).T
     bias_own = lax.dynamic_index_in_dim(rest[:, :, 12:], c, 2, keepdims=False)

time: 163 us -> 176 us (1.080)
  blocking collectives: 23.2 us -> 44.2 us
  starting transfers between devices: 51.5 us -> 35.2 us
  other arithmetic: 5.79 us -> 10.7 us
  local copies, waits for them, and re-layouts: 23.5 us -> 26.8 us
    all_gather x0 -> x1, blocking collectives: none -> 11.2 us  [per_device(): w_head = lax.all_gather(mine, 'a', axis=0, tiled=True)]
    all_gather x8, blocking collectives: 20.6 us -> 30.4 us  [both_cores(): return lax.all_gather(x, 'c', axis=0, tiled=False)]
    all_to_all x1 -> x0, starting transfers between devices: 6.57 us -> none  [per_device(): w_head = lax.all_to_all(copies, 'z', 0, 0, tiled=True).reshape(D, 192)]
    all_to_all x1, starting transfers between devices: 17.1 us -> 11.4 us  [per_device(): came = lax.all_to_all(message, CHIPS, 0, 0, tiled=True)]
    ppermute x4, starting transfers between devices: 16.8 us -> 11.3 us  [around(): return lax.ppermute(x, ('y', 'c'), pairs)]
    ppermute x4, waiting for transfers between devices: 13.3 us -> 18.5 us  [around(): return lax.ppermute(x, ('y', 'c'), pairs)]
    concatenate x1, local copies, waits for them, and re-layouts: 1.16 us -> 5.56 us  [per_device(): jnp.concatenate([jnp.broadcast_to(quarter, (64, 27, 128)), jnp.zeros((64,...]
    all_to_all x1 -> x0, waiting for transfers between devices: 3.46 us -> none  [per_device(): w_head = lax.all_to_all(copies, 'z', 0, 0, tiled=True).reshape(D, 192)]
  transfers between devices with their start and end apart: 9 -> 8, of which waited for: 5 -> 3; matrix products, arithmetic and copies ran while one was open for 17% -> 22% of each run, Pallas kernels for 4% -> 4%
where the time goes in v5:
time: 176 us; the launch traced here: 175 us
  blocking collectives  44.2 us (25%)
  starting transfers between devices  35.2 us (20%)
  local copies, waits for them, and re-layouts  26.8 us (15%)
  waiting for transfers between devices  25.7 us (15%)
  between operations  15.2 us (9%)
  Pallas kernels  15 us (9%)
  other arithmetic  10.7 us (6%)
  matrix products  2.38 us (1%)
    all_gather x8, blocking collectives, both_cores(): return lax.all_gather(x, 'c', axis=0, tiled=False)  30.4 us
    ppermute x4, waiting for transfers between devices, around(): return lax.ppermute(x, ('y', 'c'), pairs)  18.5 us
    pallas_call x5, Pallas kernels, call(): pl.pallas_call(kernel, out_shape=out_shape, in_specs=[SMEM] * scalars + [...  15 us
    all_to_all x1, starting transfers between devices, per_device(): came = lax.all_to_all(message, CHIPS, 0, 0, tiled=True)  11.4 us
    ppermute x4, starting transfers between devices, around(): return lax.ppermute(x, ('y', 'c'), pairs)  11.3 us
    all_gather x1, blocking collectives, per_device(): w_head = lax.all_gather(mine, 'a', axis=0, tiled=True)  11.2 us
    all_to_all x1, waiting for transfers between devices, per_device(): parts = lax.all_to_all(tied, 'z', 0, 0, tiled=True)  7.1 us
    reshape x1, local copies, waits for them, and re-layouts, per_device(): column_triple = gathered[:, :18].reshape(3 * D, D)  6.56 us
  transfers between devices with their start and end apart: 8, of which 3 were waited for; matrix products, arithmetic and copies ran while one was open for 22% of the time, Pallas kernels for 4%

profile of v5, /device:TPU:1, one launch (start us, length us, event | category | flops | bytes accessed | tf_op | source)
XLA Modules:
  0.0 175.1 jit_solution(481620241873342726)
XLA Ops:
  7.2 0.0 copy-start
  7.2 0.0 copy-start.5
  7.2 0.0 all-gather.10.cloned.1.call-start
  7.3 0.1 pad.3.clone
  7.3 1.5 maximum_maximum_fusion
  8.8 0.0 all-gather.10.cloned.1.call-update
  8.9 1.0 convert_reduce_fusion
  9.9 1.1 fusion.25
  11.1 1.1 fusion.22
  12.1 8.6 %all_gather.59.own_ref = bf16[2,128,768]{2,1,0:T(8,128)(2,1)S(1)} all-gather(bf16[1,128,768]{2,1,0:T(8,128)(2,1)S(1)} %fusion.22), channel_id=1, replica_groups=mesh['a'=4,'z'=8,'y'=8,'c'=2] {'c'}, dimensions={0}, use_global_device_ids=true | all-gather | bytes 589824 | tf_op jit(solution)/shard_map/all_gather | solution.py:167
  20.7 1.9 %collective-permute-start = (bf16[2,128,768]{2,1,0:T(8,128)(2,1)S(1)}, bf16[2,128,768]{2,1,0:T(8,128)(2,1)S(1)}, u32[]{:S(2)}, u32[]{:S(2)}) collective-permute-start(bf16[2,128,768]{2,1,0:T(8,128)(2,1)S(1)} %all_gather.59.own_ref), channel_id=1, source_target_pairs={{0,2},{1,15},{2,4},{3,1},{4,6},{5,3},{6,8},{7,5},{8,10},{9,7},{10,... | collective-permute-start | bytes 1179656 | tf_op jit(solution)/shard_map/ppermute | solution.py:163
  22.7 0.2 reshape_reshape.3
  22.9 0.1 convolution_convert_fusion.1
  23.2 0.1 dynamic-slice_bitcast_fusion.1
  23.3 0.1 maximum_maximum_fusion.1
  23.4 0.1 broadcast_in_dim.24
  23.5 5.6 %concatenate.29 = bf16[64,48,128]{2,1,0:T(8,128)(2,1)} concatenate(bf16[64,27,128]{2,1,0:T(8,128)(2,1)S(1)} %broadcast_in_dim.24, bf16[64,5,128]{2,1,0:T(8,128)(2,1)S(1)} %broadcast_in_dim.25, bf16[64,12,128]{2,1,0:T(8,128)(2,1)S(1)} %reshape_reshape.3, bf16[64,2,128]{2,1,0:T(2,128)(2,1)S(1)} %copy.25, bf16[64,2,128]{2,1,0:T(2,128)(2,1)S(1)} %broadcast_in_dim.27), dimensions={1} | concatenate | bytes 1572864 | tf_op jit(solution)/shard_map/concatenate | solution.py:206
  29.1 11.4 %all-to-all-start = ((bf16[64,48,128]{2,1,0:T(8,128)(2,1)}), bf16[64,48,128]{2,1,0:T(8,128)(2,1)}, u32[]{:S(2)}, u32[]{:S(2)}) async-start(bf16[64,48,128]{2,1,0:T(8,128)(2,1)} %concatenate.29), calls=%async_computation | async-start | bytes 1572864 | tf_op jit(solution)/shard_map/all_to_all | solution.py:217
  40.7 0.0 collective-permute-done
  40.7 4.1 %collective-permute-start.1 = (bf16[2,128,768]{2,1,0:T(8,128)(2,1)S(1)}, bf16[2,128,768]{2,1,0:T(8,128)(2,1)S(1)}, u32[]{:S(2)}, u32[]{:S(2)}) collective-permute-start(bf16[2,128,768]{2,1,0:T(8,128)(2,1)S(1)} %collective-permute-done), channel_id=1, source_target_pairs={{0,2},{1,15},{2,4},{3,1},{4,6},{5,3},{6,8},{7,5},{8,10},{9,7},{10,... | collective-permute-start | bytes 1179656 | tf_op jit(solution)/shard_map/ppermute | solution.py:163
  44.8 2.0 %fusion.2 = bf16[1536,384]{1,0:T(8,128)(2,1)S(1)} fusion(s32[384]{0:T(512)S(1)} %get-tuple-element.53, s32[384]{0:T(512)S(1)} %get-tuple-element.54, s32[]{:T(128)S(6)} %mul.58, s32[384]{0:T(512)S(1)} %get-tuple-element.52, s32[384]{0:T(512)S(1)} %get-tuple-element.55, s32[1536]{0:T(1024)S(1)} %get-tuple-element.47, s32[1536]{0:T(1024)S(1)} %get-tuple-element.48, ...), kind=kLoop, calls=%fused_computation.5 | loop fusion | flops 10027008 | bytes 1214216 | tf_op jit(solution)/shard_map/convert_element_type | solution.py:226
  46.7 18.1 %collective-permute-done.1 = bf16[2,128,768]{2,1,0:T(8,128)(2,1)S(1)} collective-permute-done((bf16[2,128,768]{2,1,0:T(8,128)(2,1)S(1)}, bf16[2,128,768]{2,1,0:T(8,128)(2,1)S(1)}, u32[]{:S(2)}, u32[]{:S(2)}) %collective-permute-start.1) | collective-permute-done | bytes 393248 | tf_op jit(solution)/shard_map/ppermute | solution.py:163
  64.8 3.4 %collective-permute-start.2 = (bf16[2,128,768]{2,1,0:T(8,128)(2,1)S(1)}, bf16[2,128,768]{2,1,0:T(8,128)(2,1)}, u32[]{:S(2)}, u32[]{:S(2)}) collective-permute-start(bf16[2,128,768]{2,1,0:T(8,128)(2,1)S(1)} %collective-permute-done.1), channel_id=1, source_target_pairs={{0,2},{1,15},{2,4},{3,1},{4,6},{5,3},{6,8},{7,5},{8,10},{9,7},{10,... | collective-permute-start | bytes 1179656 | tf_op jit(solution)/shard_map/ppermute | solution.py:163
  68.3 2.7 %fusion.14 = (bf16[1024,384]{1,0:T(8,128)(2,1)}, bf16[1024,384]{1,0:T(8,128)(2,1)}) fusion(s32[384]{0:T(512)S(1)} %get-tuple-element.53, s32[384]{0:T(512)S(1)} %get-tuple-element.54, s32[]{:T(128)S(6)} %mul.58, s32[384]{0:T(512)S(1)} %get-tuple-element.52, s32[384]{0:T(512)S(1)} %get-tuple-element.55, s32[1024]{0:T(1024)S(1)} %get-tuple-element.59, ...), kind=kLoop, calls=%fused_computation.21 | loop fusion | flops 10223616 | bytes 1598216 | tf_op jit(solution)/shard_map/convert_element_type | solution.py:226
  70.9 0.1 pad_add_fusion.at_ref
  71.0 2.4 %all-gather = bf16[4,128,768]{2,1,0:T(8,128)(2,1)S(1)} all-gather(bf16[2,128,768]{2,1,0:T(8,128)(2,1)S(1)} %collective-permute-done), channel_id=2, replica_groups=mesh['a'=4,'z'=8,'y'=8,'c'=2] {'c'}, dimensions={0}, use_global_device_ids=true | all-gather | bytes 1179648 | tf_op jit(solution)/shard_map/all_gather | solution.py:167
  73.3 0.4 collective-permute-done.2
  73.8 5.7 %all-gather.2 = bf16[4,128,768]{2,1,0:T(8,128)(2,1)S(1)} all-gather(bf16[2,128,768]{2,1,0:T(8,128)(2,1)} %collective-permute-done.2), channel_id=4, replica_groups=mesh['a'=4,'z'=8,'y'=8,'c'=2] {'c'}, dimensions={0}, use_global_device_ids=true | all-gather | bytes 1179648 | tf_op jit(solution)/shard_map/all_gather | solution.py:167
  79.4 1.0 slice_select_fusion
  80.5 1.1 slice.80
  81.6 1.0 slice.81
  82.6 1.6 fusion.26
  84.2 0.3 fusion.20
  84.5 0.4 fusion.18
  84.9 2.0 %all_gather.60.picked_ref = bf16[2,192,384]{2,1,0:T(8,128)(2,1)S(1)} all-gather(bf16[1,192,384]{2,1,0:T(8,128)(2,1)S(1)} %pad_maximum_fusion), channel_id=1, replica_groups=mesh['a'=4,'z'=8,'y'=8,'c'=2] {'c'}, dimensions={0}, use_global_device_ids=true | all-gather | bytes 442368 | tf_op jit(solution)/shard_map/all_gather | solution.py:167
  87.0 1.9 %collective-permute-start.3 = (bf16[2,64,768]{2,1,0:T(8,128)(2,1)S(1)}, bf16[2,64,768]{2,1,0:T(8,128)(2,1)S(1)}, u32[]{:S(2)}, u32[]{:S(2)}) collective-permute-start(bf16[2,64,768]{2,1,0:T(8,128)(2,1)S(1)} %slice_select_fusion), channel_id=1, source_target_pairs={{0,2},{1,15},{2,4},{3,1},{4,6},{5,3},{6,8},{7,5},{8,10},{9,7},{10,... | collective-permute-start | bytes 589832 | tf_op jit(solution)/shard_map/ppermute | solution.py:163
  88.9 0.7 shard_map.104
  89.6 11.2 %all_gather.61.w_ref = bf16[768,192]{1,0:T(8,128)(2,1)S(1)} all-gather(bf16[192,192]{1,0:T(8,128)(2,1)S(1)} %shard_map.104), channel_id=1, replica_groups=mesh['a'=4,'z'=8,'y'=8,'c'=2] {'a'}, dimensions={0}, use_global_device_ids=true | all-gather | bytes 368640 | tf_op jit(solution)/shard_map/all_gather | solution.py:237
  100.8 4.2 %all-gather.1 = bf16[4,128,768]{2,1,0:T(8,128)(2,1)S(1)} all-gather(bf16[2,128,768]{2,1,0:T(8,128)(2,1)S(1)} %copy-done.7), channel_id=3, replica_groups=mesh['a'=4,'z'=8,'y'=8,'c'=2] {'c'}, dimensions={0}, use_global_device_ids=true | all-gather | bytes 1179648 | tf_op jit(solution)/shard_map/all_gather | solution.py:167
  105.0 2.1 %all-gather.3 = bf16[4,64,768]{2,1,0:T(8,128)(2,1)S(1)} all-gather(bf16[2,64,768]{2,1,0:T(8,128)(2,1)S(1)} %collective-permute-done.3), channel_id=5, replica_groups=mesh['a'=4,'z'=8,'y'=8,'c'=2] {'c'}, dimensions={0}, use_global_device_ids=true | all-gather | bytes 589824 | tf_op jit(solution)/shard_map/all_gather | solution.py:167
  107.1 3.8 %shard_map.105 = (bf16[8,128,128]{2,1,0:T(8,128)(2,1)}, bf16[8,128,128]{2,1,0:T(8,128)(2,1)S(1)}) custom-call(s32[2]{0:T(128)S(1)} %pad_add_fusion.at_ref, bf16[768,192]{1,0:T(8,128)(2,1)S(1)} %all_gather.61.w_ref, bf16[2,128,768]{2,1,0:T(8,128)(2,1)S(1)} %all_gather.59.own_ref, bf16[2,2,128,768]{3,2,1,0:T(8,128)(2,1)S(1)} %bitcast.81, ...), custom_call_target="tpu_custom_call" | custom-call | tf_op jit(solution)/shard_map/pallas_call | solution.py:171
  110.9 6.6 %all-to-all-start.1 = ((bf16[8,128,128]{2,1,0:T(8,128)(2,1)}), bf16[8,128,128]{2,1,0:T(8,128)(2,1)S(1)}, u32[]{:S(2)}, u32[]{:S(2)}) async-start(bf16[8,128,128]{2,1,0:T(8,128)(2,1)} %get-tuple-element.30), calls=%async_computation.1 | async-start | bytes 524288 | tf_op jit(solution)/shard_map/all_to_all | solution.py:257
  118.1 1.0 slice.86
  119.1 0.1 copy.26
  119.1 2.4 %all-gather.4 = bf16[128,14,128]{2,0,1:T(8,128)(2,1)S(1)} all-gather(bf16[64,14,128]{2,0,1:T(8,128)(2,1)S(1)} %copy.26), channel_id=6, replica_groups=mesh['a'=4,'z'=8,'y'=8,'c'=2] {'c'}, dimensions={0}, use_global_device_ids=true | all-gather | bytes 688128 | tf_op jit(solution)/shard_map/all_gather | solution.py:167
  121.6 7.1 %all-to-all-done.1.part_ref = bf16[8,128,128]{2,1,0:T(8,128)(2,1)S(1)} async-done(((bf16[8,128,128]{2,1,0:T(8,128)(2,1)}), bf16[8,128,128]{2,1,0:T(8,128)(2,1)S(1)}, u32[]{:S(2)}, u32[]{:S(2)}) %all-to-all-start.1) | async-done | bytes 262176 | tf_op jit(solution)/shard_map/all_to_all | solution.py:257
  128.7 0.2 shard_map.106
  128.9 3.1 %all-gather.5 = bf16[256,128]{1,0:T(8,128)(2,1)S(1)} all-gather(bf16[128,128]{1,0:T(8,128)(2,1)S(1)} %get-tuple-element.32), channel_id=7, replica_groups=mesh['a'=4,'z'=8,'y'=8,'c'=2] {'c'}, dimensions={0}, use_global_device_ids=true | all-gather | bytes 98304 | tf_op jit(solution)/shard_map/all_gather | solution.py:167
  132.0 1.7 shard_map.107
  133.7 5.9 %all-to-all-start.2 = ((bf16[64,16,128]{2,1,0:T(8,128)(2,1)}), bf16[64,16,128]{2,1,0:T(8,128)(2,1)S(1)}, u32[]{:S(2)}, u32[]{:S(2)}) async-start(bf16[64,16,128]{2,1,0:T(8,128)(2,1)} %bitcast.27), calls=%async_computation.2 | async-start | bytes 524288 | tf_op jit(solution)/shard_map/all_to_all | solution.py:269
  139.7 0.3 copy.28
  139.9 0.2 reshape.113
  140.2 0.4 constant_dynamic-slice_fusion
  140.6 0.2 copy.29
  140.8 0.0 all-gather.10.cloned.1.call-done
  140.8 5.1 %slice.110 = bf16[128,18,768]{2,1,0:T(8,128)(2,1)} slice(bf16[128,32,768]{2,1,0:T(8,128)(2,1)} %bitcast.90), slice={[0:128], [0:18], [0:768]} | slice | bytes 7077888 | tf_op jit(solution)/shard_map/slice | solution.py:271
  145.9 0.2 copy-done.3
  146.1 1.7 fusion.48
  147.7 0.4 reshape.111.wvo_ref
  148.1 2.3 %reshape.112.who_ref = bf16[768,768]{1,0:T(8,128)(2,1)S(1)} reshape(bf16[128,6,768]{2,1,0:T(8,128)(2,1)} %get-tuple-element.40) | data formatting | bytes 2359296 | tf_op jit(solution)/shard_map/reshape | solution.py:273
  150.5 0.0 copy-start.2
  150.5 6.6 %reshape.110.wv_ref = bf16[2304,768]{1,0:T(8,128)(2,1)} reshape(bf16[128,18,768]{2,1,0:T(8,128)(2,1)} %slice.110) | data formatting | bytes 7077888 | tf_op jit(solution)/shard_map/reshape | solution.py:271
  157.1 2.6 %all-gather.7 = bf16[128,16,128]{2,1,0:T(8,128)(2,1)S(1)} all-gather(bf16[64,16,128]{2,1,0:T(8,128)(2,1)S(1)} %all-to-all-done.2), channel_id=9, replica_groups=mesh['a'=4,'z'=8,'y'=8,'c'=2] {'c'}, dimensions={0}, use_global_device_ids=true | all-gather | bytes 786432 | tf_op jit(solution)/shard_map/all_gather | solution.py:277
  159.7 8.6 %shard_map.108 = (bf16[128,768]{1,0:T(8,128)(2,1)}, bf16[128,128]{1,0:T(8,128)(2,1)}) custom-call(s32[1]{0:T(128)} %bitcast.c_ref, bf16[2,64,16,128]{3,2,1,0:T(8,128)(2,1)S(1)} %bitcast.84, bf16[768,128]{1,0:T(8,128)(2,1)S(1)} %bitcast.86, bf16[768,768]{1,0:T(8,128)(2,1)S(1)} %reshape.112.who_ref, bf16[2304,768]{1,0:T(8,128)(2,1)} %reshape.110.wv_ref, ...), custom_call_target="tpu_custom_call" | custom-call | tf_op jit(solution)/shard_map/pallas_call | solution.py:171
  (50 shorter events, 0.4 us)
Async XLA Ops:
  7.2 16.1 %copy-start = (bf16[768,18]{0,1:T(8,128)(2,1)S(1)}, bf16[768,18]{0,1:T(8,128)(2,1)}, u32[]{:S(2)}) copy-start(bf16[768,18]{0,1:T(8,128)(2,1)} %param.12) | copy-start | bytes 82948
  7.2 15.5 %copy-start.5 = (bf16[1,128,768]{2,1,0:T(8,128)(2,1)S(1)}, bf16[1,128,768]{2,1,0:T(8,128)(2,1)}, u32[]{:S(2)}) copy-start(bf16[1,128,768]{2,1,0:T(8,128)(2,1)} %param.9) | copy-start | bytes 589828
  7.2 15.7 %copy-start.1 = (bf16[1,128,128]{2,1,0:T(8,128)(2,1)S(1)}, bf16[1,128,128]{2,1,0:T(8,128)(2,1)}, u32[]{:S(2)}) copy-start(bf16[1,128,128]{2,1,0:T(8,128)(2,1)} %param.11) | copy-start | bytes 98308
  7.2 15.7 %copy-start.8 = (bf16[128,12]{0,1:T(8,128)(2,1)S(1)}, bf16[128,12]{0,1:T(8,128)(2,1)}, u32[]{:S(2)}) copy-start(bf16[128,12]{0,1:T(8,128)(2,1)} %param.16) | copy-start | bytes 9220
  7.2 133.6 %all-gather.10.cloned.1.call-start = ((), (), s32[]{:S(2)}) async-start(), calls=%async_computation.3 | async-start | bytes 6340608 | tf_op jit(solution)/shard_map/all_gather | solution.py:192
  20.7 19.9 %collective-permute-start = (bf16[2,128,768]{2,1,0:T(8,128)(2,1)S(1)}, bf16[2,128,768]{2,1,0:T(8,128)(2,1)S(1)}, u32[]{:S(2)}, u32[]{:S(2)}) collective-permute-start(bf16[2,128,768]{2,1,0:T(8,128)(2,1)S(1)} %all_gather.59.own_ref), channel_id=1, source_target_pairs={{0,2},{1,15},{2,4},{3,1},{4,6},{5,3},{6,8},{7,5},{8,10},{9,7},{10,... | collective-permute-start | bytes 1179656 | tf_op jit(solution)/shard_map/ppermute | solution.py:163
  29.1 51.4 %all-to-all-start = ((bf16[64,48,128]{2,1,0:T(8,128)(2,1)}), bf16[64,48,128]{2,1,0:T(8,128)(2,1)}, u32[]{:S(2)}, u32[]{:S(2)}) async-start(bf16[64,48,128]{2,1,0:T(8,128)(2,1)} %concatenate.29), calls=%async_computation | async-start | bytes 1572864 | tf_op jit(solution)/shard_map/all_to_all | solution.py:217
  40.7 24.1 %collective-permute-start.1 = (bf16[2,128,768]{2,1,0:T(8,128)(2,1)S(1)}, bf16[2,128,768]{2,1,0:T(8,128)(2,1)S(1)}, u32[]{:S(2)}, u32[]{:S(2)}) collective-permute-start(bf16[2,128,768]{2,1,0:T(8,128)(2,1)S(1)} %collective-permute-done), channel_id=1, source_target_pairs={{0,2},{1,15},{2,4},{3,1},{4,6},{5,3},{6,8},{7,5},{8,10},{9,7},{10,... | collective-permute-start | bytes 1179656 | tf_op jit(solution)/shard_map/ppermute | solution.py:163
  64.8 8.5 %copy-start.6 = (bf16[2,128,768]{2,1,0:T(8,128)(2,1)}, bf16[2,128,768]{2,1,0:T(8,128)(2,1)S(1)}, u32[]{:S(2)}) copy-start(bf16[2,128,768]{2,1,0:T(8,128)(2,1)S(1)} %collective-permute-done.1) | copy-start | bytes 1179652
  64.8 8.9 %collective-permute-start.2 = (bf16[2,128,768]{2,1,0:T(8,128)(2,1)S(1)}, bf16[2,128,768]{2,1,0:T(8,128)(2,1)}, u32[]{:S(2)}, u32[]{:S(2)}) collective-permute-start(bf16[2,128,768]{2,1,0:T(8,128)(2,1)S(1)} %collective-permute-done.1), channel_id=1, source_target_pairs={{0,2},{1,15},{2,4},{3,1},{4,6},{5,3},{6,8},{7,5},{8,10},{9,7},{10,... | collective-permute-start | bytes 1179656 | tf_op jit(solution)/shard_map/ppermute | solution.py:163
  80.5 3.7 %copy-start.4 = (bf16[1024,384]{1,0:T(8,128)(2,1)S(1)}, bf16[1024,384]{1,0:T(8,128)(2,1)}, u32[]{:S(2)}) copy-start(bf16[1024,384]{1,0:T(8,128)(2,1)} %get-tuple-element.24) | copy-start | bytes 2359300
  84.5 16.3 %copy-start.7 = (bf16[2,128,768]{2,1,0:T(8,128)(2,1)S(1)}, bf16[2,128,768]{2,1,0:T(8,128)(2,1)}, u32[]{:S(2)}) copy-start(bf16[2,128,768]{2,1,0:T(8,128)(2,1)} %copy-done.6) | copy-start | bytes 1179652
  87.0 18.0 %collective-permute-start.3 = (bf16[2,64,768]{2,1,0:T(8,128)(2,1)S(1)}, bf16[2,64,768]{2,1,0:T(8,128)(2,1)S(1)}, u32[]{:S(2)}, u32[]{:S(2)}) collective-permute-start(bf16[2,64,768]{2,1,0:T(8,128)(2,1)S(1)} %slice_select_fusion), channel_id=1, source_target_pairs={{0,2},{1,15},{2,4},{3,1},{4,6},{5,3},{6,8},{7,5},{8,10},{9,7},{10,... | collective-permute-start | bytes 589832 | tf_op jit(solution)/shard_map/ppermute | solution.py:163
  110.9 17.8 %all-to-all-start.1 = ((bf16[8,128,128]{2,1,0:T(8,128)(2,1)}), bf16[8,128,128]{2,1,0:T(8,128)(2,1)S(1)}, u32[]{:S(2)}, u32[]{:S(2)}) async-start(bf16[8,128,128]{2,1,0:T(8,128)(2,1)} %get-tuple-element.30), calls=%async_computation.1 | async-start | bytes 524288 | tf_op jit(solution)/shard_map/all_to_all | solution.py:257
  133.7 23.3 %all-to-all-start.2 = ((bf16[64,16,128]{2,1,0:T(8,128)(2,1)}), bf16[64,16,128]{2,1,0:T(8,128)(2,1)S(1)}, u32[]{:S(2)}, u32[]{:S(2)}) async-start(bf16[64,16,128]{2,1,0:T(8,128)(2,1)} %bitcast.27), calls=%async_computation.2 | async-start | bytes 524288 | tf_op jit(solution)/shard_map/all_to_all | solution.py:269
  140.8 5.2 %copy-start.3 = (bf16[4096,768]{1,0:T(8,128)(2,1)S(1)}, bf16[4096,768]{1,0:T(8,128)(2,1)}, u32[]{:S(2)}) copy-start(bf16[4096,768]{1,0:T(8,128)(2,1)} %all-gather.10.cloned.1.call-done) | copy-start | bytes 18874372
  150.5 9.2 %copy-start.2 = (bf16[12,128]{1,0:T(8,128)(2,1)S(1)}, bf16[12,128]{1,0:T(8,128)(2,1)}, u32[]{:S(2)}) copy-start(bf16[12,128]{1,0:T(8,128)(2,1)} %cw_ref.1) | copy-start | bytes 9220
Sparse Core Ops, SparseCore 0:
  11.7 102.2 all-gather.9

commit v6 on v2

--- a/solution.py
+++ b/solution.py
@@ -1,5 +1,3 @@
-import functools
-
 import jax
 import jax.numpy as jnp
 from jax import lax
@@ -18,7 +16,7 @@
 
 
 def params():
-    return pltpu.CompilerParams(vmem_limit_bytes=48 << 20)
+    return pltpu.CompilerParams(vmem_limit_bytes=28 << 20)
 
 
 def dot_nt(a, b):
@@ -39,23 +37,21 @@
     return (x - center) * lax.rsqrt(spread + 1e-05)
 
 
-def project_and_tie(y_ref, w_ref, *refs):
-    row_refs, (left_ref, right_ref, tied_ref, v_ref) = refs[:5], refs[5:]
+def project_and_tie(at_ref, w_ref, own_ref, one_ref, two_ref, three_ref, four_ref, tied_ref, v_ref):
     w = w_ref[...]
     lane = lax.broadcasted_iota(jnp.int32, (L, 2 * E), 1)
-    offsets = (0, -1, 1, -2, 2, -3, 3, 4)
+    y, c = at_ref[0], at_ref[1]
+    step = 2 * c - 1
+    rows = [(own_ref, None, 0, c), (four_ref, None, 4, 1 - c)]
+    for n, ref in enumerate((one_ref, two_ref, three_ref)):
+        rows += [(ref, core, (n + 1) * step, core) for core in range(2)]
     tied = [jnp.zeros((L, L), F32), jnp.zeros((L, L), F32)]
-    for n, offset in enumerate(offsets):
-        if n < 5:
-            x = row_refs[n][...]
-        elif n < 7:
-            x = refs[n][:L]
-        else:
-            x = jnp.concatenate([left_ref[L:], right_ref[L:]], axis=0)
+    for ref, core, offset, source in rows:
+        x = ref[...] if core is None else ref[core]
         packed = jnp.dot(x, w, preferred_element_type=F32)
         q = packed[:, : 2 * E] * E**-0.5
         k = packed[:, 2 * E : 4 * E].astype(BF)
-        v_ref[lax.rem(y_ref[0] + (8 + offset), 8)] = packed[:, 4 * E :].astype(BF)
+        v_ref[2 * lax.rem(y + 8 + offset, 4) + source] = packed[:, 4 * E :].astype(BF)
         tied[0] += dot_nt(jnp.where(lane < E, q, 0.0).astype(BF), k)
         tied[1] += dot_nt(jnp.where(lane < E, 0.0, q).astype(BF), k)
     for h in range(2):
@@ -104,12 +100,25 @@
     low = lane < E
     early = lax.rem(row, 8) < 4
 
+    slot = lax.rem(lax.broadcasted_iota(jnp.int32, (E, L), 0), 8)
+
     def tile(c, z, y):
         both = bl_ref[c, z * 8 + y].astype(F32)
         return jnp.where(mine == 0, both[:8], both[8:])
 
-    tiles = [[tile(c, z, y) for c in range(2) for z in range(8)] for y in range(8)]
-    blocks = [jnp.concatenate(t, axis=0) for t in tiles]
+    def block(y):
+        left, right = (jnp.concatenate([tile(c, z, y) for z in range(8)], axis=0) for c in range(2))
+        halves = []
+        for high in range(2):
+            from_left = jnp.zeros((E, L), jnp.bool_)
+            for s in range(8):
+                away = (4 * high + s // 2 - y) % 8
+                if away > 4 or (away == 0 and s % 2 == 0) or (away == 4 and s % 2 == 1):
+                    from_left = jnp.logical_or(from_left, slot == s)
+            halves.append(jnp.where(from_left, left, right))
+        return jnp.concatenate(halves, axis=0)
+
+    blocks = [block(y) for y in range(8)]
     parts = []
     for n in range(2):
         e0, o0, e1, o1 = blocks[4 * n : 4 * n + 4]
@@ -137,13 +146,13 @@
     mixed = jnp.concatenate(mixed, axis=0)
 
     result = (updated + jnp.dot(wvo_ref[...], mixed, preferred_element_type=F32)).astype(BF)
-    place = (lax.rem(row, 2) * E + row // 2 == lane).astype(BF)
+    place = (row // 8 % 2 * E + row // 16 * 8 + row % 8 == lane).astype(BF)
     out_ref[...] = dot_nt(place, result).astype(BF)
 
     one = lax.broadcasted_iota(jnp.int32, (1, L), 1) < E
     lines = []
     for n in range(4):
-        e, o = tiles[2 * n][0], tiles[2 * n + 1][0]
+        e, o = tile(0, 0, 2 * n), tile(0, 0, 2 * n + 1)
         re, ro = pltpu.roll(e, E, 1), pltpu.roll(o, E, 1)
         lines.append(jnp.where(one, re[4:5], e[5:6]))
         lines.append(jnp.where(one, re[6:7], e[7:8]))
@@ -156,13 +165,15 @@
     pair_out_ref[...] = pair.astype(BF)
 
 
-def moved(x, step):
-    return lax.ppermute(x, "y", [(i, (i + step) % 8) for i in range(8)])
+def around(x):
+    pairs = [(2 * y + c, (y + 1 - 2 * c) % 8 * 2 + c) for y in range(8) for c in range(2)]
+    return lax.ppermute(x, ("y", "c"), pairs)
 
 
 def per_device(stack, spans, pair, w_triple, w_out, v_triple, v_out, offsets, contact_w):
     y, c = lax.axis_index("y"), lax.axis_index("c")
     y1, c1 = y[None].astype(jnp.int32), c[None].astype(jnp.int32)
+    at = jnp.concatenate([y1, c1])
     pair_own = pair.reshape(L, 128)
     own_row = stack.reshape(L, D)
 
@@ -170,7 +181,10 @@
     gathered = lax.all_gather(column_weights, ROWS, axis=0, tiled=False)
 
     normed = normalize(own_row.astype(F32)).astype(BF)
-    near = [moved(normed, step) for step in (1, -1, 2, -2)]
+    one = around(lax.all_gather(normed, "c", axis=0, tiled=False))
+    two = around(one)
+    three = around(two)
+    four = around(jnp.where(c == 0, three[1], three[0]))
 
     bias = lax.dot_general(offsets, pair_own, (((0,), (1,)), ((), ())), preferred_element_type=F32).astype(BF)
     bias_pairs = jnp.stack([bias[first_head(n) : first_head(n) + 2] for n in range(8)])
@@ -185,11 +199,7 @@
         axis=1,
     )
     came = lax.all_to_all(message, CHIPS, 0, 0, tiled=True)
-    far = [
-        moved(jnp.concatenate([near[0], near[2][: L // 2]]), 2),
-        moved(jnp.concatenate([near[1], near[3][L // 2 :]]), -2),
-    ]
-    came, *near = lax.optimization_barrier((came, *near))
+    came, one = lax.optimization_barrier((came, one))
 
     source = lax.broadcasted_iota(jnp.int32, (2048, 384), 0)
     target = lax.broadcasted_iota(jnp.int32, (2048, 384), 1)
@@ -205,7 +215,8 @@
 
     rest = lax.all_gather(came[:, 18:, :], "c", axis=0, tiled=False)
     stack_own = rest[:, :, :12].reshape(2, 64, 2, D)
-    stack_own = lax.dynamic_index_in_dim(stack_own, c, 2, keepdims=False).reshape(R, D)
+    stack_own = lax.dynamic_index_in_dim(stack_own, c, 2, keepdims=False).reshape(2, 8, 2, 4, D)
+    stack_own = stack_own.transpose(2, 1, 3, 0, 4).reshape(R, D)
     bias_own = lax.dynamic_index_in_dim(rest[:, :, 12:], c, 2, keepdims=False)
     bias_own = bias_own.transpose(1, 0, 2).reshape(L, L)
 
@@ -215,10 +226,10 @@
             jax.ShapeDtypeStruct((2, L, L), F32),
             jax.ShapeDtypeStruct((8, L, 2 * E), BF),
         ),
-        in_specs=[SMEM] + [VMEM] * 8,
+        in_specs=[SMEM] + [VMEM] * 6,
         out_specs=(VMEM, VMEM),
         compiler_params=params(),
-    )(y1, w_heads, normed, *near, *far)
+    )(at, w_heads, normed, one, two, three, four)
 
     tied = lax.all_gather(tied, "c", axis=0, tiled=False)
     tied = lax.dynamic_index_in_dim(tied, c, 1, keepdims=False)

time: 169 us -> 163 us (0.964)
  starting transfers between devices: 57.6 us -> 52.3 us
  waiting for transfers between devices: 38.3 us -> 36.4 us
    ppermute x6 -> x4, waiting for transfers between devices: 25.5 us -> 16.6 us  [around(): return lax.ppermute(x, ('y', 'c'), pairs)]
    all_to_all x1, waiting for transfers between devices: 4.98 us -> 10.6 us  [per_device(): lax.all_to_all(jnp.broadcast_to(half, (8, 48, 384)), 'z', 0, 0, tiled=True)]
    unnamed x18 -> x23, local copies, waits for them, and re-layouts: 0.32 us -> 4.53 us
    ppermute x6 -> x4, starting transfers between devices: 21.3 us -> 17.4 us  [around(): return lax.ppermute(x, ('y', 'c'), pairs)]
    all_to_all x1, starting transfers between devices: 7.28 us -> 3.41 us  [per_device(): lax.all_to_all(jnp.broadcast_to(tied, (8, L, L)), 'z', 0, 0, tiled=True)]
    all_gather x0 -> x1, blocking collectives: none -> 2.67 us  [per_device(): one = around(lax.all_gather(normed, 'c', axis=0, tiled=False))]
    all_to_all x1, starting transfers between devices: 5.15 us -> 7.78 us  [per_device(): came = lax.all_to_all(message.reshape(64, 16, 128), CHIPS, 0, 0, tiled=True)]
    pallas_call x1, Pallas kernels: 8.57 us -> 6.61 us  [per_device(): pl.pallas_call(column_block, out_shape=(jax.ShapeDtypeStruct((R, D), BF),...]
  transfers between devices with their start and end apart: 11 -> 9, of which waited for: 7 -> 4; matrix products, arithmetic and copies ran while one was open for 16% -> 15% of each run, Pallas kernels for 2% -> 3%
where the time goes in v6:
time: 163 us; the launch traced here: 162 us
  starting transfers between devices  52.3 us (32%)
  waiting for transfers between devices  36.4 us (22%)
  local copies, waits for them, and re-layouts  23.9 us (15%)
  blocking collectives  17.1 us (10%)
  between operations  15.1 us (9%)
  Pallas kernels  10.7 us (7%)
  other arithmetic  3.25 us (2%)
  matrix products  3 us (2%)
    ppermute x4, starting transfers between devices, around(): return lax.ppermute(x, ('y', 'c'), pairs)  17.4 us
    all_to_all x1, starting transfers between devices, per_device(): came = lax.all_to_all(message, CHIPS, 0, 0, tiled=True)  17.1 us
    ppermute x4, waiting for transfers between devices, around(): return lax.ppermute(x, ('y', 'c'), pairs)  16.6 us
    all_to_all x1, waiting for transfers between devices, per_device(): lax.all_to_all(jnp.broadcast_to(half, (8, 48, 384)), 'z', 0, 0, tiled=True)  10.6 us
    all_to_all x1, waiting for transfers between devices, per_device(): lax.all_to_all(jnp.broadcast_to(tied, (8, L, L)), 'z', 0, 0, tiled=True)  9.26 us
    all_to_all x1, starting transfers between devices, per_device(): came = lax.all_to_all(message.reshape(64, 16, 128), CHIPS, 0, 0, tiled=True)  7.78 us
    pallas_call x1, Pallas kernels, per_device(): pl.pallas_call(column_block, out_shape=(jax.ShapeDtypeStruct((R, D), BF),...  6.61 us
    all_to_all x1, starting transfers between devices, per_device(): lax.all_to_all(jnp.broadcast_to(half, (8, 48, 384)), 'z', 0, 0, tiled=True)  6.54 us
  transfers between devices with their start and end apart: 9, of which 4 were waited for; matrix products, arithmetic and copies ran while one was open for 15% of the time, Pallas kernels for 3%

profile of v6, /device:TPU:1, one launch (start us, length us, event | category | flops | bytes accessed | tf_op | source)
XLA Modules:
  0.0 161.7 jit_solution(18115367425102899668)
XLA Ops:
  7.2 0.0 copy-start
  7.2 0.0 copy-start.7
  7.2 0.0 all-gather.9.cloned.1.call-start
  7.2 0.1 pad.8.clone
  7.3 1.5 maximum_maximum_fusion
  8.8 0.0 all-gather.9.cloned.1.call-update
  8.8 0.9 reshape.94
  9.7 0.1 copy.35
  9.8 0.1 reshape.95
  9.9 1.1 reshape_reshape.3
  11.1 0.9 convolution_convert_fusion
  12.1 0.1 broadcast_in_dim.33
  12.2 1.0 pad_maximum_fusion
  13.2 17.1 %all-to-all-start = ((bf16[64,32,128]{2,1,0:T(8,128)(2,1)}), bf16[64,32,128]{2,1,0:T(8,128)(2,1)S(1)}, u32[]{:S(2)}, u32[]{:S(2)}) async-start(bf16[64,32,128]{2,1,0:T(8,128)(2,1)} %pad_maximum_fusion), calls=%async_computation | async-start | bytes 1048576 | tf_op jit(solution)/shard_map/all_to_all | solution.py:201
  30.3 0.1 convert_reduce_fusion
  30.5 0.2 fusion.26
  30.7 0.1 fusion.22
  30.8 2.7 %all_gather.46 = bf16[2,128,768]{2,1,0:T(8,128)(2,1)S(1)} all-gather(bf16[1,128,768]{2,1,0:T(8,128)(2,1)S(1)} %fusion.22), channel_id=1, replica_groups=mesh['a'=4,'z'=8,'y'=8,'c'=2] {'c'}, dimensions={0}, use_global_device_ids=true | all-gather | bytes 589824 | tf_op jit(solution)/shard_map/all_gather | solution.py:184
  33.5 4.4 %collective-permute-start = (bf16[2,128,768]{2,1,0:T(8,128)(2,1)S(1)}, bf16[2,128,768]{2,1,0:T(8,128)(2,1)S(1)}, u32[]{:S(2)}, u32[]{:S(2)}) collective-permute-start(bf16[2,128,768]{2,1,0:T(8,128)(2,1)S(1)} %all_gather.46), channel_id=1, source_target_pairs={{0,2},{1,15},{2,4},{3,1},{4,6},{5,3},{6,8},{7,5},{8,10},{9,7},{10,... | collective-permute-start | bytes 1179656 | tf_op jit(solution)/shard_map/ppermute | solution.py:170
  38.0 10.8 %collective-permute-done.one_ref = bf16[2,128,768]{2,1,0:T(8,128)(2,1)S(1)} collective-permute-done((bf16[2,128,768]{2,1,0:T(8,128)(2,1)S(1)}, bf16[2,128,768]{2,1,0:T(8,128)(2,1)S(1)}, u32[]{:S(2)}, u32[]{:S(2)}) %collective-permute-start) | collective-permute-done | bytes 393248 | tf_op jit(solution)/shard_map/ppermute | solution.py:170
  48.8 3.4 %collective-permute-start.1 = (bf16[2,128,768]{2,1,0:T(8,128)(2,1)S(1)}, bf16[2,128,768]{2,1,0:T(8,128)(2,1)S(1)}, u32[]{:S(2)}, u32[]{:S(2)}) collective-permute-start(bf16[2,128,768]{2,1,0:T(8,128)(2,1)S(1)} %collective-permute-done.one_ref), channel_id=1, source_target_pairs={{0,2},{1,15},{2,4},{3,1},{4,6},{5,3},{6,8},{7,5},{8,10},{9,7},{10,... | collective-permute-start | bytes 1179656 | tf_op jit(solution)/shard_map/ppermute | solution.py:170
  52.2 5.7 %collective-permute-done.1.two_ref = bf16[2,128,768]{2,1,0:T(8,128)(2,1)S(1)} collective-permute-done((bf16[2,128,768]{2,1,0:T(8,128)(2,1)S(1)}, bf16[2,128,768]{2,1,0:T(8,128)(2,1)S(1)}, u32[]{:S(2)}, u32[]{:S(2)}) %collective-permute-start.1) | collective-permute-done | bytes 393248 | tf_op jit(solution)/shard_map/ppermute | solution.py:170
  57.9 4.8 %collective-permute-start.2 = (bf16[2,128,768]{2,1,0:T(8,128)(2,1)S(1)}, bf16[2,128,768]{2,1,0:T(8,128)(2,1)S(1)}, u32[]{:S(2)}, u32[]{:S(2)}) collective-permute-start(bf16[2,128,768]{2,1,0:T(8,128)(2,1)S(1)} %collective-permute-done.1.two_ref), channel_id=1, source_target_pairs={{0,2},{1,15},{2,4},{3,1},{4,6},{5,3},{6,8},{7,5},{8,10},{9,7},{10,... | collective-permute-start | bytes 1179656 | tf_op jit(solution)/shard_map/ppermute | solution.py:170
  62.7 0.0 all-to-all-done
  62.7 2.1 %fusion.2 = bf16[128,384]{1,0:T(8,128)(2,1)S(1)} fusion(bf16[2048,128]{1,0:T(8,128)(2,1)S(1)} %bitcast.101, s32[384]{0:T(512)S(1)} %get-tuple-element.33, s32[384]{0:T(512)S(1)} %get-tuple-element.34, s32[]{:T(128)S(6)} %mul.41, s32[384]{0:T(512)S(1)} %get-tuple-element.32, s32[384]{0:T(512)S(1)} %get-tuple-element.35, s32[2048]{0:T(1024)S(1)} %get-tuple-element.27, ...), kind=kOutput, calls=%fused_computation.4 | convolution fusion | flops 212336640 | bytes 666376 | tf_op jit(solution)/shard_map/dot_general | solution.py:27
  64.8 2.4 %all-gather = bf16[192,384]{1,0:T(8,128)(2,1)S(1)} all-gather(bf16[96,384]{1,0:T(8,128)(2,1)S(1)} %slice.132), channel_id=2, replica_groups=mesh['a'=4,'z'=8,'y'=8,'c'=2] {'c'}, dimensions={0}, use_global_device_ids=true | all-gather | bytes 221184 | tf_op jit(solution)/shard_map/all_gather | solution.py:210
  67.2 0.7 broadcast_in_dim.35
  68.0 6.5 %all-to-all-start.1 = ((bf16[8,48,384]{2,1,0:T(8,128)(2,1)}), bf16[8,48,384]{2,1,0:T(8,128)(2,1)S(1)}, u32[]{:S(2)}, u32[]{:S(2)}) async-start(bf16[8,48,384]{2,1,0:T(8,128)(2,1)} %broadcast_in_dim.35), calls=%async_computation.1 | async-start | bytes 589824 | tf_op jit(solution)/shard_map/all_to_all | solution.py:213
  74.5 0.1 fusion.27.own_ref
  74.7 4.9 %collective-permute-start.3 = (bf16[128,768]{1,0:T(8,128)(2,1)S(1)}, bf16[128,768]{1,0:T(8,128)(2,1)S(1)}, u32[]{:S(2)}, u32[]{:S(2)}) collective-permute-start(bf16[128,768]{1,0:T(8,128)(2,1)S(1)} %fusion.28), channel_id=1, source_target_pairs={{0,2},{1,15},{2,4},{3,1},{4,6},{5,3},{6,8},{7,5},{8,10},{9,7},{10,... | collective-permute-start | bytes 589832 | tf_op jit(solution)/shard_map/ppermute | solution.py:170
  79.5 0.1 pad_add_fusion.at_ref
  79.6 10.6 %all-to-all-done.1 = bf16[8,48,384]{2,1,0:T(8,128)(2,1)S(1)} async-done(((bf16[8,48,384]{2,1,0:T(8,128)(2,1)}), bf16[8,48,384]{2,1,0:T(8,128)(2,1)S(1)}, u32[]{:S(2)}, u32[]{:S(2)}) %all-to-all-start.1) | async-done | bytes 294944 | tf_op jit(solution)/shard_map/all_to_all | solution.py:213
  90.2 3.1 %all-gather.1 = bf16[16,48,384]{2,1,0:T(8,128)(2,1)S(1)} all-gather(bf16[8,48,384]{2,1,0:T(8,128)(2,1)S(1)} %all-to-all-done.1), channel_id=3, replica_groups=mesh['a'=4,'z'=8,'y'=8,'c'=2] {'c'}, dimensions={0}, use_global_device_ids=true | all-gather | bytes 884736 | tf_op jit(solution)/shard_map/all_gather | solution.py:214
  93.3 2.7 %shard_map.104 = (f32[2,128,128]{2,1,0:T(8,128)S(1)}, bf16[8,128,128]{2,1,0:T(8,128)(2,1)S(1)}) custom-call(s32[2]{0:T(128)S(1)} %pad_add_fusion.at_ref, bf16[768,384]{1,0:T(8,128)(2,1)S(1)} %bitcast.90, bf16[128,768]{1,0:T(8,128)(2,1)S(1)} %fusion.27.own_ref, bf16[2,128,768]{2,1,0:T(8,128)(2,1)S(1)} %collective-permute-done.one_ref, ...), custom_call_target="tpu_custom_call" | custom-call | tf_op jit(solution)/shard_map/pallas_call | solution.py:223
  95.9 2.1 %all-gather.2 = f32[4,128,128]{2,1,0:T(8,128)S(1)} all-gather(f32[2,128,128]{2,1,0:T(8,128)S(1)} %get-tuple-element.14), channel_id=4, replica_groups=mesh['a'=4,'z'=8,'y'=8,'c'=2] {'c'}, dimensions={0}, use_global_device_ids=true | all-gather | bytes 393216 | tf_op jit(solution)/shard_map/all_gather | solution.py:234
  98.1 0.7 broadcast_in_dim.36
  98.8 3.4 %all-to-all-start.2 = ((bf16[8,128,128]{2,1,0:T(8,128)(2,1)}), bf16[8,128,128]{2,1,0:T(8,128)(2,1)S(1)}, u32[]{:S(2)}, u32[]{:S(2)}) async-start(bf16[8,128,128]{2,1,0:T(8,128)(2,1)} %broadcast_in_dim.36), calls=%async_computation.2 | async-start | bytes 524288 | tf_op jit(solution)/shard_map/all_to_all | solution.py:237
  102.9 0.1 slice.81
  103.0 0.1 copy.28
  103.0 2.1 %all-gather.3 = bf16[128,14,128]{2,0,1:T(8,128)(2,1)S(1)} all-gather(bf16[64,14,128]{2,0,1:T(8,128)(2,1)S(1)} %copy.28), channel_id=5, replica_groups=mesh['a'=4,'z'=8,'y'=8,'c'=2] {'c'}, dimensions={0}, use_global_device_ids=true | all-gather | bytes 688128 | tf_op jit(solution)/shard_map/all_gather | solution.py:216
  105.2 9.3 %all-to-all-done.2.part_ref = bf16[8,128,128]{2,1,0:T(8,128)(2,1)S(1)} async-done(((bf16[8,128,128]{2,1,0:T(8,128)(2,1)}), bf16[8,128,128]{2,1,0:T(8,128)(2,1)S(1)}, u32[]{:S(2)}, u32[]{:S(2)}) %all-to-all-start.2) | async-done | bytes 262176 | tf_op jit(solution)/shard_map/all_to_all | solution.py:237
  114.5 0.2 shard_map.105
  114.7 2.1 %all-gather.4 = bf16[4,128,128]{2,1,0:T(8,128)(2,1)S(1)} all-gather(bf16[2,128,128]{2,1,0:T(8,128)(2,1)S(1)} %shard_map.105), channel_id=6, replica_groups=mesh['a'=4,'z'=8,'y'=8,'c'=2] {'c'}, dimensions={0}, use_global_device_ids=true | all-gather | bytes 196608 | tf_op jit(solution)/shard_map/all_gather | solution.py:245
  116.8 1.2 shard_map.106
  118.0 7.8 %all-to-all-start.3 = ((bf16[64,16,128]{2,1,0:T(8,128)(2,1)}), bf16[64,16,128]{2,1,0:T(8,128)(2,1)}, u32[]{:S(2)}, u32[]{:S(2)}) async-start(bf16[64,16,128]{2,1,0:T(8,128)(2,1)} %bitcast.29), calls=%async_computation.3 | async-start | bytes 524288 | tf_op jit(solution)/shard_map/all_to_all | solution.py:254
  125.8 0.3 copy.30
  126.1 0.2 reshape.106
  126.3 0.4 constant_dynamic-slice_fusion
  126.7 0.3 copy.31
  127.1 0.1 copy.32
  127.2 0.1 reshape.108
  127.3 0.8 copy.33
  128.1 5.1 %slice.99 = bf16[128,18,768]{2,1,0:T(8,128)(2,1)} slice(bf16[128,32,768]{2,1,0:T(8,128)(2,1)} %bitcast.96), slice={[0:128], [0:18], [0:768]} | slice | bytes 7077888 | tf_op jit(solution)/shard_map/slice | solution.py:255
  133.2 0.2 copy-done.6
  133.4 0.5 fusion.48
  133.8 1.2 reshape.104.wvo_ref
  135.1 1.3 reshape.105.who_ref
  136.3 5.0 %reshape.103.wv_ref = bf16[2304,768]{1,0:T(8,128)(2,1)S(1)} reshape(bf16[128,18,768]{2,1,0:T(8,128)(2,1)} %slice.99) | data formatting | bytes 7077888 | tf_op jit(solution)/shard_map/reshape | solution.py:255
  141.4 2.7 %all-gather.6 = bf16[128,16,128]{2,1,0:T(8,128)(2,1)S(1)} all-gather(bf16[64,16,128]{2,1,0:T(8,128)(2,1)} %all-to-all-done.3), channel_id=8, replica_groups=mesh['a'=4,'z'=8,'y'=8,'c'=2] {'c'}, dimensions={0}, use_global_device_ids=true | all-gather | bytes 786432 | tf_op jit(solution)/shard_map/all_gather | solution.py:261
  144.0 1.3 copy-done.1
  145.3 1.3 copy-done.2
  146.6 0.9 copy-done.3
  147.5 0.8 copy-done.4
  148.3 6.6 %shard_map.107 = (bf16[128,768]{1,0:T(8,128)(2,1)}, bf16[128,128]{1,0:T(8,128)(2,1)}) custom-call(s32[1]{0:T(128)} %bitcast.c_ref, bf16[2,64,16,128]{3,2,1,0:T(8,128)(2,1)S(1)} %bitcast.91, bf16[768,128]{1,0:T(8,128)(2,1)S(1)} %bitcast.92, bf16[768,768]{1,0:T(8,128)(2,1)S(1)} %copy-done.2, bf16[2304,768]{1,0:T(8,128)(2,1)S(1)} %reshape.103.wv_ref, ...), custom_call_target="tpu_custom_call" | custom-call | tf_op jit(solution)/shard_map/pallas_call | solution.py:263
  (41 shorter events, 0.4 us)
Async XLA Ops:
  7.2 3.9 %copy-start = (bf16[128,12]{0,1:T(8,128)(2,1)S(1)}, bf16[128,12]{0,1:T(8,128)(2,1)}, u32[]{:S(2)}) copy-start(bf16[128,12]{0,1:T(8,128)(2,1)} %param.16) | copy-start | bytes 9220
  7.2 23.1 %copy-start.7 = (bf16[1,128,768]{2,1,0:T(8,128)(2,1)S(1)}, bf16[1,128,768]{2,1,0:T(8,128)(2,1)}, u32[]{:S(2)}) copy-start(bf16[1,128,768]{2,1,0:T(8,128)(2,1)} %param.9) | copy-start | bytes 589828
  7.2 120.9 %all-gather.9.cloned.1.call-start = ((), (), s32[]{:S(2)}) async-start(), calls=%async_computation.4 | async-start | bytes 6340608 | tf_op jit(solution)/shard_map/all_gather | solution.py:181
  13.2 49.5 %all-to-all-start = ((bf16[64,32,128]{2,1,0:T(8,128)(2,1)}), bf16[64,32,128]{2,1,0:T(8,128)(2,1)S(1)}, u32[]{:S(2)}, u32[]{:S(2)}) async-start(bf16[64,32,128]{2,1,0:T(8,128)(2,1)} %pad_maximum_fusion), calls=%async_computation | async-start | bytes 1048576 | tf_op jit(solution)/shard_map/all_to_all | solution.py:201
  33.5 15.3 %collective-permute-start = (bf16[2,128,768]{2,1,0:T(8,128)(2,1)S(1)}, bf16[2,128,768]{2,1,0:T(8,128)(2,1)S(1)}, u32[]{:S(2)}, u32[]{:S(2)}) collective-permute-start(bf16[2,128,768]{2,1,0:T(8,128)(2,1)S(1)} %all_gather.46), channel_id=1, source_target_pairs={{0,2},{1,15},{2,4},{3,1},{4,6},{5,3},{6,8},{7,5},{8,10},{9,7},{10,... | collective-permute-start | bytes 1179656 | tf_op jit(solution)/shard_map/ppermute | solution.py:170
  48.8 9.1 %collective-permute-start.1 = (bf16[2,128,768]{2,1,0:T(8,128)(2,1)S(1)}, bf16[2,128,768]{2,1,0:T(8,128)(2,1)S(1)}, u32[]{:S(2)}, u32[]{:S(2)}) collective-permute-start(bf16[2,128,768]{2,1,0:T(8,128)(2,1)S(1)} %collective-permute-done.one_ref), channel_id=1, source_target_pairs={{0,2},{1,15},{2,4},{3,1},{4,6},{5,3},{6,8},{7,5},{8,10},{9,7},{10,... | collective-permute-start | bytes 1179656 | tf_op jit(solution)/shard_map/ppermute | solution.py:170
  57.9 16.7 %collective-permute-start.2 = (bf16[2,128,768]{2,1,0:T(8,128)(2,1)S(1)}, bf16[2,128,768]{2,1,0:T(8,128)(2,1)S(1)}, u32[]{:S(2)}, u32[]{:S(2)}) collective-permute-start(bf16[2,128,768]{2,1,0:T(8,128)(2,1)S(1)} %collective-permute-done.1.two_ref), channel_id=1, source_target_pairs={{0,2},{1,15},{2,4},{3,1},{4,6},{5,3},{6,8},{7,5},{8,10},{9,7},{10,... | collective-permute-start | bytes 1179656 | tf_op jit(solution)/shard_map/ppermute | solution.py:170
  68.0 22.2 %all-to-all-start.1 = ((bf16[8,48,384]{2,1,0:T(8,128)(2,1)}), bf16[8,48,384]{2,1,0:T(8,128)(2,1)S(1)}, u32[]{:S(2)}, u32[]{:S(2)}) async-start(bf16[8,48,384]{2,1,0:T(8,128)(2,1)} %broadcast_in_dim.35), calls=%async_computation.1 | async-start | bytes 589824 | tf_op jit(solution)/shard_map/all_to_all | solution.py:213
  74.7 18.6 %collective-permute-start.3 = (bf16[128,768]{1,0:T(8,128)(2,1)S(1)}, bf16[128,768]{1,0:T(8,128)(2,1)S(1)}, u32[]{:S(2)}, u32[]{:S(2)}) collective-permute-start(bf16[128,768]{1,0:T(8,128)(2,1)S(1)} %fusion.28), channel_id=1, source_target_pairs={{0,2},{1,15},{2,4},{3,1},{4,6},{5,3},{6,8},{7,5},{8,10},{9,7},{10,... | collective-permute-start | bytes 589832 | tf_op jit(solution)/shard_map/ppermute | solution.py:170
  98.8 15.7 %all-to-all-start.2 = ((bf16[8,128,128]{2,1,0:T(8,128)(2,1)}), bf16[8,128,128]{2,1,0:T(8,128)(2,1)S(1)}, u32[]{:S(2)}, u32[]{:S(2)}) async-start(bf16[8,128,128]{2,1,0:T(8,128)(2,1)} %broadcast_in_dim.36), calls=%async_computation.2 | async-start | bytes 524288 | tf_op jit(solution)/shard_map/all_to_all | solution.py:237
  118.0 23.4 %all-to-all-start.3 = ((bf16[64,16,128]{2,1,0:T(8,128)(2,1)}), bf16[64,16,128]{2,1,0:T(8,128)(2,1)}, u32[]{:S(2)}, u32[]{:S(2)}) async-start(bf16[64,16,128]{2,1,0:T(8,128)(2,1)} %bitcast.29), calls=%async_computation.3 | async-start | bytes 524288 | tf_op jit(solution)/shard_map/all_to_all | solution.py:254
  128.1 5.3 %copy-start.6 = (bf16[4096,768]{1,0:T(8,128)(2,1)S(1)}, bf16[4096,768]{1,0:T(8,128)(2,1)}, u32[]{:S(2)}) copy-start(bf16[4096,768]{1,0:T(8,128)(2,1)} %all-gather.9.cloned.1.call-done) | copy-start | bytes 18874372
  136.3 7.7 %copy-start.5 = (bf16[12,128]{1,0:T(8,128)(2,1)S(1)}, bf16[12,128]{1,0:T(8,128)(2,1)}, u32[]{:S(2)}) copy-start(bf16[12,128]{1,0:T(8,128)(2,1)} %cw_ref.1) | copy-start | bytes 9220
  144.0 1.3 copy-start.1
  145.3 1.3 copy-start.2
  146.6 0.9 copy-start.3
  147.5 0.8 copy-start.4
Sparse Core Ops, SparseCore 0:
  11.2 101.6 all-gather.8

commit v7 on v6

--- a/solution.py
+++ b/solution.py
@@ -15,8 +15,11 @@
 SMEM = pl.BlockSpec(memory_space=pltpu.SMEM)
 
 
-def params():
-    return pltpu.CompilerParams(vmem_limit_bytes=28 << 20)
+def params(mib=16):
+    return pltpu.CompilerParams(vmem_limit_bytes=mib << 20)
+
+
+ANY = pl.BlockSpec(memory_space=pl.ANY)
 
 
 def dot_nt(a, b):
@@ -93,7 +96,12 @@
     out_ref[...] = held[...].astype(BF)
 
 
-def column_block(c_ref, bl_ref, stack_ref, who_ref, wv_ref, wvo_ref, pair_ref, cw_ref, out_ref, pair_out_ref):
+def column_block(c_ref, bl_ref, *refs):
+    far_refs, (out_ref, pair_out_ref), held, sems = refs[:6], refs[6:8], refs[8:14], refs[14]
+    copies = [pltpu.make_async_copy(far_refs[n], held[n], sems.at[n]) for n in range(6)]
+    for copy in copies:
+        copy.start()
+    stack_ref, who_ref, wv_ref, wvo_ref, pair_ref, cw_ref = held
     mine = c_ref[0]
     lane = lax.broadcasted_iota(jnp.int32, (L, L), 1)
     row = lax.broadcasted_iota(jnp.int32, (L, L), 0)
@@ -128,10 +136,13 @@
         parts.append(jnp.where(jnp.logical_and(low, early), re1, o1))
     blended = jnp.concatenate(parts, axis=1).astype(BF)
 
+    copies[0].wait()
+    copies[1].wait()
     updated = (dot_nt(who_ref[...], blended) + stack_ref[...].astype(F32)).astype(BF).astype(F32)
     center = jnp.mean(updated, axis=0, keepdims=True)
     spread = jnp.mean(jnp.square(updated - center), axis=0, keepdims=True)
     normed = ((updated - center) * lax.rsqrt(spread + 1e-05)).astype(BF)
+    copies[2].wait()
     packed = jnp.dot(wv_ref[...], normed, preferred_element_type=F32)
 
     mixed = []
@@ -145,6 +156,7 @@
         mixed.append(jnp.dot(v, probs, preferred_element_type=F32).astype(BF))
     mixed = jnp.concatenate(mixed, axis=0)
 
+    copies[3].wait()
     result = (updated + jnp.dot(wvo_ref[...], mixed, preferred_element_type=F32)).astype(BF)
     place = (row // 8 % 2 * E + row // 16 * 8 + row % 8 == lane).astype(BF)
     out_ref[...] = dot_nt(place, result).astype(BF)
@@ -157,6 +169,8 @@
         lines.append(jnp.where(one, re[4:5], e[5:6]))
         lines.append(jnp.where(one, re[6:7], e[7:8]))
         lines.append(jnp.where(one, o[2:3], ro[3:4]))
+    copies[4].wait()
+    copies[5].wait()
     scores = jnp.concatenate(lines + [jnp.zeros((L - H, L), F32)], axis=0).T
     weights = jnp.concatenate([cw_ref[...].astype(F32), jnp.zeros((L - H, L), F32)], axis=0)
     pair = pair_ref[...].astype(F32) + jnp.dot(
@@ -183,8 +197,6 @@
     normed = normalize(own_row.astype(F32)).astype(BF)
     one = around(lax.all_gather(normed, "c", axis=0, tiled=False))
     two = around(one)
-    three = around(two)
-    four = around(jnp.where(c == 0, three[1], three[0]))
 
     bias = lax.dot_general(offsets, pair_own, (((0,), (1,)), ((), ())), preferred_element_type=F32).astype(BF)
     bias_pairs = jnp.stack([bias[first_head(n) : first_head(n) + 2] for n in range(8)])
@@ -199,17 +211,18 @@
         axis=1,
     )
     came = lax.all_to_all(message, CHIPS, 0, 0, tiled=True)
-    came, one = lax.optimization_barrier((came, one))
-
     source = lax.broadcasted_iota(jnp.int32, (2048, 384), 0)
     target = lax.broadcasted_iota(jnp.int32, (2048, 384), 1)
     column = (source // 32 * 2 + c) * 18 + source % 32
     wanted = target // 128 * D + first_head(y) * E + target % 128
     pick = jnp.logical_and(column == wanted, source % 32 < 18).astype(BF)
+    came, one, pick = lax.optimization_barrier((came, one, pick))
     picked = dot_tn(came.reshape(2048, 128), pick)[:96].astype(BF)
     picked = lax.all_gather(picked, "c", axis=0, tiled=False)
     half = lax.dynamic_slice_in_dim(picked, c * 48, 48, axis=1)
-    half = half[0] + half[1]
+    half, two = lax.optimization_barrier((half[0] + half[1], two))
+    three = around(two)
+    four = around(jnp.where(c == 0, three[1], three[0]))
     over_z = lax.all_to_all(jnp.broadcast_to(half, (8, 48, 384)), "z", 0, 0, tiled=True)
     w_heads = lax.all_gather(over_z, "c", axis=0, tiled=False).reshape(D, 384)
 
@@ -263,9 +276,18 @@
     alignment, pair_out = pl.pallas_call(
         column_block,
         out_shape=(jax.ShapeDtypeStruct((R, D), BF), jax.ShapeDtypeStruct((L, 128), BF)),
-        in_specs=[SMEM] + [VMEM] * 7,
+        in_specs=[SMEM, VMEM] + [ANY] * 6,
         out_specs=(VMEM, VMEM),
-        compiler_params=params(),
+        scratch_shapes=[
+            pltpu.VMEM((D, R), BF),
+            pltpu.VMEM((D, D), BF),
+            pltpu.VMEM((3 * D, D), BF),
+            pltpu.VMEM((D, D), BF),
+            pltpu.VMEM((L, 128), BF),
+            pltpu.VMEM((H, 128), BF),
+            pltpu.SemaphoreType.DMA((6,)),
+        ],
+        compiler_params=params(56),
     )(c1, blended, stack_own.T, row_out, column_triple, column_out, pair_own, contact_w)
     return alignment.reshape(R, 1, D), pair_out.reshape(1, L, 128)
 

time: 163 us -> 157 us (0.963)
  waiting for transfers between devices: 36.4 us -> 29.2 us
  Pallas kernels: 10.7 us -> 13.5 us
  local copies, waits for them, and re-layouts: 23.9 us -> 21.2 us
  blocking collectives: 17.1 us -> 19.8 us
  starting transfers between devices: 52.3 us -> 49.7 us
  other arithmetic: 3.25 us -> 5.83 us
  matrix products: 3 us -> 1.36 us
    ppermute x4, waiting for transfers between devices: 16.6 us -> 11.8 us  [around(): return lax.ppermute(x, ('y', 'c'), pairs)]
    unnamed x23 -> x13, local copies, waits for them, and re-layouts: 4.53 us -> 0.32 us
    all_to_all x1, waiting for transfers between devices: 10.6 us -> 7.29 us  [per_device(): lax.all_to_all(jnp.broadcast_to(half, (8, 48, 384)), 'z', 0, 0, tiled=True)]
    ppermute x4, starting transfers between devices: 17.4 us -> 14.3 us  [around(): return lax.ppermute(x, ('y', 'c'), pairs)]
    pallas_call x1, Pallas kernels: 6.61 us -> 9.44 us  [per_device(): pl.pallas_call(column_block, out_shape=(jax.ShapeDtypeStruct((R, D), BF),...]
    convert_element_type x0 -> x1, other arithmetic: none -> 2.59 us  [per_device(): pick = jnp.logical_and(column == wanted, source % 32 < 18).astype(BF)]
    all_gather x1, blocking collectives: 3.06 us -> 5.48 us  [per_device(): w_heads = lax.all_gather(over_z, 'c', axis=0, tiled=False).reshape(D, 384)]
    all_to_all x1, starting transfers between devices: 3.41 us -> 5.23 us  [per_device(): lax.all_to_all(jnp.broadcast_to(tied, (8, L, L)), 'z', 0, 0, tiled=True)]
  transfers between devices with their start and end apart: 9 -> 9, of which waited for: 4 -> 4; matrix products, arithmetic and copies ran while one was open for 15% -> 17% of each run, Pallas kernels for 3% -> 3%
where the time goes in v7:
time: 157 us; the launch traced here: 156 us
  starting transfers between devices  49.7 us (32%)
  waiting for transfers between devices  29.2 us (19%)
  local copies, waits for them, and re-layouts  21.2 us (14%)
  blocking collectives  19.8 us (13%)
  between operations  15.1 us (10%)
  Pallas kernels  13.5 us (9%)
  other arithmetic  5.83 us (4%)
    all_to_all x1, starting transfers between devices, per_device(): came = lax.all_to_all(message, CHIPS, 0, 0, tiled=True)  17.1 us
    ppermute x4, starting transfers between devices, around(): return lax.ppermute(x, ('y', 'c'), pairs)  14.3 us
    ppermute x4, waiting for transfers between devices, around(): return lax.ppermute(x, ('y', 'c'), pairs)  11.8 us
    all_to_all x1, waiting for transfers between devices, per_device(): lax.all_to_all(jnp.broadcast_to(tied, (8, L, L)), 'z', 0, 0, tiled=True)  10.1 us
    pallas_call x1, Pallas kernels, per_device(): pl.pallas_call(column_block, out_shape=(jax.ShapeDtypeStruct((R, D), BF),...  9.44 us
    all_to_all x1, waiting for transfers between devices, per_device(): lax.all_to_all(jnp.broadcast_to(half, (8, 48, 384)), 'z', 0, 0, tiled=True)  7.29 us
    reshape x1, local copies, waits for them, and re-layouts, per_device(): column_triple = gathered[:, :18].reshape(3 * D, D)  6.56 us
    all_to_all x1, starting transfers between devices, per_device(): lax.all_to_all(jnp.broadcast_to(half, (8, 48, 384)), 'z', 0, 0, tiled=True)  6.54 us
  transfers between devices with their start and end apart: 9, of which 4 were waited for; matrix products, arithmetic and copies ran while one was open for 17% of the time, Pallas kernels for 3%

profile of v7, /device:TPU:1, one launch (start us, length us, event | category | flops | bytes accessed | tf_op | source)
XLA Modules:
  0.0 155.8 jit_solution(6371596387305758841)
XLA Ops:
  7.2 0.0 copy-start
  7.2 0.0 copy-start.2
  7.2 0.0 all-gather.9.cloned.1.call-start
  7.2 0.1 pad.8.clone
  7.3 1.5 maximum_maximum_fusion
  8.8 0.0 all-gather.9.cloned.1.call-update
  8.8 0.9 reshape.94
  9.7 0.1 copy.35
  9.8 0.1 reshape.95
  10.0 1.1 reshape_reshape.3
  11.1 0.9 convolution_convert_fusion
  12.1 0.1 broadcast_in_dim.33
  12.2 1.0 pad_maximum_fusion
  13.2 17.1 %all-to-all-start = ((bf16[64,32,128]{2,1,0:T(8,128)(2,1)}), bf16[64,32,128]{2,1,0:T(8,128)(2,1)S(1)}, u32[]{:S(2)}, u32[]{:S(2)}) async-start(bf16[64,32,128]{2,1,0:T(8,128)(2,1)} %pad_maximum_fusion), calls=%async_computation | async-start | bytes 1048576 | tf_op jit(solution)/shard_map/all_to_all | solution.py:213
  30.3 0.1 convert_reduce_fusion
  30.5 0.2 fusion.8
  30.7 0.1 fusion.4
  30.8 2.7 %all_gather.46 = bf16[2,128,768]{2,1,0:T(8,128)(2,1)S(1)} all-gather(bf16[1,128,768]{2,1,0:T(8,128)(2,1)S(1)} %fusion.4), channel_id=1, replica_groups=mesh['a'=4,'z'=8,'y'=8,'c'=2] {'c'}, dimensions={0}, use_global_device_ids=true | all-gather | bytes 589824 | tf_op jit(solution)/shard_map/all_gather | solution.py:198
  33.5 4.4 %collective-permute-start = (bf16[2,128,768]{2,1,0:T(8,128)(2,1)S(1)}, bf16[2,128,768]{2,1,0:T(8,128)(2,1)S(1)}, u32[]{:S(2)}, u32[]{:S(2)}) collective-permute-start(bf16[2,128,768]{2,1,0:T(8,128)(2,1)S(1)} %all_gather.46), channel_id=1, source_target_pairs={{0,2},{1,15},{2,4},{3,1},{4,6},{5,3},{6,8},{7,5},{8,10},{9,7},{10,... | collective-permute-start | bytes 1179656 | tf_op jit(solution)/shard_map/ppermute | solution.py:184
  38.0 2.6 %fusion.2 = bf16[2048,384]{1,0:T(8,128)(2,1)S(1)} fusion(s32[384]{0:T(512)S(1)} %get-tuple-element.39, s32[384]{0:T(512)S(1)} %get-tuple-element.40, s32[]{:T(128)S(6)} %mul.41, s32[384]{0:T(512)S(1)} %get-tuple-element.38, s32[384]{0:T(512)S(1)} %get-tuple-element.41, s32[2048]{0:T(1024)S(1)} %get-tuple-element.33, s32[2048]{0:T(1024)S(1)} %get-tuple-element.34, ...), kind=kLoop, calls=%fused_computation.4 | loop fusion | flops 11796480 | bytes 1616648 | tf_op jit(solution)/shard_map/convert_element_type | solution.py:218
  40.6 8.2 %collective-permute-done.one_ref = bf16[2,128,768]{2,1,0:T(8,128)(2,1)S(1)} collective-permute-done((bf16[2,128,768]{2,1,0:T(8,128)(2,1)S(1)}, bf16[2,128,768]{2,1,0:T(8,128)(2,1)S(1)}, u32[]{:S(2)}, u32[]{:S(2)}) %collective-permute-start) | collective-permute-done | bytes 393248 | tf_op jit(solution)/shard_map/ppermute | solution.py:184
  48.8 3.2 %collective-permute-start.1 = (bf16[2,128,768]{2,1,0:T(8,128)(2,1)S(1)}, bf16[2,128,768]{2,1,0:T(8,128)(2,1)S(1)}, u32[]{:S(2)}, u32[]{:S(2)}) collective-permute-start(bf16[2,128,768]{2,1,0:T(8,128)(2,1)S(1)} %collective-permute-done.one_ref), channel_id=1, source_target_pairs={{0,2},{1,15},{2,4},{3,1},{4,6},{5,3},{6,8},{7,5},{8,10},{9,7},{10,... | collective-permute-start | bytes 1179656 | tf_op jit(solution)/shard_map/ppermute | solution.py:184
  52.0 0.0 all-to-all-done
  52.0 0.5 fusion.28
  52.5 1.9 %all-gather = bf16[192,384]{1,0:T(8,128)(2,1)S(1)} all-gather(bf16[96,384]{1,0:T(8,128)(2,1)S(1)} %slice.132), channel_id=2, replica_groups=mesh['a'=4,'z'=8,'y'=8,'c'=2] {'c'}, dimensions={0}, use_global_device_ids=true | all-gather | bytes 221184 | tf_op jit(solution)/shard_map/all_gather | solution.py:221
  54.4 3.6 %collective-permute-done.1.two_ref = bf16[2,128,768]{2,1,0:T(8,128)(2,1)S(1)} collective-permute-done((bf16[2,128,768]{2,1,0:T(8,128)(2,1)S(1)}, bf16[2,128,768]{2,1,0:T(8,128)(2,1)S(1)}, u32[]{:S(2)}, u32[]{:S(2)}) %collective-permute-start.1) | collective-permute-done | bytes 393248 | tf_op jit(solution)/shard_map/ppermute | solution.py:184
  58.0 4.0 %collective-permute-start.2 = (bf16[2,128,768]{2,1,0:T(8,128)(2,1)S(1)}, bf16[2,128,768]{2,1,0:T(8,128)(2,1)S(1)}, u32[]{:S(2)}, u32[]{:S(2)}) collective-permute-start(bf16[2,128,768]{2,1,0:T(8,128)(2,1)S(1)} %collective-permute-done.1.two_ref), channel_id=1, source_target_pairs={{0,2},{1,15},{2,4},{3,1},{4,6},{5,3},{6,8},{7,5},{8,10},{9,7},{10,... | collective-permute-start | bytes 1179656 | tf_op jit(solution)/shard_map/ppermute | solution.py:184
  62.0 0.8 broadcast_in_dim.35
  62.7 6.5 %all-to-all-start.1 = ((bf16[8,48,384]{2,1,0:T(8,128)(2,1)}), bf16[8,48,384]{2,1,0:T(8,128)(2,1)S(1)}, u32[]{:S(2)}, u32[]{:S(2)}) async-start(bf16[8,48,384]{2,1,0:T(8,128)(2,1)} %broadcast_in_dim.35), calls=%async_computation.1 | async-start | bytes 589824 | tf_op jit(solution)/shard_map/all_to_all | solution.py:226
  69.3 0.1 fusion.9.own_ref
  69.4 0.0 collective-permute-done.2.three_ref
  69.5 2.7 %collective-permute-start.3 = (bf16[128,768]{1,0:T(8,128)(2,1)S(1)}, bf16[128,768]{1,0:T(8,128)(2,1)S(1)}, u32[]{:S(2)}, u32[]{:S(2)}) collective-permute-start(bf16[128,768]{1,0:T(8,128)(2,1)S(1)} %fusion.10), channel_id=1, source_target_pairs={{0,2},{1,15},{2,4},{3,1},{4,6},{5,3},{6,8},{7,5},{8,10},{9,7},{10,... | collective-permute-start | bytes 589832 | tf_op jit(solution)/shard_map/ppermute | solution.py:184
  72.2 0.1 pad_add_fusion.at_ref
  72.3 7.3 %all-to-all-done.1 = bf16[8,48,384]{2,1,0:T(8,128)(2,1)S(1)} async-done(((bf16[8,48,384]{2,1,0:T(8,128)(2,1)}), bf16[8,48,384]{2,1,0:T(8,128)(2,1)S(1)}, u32[]{:S(2)}, u32[]{:S(2)}) %all-to-all-start.1) | async-done | bytes 294944 | tf_op jit(solution)/shard_map/all_to_all | solution.py:226
  79.6 5.5 %all-gather.1 = bf16[16,48,384]{2,1,0:T(8,128)(2,1)S(1)} all-gather(bf16[8,48,384]{2,1,0:T(8,128)(2,1)S(1)} %all-to-all-done.1), channel_id=3, replica_groups=mesh['a'=4,'z'=8,'y'=8,'c'=2] {'c'}, dimensions={0}, use_global_device_ids=true | all-gather | bytes 884736 | tf_op jit(solution)/shard_map/all_gather | solution.py:227
  85.0 0.0 collective-permute-done.3.four_ref
  85.0 2.7 %shard_map.104 = (f32[2,128,128]{2,1,0:T(8,128)S(1)}, bf16[8,128,128]{2,1,0:T(8,128)(2,1)S(1)}) custom-call(s32[2]{0:T(128)S(1)} %pad_add_fusion.at_ref, bf16[768,384]{1,0:T(8,128)(2,1)S(1)} %bitcast.91, bf16[128,768]{1,0:T(8,128)(2,1)S(1)} %fusion.9.own_ref, bf16[2,128,768]{2,1,0:T(8,128)(2,1)S(1)} %collective-permute-done.one_ref, ...), custom_call_target="tpu_custom_call" | custom-call | tf_op jit(solution)/shard_map/pallas_call | solution.py:236
  87.7 2.0 %all-gather.2 = f32[4,128,128]{2,1,0:T(8,128)S(1)} all-gather(f32[2,128,128]{2,1,0:T(8,128)S(1)} %get-tuple-element.20), channel_id=4, replica_groups=mesh['a'=4,'z'=8,'y'=8,'c'=2] {'c'}, dimensions={0}, use_global_device_ids=true | all-gather | bytes 393216 | tf_op jit(solution)/shard_map/all_gather | solution.py:247
  89.7 0.7 broadcast_in_dim.36
  90.5 5.2 %all-to-all-start.2 = ((bf16[8,128,128]{2,1,0:T(8,128)(2,1)}), bf16[8,128,128]{2,1,0:T(8,128)(2,1)S(1)}, u32[]{:S(2)}, u32[]{:S(2)}) async-start(bf16[8,128,128]{2,1,0:T(8,128)(2,1)} %broadcast_in_dim.36), calls=%async_computation.2 | async-start | bytes 524288 | tf_op jit(solution)/shard_map/all_to_all | solution.py:250
  96.4 0.1 slice.81
  96.5 0.1 copy.28
  96.5 2.6 %all-gather.3 = bf16[128,14,128]{2,0,1:T(8,128)(2,1)S(1)} all-gather(bf16[64,14,128]{2,0,1:T(8,128)(2,1)S(1)} %copy.28), channel_id=5, replica_groups=mesh['a'=4,'z'=8,'y'=8,'c'=2] {'c'}, dimensions={0}, use_global_device_ids=true | all-gather | bytes 688128 | tf_op jit(solution)/shard_map/all_gather | solution.py:229
  99.1 10.1 %all-to-all-done.2.part_ref = bf16[8,128,128]{2,1,0:T(8,128)(2,1)S(1)} async-done(((bf16[8,128,128]{2,1,0:T(8,128)(2,1)}), bf16[8,128,128]{2,1,0:T(8,128)(2,1)S(1)}, u32[]{:S(2)}, u32[]{:S(2)}) %all-to-all-start.2) | async-done | bytes 262176 | tf_op jit(solution)/shard_map/all_to_all | solution.py:250
  109.2 0.2 shard_map.105
  109.5 2.4 %all-gather.4 = bf16[4,128,128]{2,1,0:T(8,128)(2,1)S(1)} all-gather(bf16[2,128,128]{2,1,0:T(8,128)(2,1)S(1)} %shard_map.105), channel_id=6, replica_groups=mesh['a'=4,'z'=8,'y'=8,'c'=2] {'c'}, dimensions={0}, use_global_device_ids=true | all-gather | bytes 196608 | tf_op jit(solution)/shard_map/all_gather | solution.py:258
  111.9 1.2 shard_map.106
  113.1 6.5 %all-to-all-start.3 = ((bf16[64,16,128]{2,1,0:T(8,128)(2,1)}), bf16[64,16,128]{2,1,0:T(8,128)(2,1)S(1)}, u32[]{:S(2)}, u32[]{:S(2)}) async-start(bf16[64,16,128]{2,1,0:T(8,128)(2,1)} %bitcast.29), calls=%async_computation.3 | async-start | bytes 524288 | tf_op jit(solution)/shard_map/all_to_all | solution.py:267
  119.6 0.3 copy.30
  119.9 0.2 reshape.106
  120.2 0.4 constant_dynamic-slice_fusion
  120.6 0.3 copy.31
  120.9 0.1 copy.32
  121.0 0.1 reshape.108
  121.1 0.8 copy.33
  121.9 5.0 %slice.99 = bf16[128,18,768]{2,1,0:T(8,128)(2,1)} slice(bf16[128,32,768]{2,1,0:T(8,128)(2,1)} %bitcast.94), slice={[0:128], [0:18], [0:768]} | slice | bytes 7077888 | tf_op jit(solution)/shard_map/slice | solution.py:268
  127.0 0.2 copy-done.1
  127.2 0.5 fusion.27
  127.7 1.3 reshape.104.refs_3_
  128.9 1.2 reshape.105.refs_1_
  130.2 6.6 %reshape.103.refs_2_ = bf16[2304,768]{1,0:T(8,128)(2,1)} reshape(bf16[128,18,768]{2,1,0:T(8,128)(2,1)} %slice.99) | data formatting | bytes 7077888 | tf_op jit(solution)/shard_map/reshape | solution.py:268
  136.7 0.0 all-to-all-done.3
  136.7 2.7 %all-gather.6 = bf16[128,16,128]{2,1,0:T(8,128)(2,1)} all-gather(bf16[64,16,128]{2,1,0:T(8,128)(2,1)S(1)} %all-to-all-done.3), channel_id=8, replica_groups=mesh['a'=4,'z'=8,'y'=8,'c'=2] {'c'}, dimensions={0}, use_global_device_ids=true | all-gather | bytes 786432 | tf_op jit(solution)/shard_map/all_gather | solution.py:274
  139.5 9.4 %shard_map.107 = (bf16[128,768]{1,0:T(8,128)(2,1)}, bf16[128,128]{1,0:T(8,128)(2,1)}) custom-call(s32[1]{0:T(128)} %bitcast.c_ref, bf16[2,64,16,128]{3,2,1,0:T(8,128)(2,1)} %bitcast.97, bf16[768,128]{1,0:T(8,128)(2,1)} %bitcast.101, bf16[768,768]{1,0:T(8,128)(2,1)} %reshape.105.refs_1_, bf16[2304,768]{1,0:T(8,128)(2,1)} %reshape.103.refs_2_, ...), custom_call_target="tpu_custom_call" | custom-call | tf_op jit(solution)/shard_map/pallas_call | solution.py:276
  (32 shorter events, 0.3 us)
Async XLA Ops:
  7.2 3.9 %copy-start = (bf16[128,12]{0,1:T(8,128)(2,1)S(1)}, bf16[128,12]{0,1:T(8,128)(2,1)}, u32[]{:S(2)}) copy-start(bf16[128,12]{0,1:T(8,128)(2,1)} %param.16) | copy-start | bytes 9220
  7.2 23.1 %copy-start.2 = (bf16[1,128,768]{2,1,0:T(8,128)(2,1)S(1)}, bf16[1,128,768]{2,1,0:T(8,128)(2,1)}, u32[]{:S(2)}) copy-start(bf16[1,128,768]{2,1,0:T(8,128)(2,1)} %param.9) | copy-start | bytes 589828
  7.2 114.7 %all-gather.9.cloned.1.call-start = ((), (), s32[]{:S(2)}) async-start(), calls=%async_computation.4 | async-start | bytes 6340608 | tf_op jit(solution)/shard_map/all_gather | solution.py:195
  13.2 38.8 %all-to-all-start = ((bf16[64,32,128]{2,1,0:T(8,128)(2,1)}), bf16[64,32,128]{2,1,0:T(8,128)(2,1)S(1)}, u32[]{:S(2)}, u32[]{:S(2)}) async-start(bf16[64,32,128]{2,1,0:T(8,128)(2,1)} %pad_maximum_fusion), calls=%async_computation | async-start | bytes 1048576 | tf_op jit(solution)/shard_map/all_to_all | solution.py:213
  33.5 15.3 %collective-permute-start = (bf16[2,128,768]{2,1,0:T(8,128)(2,1)S(1)}, bf16[2,128,768]{2,1,0:T(8,128)(2,1)S(1)}, u32[]{:S(2)}, u32[]{:S(2)}) collective-permute-start(bf16[2,128,768]{2,1,0:T(8,128)(2,1)S(1)} %all_gather.46), channel_id=1, source_target_pairs={{0,2},{1,15},{2,4},{3,1},{4,6},{5,3},{6,8},{7,5},{8,10},{9,7},{10,... | collective-permute-start | bytes 1179656 | tf_op jit(solution)/shard_map/ppermute | solution.py:184
  48.8 9.2 %collective-permute-start.1 = (bf16[2,128,768]{2,1,0:T(8,128)(2,1)S(1)}, bf16[2,128,768]{2,1,0:T(8,128)(2,1)S(1)}, u32[]{:S(2)}, u32[]{:S(2)}) collective-permute-start(bf16[2,128,768]{2,1,0:T(8,128)(2,1)S(1)} %collective-permute-done.one_ref), channel_id=1, source_target_pairs={{0,2},{1,15},{2,4},{3,1},{4,6},{5,3},{6,8},{7,5},{8,10},{9,7},{10,... | collective-permute-start | bytes 1179656 | tf_op jit(solution)/shard_map/ppermute | solution.py:184
  58.0 11.4 %collective-permute-start.2 = (bf16[2,128,768]{2,1,0:T(8,128)(2,1)S(1)}, bf16[2,128,768]{2,1,0:T(8,128)(2,1)S(1)}, u32[]{:S(2)}, u32[]{:S(2)}) collective-permute-start(bf16[2,128,768]{2,1,0:T(8,128)(2,1)S(1)} %collective-permute-done.1.two_ref), channel_id=1, source_target_pairs={{0,2},{1,15},{2,4},{3,1},{4,6},{5,3},{6,8},{7,5},{8,10},{9,7},{10,... | collective-permute-start | bytes 1179656 | tf_op jit(solution)/shard_map/ppermute | solution.py:184
  62.7 16.8 %all-to-all-start.1 = ((bf16[8,48,384]{2,1,0:T(8,128)(2,1)}), bf16[8,48,384]{2,1,0:T(8,128)(2,1)S(1)}, u32[]{:S(2)}, u32[]{:S(2)}) async-start(bf16[8,48,384]{2,1,0:T(8,128)(2,1)} %broadcast_in_dim.35), calls=%async_computation.1 | async-start | bytes 589824 | tf_op jit(solution)/shard_map/all_to_all | solution.py:226
  69.5 15.6 %collective-permute-start.3 = (bf16[128,768]{1,0:T(8,128)(2,1)S(1)}, bf16[128,768]{1,0:T(8,128)(2,1)S(1)}, u32[]{:S(2)}, u32[]{:S(2)}) collective-permute-start(bf16[128,768]{1,0:T(8,128)(2,1)S(1)} %fusion.10), channel_id=1, source_target_pairs={{0,2},{1,15},{2,4},{3,1},{4,6},{5,3},{6,8},{7,5},{8,10},{9,7},{10,... | collective-permute-start | bytes 589832 | tf_op jit(solution)/shard_map/ppermute | solution.py:184
  90.5 18.8 %all-to-all-start.2 = ((bf16[8,128,128]{2,1,0:T(8,128)(2,1)}), bf16[8,128,128]{2,1,0:T(8,128)(2,1)S(1)}, u32[]{:S(2)}, u32[]{:S(2)}) async-start(bf16[8,128,128]{2,1,0:T(8,128)(2,1)} %broadcast_in_dim.36), calls=%async_computation.2 | async-start | bytes 524288 | tf_op jit(solution)/shard_map/all_to_all | solution.py:250
  113.1 23.6 %all-to-all-start.3 = ((bf16[64,16,128]{2,1,0:T(8,128)(2,1)}), bf16[64,16,128]{2,1,0:T(8,128)(2,1)S(1)}, u32[]{:S(2)}, u32[]{:S(2)}) async-start(bf16[64,16,128]{2,1,0:T(8,128)(2,1)} %bitcast.29), calls=%async_computation.3 | async-start | bytes 524288 | tf_op jit(solution)/shard_map/all_to_all | solution.py:267
  121.9 5.3 %copy-start.1 = (bf16[4096,768]{1,0:T(8,128)(2,1)S(1)}, bf16[4096,768]{1,0:T(8,128)(2,1)}, u32[]{:S(2)}) copy-start(bf16[4096,768]{1,0:T(8,128)(2,1)} %all-gather.9.cloned.1.call-done) | copy-start | bytes 18874372
Sparse Core Ops, SparseCore 0:
  11.7 99.1 all-gather.8

commit v8 on v6

--- a/solution.py
+++ b/solution.py
@@ -13,10 +13,11 @@
 BF, F32 = jnp.bfloat16, jnp.float32
 VMEM = pl.BlockSpec(memory_space=pltpu.VMEM)
 SMEM = pl.BlockSpec(memory_space=pltpu.SMEM)
-
-
-def params():
-    return pltpu.CompilerParams(vmem_limit_bytes=28 << 20)
+ANY = pl.BlockSpec(memory_space=pl.ANY)
+
+
+def params(mib=16):
+    return pltpu.CompilerParams(vmem_limit_bytes=mib << 20)
 
 
 def dot_nt(a, b):
@@ -93,7 +94,11 @@
     out_ref[...] = held[...].astype(BF)
 
 
-def column_block(c_ref, bl_ref, stack_ref, who_ref, wv_ref, wvo_ref, pair_ref, cw_ref, out_ref, pair_out_ref):
+def column_block(
+    c_ref, bl_ref, stack_ref, who_ref, far_ref, wvo_ref, pair_ref, cw_ref, out_ref, pair_out_ref, wv_ref, sem
+):
+    copy = pltpu.make_async_copy(far_ref, wv_ref, sem)
+    copy.start()
     mine = c_ref[0]
     lane = lax.broadcasted_iota(jnp.int32, (L, L), 1)
     row = lax.broadcasted_iota(jnp.int32, (L, L), 0)
@@ -132,6 +137,7 @@
     center = jnp.mean(updated, axis=0, keepdims=True)
     spread = jnp.mean(jnp.square(updated - center), axis=0, keepdims=True)
     normed = ((updated - center) * lax.rsqrt(spread + 1e-05)).astype(BF)
+    copy.wait()
     packed = jnp.dot(wv_ref[...], normed, preferred_element_type=F32)
 
     mixed = []
@@ -183,8 +189,6 @@
     normed = normalize(own_row.astype(F32)).astype(BF)
     one = around(lax.all_gather(normed, "c", axis=0, tiled=False))
     two = around(one)
-    three = around(two)
-    four = around(jnp.where(c == 0, three[1], three[0]))
 
     bias = lax.dot_general(offsets, pair_own, (((0,), (1,)), ((), ())), preferred_element_type=F32).astype(BF)
     bias_pairs = jnp.stack([bias[first_head(n) : first_head(n) + 2] for n in range(8)])
@@ -199,17 +203,18 @@
         axis=1,
     )
     came = lax.all_to_all(message, CHIPS, 0, 0, tiled=True)
-    came, one = lax.optimization_barrier((came, one))
-
     source = lax.broadcasted_iota(jnp.int32, (2048, 384), 0)
     target = lax.broadcasted_iota(jnp.int32, (2048, 384), 1)
     column = (source // 32 * 2 + c) * 18 + source % 32
     wanted = target // 128 * D + first_head(y) * E + target % 128
     pick = jnp.logical_and(column == wanted, source % 32 < 18).astype(BF)
+    came, one, pick = lax.optimization_barrier((came, one, pick))
     picked = dot_tn(came.reshape(2048, 128), pick)[:96].astype(BF)
     picked = lax.all_gather(picked, "c", axis=0, tiled=False)
     half = lax.dynamic_slice_in_dim(picked, c * 48, 48, axis=1)
-    half = half[0] + half[1]
+    half, two = lax.optimization_barrier((half[0] + half[1], two))
+    three = around(two)
+    four = around(jnp.where(c == 0, three[1], three[0]))
     over_z = lax.all_to_all(jnp.broadcast_to(half, (8, 48, 384)), "z", 0, 0, tiled=True)
     w_heads = lax.all_gather(over_z, "c", axis=0, tiled=False).reshape(D, 384)
 
@@ -255,17 +260,16 @@
     column_triple = gathered[:, :18].reshape(3 * D, D)
     column_out = gathered[:, 18:24].reshape(D, D)
     row_out = gathered[:, 24:30].reshape(D, D)
-    came, column_triple, column_out, row_out = lax.optimization_barrier(
-        (came, column_triple, column_out, row_out)
-    )
+    came, column_triple = lax.optimization_barrier((came, column_triple))
     blended = lax.all_gather(came, "c", axis=0, tiled=False)
 
     alignment, pair_out = pl.pallas_call(
         column_block,
         out_shape=(jax.ShapeDtypeStruct((R, D), BF), jax.ShapeDtypeStruct((L, 128), BF)),
-        in_specs=[SMEM] + [VMEM] * 7,
+        in_specs=[SMEM] + [VMEM] * 3 + [ANY] + [VMEM] * 3,
         out_specs=(VMEM, VMEM),
-        compiler_params=params(),
+        scratch_shapes=[pltpu.VMEM((3 * D, D), BF), pltpu.SemaphoreType.DMA],
+        compiler_params=params(48),
     )(c1, blended, stack_own.T, row_out, column_triple, column_out, pair_own, contact_w)
     return alignment.reshape(R, 1, D), pair_out.reshape(1, L, 128)
 

time: 163 us -> 158 us (0.969)
  waiting for transfers between devices: 36.4 us -> 29.4 us
  starting transfers between devices: 52.3 us -> 49.7 us
  other arithmetic: 3.25 us -> 5.84 us
  blocking collectives: 17.1 us -> 19.5 us
  Pallas kernels: 10.7 us -> 12.6 us
  matrix products: 3 us -> 1.36 us
    ppermute x4, waiting for transfers between devices: 16.6 us -> 11.8 us  [around(): return lax.ppermute(x, ('y', 'c'), pairs)]
    unnamed x23 -> x15, local copies, waits for them, and re-layouts: 4.53 us -> 0.11 us
    all_to_all x1, waiting for transfers between devices: 10.6 us -> 7.27 us  [per_device(): lax.all_to_all(jnp.broadcast_to(half, (8, 48, 384)), 'z', 0, 0, tiled=True)]
    ppermute x4, starting transfers between devices: 17.4 us -> 14.3 us  [around(): return lax.ppermute(x, ('y', 'c'), pairs)]
    slice x1, local copies, waits for them, and re-layouts: 0.48 us -> 3.42 us  [per_device(): column_out = gathered[:, 18:24].reshape(D, D)]
    convert_element_type x0 -> x1, other arithmetic: none -> 2.59 us  [per_device(): pick = jnp.logical_and(column == wanted, source % 32 < 18).astype(BF)]
    all_gather x1, blocking collectives: 3.06 us -> 5.46 us  [per_device(): w_heads = lax.all_gather(over_z, 'c', axis=0, tiled=False).reshape(D, 384)]
    pallas_call x1, Pallas kernels: 6.61 us -> 8.49 us  [per_device(): pl.pallas_call(column_block, out_shape=(jax.ShapeDtypeStruct((R, D), BF),...]
  transfers between devices with their start and end apart: 9 -> 9, of which waited for: 4 -> 4; matrix products, arithmetic and copies ran while one was open for 15% -> 17% of each run, Pallas kernels for 3% -> 3%
where the time goes in v8:
time: 158 us; the launch traced here: 157 us
  starting transfers between devices  49.7 us (31%)
  waiting for transfers between devices  29.4 us (19%)
  local copies, waits for them, and re-layouts  23.4 us (15%)
  blocking collectives  19.5 us (12%)
  between operations  15.1 us (10%)
  Pallas kernels  12.6 us (8%)
  other arithmetic  5.84 us (4%)
    all_to_all x1, starting transfers between devices, per_device(): came = lax.all_to_all(message, CHIPS, 0, 0, tiled=True)  17.1 us
    ppermute x4, starting transfers between devices, around(): return lax.ppermute(x, ('y', 'c'), pairs)  14.3 us
    ppermute x4, waiting for transfers between devices, around(): return lax.ppermute(x, ('y', 'c'), pairs)  11.8 us
    all_to_all x1, waiting for transfers between devices, per_device(): lax.all_to_all(jnp.broadcast_to(tied, (8, L, L)), 'z', 0, 0, tiled=True)  10.2 us
    pallas_call x1, Pallas kernels, per_device(): pl.pallas_call(column_block, out_shape=(jax.ShapeDtypeStruct((R, D), BF),...  8.49 us
    all_to_all x1, waiting for transfers between devices, per_device(): lax.all_to_all(jnp.broadcast_to(half, (8, 48, 384)), 'z', 0, 0, tiled=True)  7.27 us
    reshape x1, local copies, waits for them, and re-layouts, per_device(): column_triple = gathered[:, :18].reshape(3 * D, D)  6.57 us
    all_to_all x1, starting transfers between devices, per_device(): lax.all_to_all(jnp.broadcast_to(half, (8, 48, 384)), 'z', 0, 0, tiled=True)  6.5 us
  transfers between devices with their start and end apart: 9, of which 4 were waited for; matrix products, arithmetic and copies ran while one was open for 17% of the time, Pallas kernels for 3%

profile of v8, /device:TPU:1, one launch (start us, length us, event | category | flops | bytes accessed | tf_op | source)
XLA Modules:
  0.0 156.9 jit_solution(7687113566103319596)
XLA Ops:
  7.2 0.0 copy-start
  7.2 0.0 copy-start.3
  7.2 0.0 all-gather.9.cloned.1.call-start
  7.2 0.1 pad.8.clone
  7.3 1.5 maximum_maximum_fusion
  8.8 0.0 all-gather.9.cloned.1.call-update
  8.8 0.9 reshape.94
  9.7 0.1 copy.35
  9.8 0.1 reshape.95
  10.0 1.1 reshape_reshape.3
  11.1 0.9 convolution_convert_fusion
  12.1 0.1 broadcast_in_dim.33
  12.2 1.0 pad_maximum_fusion
  13.2 17.1 %all-to-all-start = ((bf16[64,32,128]{2,1,0:T(8,128)(2,1)}), bf16[64,32,128]{2,1,0:T(8,128)(2,1)S(1)}, u32[]{:S(2)}, u32[]{:S(2)}) async-start(bf16[64,32,128]{2,1,0:T(8,128)(2,1)} %pad_maximum_fusion), calls=%async_computation | async-start | bytes 1048576 | tf_op jit(solution)/shard_map/all_to_all | solution.py:205
  30.3 0.1 convert_reduce_fusion
  30.5 0.2 fusion.8
  30.7 0.1 fusion.4
  30.8 2.7 %all_gather.46 = bf16[2,128,768]{2,1,0:T(8,128)(2,1)S(1)} all-gather(bf16[1,128,768]{2,1,0:T(8,128)(2,1)S(1)} %fusion.4), channel_id=1, replica_groups=mesh['a'=4,'z'=8,'y'=8,'c'=2] {'c'}, dimensions={0}, use_global_device_ids=true | all-gather | bytes 589824 | tf_op jit(solution)/shard_map/all_gather | solution.py:190
  33.5 4.4 %collective-permute-start = (bf16[2,128,768]{2,1,0:T(8,128)(2,1)S(1)}, bf16[2,128,768]{2,1,0:T(8,128)(2,1)S(1)}, u32[]{:S(2)}, u32[]{:S(2)}) collective-permute-start(bf16[2,128,768]{2,1,0:T(8,128)(2,1)S(1)} %all_gather.46), channel_id=1, source_target_pairs={{0,2},{1,15},{2,4},{3,1},{4,6},{5,3},{6,8},{7,5},{8,10},{9,7},{10,... | collective-permute-start | bytes 1179656 | tf_op jit(solution)/shard_map/ppermute | solution.py:176
  38.0 2.6 %fusion.2 = bf16[2048,384]{1,0:T(8,128)(2,1)S(1)} fusion(s32[384]{0:T(512)S(1)} %get-tuple-element.35, s32[384]{0:T(512)S(1)} %get-tuple-element.36, s32[]{:T(128)S(6)} %mul.41, s32[384]{0:T(512)S(1)} %get-tuple-element.34, s32[384]{0:T(512)S(1)} %get-tuple-element.37, s32[2048]{0:T(1024)S(1)} %get-tuple-element.29, s32[2048]{0:T(1024)S(1)} %get-tuple-element.30, ...), kind=kLoop, calls=%fused_computation.4 | loop fusion | flops 11796480 | bytes 1616648 | tf_op jit(solution)/shard_map/convert_element_type | solution.py:210
  40.6 8.2 %collective-permute-done.one_ref = bf16[2,128,768]{2,1,0:T(8,128)(2,1)S(1)} collective-permute-done((bf16[2,128,768]{2,1,0:T(8,128)(2,1)S(1)}, bf16[2,128,768]{2,1,0:T(8,128)(2,1)S(1)}, u32[]{:S(2)}, u32[]{:S(2)}) %collective-permute-start) | collective-permute-done | bytes 393248 | tf_op jit(solution)/shard_map/ppermute | solution.py:176
  48.8 3.2 %collective-permute-start.1 = (bf16[2,128,768]{2,1,0:T(8,128)(2,1)S(1)}, bf16[2,128,768]{2,1,0:T(8,128)(2,1)S(1)}, u32[]{:S(2)}, u32[]{:S(2)}) collective-permute-start(bf16[2,128,768]{2,1,0:T(8,128)(2,1)S(1)} %collective-permute-done.one_ref), channel_id=1, source_target_pairs={{0,2},{1,15},{2,4},{3,1},{4,6},{5,3},{6,8},{7,5},{8,10},{9,7},{10,... | collective-permute-start | bytes 1179656 | tf_op jit(solution)/shard_map/ppermute | solution.py:176
  52.0 0.0 all-to-all-done
  52.0 0.5 fusion.28
  52.5 1.9 %all-gather = bf16[192,384]{1,0:T(8,128)(2,1)S(1)} all-gather(bf16[96,384]{1,0:T(8,128)(2,1)S(1)} %slice.132), channel_id=2, replica_groups=mesh['a'=4,'z'=8,'y'=8,'c'=2] {'c'}, dimensions={0}, use_global_device_ids=true | all-gather | bytes 221184 | tf_op jit(solution)/shard_map/all_gather | solution.py:213
  54.4 3.6 %collective-permute-done.1.two_ref = bf16[2,128,768]{2,1,0:T(8,128)(2,1)S(1)} collective-permute-done((bf16[2,128,768]{2,1,0:T(8,128)(2,1)S(1)}, bf16[2,128,768]{2,1,0:T(8,128)(2,1)S(1)}, u32[]{:S(2)}, u32[]{:S(2)}) %collective-permute-start.1) | collective-permute-done | bytes 393248 | tf_op jit(solution)/shard_map/ppermute | solution.py:176
  58.0 4.0 %collective-permute-start.2 = (bf16[2,128,768]{2,1,0:T(8,128)(2,1)S(1)}, bf16[2,128,768]{2,1,0:T(8,128)(2,1)S(1)}, u32[]{:S(2)}, u32[]{:S(2)}) collective-permute-start(bf16[2,128,768]{2,1,0:T(8,128)(2,1)S(1)} %collective-permute-done.1.two_ref), channel_id=1, source_target_pairs={{0,2},{1,15},{2,4},{3,1},{4,6},{5,3},{6,8},{7,5},{8,10},{9,7},{10,... | collective-permute-start | bytes 1179656 | tf_op jit(solution)/shard_map/ppermute | solution.py:176
  62.0 0.8 broadcast_in_dim.35
  62.7 6.5 %all-to-all-start.1 = ((bf16[8,48,384]{2,1,0:T(8,128)(2,1)}), bf16[8,48,384]{2,1,0:T(8,128)(2,1)S(1)}, u32[]{:S(2)}, u32[]{:S(2)}) async-start(bf16[8,48,384]{2,1,0:T(8,128)(2,1)} %broadcast_in_dim.35), calls=%async_computation.1 | async-start | bytes 589824 | tf_op jit(solution)/shard_map/all_to_all | solution.py:218
  69.2 0.1 fusion.9.own_ref
  69.4 0.0 collective-permute-done.2.three_ref
  69.4 2.8 %collective-permute-start.3 = (bf16[128,768]{1,0:T(8,128)(2,1)S(1)}, bf16[128,768]{1,0:T(8,128)(2,1)S(1)}, u32[]{:S(2)}, u32[]{:S(2)}) collective-permute-start(bf16[128,768]{1,0:T(8,128)(2,1)S(1)} %fusion.10), channel_id=1, source_target_pairs={{0,2},{1,15},{2,4},{3,1},{4,6},{5,3},{6,8},{7,5},{8,10},{9,7},{10,... | collective-permute-start | bytes 589832 | tf_op jit(solution)/shard_map/ppermute | solution.py:176
  72.2 0.1 pad_add_fusion.at_ref
  72.3 7.3 %all-to-all-done.1 = bf16[8,48,384]{2,1,0:T(8,128)(2,1)S(1)} async-done(((bf16[8,48,384]{2,1,0:T(8,128)(2,1)}), bf16[8,48,384]{2,1,0:T(8,128)(2,1)S(1)}, u32[]{:S(2)}, u32[]{:S(2)}) %all-to-all-start.1) | async-done | bytes 294944 | tf_op jit(solution)/shard_map/all_to_all | solution.py:218
  79.5 5.5 %all-gather.1 = bf16[16,48,384]{2,1,0:T(8,128)(2,1)S(1)} all-gather(bf16[8,48,384]{2,1,0:T(8,128)(2,1)S(1)} %all-to-all-done.1), channel_id=3, replica_groups=mesh['a'=4,'z'=8,'y'=8,'c'=2] {'c'}, dimensions={0}, use_global_device_ids=true | all-gather | bytes 884736 | tf_op jit(solution)/shard_map/all_gather | solution.py:219
  85.0 0.0 collective-permute-done.3.four_ref
  85.0 2.7 %shard_map.104 = (f32[2,128,128]{2,1,0:T(8,128)S(1)}, bf16[8,128,128]{2,1,0:T(8,128)(2,1)S(1)}) custom-call(s32[2]{0:T(128)S(1)} %pad_add_fusion.at_ref, bf16[768,384]{1,0:T(8,128)(2,1)S(1)} %bitcast.91, bf16[128,768]{1,0:T(8,128)(2,1)S(1)} %fusion.9.own_ref, bf16[2,128,768]{2,1,0:T(8,128)(2,1)S(1)} %collective-permute-done.one_ref, ...), custom_call_target="tpu_custom_call" | custom-call | tf_op jit(solution)/shard_map/pallas_call | solution.py:228
  87.7 2.0 %all-gather.2 = f32[4,128,128]{2,1,0:T(8,128)S(1)} all-gather(f32[2,128,128]{2,1,0:T(8,128)S(1)} %get-tuple-element.18), channel_id=4, replica_groups=mesh['a'=4,'z'=8,'y'=8,'c'=2] {'c'}, dimensions={0}, use_global_device_ids=true | all-gather | bytes 393216 | tf_op jit(solution)/shard_map/all_gather | solution.py:239
  89.7 0.8 broadcast_in_dim.36
  90.4 5.3 %all-to-all-start.2 = ((bf16[8,128,128]{2,1,0:T(8,128)(2,1)}), bf16[8,128,128]{2,1,0:T(8,128)(2,1)S(1)}, u32[]{:S(2)}, u32[]{:S(2)}) async-start(bf16[8,128,128]{2,1,0:T(8,128)(2,1)} %broadcast_in_dim.36), calls=%async_computation.2 | async-start | bytes 524288 | tf_op jit(solution)/shard_map/all_to_all | solution.py:242
  96.4 0.1 slice.81
  96.5 0.1 copy.28
  96.5 2.5 %all-gather.3 = bf16[128,14,128]{2,0,1:T(8,128)(2,1)S(1)} all-gather(bf16[64,14,128]{2,0,1:T(8,128)(2,1)S(1)} %copy.28), channel_id=5, replica_groups=mesh['a'=4,'z'=8,'y'=8,'c'=2] {'c'}, dimensions={0}, use_global_device_ids=true | all-gather | bytes 688128 | tf_op jit(solution)/shard_map/all_gather | solution.py:221
  99.1 10.2 %all-to-all-done.2.part_ref = bf16[8,128,128]{2,1,0:T(8,128)(2,1)S(1)} async-done(((bf16[8,128,128]{2,1,0:T(8,128)(2,1)}), bf16[8,128,128]{2,1,0:T(8,128)(2,1)S(1)}, u32[]{:S(2)}, u32[]{:S(2)}) %all-to-all-start.2) | async-done | bytes 262176 | tf_op jit(solution)/shard_map/all_to_all | solution.py:242
  109.3 0.2 shard_map.105
  109.5 2.4 %all-gather.4 = bf16[4,128,128]{2,1,0:T(8,128)(2,1)S(1)} all-gather(bf16[2,128,128]{2,1,0:T(8,128)(2,1)S(1)} %shard_map.105), channel_id=6, replica_groups=mesh['a'=4,'z'=8,'y'=8,'c'=2] {'c'}, dimensions={0}, use_global_device_ids=true | all-gather | bytes 196608 | tf_op jit(solution)/shard_map/all_gather | solution.py:250
  111.9 1.2 shard_map.106
  113.2 6.4 %all-to-all-start.3 = ((bf16[64,16,128]{2,1,0:T(8,128)(2,1)}), bf16[64,16,128]{2,1,0:T(8,128)(2,1)S(1)}, u32[]{:S(2)}, u32[]{:S(2)}) async-start(bf16[64,16,128]{2,1,0:T(8,128)(2,1)} %bitcast.29), calls=%async_computation.3 | async-start | bytes 524288 | tf_op jit(solution)/shard_map/all_to_all | solution.py:259
  119.6 0.3 copy.30
  119.9 0.2 reshape.104
  120.1 0.4 constant_dynamic-slice_fusion
  120.6 0.3 copy.31
  120.9 0.1 copy.32
  121.0 0.1 reshape.106
  121.1 0.2 copy.33
  121.3 0.0 all-gather.9.cloned.1.call-done
  121.3 4.9 %slice.99 = bf16[128,18,768]{2,1,0:T(8,128)(2,1)} slice(bf16[128,32,768]{2,1,0:T(8,128)(2,1)} %bitcast.97), slice={[0:128], [0:18], [0:768]} | slice | bytes 7077888 | tf_op jit(solution)/shard_map/slice | solution.py:260
  126.2 6.6 %reshape.103.far_ref = bf16[2304,768]{1,0:T(8,128)(2,1)} reshape(bf16[128,18,768]{2,1,0:T(8,128)(2,1)} %slice.99) | data formatting | bytes 7077888 | tf_op jit(solution)/shard_map/reshape | solution.py:260
  132.8 3.4 %fusion.27 = (bf16[128,6,768]{2,1,0:T(8,128)(2,1)S(1)}, bf16[128,6,768]{2,1,0:T(8,128)(2,1)}) fusion(bf16[128,32,768]{2,1,0:T(8,128)(2,1)} %bitcast.98), kind=kLoop, calls=%fused_computation.70 | loop fusion | bytes 4718592 | tf_op jit(solution)/shard_map/slice | solution.py:261
  136.2 0.4 reshape.108.wvo_ref
  136.6 0.0 all-to-all-done.3
  136.6 2.6 %all-gather.6 = bf16[128,16,128]{2,1,0:T(8,128)(2,1)S(1)} all-gather(bf16[64,16,128]{2,1,0:T(8,128)(2,1)S(1)} %all-to-all-done.3), channel_id=8, replica_groups=mesh['a'=4,'z'=8,'y'=8,'c'=2] {'c'}, dimensions={0}, use_global_device_ids=true | all-gather | bytes 786432 | tf_op jit(solution)/shard_map/all_gather | solution.py:264
  139.2 2.3 %reshape.107.who_ref = bf16[768,768]{1,0:T(8,128)(2,1)S(1)} reshape(bf16[128,6,768]{2,1,0:T(8,128)(2,1)} %get-tuple-element.25) | data formatting | bytes 2359296 | tf_op jit(solution)/shard_map/reshape | solution.py:262
  141.6 8.5 %shard_map.107 = (bf16[128,768]{1,0:T(8,128)(2,1)}, bf16[128,128]{1,0:T(8,128)(2,1)}) custom-call(s32[1]{0:T(128)} %bitcast.c_ref, bf16[2,64,16,128]{3,2,1,0:T(8,128)(2,1)S(1)} %bitcast.92, bf16[768,128]{1,0:T(8,128)(2,1)S(1)} %bitcast.93, bf16[768,768]{1,0:T(8,128)(2,1)S(1)} %reshape.107.who_ref, bf16[2304,768]{1,0:T(8,128)(2,1)} %reshape.103.far_ref, ...), custom_call_target="tpu_custom_call" | custom-call | tf_op jit(solution)/shard_map/pallas_call | solution.py:266
  (34 shorter events, 0.3 us)
Async XLA Ops:
  7.2 3.9 %copy-start = (bf16[128,12]{0,1:T(8,128)(2,1)S(1)}, bf16[128,12]{0,1:T(8,128)(2,1)}, u32[]{:S(2)}) copy-start(bf16[128,12]{0,1:T(8,128)(2,1)} %param.16) | copy-start | bytes 9220
  7.2 23.1 %copy-start.3 = (bf16[1,128,768]{2,1,0:T(8,128)(2,1)S(1)}, bf16[1,128,768]{2,1,0:T(8,128)(2,1)}, u32[]{:S(2)}) copy-start(bf16[1,128,768]{2,1,0:T(8,128)(2,1)} %param.9) | copy-start | bytes 589828
  7.2 114.1 %all-gather.9.cloned.1.call-start = ((), (), s32[]{:S(2)}) async-start(), calls=%async_computation.4 | async-start | bytes 6340608 | tf_op jit(solution)/shard_map/all_gather | solution.py:187
  13.2 38.8 %all-to-all-start = ((bf16[64,32,128]{2,1,0:T(8,128)(2,1)}), bf16[64,32,128]{2,1,0:T(8,128)(2,1)S(1)}, u32[]{:S(2)}, u32[]{:S(2)}) async-start(bf16[64,32,128]{2,1,0:T(8,128)(2,1)} %pad_maximum_fusion), calls=%async_computation | async-start | bytes 1048576 | tf_op jit(solution)/shard_map/all_to_all | solution.py:205
  33.5 15.3 %collective-permute-start = (bf16[2,128,768]{2,1,0:T(8,128)(2,1)S(1)}, bf16[2,128,768]{2,1,0:T(8,128)(2,1)S(1)}, u32[]{:S(2)}, u32[]{:S(2)}) collective-permute-start(bf16[2,128,768]{2,1,0:T(8,128)(2,1)S(1)} %all_gather.46), channel_id=1, source_target_pairs={{0,2},{1,15},{2,4},{3,1},{4,6},{5,3},{6,8},{7,5},{8,10},{9,7},{10,... | collective-permute-start | bytes 1179656 | tf_op jit(solution)/shard_map/ppermute | solution.py:176
  48.8 9.2 %collective-permute-start.1 = (bf16[2,128,768]{2,1,0:T(8,128)(2,1)S(1)}, bf16[2,128,768]{2,1,0:T(8,128)(2,1)S(1)}, u32[]{:S(2)}, u32[]{:S(2)}) collective-permute-start(bf16[2,128,768]{2,1,0:T(8,128)(2,1)S(1)} %collective-permute-done.one_ref), channel_id=1, source_target_pairs={{0,2},{1,15},{2,4},{3,1},{4,6},{5,3},{6,8},{7,5},{8,10},{9,7},{10,... | collective-permute-start | bytes 1179656 | tf_op jit(solution)/shard_map/ppermute | solution.py:176
  58.0 11.4 %collective-permute-start.2 = (bf16[2,128,768]{2,1,0:T(8,128)(2,1)S(1)}, bf16[2,128,768]{2,1,0:T(8,128)(2,1)S(1)}, u32[]{:S(2)}, u32[]{:S(2)}) collective-permute-start(bf16[2,128,768]{2,1,0:T(8,128)(2,1)S(1)} %collective-permute-done.1.two_ref), channel_id=1, source_target_pairs={{0,2},{1,15},{2,4},{3,1},{4,6},{5,3},{6,8},{7,5},{8,10},{9,7},{10,... | collective-permute-start | bytes 1179656 | tf_op jit(solution)/shard_map/ppermute | solution.py:176
  62.7 16.8 %all-to-all-start.1 = ((bf16[8,48,384]{2,1,0:T(8,128)(2,1)}), bf16[8,48,384]{2,1,0:T(8,128)(2,1)S(1)}, u32[]{:S(2)}, u32[]{:S(2)}) async-start(bf16[8,48,384]{2,1,0:T(8,128)(2,1)} %broadcast_in_dim.35), calls=%async_computation.1 | async-start | bytes 589824 | tf_op jit(solution)/shard_map/all_to_all | solution.py:218
  69.4 15.6 %collective-permute-start.3 = (bf16[128,768]{1,0:T(8,128)(2,1)S(1)}, bf16[128,768]{1,0:T(8,128)(2,1)S(1)}, u32[]{:S(2)}, u32[]{:S(2)}) collective-permute-start(bf16[128,768]{1,0:T(8,128)(2,1)S(1)} %fusion.10), channel_id=1, source_target_pairs={{0,2},{1,15},{2,4},{3,1},{4,6},{5,3},{6,8},{7,5},{8,10},{9,7},{10,... | collective-permute-start | bytes 589832 | tf_op jit(solution)/shard_map/ppermute | solution.py:176
  90.4 18.9 %all-to-all-start.2 = ((bf16[8,128,128]{2,1,0:T(8,128)(2,1)}), bf16[8,128,128]{2,1,0:T(8,128)(2,1)S(1)}, u32[]{:S(2)}, u32[]{:S(2)}) async-start(bf16[8,128,128]{2,1,0:T(8,128)(2,1)} %broadcast_in_dim.36), calls=%async_computation.2 | async-start | bytes 524288 | tf_op jit(solution)/shard_map/all_to_all | solution.py:242
  113.2 23.5 %all-to-all-start.3 = ((bf16[64,16,128]{2,1,0:T(8,128)(2,1)}), bf16[64,16,128]{2,1,0:T(8,128)(2,1)S(1)}, u32[]{:S(2)}, u32[]{:S(2)}) async-start(bf16[64,16,128]{2,1,0:T(8,128)(2,1)} %bitcast.29), calls=%async_computation.3 | async-start | bytes 524288 | tf_op jit(solution)/shard_map/all_to_all | solution.py:259
  136.2 5.4 %copy-start.1 = (bf16[1,128,128]{2,1,0:T(8,128)(2,1)S(1)}, bf16[1,128,128]{2,1,0:T(8,128)(2,1)}, u32[]{:S(2)}) copy-start(bf16[1,128,128]{2,1,0:T(8,128)(2,1)} %param.11) | copy-start | bytes 98308
  136.2 5.4 %copy-start.2 = (bf16[12,128]{1,0:T(8,128)(2,1)S(1)}, bf16[12,128]{1,0:T(8,128)(2,1)}, u32[]{:S(2)}) copy-start(bf16[12,128]{1,0:T(8,128)(2,1)} %cw_ref.1) | copy-start | bytes 9220
Sparse Core Ops, SparseCore 0:
  11.7 99.0 all-gather.8

commit v9 on v8

--- a/solution.py
+++ b/solution.py
@@ -94,11 +94,35 @@
     out_ref[...] = held[...].astype(BF)
 
 
-def column_block(
-    c_ref, bl_ref, stack_ref, who_ref, far_ref, wvo_ref, pair_ref, cw_ref, out_ref, pair_out_ref, wv_ref, sem
-):
-    copy = pltpu.make_async_copy(far_ref, wv_ref, sem)
-    copy.start()
+def pack(far_ref, out_ref, held, packed, in_sems, out_sems):
+    copies = [
+        pltpu.make_async_copy(far_ref.at[pl.ds(16 * n, 16)], held.at[pl.ds(16 * n, 16)], in_sems.at[n])
+        for n in range(8)
+    ]
+    for copy in copies:
+        copy.start()
+    sent = []
+    for n in range(8):
+        copies[n].wait()
+        for d in range(16 * n, 16 * n + 16):
+            packed[18 * d : 18 * d + 18, :] = held[d, 0:18, :]
+            packed[3 * D + 6 * d : 3 * D + 6 * d + 6, :] = held[d, 18:24, :]
+            packed[4 * D + 6 * d : 4 * D + 6 * d + 6, :] = held[d, 24:30, :]
+        for m, (start, rows) in enumerate(((288 * n, 288), (3 * D + 96 * n, 96), (4 * D + 96 * n, 96))):
+            part = pl.ds(start, rows)
+            sent.append(pltpu.make_async_copy(packed.at[part], out_ref.at[part], out_sems.at[3 * n + m]))
+            sent[-1].start()
+    for copy in sent:
+        copy.wait()
+
+
+def column_block(c_ref, bl_ref, stack_ref, far_ref, pair_ref, cw_ref, out_ref, pair_out_ref, w_ref, sems):
+    order = (8, 9, 0, 1, 2, 3, 4, 5, 6, 7)
+    copies = []
+    for n, m in enumerate(order):
+        part = pl.ds(384 * m, 384)
+        copies.append(pltpu.make_async_copy(far_ref.at[part], w_ref.at[part], sems.at[n]))
+        copies[n].start()
     mine = c_ref[0]
     lane = lax.broadcasted_iota(jnp.int32, (L, L), 1)
     row = lax.broadcasted_iota(jnp.int32, (L, L), 0)
@@ -133,12 +157,15 @@
         parts.append(jnp.where(jnp.logical_and(low, early), re1, o1))
     blended = jnp.concatenate(parts, axis=1).astype(BF)
 
-    updated = (dot_nt(who_ref[...], blended) + stack_ref[...].astype(F32)).astype(BF).astype(F32)
+    for copy in copies[:2]:
+        copy.wait()
+    updated = (dot_nt(w_ref[4 * D :], blended) + stack_ref[...].astype(F32)).astype(BF).astype(F32)
     center = jnp.mean(updated, axis=0, keepdims=True)
     spread = jnp.mean(jnp.square(updated - center), axis=0, keepdims=True)
     normed = ((updated - center) * lax.rsqrt(spread + 1e-05)).astype(BF)
-    copy.wait()
-    packed = jnp.dot(wv_ref[...], normed, preferred_element_type=F32)
+    for copy in copies[2:8]:
+        copy.wait()
+    packed = jnp.dot(w_ref[: 3 * D], normed, preferred_element_type=F32)
 
     mixed = []
     for h in range(H):
@@ -151,7 +178,9 @@
         mixed.append(jnp.dot(v, probs, preferred_element_type=F32).astype(BF))
     mixed = jnp.concatenate(mixed, axis=0)
 
-    result = (updated + jnp.dot(wvo_ref[...], mixed, preferred_element_type=F32)).astype(BF)
+    for copy in copies[8:]:
+        copy.wait()
+    result = (updated + jnp.dot(w_ref[3 * D : 4 * D], mixed, preferred_element_type=F32)).astype(BF)
     place = (row // 8 % 2 * E + row // 16 * 8 + row % 8 == lane).astype(BF)
     out_ref[...] = dot_nt(place, result).astype(BF)
 
@@ -257,20 +286,30 @@
         compiler_params=params(),
     )(y1, heads, values)
     came = lax.all_to_all(message.reshape(64, 16, 128), CHIPS, 0, 0, tiled=True)
-    column_triple = gathered[:, :18].reshape(3 * D, D)
-    column_out = gathered[:, 18:24].reshape(D, D)
-    row_out = gathered[:, 24:30].reshape(D, D)
-    came, column_triple = lax.optimization_barrier((came, column_triple))
+    column_weights = pl.pallas_call(
+        pack,
+        out_shape=jax.ShapeDtypeStruct((5 * D, D), BF),
+        in_specs=[ANY],
+        out_specs=ANY,
+        scratch_shapes=[
+            pltpu.VMEM((128, 32, D), BF),
+            pltpu.VMEM((5 * D, D), BF),
+            pltpu.SemaphoreType.DMA((8,)),
+            pltpu.SemaphoreType.DMA((24,)),
+        ],
+        compiler_params=params(56),
+    )(gathered)
+    came, column_weights = lax.optimization_barrier((came, column_weights))
     blended = lax.all_gather(came, "c", axis=0, tiled=False)
 
     alignment, pair_out = pl.pallas_call(
         column_block,
         out_shape=(jax.ShapeDtypeStruct((R, D), BF), jax.ShapeDtypeStruct((L, 128), BF)),
-        in_specs=[SMEM] + [VMEM] * 3 + [ANY] + [VMEM] * 3,
+        in_specs=[SMEM, VMEM, VMEM, ANY, VMEM, VMEM],
         out_specs=(VMEM, VMEM),
-        scratch_shapes=[pltpu.VMEM((3 * D, D), BF), pltpu.SemaphoreType.DMA],
-        compiler_params=params(48),
-    )(c1, blended, stack_own.T, row_out, column_triple, column_out, pair_own, contact_w)
+        scratch_shapes=[pltpu.VMEM((5 * D, D), BF), pltpu.SemaphoreType.DMA((10,))],
+        compiler_params=params(52),
+    )(c1, blended, stack_own.T, column_weights, pair_own, contact_w)
     return alignment.reshape(R, 1, D), pair_out.reshape(1, L, 128)
 
 

time: 158 us -> 153 us (0.968)
  local copies, waits for them, and re-layouts: 23.4 us -> 5.83 us
  waiting for transfers between devices: 29.4 us -> 35.2 us
  Pallas kernels: 12.6 us -> 17.9 us
  blocking collectives: 19.5 us -> 21.6 us
    reshape x3 -> x0, local copies, waits for them, and re-layouts: 9.3 us -> none  [the longest x1 6.57 us: per_device(): column_triple = gathered[:, :18].reshape(3 * D, D)]
    slice x2 -> x0, local copies, waits for them, and re-layouts: 8.31 us -> none  [the longest x1 4.89 us: per_device(): column_triple = gathered[:, :18].reshape(3 * D, D)]
    all_to_all x1, waiting for transfers between devices: 0.01 us -> 5.77 us  [per_device(): came = lax.all_to_all(message.reshape(64, 16, 128), CHIPS, 0, 0, tiled=True)]
    pallas_call x0 -> x1, Pallas kernels: none -> 5.62 us  [per_device(): pl.pallas_call(pack, out_shape=jax.ShapeDtypeStruct((5 * D, D), BF), in_s...]
    all_gather x1, blocking collectives: 2.62 us -> 4.72 us  [per_device(): blended = lax.all_gather(came, 'c', axis=0, tiled=False)]
  transfers between devices with their start and end apart: 9 -> 9, of which waited for: 4 -> 5; matrix products, arithmetic and copies ran while one was open for 17% -> 7% of each run, Pallas kernels for 3% -> 6%
where the time goes in v9:
time: 153 us; the launch traced here: 152 us
  starting transfers between devices  49.6 us (32%)
  waiting for transfers between devices  35.2 us (23%)
  blocking collectives  21.6 us (14%)
  Pallas kernels  17.9 us (12%)
  between operations  15.2 us (10%)
  local copies, waits for them, and re-layouts  5.83 us (4%)
  other arithmetic  5.83 us (4%)
    all_to_all x1, starting transfers between devices, per_device(): came = lax.all_to_all(message, CHIPS, 0, 0, tiled=True)  17.1 us
    ppermute x4, starting transfers between devices, around(): return lax.ppermute(x, ('y', 'c'), pairs)  14.2 us
    ppermute x4, waiting for transfers between devices, around(): return lax.ppermute(x, ('y', 'c'), pairs)  11.8 us
    all_to_all x1, waiting for transfers between devices, per_device(): lax.all_to_all(jnp.broadcast_to(tied, (8, L, L)), 'z', 0, 0, tiled=True)  10.3 us
    pallas_call x1, Pallas kernels, per_device(): pl.pallas_call(column_block, out_shape=(jax.ShapeDtypeStruct((R, D), BF),...  8.13 us
    all_to_all x1, waiting for transfers between devices, per_device(): lax.all_to_all(jnp.broadcast_to(half, (8, 48, 384)), 'z', 0, 0, tiled=True)  7.35 us
    all_to_all x1, starting transfers between devices, per_device(): lax.all_to_all(jnp.broadcast_to(half, (8, 48, 384)), 'z', 0, 0, tiled=True)  6.55 us
    all_to_all x1, starting transfers between devices, per_device(): came = lax.all_to_all(message.reshape(64, 16, 128), CHIPS, 0, 0, tiled=True)  6.43 us
  transfers between devices with their start and end apart: 9, of which 5 were waited for; matrix products, arithmetic and copies ran while one was open for 7% of the time, Pallas kernels for 6%

profile of v9, /device:TPU:1, one launch (start us, length us, event | category | flops | bytes accessed | tf_op | source)
XLA Modules:
  0.0 152.5 jit_solution(14399020387143681334)
XLA Ops:
  7.2 0.0 copy-start
  7.2 0.0 copy-start.3
  7.2 0.0 all-gather.9.cloned.1.call-start
  7.2 0.1 pad.8.clone
  7.3 1.5 maximum_maximum_fusion
  8.8 0.0 all-gather.9.cloned.1.call-update
  8.8 0.9 reshape.85
  9.7 0.1 copy.35
  9.8 0.1 reshape.86
  10.0 1.1 reshape_reshape.3
  11.1 0.9 convolution_convert_fusion
  12.1 0.1 broadcast_in_dim.33
  12.2 1.0 pad_maximum_fusion
  13.2 17.1 %all-to-all-start = ((bf16[64,32,128]{2,1,0:T(8,128)(2,1)}), bf16[64,32,128]{2,1,0:T(8,128)(2,1)S(1)}, u32[]{:S(2)}, u32[]{:S(2)}) async-start(bf16[64,32,128]{2,1,0:T(8,128)(2,1)} %pad_maximum_fusion), calls=%async_computation | async-start | bytes 1048576 | tf_op jit(solution)/shard_map/all_to_all | solution.py:234
  30.3 0.0 copy-done.3
  30.3 0.1 convert_reduce_fusion
  30.5 0.2 fusion.8
  30.7 0.1 fusion.4
  30.8 2.7 %all_gather.46 = bf16[2,128,768]{2,1,0:T(8,128)(2,1)S(1)} all-gather(bf16[1,128,768]{2,1,0:T(8,128)(2,1)S(1)} %fusion.4), channel_id=1, replica_groups=mesh['a'=4,'z'=8,'y'=8,'c'=2] {'c'}, dimensions={0}, use_global_device_ids=true | all-gather | bytes 589824 | tf_op jit(solution)/shard_map/all_gather | solution.py:219
  33.5 4.4 %collective-permute-start = (bf16[2,128,768]{2,1,0:T(8,128)(2,1)S(1)}, bf16[2,128,768]{2,1,0:T(8,128)(2,1)S(1)}, u32[]{:S(2)}, u32[]{:S(2)}) collective-permute-start(bf16[2,128,768]{2,1,0:T(8,128)(2,1)S(1)} %all_gather.46), channel_id=1, source_target_pairs={{0,2},{1,15},{2,4},{3,1},{4,6},{5,3},{6,8},{7,5},{8,10},{9,7},{10,... | collective-permute-start | bytes 1179656 | tf_op jit(solution)/shard_map/ppermute | solution.py:205
  38.0 2.6 %fusion.2 = bf16[2048,384]{1,0:T(8,128)(2,1)S(1)} fusion(s32[384]{0:T(512)S(1)} %get-tuple-element.33, s32[384]{0:T(512)S(1)} %get-tuple-element.34, s32[]{:T(128)S(6)} %mul.41, s32[384]{0:T(512)S(1)} %get-tuple-element.32, s32[384]{0:T(512)S(1)} %get-tuple-element.35, s32[2048]{0:T(1024)S(1)} %get-tuple-element.27, s32[2048]{0:T(1024)S(1)} %get-tuple-element.28, ...), kind=kLoop, calls=%fused_computation.4 | loop fusion | flops 11796480 | bytes 1616648 | tf_op jit(solution)/shard_map/convert_element_type | solution.py:239
  40.6 8.2 %collective-permute-done.one_ref = bf16[2,128,768]{2,1,0:T(8,128)(2,1)S(1)} collective-permute-done((bf16[2,128,768]{2,1,0:T(8,128)(2,1)S(1)}, bf16[2,128,768]{2,1,0:T(8,128)(2,1)S(1)}, u32[]{:S(2)}, u32[]{:S(2)}) %collective-permute-start) | collective-permute-done | bytes 393248 | tf_op jit(solution)/shard_map/ppermute | solution.py:205
  48.8 3.2 %collective-permute-start.1 = (bf16[2,128,768]{2,1,0:T(8,128)(2,1)S(1)}, bf16[2,128,768]{2,1,0:T(8,128)(2,1)S(1)}, u32[]{:S(2)}, u32[]{:S(2)}) collective-permute-start(bf16[2,128,768]{2,1,0:T(8,128)(2,1)S(1)} %collective-permute-done.one_ref), channel_id=1, source_target_pairs={{0,2},{1,15},{2,4},{3,1},{4,6},{5,3},{6,8},{7,5},{8,10},{9,7},{10,... | collective-permute-start | bytes 1179656 | tf_op jit(solution)/shard_map/ppermute | solution.py:205
  52.0 0.0 all-to-all-done
  52.0 0.5 fusion.27
  52.5 1.9 %all-gather = bf16[192,384]{1,0:T(8,128)(2,1)S(1)} all-gather(bf16[96,384]{1,0:T(8,128)(2,1)S(1)} %slice.117), channel_id=2, replica_groups=mesh['a'=4,'z'=8,'y'=8,'c'=2] {'c'}, dimensions={0}, use_global_device_ids=true | all-gather | bytes 221184 | tf_op jit(solution)/shard_map/all_gather | solution.py:242
  54.4 0.0 copy-done.4
  54.5 3.5 %collective-permute-done.1.two_ref = bf16[2,128,768]{2,1,0:T(8,128)(2,1)S(1)} collective-permute-done((bf16[2,128,768]{2,1,0:T(8,128)(2,1)S(1)}, bf16[2,128,768]{2,1,0:T(8,128)(2,1)S(1)}, u32[]{:S(2)}, u32[]{:S(2)}) %collective-permute-start.1) | collective-permute-done | bytes 393248 | tf_op jit(solution)/shard_map/ppermute | solution.py:205
  58.0 4.0 %collective-permute-start.2 = (bf16[2,128,768]{2,1,0:T(8,128)(2,1)S(1)}, bf16[2,128,768]{2,1,0:T(8,128)(2,1)S(1)}, u32[]{:S(2)}, u32[]{:S(2)}) collective-permute-start(bf16[2,128,768]{2,1,0:T(8,128)(2,1)S(1)} %collective-permute-done.1.two_ref), channel_id=1, source_target_pairs={{0,2},{1,15},{2,4},{3,1},{4,6},{5,3},{6,8},{7,5},{8,10},{9,7},{10,... | collective-permute-start | bytes 1179656 | tf_op jit(solution)/shard_map/ppermute | solution.py:205
  62.0 0.8 broadcast_in_dim.35
  62.8 6.6 %all-to-all-start.1 = ((bf16[8,48,384]{2,1,0:T(8,128)(2,1)}), bf16[8,48,384]{2,1,0:T(8,128)(2,1)S(1)}, u32[]{:S(2)}, u32[]{:S(2)}) async-start(bf16[8,48,384]{2,1,0:T(8,128)(2,1)} %broadcast_in_dim.35), calls=%async_computation.1 | async-start | bytes 589824 | tf_op jit(solution)/shard_map/all_to_all | solution.py:247
  69.3 0.1 fusion.9.own_ref
  69.4 0.0 collective-permute-done.2.three_ref
  69.5 2.7 %collective-permute-start.3 = (bf16[128,768]{1,0:T(8,128)(2,1)S(1)}, bf16[128,768]{1,0:T(8,128)(2,1)S(1)}, u32[]{:S(2)}, u32[]{:S(2)}) collective-permute-start(bf16[128,768]{1,0:T(8,128)(2,1)S(1)} %fusion.10), channel_id=1, source_target_pairs={{0,2},{1,15},{2,4},{3,1},{4,6},{5,3},{6,8},{7,5},{8,10},{9,7},{10,... | collective-permute-start | bytes 589832 | tf_op jit(solution)/shard_map/ppermute | solution.py:205
  72.2 0.1 pad_add_fusion.at_ref
  72.3 7.3 %all-to-all-done.1 = bf16[8,48,384]{2,1,0:T(8,128)(2,1)S(1)} async-done(((bf16[8,48,384]{2,1,0:T(8,128)(2,1)}), bf16[8,48,384]{2,1,0:T(8,128)(2,1)S(1)}, u32[]{:S(2)}, u32[]{:S(2)}) %all-to-all-start.1) | async-done | bytes 294944 | tf_op jit(solution)/shard_map/all_to_all | solution.py:247
  79.6 5.4 %all-gather.1 = bf16[16,48,384]{2,1,0:T(8,128)(2,1)S(1)} all-gather(bf16[8,48,384]{2,1,0:T(8,128)(2,1)S(1)} %all-to-all-done.1), channel_id=3, replica_groups=mesh['a'=4,'z'=8,'y'=8,'c'=2] {'c'}, dimensions={0}, use_global_device_ids=true | all-gather | bytes 884736 | tf_op jit(solution)/shard_map/all_gather | solution.py:248
  85.0 0.0 collective-permute-done.3.four_ref
  85.0 2.7 %shard_map.104 = (f32[2,128,128]{2,1,0:T(8,128)S(1)}, bf16[8,128,128]{2,1,0:T(8,128)(2,1)S(1)}) custom-call(s32[2]{0:T(128)S(1)} %pad_add_fusion.at_ref, bf16[768,384]{1,0:T(8,128)(2,1)S(1)} %bitcast.91, bf16[128,768]{1,0:T(8,128)(2,1)S(1)} %fusion.9.own_ref, bf16[2,128,768]{2,1,0:T(8,128)(2,1)S(1)} %collective-permute-done.one_ref, ...), custom_call_target="tpu_custom_call" | custom-call | tf_op jit(solution)/shard_map/pallas_call | solution.py:257
  87.7 2.1 %all-gather.2 = f32[4,128,128]{2,1,0:T(8,128)S(1)} all-gather(f32[2,128,128]{2,1,0:T(8,128)S(1)} %get-tuple-element.18), channel_id=4, replica_groups=mesh['a'=4,'z'=8,'y'=8,'c'=2] {'c'}, dimensions={0}, use_global_device_ids=true | all-gather | bytes 393216 | tf_op jit(solution)/shard_map/all_gather | solution.py:268
  89.8 0.7 broadcast_in_dim.36
  90.5 5.2 %all-to-all-start.2 = ((bf16[8,128,128]{2,1,0:T(8,128)(2,1)}), bf16[8,128,128]{2,1,0:T(8,128)(2,1)S(1)}, u32[]{:S(2)}, u32[]{:S(2)}) async-start(bf16[8,128,128]{2,1,0:T(8,128)(2,1)} %broadcast_in_dim.36), calls=%async_computation.2 | async-start | bytes 524288 | tf_op jit(solution)/shard_map/all_to_all | solution.py:271
  96.4 0.1 slice.72
  96.5 0.1 copy.28
  96.5 2.4 %all-gather.3 = bf16[128,14,128]{2,0,1:T(8,128)(2,1)S(1)} all-gather(bf16[64,14,128]{2,0,1:T(8,128)(2,1)S(1)} %copy.28), channel_id=5, replica_groups=mesh['a'=4,'z'=8,'y'=8,'c'=2] {'c'}, dimensions={0}, use_global_device_ids=true | all-gather | bytes 688128 | tf_op jit(solution)/shard_map/all_gather | solution.py:250
  99.0 10.3 %all-to-all-done.2.part_ref = bf16[8,128,128]{2,1,0:T(8,128)(2,1)S(1)} async-done(((bf16[8,128,128]{2,1,0:T(8,128)(2,1)}), bf16[8,128,128]{2,1,0:T(8,128)(2,1)S(1)}, u32[]{:S(2)}, u32[]{:S(2)}) %all-to-all-start.2) | async-done | bytes 262176 | tf_op jit(solution)/shard_map/all_to_all | solution.py:271
  109.3 0.2 shard_map.105
  109.5 2.4 %all-gather.4 = bf16[4,128,128]{2,1,0:T(8,128)(2,1)S(1)} all-gather(bf16[2,128,128]{2,1,0:T(8,128)(2,1)S(1)} %shard_map.105), channel_id=6, replica_groups=mesh['a'=4,'z'=8,'y'=8,'c'=2] {'c'}, dimensions={0}, use_global_device_ids=true | all-gather | bytes 196608 | tf_op jit(solution)/shard_map/all_gather | solution.py:279
  111.9 1.2 shard_map.106
  113.2 6.4 %all-to-all-start.3 = ((bf16[64,16,128]{2,1,0:T(8,128)(2,1)}), bf16[64,16,128]{2,1,0:T(8,128)(2,1)S(1)}, u32[]{:S(2)}, u32[]{:S(2)}) async-start(bf16[64,16,128]{2,1,0:T(8,128)(2,1)} %bitcast.29), calls=%async_computation.3 | async-start | bytes 524288 | tf_op jit(solution)/shard_map/all_to_all | solution.py:288
  119.6 0.3 copy.30
  119.9 0.2 reshape.94
  120.1 0.4 constant_dynamic-slice_fusion
  120.6 0.3 copy.31
  120.9 0.1 copy.32
  121.0 0.1 reshape.96
  121.1 0.2 copy.33
  121.3 0.0 all-gather.9.cloned.1.call-done
  121.3 0.0 copy-start.1
  121.3 0.0 copy-start.2
  121.3 5.6 %shard_map.107.far_ref = bf16[3840,768]{1,0:T(8,128)(2,1)} custom-call(bf16[128,32,768]{2,1,0:T(8,128)(2,1)} %bitcast.97), custom_call_target="tpu_custom_call" | custom-call | tf_op jit(solution)/shard_map/pallas_call | solution.py:289
  127.0 5.8 %all-to-all-done.3 = bf16[64,16,128]{2,1,0:T(8,128)(2,1)S(1)} async-done(((bf16[64,16,128]{2,1,0:T(8,128)(2,1)}), bf16[64,16,128]{2,1,0:T(8,128)(2,1)S(1)}, u32[]{:S(2)}, u32[]{:S(2)}) %all-to-all-start.3) | async-done | bytes 262176 | tf_op jit(solution)/shard_map/all_to_all | solution.py:288
  132.7 4.7 %all-gather.6 = bf16[128,16,128]{2,1,0:T(8,128)(2,1)S(1)} all-gather(bf16[64,16,128]{2,1,0:T(8,128)(2,1)S(1)} %all-to-all-done.3), channel_id=8, replica_groups=mesh['a'=4,'z'=8,'y'=8,'c'=2] {'c'}, dimensions={0}, use_global_device_ids=true | all-gather | bytes 786432 | tf_op jit(solution)/shard_map/all_gather | solution.py:303
  137.5 8.1 %shard_map.108 = (bf16[128,768]{1,0:T(8,128)(2,1)}, bf16[128,128]{1,0:T(8,128)(2,1)}) custom-call(s32[1]{0:T(128)} %bitcast.c_ref, bf16[2,64,16,128]{3,2,1,0:T(8,128)(2,1)S(1)} %bitcast.92, bf16[768,128]{1,0:T(8,128)(2,1)S(1)} %bitcast.93, bf16[3840,768]{1,0:T(8,128)(2,1)} %shard_map.107.far_ref, bf16[128,128]{1,0:T(8,128)(2,1)S(1)} %bitcast.95, ...), custom_call_target="tpu_custom_call" | custom-call | tf_op jit(solution)/shard_map/pallas_call | solution.py:305
  (34 shorter events, 0.3 us)
Async XLA Ops:
  7.2 3.9 %copy-start = (bf16[128,12]{0,1:T(8,128)(2,1)S(1)}, bf16[128,12]{0,1:T(8,128)(2,1)}, u32[]{:S(2)}) copy-start(bf16[128,12]{0,1:T(8,128)(2,1)} %param.16) | copy-start | bytes 9220
  7.2 23.1 %copy-start.3 = (bf16[1,128,768]{2,1,0:T(8,128)(2,1)S(1)}, bf16[1,128,768]{2,1,0:T(8,128)(2,1)}, u32[]{:S(2)}) copy-start(bf16[1,128,768]{2,1,0:T(8,128)(2,1)} %param.9) | copy-start | bytes 589828
  7.2 114.1 %all-gather.9.cloned.1.call-start = ((), (), s32[]{:S(2)}) async-start(), calls=%async_computation.4 | async-start | bytes 6340608 | tf_op jit(solution)/shard_map/all_gather | solution.py:216
  13.2 38.8 %all-to-all-start = ((bf16[64,32,128]{2,1,0:T(8,128)(2,1)}), bf16[64,32,128]{2,1,0:T(8,128)(2,1)S(1)}, u32[]{:S(2)}, u32[]{:S(2)}) async-start(bf16[64,32,128]{2,1,0:T(8,128)(2,1)} %pad_maximum_fusion), calls=%async_computation | async-start | bytes 1048576 | tf_op jit(solution)/shard_map/all_to_all | solution.py:234
  33.5 15.3 %collective-permute-start = (bf16[2,128,768]{2,1,0:T(8,128)(2,1)S(1)}, bf16[2,128,768]{2,1,0:T(8,128)(2,1)S(1)}, u32[]{:S(2)}, u32[]{:S(2)}) collective-permute-start(bf16[2,128,768]{2,1,0:T(8,128)(2,1)S(1)} %all_gather.46), channel_id=1, source_target_pairs={{0,2},{1,15},{2,4},{3,1},{4,6},{5,3},{6,8},{7,5},{8,10},{9,7},{10,... | collective-permute-start | bytes 1179656 | tf_op jit(solution)/shard_map/ppermute | solution.py:205
  48.8 9.2 %collective-permute-start.1 = (bf16[2,128,768]{2,1,0:T(8,128)(2,1)S(1)}, bf16[2,128,768]{2,1,0:T(8,128)(2,1)S(1)}, u32[]{:S(2)}, u32[]{:S(2)}) collective-permute-start(bf16[2,128,768]{2,1,0:T(8,128)(2,1)S(1)} %collective-permute-done.one_ref), channel_id=1, source_target_pairs={{0,2},{1,15},{2,4},{3,1},{4,6},{5,3},{6,8},{7,5},{8,10},{9,7},{10,... | collective-permute-start | bytes 1179656 | tf_op jit(solution)/shard_map/ppermute | solution.py:205
  52.0 2.4 %copy-start.4 = (bf16[64,32,128]{2,1,0:T(8,128)(2,1)}, bf16[64,32,128]{2,1,0:T(8,128)(2,1)S(1)}, u32[]{:S(2)}) copy-start(bf16[64,32,128]{2,1,0:T(8,128)(2,1)S(1)} %all-to-all-done) | copy-start | bytes 1572868
  58.0 11.5 %collective-permute-start.2 = (bf16[2,128,768]{2,1,0:T(8,128)(2,1)S(1)}, bf16[2,128,768]{2,1,0:T(8,128)(2,1)S(1)}, u32[]{:S(2)}, u32[]{:S(2)}) collective-permute-start(bf16[2,128,768]{2,1,0:T(8,128)(2,1)S(1)} %collective-permute-done.1.two_ref), channel_id=1, source_target_pairs={{0,2},{1,15},{2,4},{3,1},{4,6},{5,3},{6,8},{7,5},{8,10},{9,7},{10,... | collective-permute-start | bytes 1179656 | tf_op jit(solution)/shard_map/ppermute | solution.py:205
  62.0 34.4 %copy-start.5 = (bf16[64,32,128]{2,1,0:T(8,128)(2,1)S(1)}, bf16[64,32,128]{2,1,0:T(8,128)(2,1)}, u32[]{:S(2)}) copy-start(bf16[64,32,128]{2,1,0:T(8,128)(2,1)} %copy-done.4) | copy-start | bytes 1572868
  62.8 16.9 %all-to-all-start.1 = ((bf16[8,48,384]{2,1,0:T(8,128)(2,1)}), bf16[8,48,384]{2,1,0:T(8,128)(2,1)S(1)}, u32[]{:S(2)}, u32[]{:S(2)}) async-start(bf16[8,48,384]{2,1,0:T(8,128)(2,1)} %broadcast_in_dim.35), calls=%async_computation.1 | async-start | bytes 589824 | tf_op jit(solution)/shard_map/all_to_all | solution.py:247
  69.5 15.6 %collective-permute-start.3 = (bf16[128,768]{1,0:T(8,128)(2,1)S(1)}, bf16[128,768]{1,0:T(8,128)(2,1)S(1)}, u32[]{:S(2)}, u32[]{:S(2)}) collective-permute-start(bf16[128,768]{1,0:T(8,128)(2,1)S(1)} %fusion.10), channel_id=1, source_target_pairs={{0,2},{1,15},{2,4},{3,1},{4,6},{5,3},{6,8},{7,5},{8,10},{9,7},{10,... | collective-permute-start | bytes 589832 | tf_op jit(solution)/shard_map/ppermute | solution.py:205
  90.5 18.8 %all-to-all-start.2 = ((bf16[8,128,128]{2,1,0:T(8,128)(2,1)}), bf16[8,128,128]{2,1,0:T(8,128)(2,1)S(1)}, u32[]{:S(2)}, u32[]{:S(2)}) async-start(bf16[8,128,128]{2,1,0:T(8,128)(2,1)} %broadcast_in_dim.36), calls=%async_computation.2 | async-start | bytes 524288 | tf_op jit(solution)/shard_map/all_to_all | solution.py:271
  113.2 19.6 %all-to-all-start.3 = ((bf16[64,16,128]{2,1,0:T(8,128)(2,1)}), bf16[64,16,128]{2,1,0:T(8,128)(2,1)S(1)}, u32[]{:S(2)}, u32[]{:S(2)}) async-start(bf16[64,16,128]{2,1,0:T(8,128)(2,1)} %bitcast.29), calls=%async_computation.3 | async-start | bytes 524288 | tf_op jit(solution)/shard_map/all_to_all | solution.py:288
  121.3 16.1 %copy-start.1 = (bf16[1,128,128]{2,1,0:T(8,128)(2,1)S(1)}, bf16[1,128,128]{2,1,0:T(8,128)(2,1)}, u32[]{:S(2)}) copy-start(bf16[1,128,128]{2,1,0:T(8,128)(2,1)} %param.11) | copy-start | bytes 98308
  121.3 16.1 %copy-start.2 = (bf16[12,128]{1,0:T(8,128)(2,1)S(1)}, bf16[12,128]{1,0:T(8,128)(2,1)}, u32[]{:S(2)}) copy-start(bf16[12,128]{1,0:T(8,128)(2,1)} %cw_ref.1) | copy-start | bytes 9220
Sparse Core Ops, SparseCore 0:
  11.7 98.8 all-gather.8

commit v10 on v9

--- a/solution.py
+++ b/solution.py
@@ -70,27 +70,31 @@
     out_ref[1] = scores.astype(BF)
 
 
-def blend(y_ref, probs_ref, v_ref, out_ref, held):
-    lane = lax.broadcasted_iota(jnp.int32, (L, 2 * E), 1)
+def blend(at_ref, probs_ref, v_ref, out_ref, held):
+    half = L // 2
+    lane = lax.broadcasted_iota(jnp.int32, (half, 2 * E), 1)
     low = lane < E
-    odd = lax.rem(y_ref[0], 2) == 1
-    plain = [probs_ref[h, 1].astype(F32) for h in range(2)]
+    odd = lax.rem(at_ref[0], 2) == 1
+    pick = (2 * lax.broadcasted_iota(jnp.int32, (half, L), 0) + at_ref[1] == lane).astype(BF)
+    probs = [jnp.dot(pick, probs_ref[h, 0], preferred_element_type=F32).astype(BF) for h in range(2)]
+    plain = [jnp.dot(pick, probs_ref[h, 1], preferred_element_type=F32) for h in range(2)]
     moved = [pltpu.roll(s, E, 1) for s in plain]
-    for n in range(8):
-        v = v_ref[n]
-        o = jnp.where(
-            low,
-            jnp.dot(probs_ref[0, 0], v, preferred_element_type=F32),
-            jnp.dot(probs_ref[1, 0], v, preferred_element_type=F32),
-        )
-        h, half = (n % 4) // 2, n % 2
-        if n < 4:
-            extra = moved[h] if half else plain[h]
-            o = jnp.where(jnp.logical_and(low, odd), extra, o)
-        else:
-            extra = plain[h] if half else moved[h]
-            o = jnp.where(jnp.logical_or(low, odd), o, extra)
-        held[:, n, :] = o
+    for core in range(2):
+        for n in range(8):
+            v = v_ref[core, n]
+            o = jnp.where(
+                low,
+                jnp.dot(probs[0], v, preferred_element_type=F32),
+                jnp.dot(probs[1], v, preferred_element_type=F32),
+            )
+            h, second = (n % 4) // 2, n % 2
+            if n < 4:
+                extra = moved[h] if second else plain[h]
+                o = jnp.where(jnp.logical_and(low, odd), extra, o)
+            else:
+                extra = plain[h] if second else moved[h]
+                o = jnp.where(jnp.logical_or(low, odd), o, extra)
+            held[:, 8 * core + n, :] = o
     out_ref[...] = held[...].astype(BF)
 
 
@@ -116,14 +120,13 @@
         copy.wait()
 
 
-def column_block(c_ref, bl_ref, stack_ref, far_ref, pair_ref, cw_ref, out_ref, pair_out_ref, w_ref, sems):
+def column_block(bl_ref, stack_ref, far_ref, pair_ref, cw_ref, out_ref, pair_out_ref, w_ref, sems):
     order = (8, 9, 0, 1, 2, 3, 4, 5, 6, 7)
     copies = []
     for n, m in enumerate(order):
         part = pl.ds(384 * m, 384)
         copies.append(pltpu.make_async_copy(far_ref.at[part], w_ref.at[part], sems.at[n]))
         copies[n].start()
-    mine = c_ref[0]
     lane = lax.broadcasted_iota(jnp.int32, (L, L), 1)
     row = lax.broadcasted_iota(jnp.int32, (L, L), 0)
     low = lane < E
@@ -132,8 +135,7 @@
     slot = lax.rem(lax.broadcasted_iota(jnp.int32, (E, L), 0), 8)
 
     def tile(c, z, y):
-        both = bl_ref[c, z * 8 + y].astype(F32)
-        return jnp.where(mine == 0, both[:8], both[8:])
+        return bl_ref[z * 8 + y].astype(F32)[8 * c : 8 * c + 8]
 
     def block(y):
         left, right = (jnp.concatenate([tile(c, z, y) for z in range(8)], axis=0) for c in range(2))
@@ -241,8 +243,8 @@
     picked = dot_tn(came.reshape(2048, 128), pick)[:96].astype(BF)
     picked = lax.all_gather(picked, "c", axis=0, tiled=False)
     half = lax.dynamic_slice_in_dim(picked, c * 48, 48, axis=1)
-    half, two = lax.optimization_barrier((half[0] + half[1], two))
-    three = around(two)
+    half = half[0] + half[1]
+    three = around(lax.optimization_barrier((half, two))[1])
     four = around(jnp.where(c == 0, three[1], three[0]))
     over_z = lax.all_to_all(jnp.broadcast_to(half, (8, 48, 384)), "z", 0, 0, tiled=True)
     w_heads = lax.all_gather(over_z, "c", axis=0, tiled=False).reshape(D, 384)
@@ -279,13 +281,13 @@
     heads = lax.all_gather(head, "c", axis=0, tiled=False)
     message = pl.pallas_call(
         blend,
-        out_shape=jax.ShapeDtypeStruct((L, 8, 2 * E), BF),
+        out_shape=jax.ShapeDtypeStruct((L // 2, 16, 2 * E), BF),
         in_specs=[SMEM, VMEM, VMEM],
         out_specs=VMEM,
-        scratch_shapes=[pltpu.VMEM((L, 8, 2 * E), F32)],
+        scratch_shapes=[pltpu.VMEM((L // 2, 16, 2 * E), F32)],
         compiler_params=params(),
-    )(y1, heads, values)
-    came = lax.all_to_all(message.reshape(64, 16, 128), CHIPS, 0, 0, tiled=True)
+    )(at, heads, lax.all_gather(values, "c", axis=0, tiled=False))
+    came = lax.all_to_all(message, CHIPS, 0, 0, tiled=True)
     column_weights = pl.pallas_call(
         pack,
         out_shape=jax.ShapeDtypeStruct((5 * D, D), BF),
@@ -299,17 +301,16 @@
         ],
         compiler_params=params(56),
     )(gathered)
-    came, column_weights = lax.optimization_barrier((came, column_weights))
-    blended = lax.all_gather(came, "c", axis=0, tiled=False)
+    blended, column_weights = lax.optimization_barrier((came, column_weights))
 
     alignment, pair_out = pl.pallas_call(
         column_block,
         out_shape=(jax.ShapeDtypeStruct((R, D), BF), jax.ShapeDtypeStruct((L, 128), BF)),
-        in_specs=[SMEM, VMEM, VMEM, ANY, VMEM, VMEM],
+        in_specs=[VMEM, VMEM, ANY, VMEM, VMEM],
         out_specs=(VMEM, VMEM),
         scratch_shapes=[pltpu.VMEM((5 * D, D), BF), pltpu.SemaphoreType.DMA((10,))],
         compiler_params=params(52),
-    )(c1, blended, stack_own.T, column_weights, pair_own, contact_w)
+    )(blended, stack_own.T, column_weights, pair_own, contact_w)
     return alignment.reshape(R, 1, D), pair_out.reshape(1, L, 128)
 
 

time: 153 us -> 150 us (0.980)
  waiting for transfers between devices: 35.2 us -> 32.5 us
  blocking collectives: 21.6 us -> 19.4 us
    all_to_all x1 -> x2, starting transfers between devices: 17.1 us -> 23.7 us  [per_device(): came = lax.all_to_all(message, CHIPS, 0, 0, tiled=True)]
    all_to_all x1 -> x0, starting transfers between devices: 6.43 us -> none  [per_device(): came = lax.all_to_all(message.reshape(64, 16, 128), CHIPS, 0, 0, tiled=True)]
    all_to_all x1 -> x0, waiting for transfers between devices: 5.77 us -> none  [per_device(): came = lax.all_to_all(message.reshape(64, 16, 128), CHIPS, 0, 0, tiled=True)]
    all_to_all x1 -> x2, waiting for transfers between devices: 0.01 us -> 5.57 us  [per_device(): came = lax.all_to_all(message, CHIPS, 0, 0, tiled=True)]
    all_to_all x1, waiting for transfers between devices: 10.3 us -> 7.86 us  [per_device(): lax.all_to_all(jnp.broadcast_to(tied, (8, L, L)), 'z', 0, 0, tiled=True)]
    all_gather x1, blocking collectives: 4.72 us -> 2.39 us  [per_device(): lax.all_gather(values, 'c', axis=0, tiled=False)]
  transfers between devices with their start and end apart: 9 -> 9, of which waited for: 5 -> 5; matrix products, arithmetic and copies ran while one was open for 7% -> 8% of each run, Pallas kernels for 6% -> 7%
where the time goes in v10:
time: 150 us; the launch traced here: 148 us
  starting transfers between devices  49.7 us (33%)
  waiting for transfers between devices  32.5 us (22%)
  blocking collectives  19.4 us (13%)
  Pallas kernels  18.5 us (12%)
  between operations  15.2 us (10%)
  local copies, waits for them, and re-layouts  5.83 us (4%)
  other arithmetic  5.83 us (4%)
    all_to_all x2, starting transfers between devices, per_device(): came = lax.all_to_all(message, CHIPS, 0, 0, tiled=True)  23.7 us
    ppermute x4, starting transfers between devices, around(): return lax.ppermute(x, ('y', 'c'), pairs)  14.3 us
    ppermute x4, waiting for transfers between devices, around(): return lax.ppermute(x, ('y', 'c'), pairs)  11.8 us
    pallas_call x1, Pallas kernels, per_device(): pl.pallas_call(column_block, out_shape=(jax.ShapeDtypeStruct((R, D), BF),...  8.12 us
    all_to_all x1, waiting for transfers between devices, per_device(): lax.all_to_all(jnp.broadcast_to(tied, (8, L, L)), 'z', 0, 0, tiled=True)  7.86 us
    all_to_all x1, waiting for transfers between devices, per_device(): lax.all_to_all(jnp.broadcast_to(half, (8, 48, 384)), 'z', 0, 0, tiled=True)  7.27 us
    all_to_all x1, starting transfers between devices, per_device(): lax.all_to_all(jnp.broadcast_to(half, (8, 48, 384)), 'z', 0, 0, tiled=True)  6.5 us
    pallas_call x1, Pallas kernels, per_device(): pl.pallas_call(pack, out_shape=jax.ShapeDtypeStruct((5 * D, D), BF), in_s...  5.62 us
  transfers between devices with their start and end apart: 9, of which 5 were waited for; matrix products, arithmetic and copies ran while one was open for 8% of the time, Pallas kernels for 7%

profile of v10, /device:TPU:1, one launch (start us, length us, event | category | flops | bytes accessed | tf_op | source)
XLA Modules:
  0.0 148.3 jit_solution(9905962147673256045)
XLA Ops:
  7.2 0.0 copy-start
  7.2 0.0 copy-start.3
  7.2 0.0 all-gather.9.cloned.1.call-start
  7.2 0.1 pad.8.clone
  7.3 1.5 %maximum_maximum_fusion = bf16[32,768]{1,0:T(8,128)(2,1)} fusion(bf16[6,768]{1,0:T(8,128)(2,1)} %bitcast.108, bf16[6,768]{1,0:T(8,128)(2,1)} %bitcast.109, bf16[18,768]{1,0:T(8,128)(2,1)} %bitcast.106, bf16[32]{0:T(256)(128)(2,1)S(1)} %pad.8.clone), kind=kLoop, calls=%fused_computation.23 | loop fusion | flops 196608 | bytes 95296 | tf_op jit(solution)/shard_map/concatenate | solution.py:217
  8.8 0.0 all-gather.9.cloned.1.call-update
  8.8 0.9 reshape.82
  9.7 0.1 copy.35
  9.8 0.1 reshape.83
  10.0 1.1 reshape_reshape.3
  11.1 0.0 copy-done
  11.1 0.9 convolution_convert_fusion
  12.1 0.1 broadcast_in_dim.33
  12.2 1.0 pad_maximum_fusion
  13.2 17.1 %all-to-all-start = ((bf16[64,32,128]{2,1,0:T(8,128)(2,1)}), bf16[64,32,128]{2,1,0:T(8,128)(2,1)S(1)}, u32[]{:S(2)}, u32[]{:S(2)}) async-start(bf16[64,32,128]{2,1,0:T(8,128)(2,1)} %pad_maximum_fusion), calls=%async_computation | async-start | bytes 1048576 | tf_op jit(solution)/shard_map/all_to_all | solution.py:236
  30.3 0.0 copy-done.3
  30.3 0.1 convert_reduce_fusion
  30.5 0.2 fusion.8
  30.7 0.1 fusion.4
  30.8 2.7 %all_gather.46 = bf16[2,128,768]{2,1,0:T(8,128)(2,1)S(1)} all-gather(bf16[1,128,768]{2,1,0:T(8,128)(2,1)S(1)} %fusion.4), channel_id=1, replica_groups=mesh['a'=4,'z'=8,'y'=8,'c'=2] {'c'}, dimensions={0}, use_global_device_ids=true | all-gather | bytes 589824 | tf_op jit(solution)/shard_map/all_gather | solution.py:221
  33.5 4.4 %collective-permute-start = (bf16[2,128,768]{2,1,0:T(8,128)(2,1)S(1)}, bf16[2,128,768]{2,1,0:T(8,128)(2,1)S(1)}, u32[]{:S(2)}, u32[]{:S(2)}) collective-permute-start(bf16[2,128,768]{2,1,0:T(8,128)(2,1)S(1)} %all_gather.46), channel_id=1, source_target_pairs={{0,2},{1,15},{2,4},{3,1},{4,6},{5,3},{6,8},{7,5},{8,10},{9,7},{10,... | collective-permute-start | bytes 1179656 | tf_op jit(solution)/shard_map/ppermute | solution.py:207
  38.0 2.6 %fusion.2 = bf16[2048,384]{1,0:T(8,128)(2,1)S(1)} fusion(s32[384]{0:T(512)S(1)} %get-tuple-element.31, s32[384]{0:T(512)S(1)} %get-tuple-element.32, s32[]{:T(128)S(6)} %mul.41, s32[384]{0:T(512)S(1)} %get-tuple-element.30, s32[384]{0:T(512)S(1)} %get-tuple-element.33, s32[2048]{0:T(1024)S(1)} %get-tuple-element.25, s32[2048]{0:T(1024)S(1)} %get-tuple-element.26, ...), kind=kLoop, calls=%fused_computation.4 | loop fusion | flops 11796480 | bytes 1616648 | tf_op jit(solution)/shard_map/convert_element_type | solution.py:241
  40.6 8.2 %collective-permute-done.one_ref = bf16[2,128,768]{2,1,0:T(8,128)(2,1)S(1)} collective-permute-done((bf16[2,128,768]{2,1,0:T(8,128)(2,1)S(1)}, bf16[2,128,768]{2,1,0:T(8,128)(2,1)S(1)}, u32[]{:S(2)}, u32[]{:S(2)}) %collective-permute-start) | collective-permute-done | bytes 393248 | tf_op jit(solution)/shard_map/ppermute | solution.py:207
  48.8 3.2 %collective-permute-start.1 = (bf16[2,128,768]{2,1,0:T(8,128)(2,1)S(1)}, bf16[2,128,768]{2,1,0:T(8,128)(2,1)S(1)}, u32[]{:S(2)}, u32[]{:S(2)}) collective-permute-start(bf16[2,128,768]{2,1,0:T(8,128)(2,1)S(1)} %collective-permute-done.one_ref), channel_id=1, source_target_pairs={{0,2},{1,15},{2,4},{3,1},{4,6},{5,3},{6,8},{7,5},{8,10},{9,7},{10,... | collective-permute-start | bytes 1179656 | tf_op jit(solution)/shard_map/ppermute | solution.py:207
  52.0 0.0 all-to-all-done
  52.0 0.5 fusion.27
  52.5 1.9 %all-gather = bf16[192,384]{1,0:T(8,128)(2,1)S(1)} all-gather(bf16[96,384]{1,0:T(8,128)(2,1)S(1)} %slice.117), channel_id=2, replica_groups=mesh['a'=4,'z'=8,'y'=8,'c'=2] {'c'}, dimensions={0}, use_global_device_ids=true | all-gather | bytes 221184 | tf_op jit(solution)/shard_map/all_gather | solution.py:244
  54.5 3.5 %collective-permute-done.1.two_ref = bf16[2,128,768]{2,1,0:T(8,128)(2,1)S(1)} collective-permute-done((bf16[2,128,768]{2,1,0:T(8,128)(2,1)S(1)}, bf16[2,128,768]{2,1,0:T(8,128)(2,1)S(1)}, u32[]{:S(2)}, u32[]{:S(2)}) %collective-permute-start.1) | collective-permute-done | bytes 393248 | tf_op jit(solution)/shard_map/ppermute | solution.py:207
  58.0 4.0 %collective-permute-start.2 = (bf16[2,128,768]{2,1,0:T(8,128)(2,1)S(1)}, bf16[2,128,768]{2,1,0:T(8,128)(2,1)S(1)}, u32[]{:S(2)}, u32[]{:S(2)}) collective-permute-start(bf16[2,128,768]{2,1,0:T(8,128)(2,1)S(1)} %collective-permute-done.1.two_ref), channel_id=1, source_target_pairs={{0,2},{1,15},{2,4},{3,1},{4,6},{5,3},{6,8},{7,5},{8,10},{9,7},{10,... | collective-permute-start | bytes 1179656 | tf_op jit(solution)/shard_map/ppermute | solution.py:207
  62.0 0.8 broadcast_in_dim.35
  62.8 6.5 %all-to-all-start.1 = ((bf16[8,48,384]{2,1,0:T(8,128)(2,1)}), bf16[8,48,384]{2,1,0:T(8,128)(2,1)S(1)}, u32[]{:S(2)}, u32[]{:S(2)}) async-start(bf16[8,48,384]{2,1,0:T(8,128)(2,1)} %broadcast_in_dim.35), calls=%async_computation.1 | async-start | bytes 589824 | tf_op jit(solution)/shard_map/all_to_all | solution.py:249
  69.3 0.1 fusion.9.own_ref
  69.4 0.0 collective-permute-done.2.three_ref
  69.4 2.8 %collective-permute-start.3 = (bf16[128,768]{1,0:T(8,128)(2,1)S(1)}, bf16[128,768]{1,0:T(8,128)(2,1)S(1)}, u32[]{:S(2)}, u32[]{:S(2)}) collective-permute-start(bf16[128,768]{1,0:T(8,128)(2,1)S(1)} %fusion.10), channel_id=1, source_target_pairs={{0,2},{1,15},{2,4},{3,1},{4,6},{5,3},{6,8},{7,5},{8,10},{9,7},{10,... | collective-permute-start | bytes 589832 | tf_op jit(solution)/shard_map/ppermute | solution.py:207
  72.2 0.1 pad_add_fusion.at_ref
  72.3 7.3 %all-to-all-done.1 = bf16[8,48,384]{2,1,0:T(8,128)(2,1)S(1)} async-done(((bf16[8,48,384]{2,1,0:T(8,128)(2,1)}), bf16[8,48,384]{2,1,0:T(8,128)(2,1)S(1)}, u32[]{:S(2)}, u32[]{:S(2)}) %all-to-all-start.1) | async-done | bytes 294944 | tf_op jit(solution)/shard_map/all_to_all | solution.py:249
  79.5 5.5 %all-gather.1 = bf16[16,48,384]{2,1,0:T(8,128)(2,1)S(1)} all-gather(bf16[8,48,384]{2,1,0:T(8,128)(2,1)S(1)} %all-to-all-done.1), channel_id=3, replica_groups=mesh['a'=4,'z'=8,'y'=8,'c'=2] {'c'}, dimensions={0}, use_global_device_ids=true | all-gather | bytes 884736 | tf_op jit(solution)/shard_map/all_gather | solution.py:250
  85.0 0.0 collective-permute-done.3.four_ref
  85.0 2.7 %shard_map.104 = (f32[2,128,128]{2,1,0:T(8,128)S(1)}, bf16[8,128,128]{2,1,0:T(8,128)(2,1)S(1)}) custom-call(s32[2]{0:T(128)S(1)} %pad_add_fusion.at_ref, bf16[768,384]{1,0:T(8,128)(2,1)S(1)} %bitcast.90, bf16[128,768]{1,0:T(8,128)(2,1)S(1)} %fusion.9.own_ref, bf16[2,128,768]{2,1,0:T(8,128)(2,1)S(1)} %collective-permute-done.one_ref, ...), custom_call_target="tpu_custom_call" | custom-call | tf_op jit(solution)/shard_map/pallas_call | solution.py:259
  87.7 2.0 %all-gather.2 = f32[4,128,128]{2,1,0:T(8,128)S(1)} all-gather(f32[2,128,128]{2,1,0:T(8,128)S(1)} %get-tuple-element.16), channel_id=4, replica_groups=mesh['a'=4,'z'=8,'y'=8,'c'=2] {'c'}, dimensions={0}, use_global_device_ids=true | all-gather | bytes 393216 | tf_op jit(solution)/shard_map/all_gather | solution.py:270
  89.8 0.7 broadcast_in_dim.36
  90.5 5.2 %all-to-all-start.2 = ((bf16[8,128,128]{2,1,0:T(8,128)(2,1)}), bf16[8,128,128]{2,1,0:T(8,128)(2,1)S(1)}, u32[]{:S(2)}, u32[]{:S(2)}) async-start(bf16[8,128,128]{2,1,0:T(8,128)(2,1)} %broadcast_in_dim.36), calls=%async_computation.2 | async-start | bytes 524288 | tf_op jit(solution)/shard_map/all_to_all | solution.py:273
  96.4 0.1 slice.72
  96.4 0.1 copy.28
  96.5 2.5 %all-gather.3 = bf16[128,14,128]{2,0,1:T(8,128)(2,1)S(1)} all-gather(bf16[64,14,128]{2,0,1:T(8,128)(2,1)S(1)} %copy.28), channel_id=5, replica_groups=mesh['a'=4,'z'=8,'y'=8,'c'=2] {'c'}, dimensions={0}, use_global_device_ids=true | all-gather | bytes 688128 | tf_op jit(solution)/shard_map/all_gather | solution.py:252
  99.1 2.4 %all-gather.5 = bf16[16,128,128]{2,1,0:T(8,128)(2,1)S(1)} all-gather(bf16[8,128,128]{2,1,0:T(8,128)(2,1)S(1)} %get-tuple-element.17), channel_id=7, replica_groups=mesh['a'=4,'z'=8,'y'=8,'c'=2] {'c'}, dimensions={0}, use_global_device_ids=true | all-gather | bytes 786432 | tf_op jit(solution)/shard_map/all_gather | solution.py:289
  101.5 7.9 %all-to-all-done.2.part_ref = bf16[8,128,128]{2,1,0:T(8,128)(2,1)S(1)} async-done(((bf16[8,128,128]{2,1,0:T(8,128)(2,1)}), bf16[8,128,128]{2,1,0:T(8,128)(2,1)S(1)}, u32[]{:S(2)}, u32[]{:S(2)}) %all-to-all-start.2) | async-done | bytes 262176 | tf_op jit(solution)/shard_map/all_to_all | solution.py:273
  109.3 0.2 shard_map.105
  109.5 2.4 %all-gather.4 = bf16[4,128,128]{2,1,0:T(8,128)(2,1)S(1)} all-gather(bf16[2,128,128]{2,1,0:T(8,128)(2,1)S(1)} %shard_map.105), channel_id=6, replica_groups=mesh['a'=4,'z'=8,'y'=8,'c'=2] {'c'}, dimensions={0}, use_global_device_ids=true | all-gather | bytes 196608 | tf_op jit(solution)/shard_map/all_gather | solution.py:281
  111.9 1.9 %shard_map.106 = bf16[64,16,128]{2,1,0:T(8,128)(2,1)} custom-call(s32[2]{0:T(128)S(1)} %pad_add_fusion.at_ref, bf16[2,2,128,128]{3,2,1,0:T(8,128)(2,1)S(1)} %bitcast.93, bf16[2,8,128,128]{3,2,1,0:T(8,128)(2,1)S(1)} %bitcast.91), custom_call_target="tpu_custom_call" | custom-call | tf_op jit(solution)/shard_map/pallas_call | solution.py:282
  113.8 6.6 %all-to-all-start.3 = ((bf16[64,16,128]{2,1,0:T(8,128)(2,1)}), bf16[64,16,128]{2,1,0:T(8,128)(2,1)S(1)}, u32[]{:S(2)}, u32[]{:S(2)}) async-start(bf16[64,16,128]{2,1,0:T(8,128)(2,1)} %shard_map.106), calls=%async_computation.3 | async-start | bytes 524288 | tf_op jit(solution)/shard_map/all_to_all | solution.py:290
  120.5 0.3 copy.30
  120.7 0.2 reshape.90
  121.0 0.4 constant_dynamic-slice_fusion
  121.4 0.3 copy.31
  121.7 0.1 copy.32
  121.8 0.1 reshape.92
  121.9 0.2 copy.33
  122.1 0.0 all-gather.9.cloned.1.call-done
  122.1 0.0 copy-start.1
  122.1 0.0 copy-start.2
  122.2 5.6 %shard_map.107.far_ref = bf16[3840,768]{1,0:T(8,128)(2,1)} custom-call(bf16[128,32,768]{2,1,0:T(8,128)(2,1)} %bitcast.96), custom_call_target="tpu_custom_call" | custom-call | tf_op jit(solution)/shard_map/pallas_call | solution.py:291
  127.8 5.6 %all-to-all-done.3.bl_ref = bf16[64,16,128]{2,1,0:T(8,128)(2,1)S(1)} async-done(((bf16[64,16,128]{2,1,0:T(8,128)(2,1)}), bf16[64,16,128]{2,1,0:T(8,128)(2,1)S(1)}, u32[]{:S(2)}, u32[]{:S(2)}) %all-to-all-start.3) | async-done | bytes 262176 | tf_op jit(solution)/shard_map/all_to_all | solution.py:290
  133.4 8.1 %shard_map.108 = (bf16[128,768]{1,0:T(8,128)(2,1)}, bf16[128,128]{1,0:T(8,128)(2,1)}) custom-call(bf16[64,16,128]{2,1,0:T(8,128)(2,1)S(1)} %all-to-all-done.3.bl_ref, bf16[768,128]{1,0:T(8,128)(2,1)S(1)} %bitcast.92, bf16[3840,768]{1,0:T(8,128)(2,1)} %shard_map.107.far_ref, bf16[128,128]{1,0:T(8,128)(2,1)S(1)} %bitcast.94, bf16[12,128]{1,0:T(8,128)(2,1)S(1)} %copy-done.2), custom_call_target="tpu_custom_call" | custom-call | tf_op jit(solution)/shard_map/pallas_call | solution.py:306
  (34 shorter events, 0.3 us)
Async XLA Ops:
  7.2 3.9 %copy-start = (bf16[128,12]{0,1:T(8,128)(2,1)S(1)}, bf16[128,12]{0,1:T(8,128)(2,1)}, u32[]{:S(2)}) copy-start(bf16[128,12]{0,1:T(8,128)(2,1)} %param.16) | copy-start | bytes 9220
  7.2 23.1 %copy-start.3 = (bf16[1,128,768]{2,1,0:T(8,128)(2,1)S(1)}, bf16[1,128,768]{2,1,0:T(8,128)(2,1)}, u32[]{:S(2)}) copy-start(bf16[1,128,768]{2,1,0:T(8,128)(2,1)} %param.9) | copy-start | bytes 589828
  7.2 114.9 %all-gather.9.cloned.1.call-start = ((), (), s32[]{:S(2)}) async-start(), calls=%async_computation.4 | async-start | bytes 6340608 | tf_op jit(solution)/shard_map/all_gather | solution.py:218
  13.2 38.8 %all-to-all-start = ((bf16[64,32,128]{2,1,0:T(8,128)(2,1)}), bf16[64,32,128]{2,1,0:T(8,128)(2,1)S(1)}, u32[]{:S(2)}, u32[]{:S(2)}) async-start(bf16[64,32,128]{2,1,0:T(8,128)(2,1)} %pad_maximum_fusion), calls=%async_computation | async-start | bytes 1048576 | tf_op jit(solution)/shard_map/all_to_all | solution.py:236
  33.5 15.3 %collective-permute-start = (bf16[2,128,768]{2,1,0:T(8,128)(2,1)S(1)}, bf16[2,128,768]{2,1,0:T(8,128)(2,1)S(1)}, u32[]{:S(2)}, u32[]{:S(2)}) collective-permute-start(bf16[2,128,768]{2,1,0:T(8,128)(2,1)S(1)} %all_gather.46), channel_id=1, source_target_pairs={{0,2},{1,15},{2,4},{3,1},{4,6},{5,3},{6,8},{7,5},{8,10},{9,7},{10,... | collective-permute-start | bytes 1179656 | tf_op jit(solution)/shard_map/ppermute | solution.py:207
  48.8 9.2 %collective-permute-start.1 = (bf16[2,128,768]{2,1,0:T(8,128)(2,1)S(1)}, bf16[2,128,768]{2,1,0:T(8,128)(2,1)S(1)}, u32[]{:S(2)}, u32[]{:S(2)}) collective-permute-start(bf16[2,128,768]{2,1,0:T(8,128)(2,1)S(1)} %collective-permute-done.one_ref), channel_id=1, source_target_pairs={{0,2},{1,15},{2,4},{3,1},{4,6},{5,3},{6,8},{7,5},{8,10},{9,7},{10,... | collective-permute-start | bytes 1179656 | tf_op jit(solution)/shard_map/ppermute | solution.py:207
  52.0 2.4 %copy-start.4 = (bf16[64,32,128]{2,1,0:T(8,128)(2,1)}, bf16[64,32,128]{2,1,0:T(8,128)(2,1)S(1)}, u32[]{:S(2)}) copy-start(bf16[64,32,128]{2,1,0:T(8,128)(2,1)S(1)} %all-to-all-done) | copy-start | bytes 1572868
  58.0 11.4 %collective-permute-start.2 = (bf16[2,128,768]{2,1,0:T(8,128)(2,1)S(1)}, bf16[2,128,768]{2,1,0:T(8,128)(2,1)S(1)}, u32[]{:S(2)}, u32[]{:S(2)}) collective-permute-start(bf16[2,128,768]{2,1,0:T(8,128)(2,1)S(1)} %collective-permute-done.1.two_ref), channel_id=1, source_target_pairs={{0,2},{1,15},{2,4},{3,1},{4,6},{5,3},{6,8},{7,5},{8,10},{9,7},{10,... | collective-permute-start | bytes 1179656 | tf_op jit(solution)/shard_map/ppermute | solution.py:207
  62.0 34.4 %copy-start.5 = (bf16[64,32,128]{2,1,0:T(8,128)(2,1)S(1)}, bf16[64,32,128]{2,1,0:T(8,128)(2,1)}, u32[]{:S(2)}) copy-start(bf16[64,32,128]{2,1,0:T(8,128)(2,1)} %copy-done.4) | copy-start | bytes 1572868
  62.8 16.8 %all-to-all-start.1 = ((bf16[8,48,384]{2,1,0:T(8,128)(2,1)}), bf16[8,48,384]{2,1,0:T(8,128)(2,1)S(1)}, u32[]{:S(2)}, u32[]{:S(2)}) async-start(bf16[8,48,384]{2,1,0:T(8,128)(2,1)} %broadcast_in_dim.35), calls=%async_computation.1 | async-start | bytes 589824 | tf_op jit(solution)/shard_map/all_to_all | solution.py:249
  69.4 15.6 %collective-permute-start.3 = (bf16[128,768]{1,0:T(8,128)(2,1)S(1)}, bf16[128,768]{1,0:T(8,128)(2,1)S(1)}, u32[]{:S(2)}, u32[]{:S(2)}) collective-permute-start(bf16[128,768]{1,0:T(8,128)(2,1)S(1)} %fusion.10), channel_id=1, source_target_pairs={{0,2},{1,15},{2,4},{3,1},{4,6},{5,3},{6,8},{7,5},{8,10},{9,7},{10,... | collective-permute-start | bytes 589832 | tf_op jit(solution)/shard_map/ppermute | solution.py:207
  90.5 18.8 %all-to-all-start.2 = ((bf16[8,128,128]{2,1,0:T(8,128)(2,1)}), bf16[8,128,128]{2,1,0:T(8,128)(2,1)S(1)}, u32[]{:S(2)}, u32[]{:S(2)}) async-start(bf16[8,128,128]{2,1,0:T(8,128)(2,1)} %broadcast_in_dim.36), calls=%async_computation.2 | async-start | bytes 524288 | tf_op jit(solution)/shard_map/all_to_all | solution.py:273
  113.8 19.5 %all-to-all-start.3 = ((bf16[64,16,128]{2,1,0:T(8,128)(2,1)}), bf16[64,16,128]{2,1,0:T(8,128)(2,1)S(1)}, u32[]{:S(2)}, u32[]{:S(2)}) async-start(bf16[64,16,128]{2,1,0:T(8,128)(2,1)} %shard_map.106), calls=%async_computation.3 | async-start | bytes 524288 | tf_op jit(solution)/shard_map/all_to_all | solution.py:290
  122.1 11.2 %copy-start.1 = (bf16[1,128,128]{2,1,0:T(8,128)(2,1)S(1)}, bf16[1,128,128]{2,1,0:T(8,128)(2,1)}, u32[]{:S(2)}) copy-start(bf16[1,128,128]{2,1,0:T(8,128)(2,1)} %param.11) | copy-start | bytes 98308
  122.1 11.2 %copy-start.2 = (bf16[12,128]{1,0:T(8,128)(2,1)S(1)}, bf16[12,128]{1,0:T(8,128)(2,1)}, u32[]{:S(2)}) copy-start(bf16[12,128]{1,0:T(8,128)(2,1)} %cw_ref.1) | copy-start | bytes 9220
Sparse Core Ops, SparseCore 0:
  11.7 99.0 all-gather.8

commit v11 on v10

--- a/solution.py
+++ b/solution.py
@@ -38,7 +38,7 @@
     return (x - center) * lax.rsqrt(spread + 1e-05)
 
 
-def project_and_tie(at_ref, w_ref, own_ref, one_ref, two_ref, three_ref, four_ref, tied_ref, v_ref):
+def project_and_tie(at_ref, w_ref, own_ref, one_ref, two_ref, three_ref, four_ref, tied_ref, v_ref, held):
     w = w_ref[...]
     lane = lax.broadcasted_iota(jnp.int32, (L, 2 * E), 1)
     y, c = at_ref[0], at_ref[1]
@@ -56,29 +56,25 @@
         tied[0] += dot_nt(jnp.where(lane < E, q, 0.0).astype(BF), k)
         tied[1] += dot_nt(jnp.where(lane < E, 0.0, q).astype(BF), k)
     for h in range(2):
-        tied_ref[h] = tied[h] * R**-0.5
-
-
-def attend(span_ref, part_ref, bias_ref, out_ref):
-    scores = bias_ref[...].astype(F32)
-    for n in range(8):
-        scores += part_ref[n].astype(F32)
-    j = lax.broadcasted_iota(jnp.int32, (L, L), 1)
-    masked = jnp.where(j < span_ref[0], scores, -1e30)
-    e = jnp.exp(masked - jnp.max(masked, axis=1, keepdims=True))
-    out_ref[0] = (e / jnp.sum(e, axis=1, keepdims=True)).astype(BF)
-    out_ref[1] = scores.astype(BF)
-
-
-def blend(at_ref, probs_ref, v_ref, out_ref, held):
-    half = L // 2
-    lane = lax.broadcasted_iota(jnp.int32, (half, 2 * E), 1)
+        held[...] = tied[h] * R**-0.5
+        for core in range(2):
+            tied_ref[core, h] = held[pl.ds(core, L // 2, stride=2), :]
+
+
+def attend(at_ref, span_ref, part_ref, bias_ref, v_ref, out_ref, held):
+    lane = lax.broadcasted_iota(jnp.int32, (L // 2, 2 * E), 1)
     low = lane < E
     odd = lax.rem(at_ref[0], 2) == 1
-    pick = (2 * lax.broadcasted_iota(jnp.int32, (half, L), 0) + at_ref[1] == lane).astype(BF)
-    probs = [jnp.dot(pick, probs_ref[h, 0], preferred_element_type=F32).astype(BF) for h in range(2)]
-    plain = [jnp.dot(pick, probs_ref[h, 1], preferred_element_type=F32) for h in range(2)]
-    moved = [pltpu.roll(s, E, 1) for s in plain]
+    probs, plain, moved = [], [], []
+    for h in range(2):
+        scores = bias_ref[h].astype(F32)
+        for n in range(8):
+            scores += part_ref[n, h].astype(F32)
+        masked = jnp.where(lane < span_ref[0], scores, -1e30)
+        e = jnp.exp(masked - jnp.max(masked, axis=1, keepdims=True))
+        probs.append((e / jnp.sum(e, axis=1, keepdims=True)).astype(BF))
+        plain.append(scores)
+        moved.append(pltpu.roll(scores, E, 1))
     for core in range(2):
         for n in range(8):
             v = v_ref[core, n]
@@ -249,19 +245,18 @@
     over_z = lax.all_to_all(jnp.broadcast_to(half, (8, 48, 384)), "z", 0, 0, tiled=True)
     w_heads = lax.all_gather(over_z, "c", axis=0, tiled=False).reshape(D, 384)
 
-    rest = lax.all_gather(came[:, 18:, :], "c", axis=0, tiled=False)
-    stack_own = rest[:, :, :12].reshape(2, 64, 2, D)
+    stack_own = lax.all_gather(came[:, 18:30], "c", axis=0, tiled=False).reshape(2, 64, 2, D)
     stack_own = lax.dynamic_index_in_dim(stack_own, c, 2, keepdims=False).reshape(2, 8, 2, 4, D)
     stack_own = stack_own.transpose(2, 1, 3, 0, 4).reshape(R, D)
-    bias_own = lax.dynamic_index_in_dim(rest[:, :, 12:], c, 2, keepdims=False)
-    bias_own = bias_own.transpose(1, 0, 2).reshape(L, L)
+    bias_own = came[:, 30:].transpose(1, 0, 2)
 
     tied, values = pl.pallas_call(
         project_and_tie,
         out_shape=(
-            jax.ShapeDtypeStruct((2, L, L), F32),
+            jax.ShapeDtypeStruct((2, 2, L // 2, L), F32),
             jax.ShapeDtypeStruct((8, L, 2 * E), BF),
         ),
+        scratch_shapes=[pltpu.VMEM((L, L), F32)],
         in_specs=[SMEM] + [VMEM] * 6,
         out_specs=(VMEM, VMEM),
         compiler_params=params(),
@@ -270,23 +265,15 @@
     tied = lax.all_gather(tied, "c", axis=0, tiled=False)
     tied = lax.dynamic_index_in_dim(tied, c, 1, keepdims=False)
     tied = (tied[0] + tied[1]).astype(BF)
-    parts = lax.all_to_all(jnp.broadcast_to(tied, (8, L, L)), "z", 0, 0, tiled=True)
-    head = pl.pallas_call(
+    parts = lax.all_to_all(jnp.broadcast_to(tied, (8, 2, L // 2, L)), "z", 0, 0, tiled=True)
+    message = pl.pallas_call(
         attend,
-        out_shape=jax.ShapeDtypeStruct((2, L, L), BF),
-        in_specs=[SMEM, VMEM, VMEM],
-        out_specs=VMEM,
-        compiler_params=params(),
-    )(spans, parts, bias_own)
-    heads = lax.all_gather(head, "c", axis=0, tiled=False)
-    message = pl.pallas_call(
-        blend,
         out_shape=jax.ShapeDtypeStruct((L // 2, 16, 2 * E), BF),
-        in_specs=[SMEM, VMEM, VMEM],
+        in_specs=[SMEM, SMEM, VMEM, VMEM, VMEM],
         out_specs=VMEM,
         scratch_shapes=[pltpu.VMEM((L // 2, 16, 2 * E), F32)],
         compiler_params=params(),
-    )(at, heads, lax.all_gather(values, "c", axis=0, tiled=False))
+    )(at, spans, parts, bias_own, lax.all_gather(values, "c", axis=0, tiled=False))
     came = lax.all_to_all(message, CHIPS, 0, 0, tiled=True)
     column_weights = pl.pallas_call(
         pack,

time: 150 us -> 148 us (0.987)
  blocking collectives: 19.4 us -> 17.5 us
    all_to_all x2, waiting for transfers between devices: 5.57 us -> 1.93 us  [per_device(): came = lax.all_to_all(message, CHIPS, 0, 0, tiled=True)]
    all_to_all x1, waiting for transfers between devices: 7.86 us -> 10.4 us  [per_device(): lax.all_to_all(jnp.broadcast_to(tied, (8, 2, L // 2, L)), 'z', 0, 0, tile...]
    all_gather x2 -> x1, blocking collectives: 4.87 us -> 3.11 us  [per_device(): lax.all_gather(came[:, 18:30], 'c', axis=0, tiled=False)]
    pallas_call x3 -> x2, Pallas kernels: 4.78 us -> 4.63 us  [the longest x1 2.7 us: per_device(): pl.pallas_call(project_and_tie, out_shape=(jax.ShapeDtypeStruct((2, 2, L...]
where the time goes in v11:
time: 148 us; the launch traced here: 145 us
  starting transfers between devices  49.4 us (33%)
  waiting for transfers between devices  31.5 us (21%)
  Pallas kernels  18.4 us (12%)
  blocking collectives  17.5 us (12%)
  between operations  15.1 us (10%)
  local copies, waits for them, and re-layouts  5.95 us (4%)
  other arithmetic  5.83 us (4%)
    all_to_all x2, starting transfers between devices, per_device(): came = lax.all_to_all(message, CHIPS, 0, 0, tiled=True)  23.3 us
    ppermute x4, starting transfers between devices, around(): return lax.ppermute(x, ('y', 'c'), pairs)  14.2 us
    ppermute x4, waiting for transfers between devices, around(): return lax.ppermute(x, ('y', 'c'), pairs)  11.8 us
    all_to_all x1, waiting for transfers between devices, per_device(): lax.all_to_all(jnp.broadcast_to(tied, (8, 2, L // 2, L)), 'z', 0, 0, tile...  10.4 us
    pallas_call x1, Pallas kernels, per_device(): pl.pallas_call(column_block, out_shape=(jax.ShapeDtypeStruct((R, D), BF),...  8.12 us
    all_to_all x1, waiting for transfers between devices, per_device(): lax.all_to_all(jnp.broadcast_to(half, (8, 48, 384)), 'z', 0, 0, tiled=True)  7.42 us
    all_to_all x1, starting transfers between devices, per_device(): lax.all_to_all(jnp.broadcast_to(half, (8, 48, 384)), 'z', 0, 0, tiled=True)  6.57 us
    pallas_call x1, Pallas kernels, per_device(): pl.pallas_call(pack, out_shape=jax.ShapeDtypeStruct((5 * D, D), BF), in_s...  5.63 us
  transfers between devices with their start and end apart: 9, of which 5 were waited for; matrix products, arithmetic and copies ran while one was open for 8% of the time, Pallas kernels for 7%

profile of v11, /device:TPU:1, one launch (start us, length us, event | category | flops | bytes accessed | tf_op | source)
XLA Modules:
  0.0 145.1 jit_solution(6933774103533209078)
XLA Ops:
  7.2 0.0 copy-start
  7.2 0.0 copy-start.3
  7.2 0.0 all-gather.8.cloned.1.call-start
  7.2 0.1 pad.8.clone
  7.3 1.5 %maximum_maximum_fusion = bf16[32,768]{1,0:T(8,128)(2,1)} fusion(bf16[6,768]{1,0:T(8,128)(2,1)} %bitcast.99, bf16[6,768]{1,0:T(8,128)(2,1)} %bitcast.100, bf16[18,768]{1,0:T(8,128)(2,1)} %bitcast.97, bf16[32]{0:T(256)(128)(2,1)S(1)} %pad.8.clone), kind=kLoop, calls=%fused_computation.23 | loop fusion | flops 196608 | bytes 95296 | tf_op jit(solution)/shard_map/concatenate | solution.py:213
  8.8 0.0 all-gather.8.cloned.1.call-update
  8.8 0.9 reshape.79
  9.7 0.1 copy.35
  9.8 0.1 reshape.80
  10.0 1.1 reshape_reshape.3
  11.1 0.0 copy-done
  11.1 0.9 convolution_convert_fusion
  12.1 0.1 broadcast_in_dim.33
  12.2 1.0 pad_maximum_fusion
  13.2 17.1 %all-to-all-start = ((bf16[64,32,128]{2,1,0:T(8,128)(2,1)}), bf16[64,32,128]{2,1,0:T(8,128)(2,1)S(1)}, u32[]{:S(2)}, u32[]{:S(2)}) async-start(bf16[64,32,128]{2,1,0:T(8,128)(2,1)} %pad_maximum_fusion), calls=%async_computation | async-start | bytes 1048576 | tf_op jit(solution)/shard_map/all_to_all | solution.py:232
  30.3 0.0 copy-done.3
  30.3 0.1 convert_reduce_fusion
  30.5 0.2 fusion.8
  30.7 0.1 fusion.4
  30.8 2.7 %all_gather.40 = bf16[2,128,768]{2,1,0:T(8,128)(2,1)S(1)} all-gather(bf16[1,128,768]{2,1,0:T(8,128)(2,1)S(1)} %fusion.4), channel_id=1, replica_groups=mesh['a'=4,'z'=8,'y'=8,'c'=2] {'c'}, dimensions={0}, use_global_device_ids=true | all-gather | bytes 589824 | tf_op jit(solution)/shard_map/all_gather | solution.py:217
  33.5 4.4 %collective-permute-start = (bf16[2,128,768]{2,1,0:T(8,128)(2,1)S(1)}, bf16[2,128,768]{2,1,0:T(8,128)(2,1)S(1)}, u32[]{:S(2)}, u32[]{:S(2)}) collective-permute-start(bf16[2,128,768]{2,1,0:T(8,128)(2,1)S(1)} %all_gather.40), channel_id=1, source_target_pairs={{0,2},{1,15},{2,4},{3,1},{4,6},{5,3},{6,8},{7,5},{8,10},{9,7},{10,... | collective-permute-start | bytes 1179656 | tf_op jit(solution)/shard_map/ppermute | solution.py:203
  38.0 2.6 %fusion.2 = bf16[2048,384]{1,0:T(8,128)(2,1)S(1)} fusion(s32[384]{0:T(512)S(1)} %get-tuple-element.31, s32[384]{0:T(512)S(1)} %get-tuple-element.32, s32[]{:T(128)S(6)} %mul.41, s32[384]{0:T(512)S(1)} %get-tuple-element.30, s32[384]{0:T(512)S(1)} %get-tuple-element.33, s32[2048]{0:T(1024)S(1)} %get-tuple-element.25, s32[2048]{0:T(1024)S(1)} %get-tuple-element.26, ...), kind=kLoop, calls=%fused_computation.4 | loop fusion | flops 11796480 | bytes 1616648 | tf_op jit(solution)/shard_map/convert_element_type | solution.py:237
  40.6 8.2 %collective-permute-done.one_ref = bf16[2,128,768]{2,1,0:T(8,128)(2,1)S(1)} collective-permute-done((bf16[2,128,768]{2,1,0:T(8,128)(2,1)S(1)}, bf16[2,128,768]{2,1,0:T(8,128)(2,1)S(1)}, u32[]{:S(2)}, u32[]{:S(2)}) %collective-permute-start) | collective-permute-done | bytes 393248 | tf_op jit(solution)/shard_map/ppermute | solution.py:203
  48.8 3.2 %collective-permute-start.1 = (bf16[2,128,768]{2,1,0:T(8,128)(2,1)S(1)}, bf16[2,128,768]{2,1,0:T(8,128)(2,1)S(1)}, u32[]{:S(2)}, u32[]{:S(2)}) collective-permute-start(bf16[2,128,768]{2,1,0:T(8,128)(2,1)S(1)} %collective-permute-done.one_ref), channel_id=1, source_target_pairs={{0,2},{1,15},{2,4},{3,1},{4,6},{5,3},{6,8},{7,5},{8,10},{9,7},{10,... | collective-permute-start | bytes 1179656 | tf_op jit(solution)/shard_map/ppermute | solution.py:203
  52.0 0.0 all-to-all-done
  52.0 0.5 fusion.27
  52.5 1.9 %all-gather = bf16[192,384]{1,0:T(8,128)(2,1)S(1)} all-gather(bf16[96,384]{1,0:T(8,128)(2,1)S(1)} %slice.113), channel_id=2, replica_groups=mesh['a'=4,'z'=8,'y'=8,'c'=2] {'c'}, dimensions={0}, use_global_device_ids=true | all-gather | bytes 221184 | tf_op jit(solution)/shard_map/all_gather | solution.py:240
  54.4 3.6 %collective-permute-done.1.two_ref = bf16[2,128,768]{2,1,0:T(8,128)(2,1)S(1)} collective-permute-done((bf16[2,128,768]{2,1,0:T(8,128)(2,1)S(1)}, bf16[2,128,768]{2,1,0:T(8,128)(2,1)S(1)}, u32[]{:S(2)}, u32[]{:S(2)}) %collective-permute-start.1) | collective-permute-done | bytes 393248 | tf_op jit(solution)/shard_map/ppermute | solution.py:203
  58.0 4.0 %collective-permute-start.2 = (bf16[2,128,768]{2,1,0:T(8,128)(2,1)S(1)}, bf16[2,128,768]{2,1,0:T(8,128)(2,1)S(1)}, u32[]{:S(2)}, u32[]{:S(2)}) collective-permute-start(bf16[2,128,768]{2,1,0:T(8,128)(2,1)S(1)} %collective-permute-done.1.two_ref), channel_id=1, source_target_pairs={{0,2},{1,15},{2,4},{3,1},{4,6},{5,3},{6,8},{7,5},{8,10},{9,7},{10,... | collective-permute-start | bytes 1179656 | tf_op jit(solution)/shard_map/ppermute | solution.py:203
  62.0 0.8 broadcast_in_dim.35
  62.7 6.6 %all-to-all-start.1 = ((bf16[8,48,384]{2,1,0:T(8,128)(2,1)}), bf16[8,48,384]{2,1,0:T(8,128)(2,1)S(1)}, u32[]{:S(2)}, u32[]{:S(2)}) async-start(bf16[8,48,384]{2,1,0:T(8,128)(2,1)} %broadcast_in_dim.35), calls=%async_computation.1 | async-start | bytes 589824 | tf_op jit(solution)/shard_map/all_to_all | solution.py:245
  69.3 0.1 fusion.9.own_ref
  69.4 0.0 collective-permute-done.2.three_ref
  69.5 2.7 %collective-permute-start.3 = (bf16[128,768]{1,0:T(8,128)(2,1)S(1)}, bf16[128,768]{1,0:T(8,128)(2,1)S(1)}, u32[]{:S(2)}, u32[]{:S(2)}) collective-permute-start(bf16[128,768]{1,0:T(8,128)(2,1)S(1)} %fusion.10), channel_id=1, source_target_pairs={{0,2},{1,15},{2,4},{3,1},{4,6},{5,3},{6,8},{7,5},{8,10},{9,7},{10,... | collective-permute-start | bytes 589832 | tf_op jit(solution)/shard_map/ppermute | solution.py:203
  72.2 0.1 pad_add_fusion.at_ref
  72.3 7.4 %all-to-all-done.1 = bf16[8,48,384]{2,1,0:T(8,128)(2,1)S(1)} async-done(((bf16[8,48,384]{2,1,0:T(8,128)(2,1)}), bf16[8,48,384]{2,1,0:T(8,128)(2,1)S(1)}, u32[]{:S(2)}, u32[]{:S(2)}) %all-to-all-start.1) | async-done | bytes 294944 | tf_op jit(solution)/shard_map/all_to_all | solution.py:245
  79.7 5.3 %all-gather.1 = bf16[16,48,384]{2,1,0:T(8,128)(2,1)S(1)} all-gather(bf16[8,48,384]{2,1,0:T(8,128)(2,1)S(1)} %all-to-all-done.1), channel_id=3, replica_groups=mesh['a'=4,'z'=8,'y'=8,'c'=2] {'c'}, dimensions={0}, use_global_device_ids=true | all-gather | bytes 884736 | tf_op jit(solution)/shard_map/all_gather | solution.py:246
  85.0 0.0 collective-permute-done.3.four_ref
  85.0 2.7 %shard_map.104 = (f32[2,2,64,128]{3,2,1,0:T(8,128)S(1)}, bf16[8,128,128]{2,1,0:T(8,128)(2,1)S(1)}) custom-call(s32[2]{0:T(128)S(1)} %pad_add_fusion.at_ref, bf16[768,384]{1,0:T(8,128)(2,1)S(1)} %bitcast.85, bf16[128,768]{1,0:T(8,128)(2,1)S(1)} %fusion.9.own_ref, bf16[2,128,768]{2,1,0:T(8,128)(2,1)S(1)} %collective-permute-done.one_ref, ...), custom_call_target="tpu_custom_call" | custom-call | tf_op jit(solution)/shard_map/pallas_call | solution.py:253
  87.7 2.0 %all-gather.2 = f32[4,2,64,128]{3,2,1,0:T(8,128)S(1)} all-gather(f32[2,2,64,128]{3,2,1,0:T(8,128)S(1)} %get-tuple-element.16), channel_id=4, replica_groups=mesh['a'=4,'z'=8,'y'=8,'c'=2] {'c'}, dimensions={0}, use_global_device_ids=true | all-gather | bytes 393216 | tf_op jit(solution)/shard_map/all_gather | solution.py:265
  89.7 0.8 broadcast_in_dim.36
  90.5 5.2 %all-to-all-start.2 = ((bf16[8,2,64,128]{3,2,1,0:T(8,128)(2,1)}), bf16[8,2,64,128]{3,2,1,0:T(8,128)(2,1)S(1)}, u32[]{:S(2)}, u32[]{:S(2)}) async-start(bf16[8,2,64,128]{3,2,1,0:T(8,128)(2,1)} %broadcast_in_dim.36), calls=%async_computation.2 | async-start | bytes 524288 | tf_op jit(solution)/shard_map/all_to_all | solution.py:268
  96.4 0.2 copy.28
  96.6 2.5 %all-gather.3 = bf16[16,128,128]{2,1,0:T(8,128)(2,1)S(1)} all-gather(bf16[8,128,128]{2,1,0:T(8,128)(2,1)S(1)} %get-tuple-element.17), channel_id=5, replica_groups=mesh['a'=4,'z'=8,'y'=8,'c'=2] {'c'}, dimensions={0}, use_global_device_ids=true | all-gather | bytes 786432 | tf_op jit(solution)/shard_map/all_gather | solution.py:276
  99.1 10.4 %all-to-all-done.2.part_ref = bf16[8,2,64,128]{3,2,1,0:T(8,128)(2,1)S(1)} async-done(((bf16[8,2,64,128]{3,2,1,0:T(8,128)(2,1)}), bf16[8,2,64,128]{3,2,1,0:T(8,128)(2,1)S(1)}, u32[]{:S(2)}, u32[]{:S(2)}) %all-to-all-start.2) | async-done | bytes 262176 | tf_op jit(solution)/shard_map/all_to_all | solution.py:268
  109.5 1.9 %shard_map.105 = bf16[64,16,128]{2,1,0:T(8,128)(2,1)} custom-call(s32[2]{0:T(128)S(1)} %pad_add_fusion.at_ref, s32[1]{0:T(128)S(6)} %copy.43.span_ref, bf16[8,2,64,128]{3,2,1,0:T(8,128)(2,1)S(1)} %all-to-all-done.2.part_ref, bf16[2,64,128]{2,1,0:T(8,128)(2,1)S(1)} %slice_bitcast_fusion.bias_ref, bf16[2,8,128,128]{3,2,1,0:T(8,128)(2,1)S(1)} %bitcast.86), custom_call_target="tpu_custom_call" | custom-call | tf_op jit(solution)/shard_map/pallas_call | solution.py:269
  111.4 6.1 %all-to-all-start.3 = ((bf16[64,16,128]{2,1,0:T(8,128)(2,1)}), bf16[64,16,128]{2,1,0:T(8,128)(2,1)S(1)}, u32[]{:S(2)}, u32[]{:S(2)}) async-start(bf16[64,16,128]{2,1,0:T(8,128)(2,1)} %shard_map.105), calls=%async_computation.3 | async-start | bytes 524288 | tf_op jit(solution)/shard_map/all_to_all | solution.py:277
  117.6 0.1 slice.70
  117.7 0.1 copy.29
  117.7 3.1 %all-gather.5 = bf16[128,12,128]{2,0,1:T(8,128)(2,1)S(1)} all-gather(bf16[64,12,128]{2,0,1:T(8,128)(2,1)S(1)} %copy.29), channel_id=7, replica_groups=mesh['a'=4,'z'=8,'y'=8,'c'=2] {'c'}, dimensions={0}, use_global_device_ids=true | all-gather | bytes 589824 | tf_op jit(solution)/shard_map/all_gather | solution.py:248
  120.8 0.3 copy.30
  121.1 0.2 reshape.86
  121.3 0.4 constant_dynamic-slice_fusion
  121.8 0.3 copy.31
  122.1 0.1 copy.32
  122.2 0.1 reshape.88
  122.3 0.2 copy.33
  122.5 0.0 all-gather.8.cloned.1.call-done
  122.5 0.0 copy-start.1
  122.5 0.0 copy-start.2
  122.5 5.6 %shard_map.106.far_ref = bf16[3840,768]{1,0:T(8,128)(2,1)} custom-call(bf16[128,32,768]{2,1,0:T(8,128)(2,1)} %bitcast.90), custom_call_target="tpu_custom_call" | custom-call | tf_op jit(solution)/shard_map/pallas_call | solution.py:278
  128.2 1.9 %all-to-all-done.3.bl_ref = bf16[64,16,128]{2,1,0:T(8,128)(2,1)S(1)} async-done(((bf16[64,16,128]{2,1,0:T(8,128)(2,1)}), bf16[64,16,128]{2,1,0:T(8,128)(2,1)S(1)}, u32[]{:S(2)}, u32[]{:S(2)}) %all-to-all-start.3) | async-done | bytes 262176 | tf_op jit(solution)/shard_map/all_to_all | solution.py:277
  130.1 0.0 copy-done.1
  130.1 8.1 %shard_map.107 = (bf16[128,768]{1,0:T(8,128)(2,1)}, bf16[128,128]{1,0:T(8,128)(2,1)}) custom-call(bf16[64,16,128]{2,1,0:T(8,128)(2,1)S(1)} %all-to-all-done.3.bl_ref, bf16[768,128]{1,0:T(8,128)(2,1)S(1)} %bitcast.87, bf16[3840,768]{1,0:T(8,128)(2,1)} %shard_map.106.far_ref, bf16[128,128]{1,0:T(8,128)(2,1)S(1)} %bitcast.88, bf16[12,128]{1,0:T(8,128)(2,1)S(1)} %copy-done.2), custom_call_target="tpu_custom_call" | custom-call | tf_op jit(solution)/shard_map/pallas_call | solution.py:293
  (26 shorter events, 0.3 us)
Async XLA Ops:
  7.2 3.9 %copy-start = (bf16[128,12]{0,1:T(8,128)(2,1)S(1)}, bf16[128,12]{0,1:T(8,128)(2,1)}, u32[]{:S(2)}) copy-start(bf16[128,12]{0,1:T(8,128)(2,1)} %param.16) | copy-start | bytes 9220
  7.2 23.1 %copy-start.3 = (bf16[1,128,768]{2,1,0:T(8,128)(2,1)S(1)}, bf16[1,128,768]{2,1,0:T(8,128)(2,1)}, u32[]{:S(2)}) copy-start(bf16[1,128,768]{2,1,0:T(8,128)(2,1)} %param.9) | copy-start | bytes 589828
  7.2 115.3 %all-gather.8.cloned.1.call-start = ((), (), s32[]{:S(2)}) async-start(), calls=%async_computation.4 | async-start | bytes 6340608 | tf_op jit(solution)/shard_map/all_gather | solution.py:214
  13.2 38.8 %all-to-all-start = ((bf16[64,32,128]{2,1,0:T(8,128)(2,1)}), bf16[64,32,128]{2,1,0:T(8,128)(2,1)S(1)}, u32[]{:S(2)}, u32[]{:S(2)}) async-start(bf16[64,32,128]{2,1,0:T(8,128)(2,1)} %pad_maximum_fusion), calls=%async_computation | async-start | bytes 1048576 | tf_op jit(solution)/shard_map/all_to_all | solution.py:232
  33.5 15.3 %collective-permute-start = (bf16[2,128,768]{2,1,0:T(8,128)(2,1)S(1)}, bf16[2,128,768]{2,1,0:T(8,128)(2,1)S(1)}, u32[]{:S(2)}, u32[]{:S(2)}) collective-permute-start(bf16[2,128,768]{2,1,0:T(8,128)(2,1)S(1)} %all_gather.40), channel_id=1, source_target_pairs={{0,2},{1,15},{2,4},{3,1},{4,6},{5,3},{6,8},{7,5},{8,10},{9,7},{10,... | collective-permute-start | bytes 1179656 | tf_op jit(solution)/shard_map/ppermute | solution.py:203
  48.8 9.2 %collective-permute-start.1 = (bf16[2,128,768]{2,1,0:T(8,128)(2,1)S(1)}, bf16[2,128,768]{2,1,0:T(8,128)(2,1)S(1)}, u32[]{:S(2)}, u32[]{:S(2)}) collective-permute-start(bf16[2,128,768]{2,1,0:T(8,128)(2,1)S(1)} %collective-permute-done.one_ref), channel_id=1, source_target_pairs={{0,2},{1,15},{2,4},{3,1},{4,6},{5,3},{6,8},{7,5},{8,10},{9,7},{10,... | collective-permute-start | bytes 1179656 | tf_op jit(solution)/shard_map/ppermute | solution.py:203
  58.0 11.5 %collective-permute-start.2 = (bf16[2,128,768]{2,1,0:T(8,128)(2,1)S(1)}, bf16[2,128,768]{2,1,0:T(8,128)(2,1)S(1)}, u32[]{:S(2)}, u32[]{:S(2)}) collective-permute-start(bf16[2,128,768]{2,1,0:T(8,128)(2,1)S(1)} %collective-permute-done.1.two_ref), channel_id=1, source_target_pairs={{0,2},{1,15},{2,4},{3,1},{4,6},{5,3},{6,8},{7,5},{8,10},{9,7},{10,... | collective-permute-start | bytes 1179656 | tf_op jit(solution)/shard_map/ppermute | solution.py:203
  62.7 16.9 %all-to-all-start.1 = ((bf16[8,48,384]{2,1,0:T(8,128)(2,1)}), bf16[8,48,384]{2,1,0:T(8,128)(2,1)S(1)}, u32[]{:S(2)}, u32[]{:S(2)}) async-start(bf16[8,48,384]{2,1,0:T(8,128)(2,1)} %broadcast_in_dim.35), calls=%async_computation.1 | async-start | bytes 589824 | tf_op jit(solution)/shard_map/all_to_all | solution.py:245
  69.5 15.5 %collective-permute-start.3 = (bf16[128,768]{1,0:T(8,128)(2,1)S(1)}, bf16[128,768]{1,0:T(8,128)(2,1)S(1)}, u32[]{:S(2)}, u32[]{:S(2)}) collective-permute-start(bf16[128,768]{1,0:T(8,128)(2,1)S(1)} %fusion.10), channel_id=1, source_target_pairs={{0,2},{1,15},{2,4},{3,1},{4,6},{5,3},{6,8},{7,5},{8,10},{9,7},{10,... | collective-permute-start | bytes 589832 | tf_op jit(solution)/shard_map/ppermute | solution.py:203
  90.5 19.0 %all-to-all-start.2 = ((bf16[8,2,64,128]{3,2,1,0:T(8,128)(2,1)}), bf16[8,2,64,128]{3,2,1,0:T(8,128)(2,1)S(1)}, u32[]{:S(2)}, u32[]{:S(2)}) async-start(bf16[8,2,64,128]{3,2,1,0:T(8,128)(2,1)} %broadcast_in_dim.36), calls=%async_computation.2 | async-start | bytes 524288 | tf_op jit(solution)/shard_map/all_to_all | solution.py:268
  111.4 18.7 %all-to-all-start.3 = ((bf16[64,16,128]{2,1,0:T(8,128)(2,1)}), bf16[64,16,128]{2,1,0:T(8,128)(2,1)S(1)}, u32[]{:S(2)}, u32[]{:S(2)}) async-start(bf16[64,16,128]{2,1,0:T(8,128)(2,1)} %shard_map.105), calls=%async_computation.3 | async-start | bytes 524288 | tf_op jit(solution)/shard_map/all_to_all | solution.py:277
  122.5 7.6 %copy-start.1 = (bf16[1,128,128]{2,1,0:T(8,128)(2,1)S(1)}, bf16[1,128,128]{2,1,0:T(8,128)(2,1)}, u32[]{:S(2)}) copy-start(bf16[1,128,128]{2,1,0:T(8,128)(2,1)} %param.11) | copy-start | bytes 98308
  122.5 7.6 %copy-start.2 = (bf16[12,128]{1,0:T(8,128)(2,1)S(1)}, bf16[12,128]{1,0:T(8,128)(2,1)}, u32[]{:S(2)}) copy-start(bf16[12,128]{1,0:T(8,128)(2,1)} %cw_ref.1) | copy-start | bytes 9220
Sparse Core Ops, SparseCore 0:
  11.7 99.1 all-gather.7

commit v12 on v11

--- a/solution.py
+++ b/solution.py
@@ -94,7 +94,7 @@
     out_ref[...] = held[...].astype(BF)
 
 
-def pack(far_ref, out_ref, held, packed, in_sems, out_sems):
+def pack(far_ref, triple_ref, out_ref, held, packed, in_sems, out_sems):
     copies = [
         pltpu.make_async_copy(far_ref.at[pl.ds(16 * n, 16)], held.at[pl.ds(16 * n, 16)], in_sems.at[n])
         for n in range(8)
@@ -106,21 +106,19 @@
         copies[n].wait()
         for d in range(16 * n, 16 * n + 16):
             packed[18 * d : 18 * d + 18, :] = held[d, 0:18, :]
-            packed[3 * D + 6 * d : 3 * D + 6 * d + 6, :] = held[d, 18:24, :]
-            packed[4 * D + 6 * d : 4 * D + 6 * d + 6, :] = held[d, 24:30, :]
-        for m, (start, rows) in enumerate(((288 * n, 288), (3 * D + 96 * n, 96), (4 * D + 96 * n, 96))):
-            part = pl.ds(start, rows)
-            sent.append(pltpu.make_async_copy(packed.at[part], out_ref.at[part], out_sems.at[3 * n + m]))
-            sent[-1].start()
+            out_ref[6 * d : 6 * d + 6, :] = held[d, 18:24, :]
+            out_ref[D + 6 * d : D + 6 * d + 6, :] = held[d, 24:30, :]
+        part = pl.ds(288 * n, 288)
+        sent.append(pltpu.make_async_copy(packed.at[part], triple_ref.at[part], out_sems.at[n]))
+        sent[n].start()
     for copy in sent:
         copy.wait()
 
 
-def column_block(bl_ref, stack_ref, far_ref, pair_ref, cw_ref, out_ref, pair_out_ref, w_ref, sems):
-    order = (8, 9, 0, 1, 2, 3, 4, 5, 6, 7)
+def column_block(bl_ref, stack_ref, outs_ref, far_ref, pair_ref, cw_ref, out_ref, pair_out_ref, w_ref, sems):
     copies = []
-    for n, m in enumerate(order):
-        part = pl.ds(384 * m, 384)
+    for n in range(6):
+        part = pl.ds(384 * n, 384)
         copies.append(pltpu.make_async_copy(far_ref.at[part], w_ref.at[part], sems.at[n]))
         copies[n].start()
     lane = lax.broadcasted_iota(jnp.int32, (L, L), 1)
@@ -155,15 +153,13 @@
         parts.append(jnp.where(jnp.logical_and(low, early), re1, o1))
     blended = jnp.concatenate(parts, axis=1).astype(BF)
 
-    for copy in copies[:2]:
-        copy.wait()
-    updated = (dot_nt(w_ref[4 * D :], blended) + stack_ref[...].astype(F32)).astype(BF).astype(F32)
+    updated = (dot_nt(outs_ref[D:], blended) + stack_ref[...].astype(F32)).astype(BF).astype(F32)
     center = jnp.mean(updated, axis=0, keepdims=True)
     spread = jnp.mean(jnp.square(updated - center), axis=0, keepdims=True)
     normed = ((updated - center) * lax.rsqrt(spread + 1e-05)).astype(BF)
-    for copy in copies[2:8]:
+    for copy in copies:
         copy.wait()
-    packed = jnp.dot(w_ref[: 3 * D], normed, preferred_element_type=F32)
+    packed = jnp.dot(w_ref[...], normed, preferred_element_type=F32)
 
     mixed = []
     for h in range(H):
@@ -176,9 +172,7 @@
         mixed.append(jnp.dot(v, probs, preferred_element_type=F32).astype(BF))
     mixed = jnp.concatenate(mixed, axis=0)
 
-    for copy in copies[8:]:
-        copy.wait()
-    result = (updated + jnp.dot(w_ref[3 * D : 4 * D], mixed, preferred_element_type=F32)).astype(BF)
+    result = (updated + jnp.dot(outs_ref[:D], mixed, preferred_element_type=F32)).astype(BF)
     place = (row // 8 % 2 * E + row // 16 * 8 + row % 8 == lane).astype(BF)
     out_ref[...] = dot_nt(place, result).astype(BF)
 
@@ -275,29 +269,29 @@
         compiler_params=params(),
     )(at, spans, parts, bias_own, lax.all_gather(values, "c", axis=0, tiled=False))
     came = lax.all_to_all(message, CHIPS, 0, 0, tiled=True)
-    column_weights = pl.pallas_call(
+    triple, outs = pl.pallas_call(
         pack,
-        out_shape=jax.ShapeDtypeStruct((5 * D, D), BF),
+        out_shape=(jax.ShapeDtypeStruct((3 * D, D), BF), jax.ShapeDtypeStruct((2 * D, D), BF)),
         in_specs=[ANY],
-        out_specs=ANY,
+        out_specs=(ANY, VMEM),
         scratch_shapes=[
             pltpu.VMEM((128, 32, D), BF),
-            pltpu.VMEM((5 * D, D), BF),
+            pltpu.VMEM((3 * D, D), BF),
             pltpu.SemaphoreType.DMA((8,)),
-            pltpu.SemaphoreType.DMA((24,)),
+            pltpu.SemaphoreType.DMA((8,)),
         ],
-        compiler_params=params(56),
+        compiler_params=params(48),
     )(gathered)
-    blended, column_weights = lax.optimization_barrier((came, column_weights))
+    blended, triple, outs = lax.optimization_barrier((came, triple, outs))
 
     alignment, pair_out = pl.pallas_call(
         column_block,
         out_shape=(jax.ShapeDtypeStruct((R, D), BF), jax.ShapeDtypeStruct((L, 128), BF)),
-        in_specs=[VMEM, VMEM, ANY, VMEM, VMEM],
+        in_specs=[VMEM, VMEM, VMEM, ANY, VMEM, VMEM],
         out_specs=(VMEM, VMEM),
-        scratch_shapes=[pltpu.VMEM((5 * D, D), BF), pltpu.SemaphoreType.DMA((10,))],
-        compiler_params=params(52),
-    )(blended, stack_own.T, column_weights, pair_own, contact_w)
+        scratch_shapes=[pltpu.VMEM((3 * D, D), BF), pltpu.SemaphoreType.DMA((6,))],
+        compiler_params=params(50),
+    )(blended, stack_own.T, outs, triple, pair_own, contact_w)
     return alignment.reshape(R, 1, D), pair_out.reshape(1, L, 128)
 
 

time: 148 us -> 148 us (level)
  local copies, waits for them, and re-layouts: 5.95 us -> 7.7 us
    unnamed x15 -> x17, local copies, waits for them, and re-layouts: 0.12 us -> 1.87 us
  transfers between devices with their start and end apart: 9 -> 9, of which waited for: 5 -> 5; matrix products, arithmetic and copies ran while one was open for 8% -> 8% of each run, Pallas kernels for 7% -> 6%
where the time goes in v12:
time: 148 us; the launch traced here: 146 us
  starting transfers between devices  49.7 us (34%)
  waiting for transfers between devices  31.3 us (21%)
  blocking collectives  17.5 us (12%)
  Pallas kernels  17.3 us (12%)
  between operations  15.1 us (10%)
  local copies, waits for them, and re-layouts  7.7 us (5%)
  other arithmetic  5.83 us (4%)
    all_to_all x2, starting transfers between devices, per_device(): came = lax.all_to_all(message, CHIPS, 0, 0, tiled=True)  23.6 us
    ppermute x4, starting transfers between devices, around(): return lax.ppermute(x, ('y', 'c'), pairs)  14.3 us
    ppermute x4, waiting for transfers between devices, around(): return lax.ppermute(x, ('y', 'c'), pairs)  11.8 us
    all_to_all x1, waiting for transfers between devices, per_device(): lax.all_to_all(jnp.broadcast_to(tied, (8, 2, L // 2, L)), 'z', 0, 0, tile...  10.3 us
    pallas_call x1, Pallas kernels, per_device(): pl.pallas_call(column_block, out_shape=(jax.ShapeDtypeStruct((R, D), BF),...  8.46 us
    all_to_all x1, waiting for transfers between devices, per_device(): lax.all_to_all(jnp.broadcast_to(half, (8, 48, 384)), 'z', 0, 0, tiled=True)  7.27 us
    all_to_all x1, starting transfers between devices, per_device(): lax.all_to_all(jnp.broadcast_to(half, (8, 48, 384)), 'z', 0, 0, tiled=True)  6.5 us
    all_gather x1, blocking collectives, per_device(): w_heads = lax.all_gather(over_z, 'c', axis=0, tiled=False).reshape(D, 384)  5.46 us
  transfers between devices with their start and end apart: 9, of which 5 were waited for; matrix products, arithmetic and copies ran while one was open for 8% of the time, Pallas kernels for 6%

profile of v12, /device:TPU:1, one launch (start us, length us, event | category | flops | bytes accessed | tf_op | source)
XLA Modules:
  0.0 145.7 jit_solution(948228464593227239)
XLA Ops:
  7.2 0.0 copy-start
  7.2 0.0 copy-start.4
  7.2 0.0 all-gather.8.cloned.1.call-start
  7.2 0.1 pad.8.clone
  7.3 1.5 %maximum_maximum_fusion = bf16[32,768]{1,0:T(8,128)(2,1)} fusion(bf16[6,768]{1,0:T(8,128)(2,1)} %bitcast.99, bf16[6,768]{1,0:T(8,128)(2,1)} %bitcast.100, bf16[18,768]{1,0:T(8,128)(2,1)} %bitcast.97, bf16[32]{0:T(256)(128)(2,1)S(1)} %pad.8.clone), kind=kLoop, calls=%fused_computation.23 | loop fusion | flops 196608 | bytes 95296 | tf_op jit(solution)/shard_map/concatenate | solution.py:207
  8.8 0.0 all-gather.8.cloned.1.call-update
  8.8 0.9 reshape.79
  9.7 0.1 copy.35
  9.8 0.1 reshape.80
  10.0 1.1 reshape_reshape.3
  11.1 0.0 copy-done
  11.1 0.9 convolution_convert_fusion
  12.1 0.1 broadcast_in_dim.33
  12.2 1.0 pad_maximum_fusion
  13.2 17.1 %all-to-all-start = ((bf16[64,32,128]{2,1,0:T(8,128)(2,1)}), bf16[64,32,128]{2,1,0:T(8,128)(2,1)S(1)}, u32[]{:S(2)}, u32[]{:S(2)}) async-start(bf16[64,32,128]{2,1,0:T(8,128)(2,1)} %pad_maximum_fusion), calls=%async_computation | async-start | bytes 1048576 | tf_op jit(solution)/shard_map/all_to_all | solution.py:226
  30.3 0.1 convert_reduce_fusion
  30.5 0.2 fusion.8
  30.7 0.1 fusion.4
  30.8 2.7 %all_gather.40 = bf16[2,128,768]{2,1,0:T(8,128)(2,1)S(1)} all-gather(bf16[1,128,768]{2,1,0:T(8,128)(2,1)S(1)} %fusion.4), channel_id=1, replica_groups=mesh['a'=4,'z'=8,'y'=8,'c'=2] {'c'}, dimensions={0}, use_global_device_ids=true | all-gather | bytes 589824 | tf_op jit(solution)/shard_map/all_gather | solution.py:211
  33.5 4.4 %collective-permute-start = (bf16[2,128,768]{2,1,0:T(8,128)(2,1)S(1)}, bf16[2,128,768]{2,1,0:T(8,128)(2,1)S(1)}, u32[]{:S(2)}, u32[]{:S(2)}) collective-permute-start(bf16[2,128,768]{2,1,0:T(8,128)(2,1)S(1)} %all_gather.40), channel_id=1, source_target_pairs={{0,2},{1,15},{2,4},{3,1},{4,6},{5,3},{6,8},{7,5},{8,10},{9,7},{10,... | collective-permute-start | bytes 1179656 | tf_op jit(solution)/shard_map/ppermute | solution.py:197
  38.0 2.6 %fusion.2 = bf16[2048,384]{1,0:T(8,128)(2,1)S(1)} fusion(s32[384]{0:T(512)S(1)} %get-tuple-element.37, s32[384]{0:T(512)S(1)} %get-tuple-element.38, s32[]{:T(128)S(6)} %mul.41, s32[384]{0:T(512)S(1)} %get-tuple-element.36, s32[384]{0:T(512)S(1)} %get-tuple-element.39, s32[2048]{0:T(1024)S(1)} %get-tuple-element.31, s32[2048]{0:T(1024)S(1)} %get-tuple-element.32, ...), kind=kLoop, calls=%fused_computation.4 | loop fusion | flops 11796480 | bytes 1616648 | tf_op jit(solution)/shard_map/convert_element_type | solution.py:231
  40.6 8.2 %collective-permute-done.one_ref = bf16[2,128,768]{2,1,0:T(8,128)(2,1)S(1)} collective-permute-done((bf16[2,128,768]{2,1,0:T(8,128)(2,1)S(1)}, bf16[2,128,768]{2,1,0:T(8,128)(2,1)S(1)}, u32[]{:S(2)}, u32[]{:S(2)}) %collective-permute-start) | collective-permute-done | bytes 393248 | tf_op jit(solution)/shard_map/ppermute | solution.py:197
  48.8 3.2 %collective-permute-start.1 = (bf16[2,128,768]{2,1,0:T(8,128)(2,1)S(1)}, bf16[2,128,768]{2,1,0:T(8,128)(2,1)S(1)}, u32[]{:S(2)}, u32[]{:S(2)}) collective-permute-start(bf16[2,128,768]{2,1,0:T(8,128)(2,1)S(1)} %collective-permute-done.one_ref), channel_id=1, source_target_pairs={{0,2},{1,15},{2,4},{3,1},{4,6},{5,3},{6,8},{7,5},{8,10},{9,7},{10,... | collective-permute-start | bytes 1179656 | tf_op jit(solution)/shard_map/ppermute | solution.py:197
  52.0 0.0 all-to-all-done
  52.0 0.5 fusion.27
  52.5 1.9 %all-gather = bf16[192,384]{1,0:T(8,128)(2,1)S(1)} all-gather(bf16[96,384]{1,0:T(8,128)(2,1)S(1)} %slice.113), channel_id=2, replica_groups=mesh['a'=4,'z'=8,'y'=8,'c'=2] {'c'}, dimensions={0}, use_global_device_ids=true | all-gather | bytes 221184 | tf_op jit(solution)/shard_map/all_gather | solution.py:234
  54.4 3.6 %collective-permute-done.1.two_ref = bf16[2,128,768]{2,1,0:T(8,128)(2,1)S(1)} collective-permute-done((bf16[2,128,768]{2,1,0:T(8,128)(2,1)S(1)}, bf16[2,128,768]{2,1,0:T(8,128)(2,1)S(1)}, u32[]{:S(2)}, u32[]{:S(2)}) %collective-permute-start.1) | collective-permute-done | bytes 393248 | tf_op jit(solution)/shard_map/ppermute | solution.py:197
  58.0 4.0 %collective-permute-start.2 = (bf16[2,128,768]{2,1,0:T(8,128)(2,1)S(1)}, bf16[2,128,768]{2,1,0:T(8,128)(2,1)S(1)}, u32[]{:S(2)}, u32[]{:S(2)}) collective-permute-start(bf16[2,128,768]{2,1,0:T(8,128)(2,1)S(1)} %collective-permute-done.1.two_ref), channel_id=1, source_target_pairs={{0,2},{1,15},{2,4},{3,1},{4,6},{5,3},{6,8},{7,5},{8,10},{9,7},{10,... | collective-permute-start | bytes 1179656 | tf_op jit(solution)/shard_map/ppermute | solution.py:197
  62.0 0.8 broadcast_in_dim.35
  62.7 6.5 %all-to-all-start.1 = ((bf16[8,48,384]{2,1,0:T(8,128)(2,1)}), bf16[8,48,384]{2,1,0:T(8,128)(2,1)S(1)}, u32[]{:S(2)}, u32[]{:S(2)}) async-start(bf16[8,48,384]{2,1,0:T(8,128)(2,1)} %broadcast_in_dim.35), calls=%async_computation.1 | async-start | bytes 589824 | tf_op jit(solution)/shard_map/all_to_all | solution.py:239
  69.2 0.1 fusion.9.own_ref
  69.4 0.0 collective-permute-done.2.three_ref
  69.4 2.8 %collective-permute-start.3 = (bf16[128,768]{1,0:T(8,128)(2,1)S(1)}, bf16[128,768]{1,0:T(8,128)(2,1)S(1)}, u32[]{:S(2)}, u32[]{:S(2)}) collective-permute-start(bf16[128,768]{1,0:T(8,128)(2,1)S(1)} %fusion.10), channel_id=1, source_target_pairs={{0,2},{1,15},{2,4},{3,1},{4,6},{5,3},{6,8},{7,5},{8,10},{9,7},{10,... | collective-permute-start | bytes 589832 | tf_op jit(solution)/shard_map/ppermute | solution.py:197
  72.2 0.1 pad_add_fusion.at_ref
  72.3 7.3 %all-to-all-done.1 = bf16[8,48,384]{2,1,0:T(8,128)(2,1)S(1)} async-done(((bf16[8,48,384]{2,1,0:T(8,128)(2,1)}), bf16[8,48,384]{2,1,0:T(8,128)(2,1)S(1)}, u32[]{:S(2)}, u32[]{:S(2)}) %all-to-all-start.1) | async-done | bytes 294944 | tf_op jit(solution)/shard_map/all_to_all | solution.py:239
  79.5 5.5 %all-gather.1 = bf16[16,48,384]{2,1,0:T(8,128)(2,1)S(1)} all-gather(bf16[8,48,384]{2,1,0:T(8,128)(2,1)S(1)} %all-to-all-done.1), channel_id=3, replica_groups=mesh['a'=4,'z'=8,'y'=8,'c'=2] {'c'}, dimensions={0}, use_global_device_ids=true | all-gather | bytes 884736 | tf_op jit(solution)/shard_map/all_gather | solution.py:240
  85.0 0.0 collective-permute-done.3.four_ref
  85.0 2.7 %shard_map.104 = (f32[2,2,64,128]{3,2,1,0:T(8,128)S(1)}, bf16[8,128,128]{2,1,0:T(8,128)(2,1)S(1)}) custom-call(s32[2]{0:T(128)S(1)} %pad_add_fusion.at_ref, bf16[768,384]{1,0:T(8,128)(2,1)S(1)} %bitcast.85, bf16[128,768]{1,0:T(8,128)(2,1)S(1)} %fusion.9.own_ref, bf16[2,128,768]{2,1,0:T(8,128)(2,1)S(1)} %collective-permute-done.one_ref, ...), custom_call_target="tpu_custom_call" | custom-call | tf_op jit(solution)/shard_map/pallas_call | solution.py:247
  87.7 2.0 %all-gather.2 = f32[4,2,64,128]{3,2,1,0:T(8,128)S(1)} all-gather(f32[2,2,64,128]{3,2,1,0:T(8,128)S(1)} %get-tuple-element.19), channel_id=4, replica_groups=mesh['a'=4,'z'=8,'y'=8,'c'=2] {'c'}, dimensions={0}, use_global_device_ids=true | all-gather | bytes 393216 | tf_op jit(solution)/shard_map/all_gather | solution.py:259
  89.7 0.8 broadcast_in_dim.36
  90.5 5.3 %all-to-all-start.2 = ((bf16[8,2,64,128]{3,2,1,0:T(8,128)(2,1)}), bf16[8,2,64,128]{3,2,1,0:T(8,128)(2,1)S(1)}, u32[]{:S(2)}, u32[]{:S(2)}) async-start(bf16[8,2,64,128]{3,2,1,0:T(8,128)(2,1)} %broadcast_in_dim.36), calls=%async_computation.2 | async-start | bytes 524288 | tf_op jit(solution)/shard_map/all_to_all | solution.py:262
  96.4 0.2 copy.28
  96.6 2.5 %all-gather.3 = bf16[16,128,128]{2,1,0:T(8,128)(2,1)S(1)} all-gather(bf16[8,128,128]{2,1,0:T(8,128)(2,1)S(1)} %get-tuple-element.20), channel_id=5, replica_groups=mesh['a'=4,'z'=8,'y'=8,'c'=2] {'c'}, dimensions={0}, use_global_device_ids=true | all-gather | bytes 786432 | tf_op jit(solution)/shard_map/all_gather | solution.py:270
  99.1 10.3 %all-to-all-done.2.part_ref = bf16[8,2,64,128]{3,2,1,0:T(8,128)(2,1)S(1)} async-done(((bf16[8,2,64,128]{3,2,1,0:T(8,128)(2,1)}), bf16[8,2,64,128]{3,2,1,0:T(8,128)(2,1)S(1)}, u32[]{:S(2)}, u32[]{:S(2)}) %all-to-all-start.2) | async-done | bytes 262176 | tf_op jit(solution)/shard_map/all_to_all | solution.py:262
  109.4 1.9 %shard_map.105 = bf16[64,16,128]{2,1,0:T(8,128)(2,1)} custom-call(s32[2]{0:T(128)S(1)} %pad_add_fusion.at_ref, s32[1]{0:T(128)S(6)} %copy.43.span_ref, bf16[8,2,64,128]{3,2,1,0:T(8,128)(2,1)S(1)} %all-to-all-done.2.part_ref, bf16[2,64,128]{2,1,0:T(8,128)(2,1)S(1)} %slice_bitcast_fusion.bias_ref, bf16[2,8,128,128]{3,2,1,0:T(8,128)(2,1)S(1)} %bitcast.86), custom_call_target="tpu_custom_call" | custom-call | tf_op jit(solution)/shard_map/pallas_call | solution.py:263
  111.3 6.4 %all-to-all-start.3 = ((bf16[64,16,128]{2,1,0:T(8,128)(2,1)}), bf16[64,16,128]{2,1,0:T(8,128)(2,1)S(1)}, u32[]{:S(2)}, u32[]{:S(2)}) async-start(bf16[64,16,128]{2,1,0:T(8,128)(2,1)} %shard_map.105), calls=%async_computation.3 | async-start | bytes 524288 | tf_op jit(solution)/shard_map/all_to_all | solution.py:271
  117.8 0.1 slice.70
  117.9 0.1 copy.29
  117.9 2.9 %all-gather.5 = bf16[128,12,128]{2,0,1:T(8,128)(2,1)S(1)} all-gather(bf16[64,12,128]{2,0,1:T(8,128)(2,1)S(1)} %copy.29), channel_id=7, replica_groups=mesh['a'=4,'z'=8,'y'=8,'c'=2] {'c'}, dimensions={0}, use_global_device_ids=true | all-gather | bytes 589824 | tf_op jit(solution)/shard_map/all_gather | solution.py:242
  120.9 0.3 copy.30
  121.1 0.2 reshape.86
  121.4 0.4 constant_dynamic-slice_fusion
  121.8 0.3 copy.31
  122.1 0.1 copy.32
  122.2 0.1 reshape.88
  122.3 0.2 copy.33
  122.5 0.0 all-gather.8.cloned.1.call-done
  122.5 0.0 copy-start.2
  122.5 0.0 copy-start.3
  122.5 4.2 %shard_map.106 = (bf16[2304,768]{1,0:T(8,128)(2,1)S(1)}, bf16[1536,768]{1,0:T(8,128)(2,1)S(1)}) custom-call(bf16[128,32,768]{2,1,0:T(8,128)(2,1)} %bitcast.90), custom_call_target="tpu_custom_call" | custom-call | tf_op jit(solution)/shard_map/pallas_call | solution.py:272
  126.7 0.0 copy-start.1
  126.7 1.8 %copy-done.1 = bf16[2304,768]{1,0:T(8,128)(2,1)} copy-done((bf16[2304,768]{1,0:T(8,128)(2,1)}, bf16[2304,768]{1,0:T(8,128)(2,1)S(1)}, u32[]{:S(2)}) %copy-start.1) | copy-done | bytes 3538968
  128.5 1.9 %all-to-all-done.3.bl_ref = bf16[64,16,128]{2,1,0:T(8,128)(2,1)S(1)} async-done(((bf16[64,16,128]{2,1,0:T(8,128)(2,1)}), bf16[64,16,128]{2,1,0:T(8,128)(2,1)S(1)}, u32[]{:S(2)}, u32[]{:S(2)}) %all-to-all-start.3) | async-done | bytes 262176 | tf_op jit(solution)/shard_map/all_to_all | solution.py:271
  130.4 8.5 %shard_map.107 = (bf16[128,768]{1,0:T(8,128)(2,1)}, bf16[128,128]{1,0:T(8,128)(2,1)}) custom-call(bf16[64,16,128]{2,1,0:T(8,128)(2,1)S(1)} %all-to-all-done.3.bl_ref, bf16[768,128]{1,0:T(8,128)(2,1)S(1)} %bitcast.87, bf16[1536,768]{1,0:T(8,128)(2,1)S(1)} %get-tuple-element.24.outs_ref, bf16[2304,768]{1,0:T(8,128)(2,1)} %copy-done.1, ...), custom_call_target="tpu_custom_call" | custom-call | tf_op jit(solution)/shard_map/pallas_call | solution.py:287
  (28 shorter events, 0.3 us)
Async XLA Ops:
  7.2 3.9 %copy-start = (bf16[128,12]{0,1:T(8,128)(2,1)S(1)}, bf16[128,12]{0,1:T(8,128)(2,1)}, u32[]{:S(2)}) copy-start(bf16[128,12]{0,1:T(8,128)(2,1)} %param.16) | copy-start | bytes 9220
  7.2 23.1 %copy-start.4 = (bf16[1,128,768]{2,1,0:T(8,128)(2,1)S(1)}, bf16[1,128,768]{2,1,0:T(8,128)(2,1)}, u32[]{:S(2)}) copy-start(bf16[1,128,768]{2,1,0:T(8,128)(2,1)} %param.9) | copy-start | bytes 589828
  7.2 115.3 %all-gather.8.cloned.1.call-start = ((), (), s32[]{:S(2)}) async-start(), calls=%async_computation.4 | async-start | bytes 6340608 | tf_op jit(solution)/shard_map/all_gather | solution.py:208
  13.2 38.8 %all-to-all-start = ((bf16[64,32,128]{2,1,0:T(8,128)(2,1)}), bf16[64,32,128]{2,1,0:T(8,128)(2,1)S(1)}, u32[]{:S(2)}, u32[]{:S(2)}) async-start(bf16[64,32,128]{2,1,0:T(8,128)(2,1)} %pad_maximum_fusion), calls=%async_computation | async-start | bytes 1048576 | tf_op jit(solution)/shard_map/all_to_all | solution.py:226
  33.5 15.3 %collective-permute-start = (bf16[2,128,768]{2,1,0:T(8,128)(2,1)S(1)}, bf16[2,128,768]{2,1,0:T(8,128)(2,1)S(1)}, u32[]{:S(2)}, u32[]{:S(2)}) collective-permute-start(bf16[2,128,768]{2,1,0:T(8,128)(2,1)S(1)} %all_gather.40), channel_id=1, source_target_pairs={{0,2},{1,15},{2,4},{3,1},{4,6},{5,3},{6,8},{7,5},{8,10},{9,7},{10,... | collective-permute-start | bytes 1179656 | tf_op jit(solution)/shard_map/ppermute | solution.py:197
  48.8 9.2 %collective-permute-start.1 = (bf16[2,128,768]{2,1,0:T(8,128)(2,1)S(1)}, bf16[2,128,768]{2,1,0:T(8,128)(2,1)S(1)}, u32[]{:S(2)}, u32[]{:S(2)}) collective-permute-start(bf16[2,128,768]{2,1,0:T(8,128)(2,1)S(1)} %collective-permute-done.one_ref), channel_id=1, source_target_pairs={{0,2},{1,15},{2,4},{3,1},{4,6},{5,3},{6,8},{7,5},{8,10},{9,7},{10,... | collective-permute-start | bytes 1179656 | tf_op jit(solution)/shard_map/ppermute | solution.py:197
  58.0 11.4 %collective-permute-start.2 = (bf16[2,128,768]{2,1,0:T(8,128)(2,1)S(1)}, bf16[2,128,768]{2,1,0:T(8,128)(2,1)S(1)}, u32[]{:S(2)}, u32[]{:S(2)}) collective-permute-start(bf16[2,128,768]{2,1,0:T(8,128)(2,1)S(1)} %collective-permute-done.1.two_ref), channel_id=1, source_target_pairs={{0,2},{1,15},{2,4},{3,1},{4,6},{5,3},{6,8},{7,5},{8,10},{9,7},{10,... | collective-permute-start | bytes 1179656 | tf_op jit(solution)/shard_map/ppermute | solution.py:197
  62.7 16.8 %all-to-all-start.1 = ((bf16[8,48,384]{2,1,0:T(8,128)(2,1)}), bf16[8,48,384]{2,1,0:T(8,128)(2,1)S(1)}, u32[]{:S(2)}, u32[]{:S(2)}) async-start(bf16[8,48,384]{2,1,0:T(8,128)(2,1)} %broadcast_in_dim.35), calls=%async_computation.1 | async-start | bytes 589824 | tf_op jit(solution)/shard_map/all_to_all | solution.py:239
  69.4 15.6 %collective-permute-start.3 = (bf16[128,768]{1,0:T(8,128)(2,1)S(1)}, bf16[128,768]{1,0:T(8,128)(2,1)S(1)}, u32[]{:S(2)}, u32[]{:S(2)}) collective-permute-start(bf16[128,768]{1,0:T(8,128)(2,1)S(1)} %fusion.10), channel_id=1, source_target_pairs={{0,2},{1,15},{2,4},{3,1},{4,6},{5,3},{6,8},{7,5},{8,10},{9,7},{10,... | collective-permute-start | bytes 589832 | tf_op jit(solution)/shard_map/ppermute | solution.py:197
  90.5 18.9 %all-to-all-start.2 = ((bf16[8,2,64,128]{3,2,1,0:T(8,128)(2,1)}), bf16[8,2,64,128]{3,2,1,0:T(8,128)(2,1)S(1)}, u32[]{:S(2)}, u32[]{:S(2)}) async-start(bf16[8,2,64,128]{3,2,1,0:T(8,128)(2,1)} %broadcast_in_dim.36), calls=%async_computation.2 | async-start | bytes 524288 | tf_op jit(solution)/shard_map/all_to_all | solution.py:262
  111.3 19.1 %all-to-all-start.3 = ((bf16[64,16,128]{2,1,0:T(8,128)(2,1)}), bf16[64,16,128]{2,1,0:T(8,128)(2,1)S(1)}, u32[]{:S(2)}, u32[]{:S(2)}) async-start(bf16[64,16,128]{2,1,0:T(8,128)(2,1)} %shard_map.105), calls=%async_computation.3 | async-start | bytes 524288 | tf_op jit(solution)/shard_map/all_to_all | solution.py:271
  122.5 7.9 %copy-start.2 = (bf16[1,128,128]{2,1,0:T(8,128)(2,1)S(1)}, bf16[1,128,128]{2,1,0:T(8,128)(2,1)}, u32[]{:S(2)}) copy-start(bf16[1,128,128]{2,1,0:T(8,128)(2,1)} %param.11) | copy-start | bytes 98308
  122.5 7.9 %copy-start.3 = (bf16[12,128]{1,0:T(8,128)(2,1)S(1)}, bf16[12,128]{1,0:T(8,128)(2,1)}, u32[]{:S(2)}) copy-start(bf16[12,128]{1,0:T(8,128)(2,1)} %cw_ref.1) | copy-start | bytes 9220
  126.7 1.8 %copy-start.1 = (bf16[2304,768]{1,0:T(8,128)(2,1)}, bf16[2304,768]{1,0:T(8,128)(2,1)S(1)}, u32[]{:S(2)}) copy-start(bf16[2304,768]{1,0:T(8,128)(2,1)S(1)} %get-tuple-element.25.far_ref) | copy-start | bytes 10616836
Sparse Core Ops, SparseCore 0:
  11.7 99.0 all-gather.7

commit v13 on v11

--- a/solution.py
+++ b/solution.py
@@ -235,7 +235,7 @@
     column = (source // 32 * 2 + c) * 18 + source % 32
     wanted = target // 128 * D + first_head(y) * E + target % 128
     pick = jnp.logical_and(column == wanted, source % 32 < 18).astype(BF)
-    came, one, pick = lax.optimization_barrier((came, one, pick))
+    came, pick = lax.optimization_barrier((came, pick))
     picked = dot_tn(came.reshape(2048, 128), pick)[:96].astype(BF)
     picked = lax.all_gather(picked, "c", axis=0, tiled=False)
     half = lax.dynamic_slice_in_dim(picked, c * 48, 48, axis=1)

time: 148 us -> 148 us (level)
  no operation moved by 1% of the time
where the time goes in v13:
time: 148 us; the launch traced here: 145 us
  starting transfers between devices  49.4 us (33%)
  waiting for transfers between devices  31.5 us (21%)
  Pallas kernels  18.4 us (12%)
  blocking collectives  17.5 us (12%)
  between operations  15.1 us (10%)
  local copies, waits for them, and re-layouts  5.95 us (4%)
  other arithmetic  5.83 us (4%)
    all_to_all x2, starting transfers between devices, per_device(): came = lax.all_to_all(message, CHIPS, 0, 0, tiled=True)  23.3 us
    ppermute x4, starting transfers between devices, around(): return lax.ppermute(x, ('y', 'c'), pairs)  14.2 us
    ppermute x4, waiting for transfers between devices, around(): return lax.ppermute(x, ('y', 'c'), pairs)  11.8 us
    all_to_all x1, waiting for transfers between devices, per_device(): lax.all_to_all(jnp.broadcast_to(tied, (8, 2, L // 2, L)), 'z', 0, 0, tile...  10.4 us
    pallas_call x1, Pallas kernels, per_device(): pl.pallas_call(column_block, out_shape=(jax.ShapeDtypeStruct((R, D), BF),...  8.12 us
    all_to_all x1, waiting for transfers between devices, per_device(): lax.all_to_all(jnp.broadcast_to(half, (8, 48, 384)), 'z', 0, 0, tiled=True)  7.42 us
    all_to_all x1, starting transfers between devices, per_device(): lax.all_to_all(jnp.broadcast_to(half, (8, 48, 384)), 'z', 0, 0, tiled=True)  6.57 us
    pallas_call x1, Pallas kernels, per_device(): pl.pallas_call(pack, out_shape=jax.ShapeDtypeStruct((5 * D, D), BF), in_s...  5.63 us
  transfers between devices with their start and end apart: 9, of which 5 were waited for; matrix products, arithmetic and copies ran while one was open for 8% of the time, Pallas kernels for 7%

profile of v13, /device:TPU:1, one launch (start us, length us, event | category | flops | bytes accessed | tf_op | source)
XLA Modules:
  0.0 145.1 jit_solution(6933774103533209078)
XLA Ops:
  7.2 0.0 copy-start
  7.2 0.0 copy-start.3
  7.2 0.0 all-gather.8.cloned.1.call-start
  7.2 0.1 pad.8.clone
  7.3 1.5 %maximum_maximum_fusion = bf16[32,768]{1,0:T(8,128)(2,1)} fusion(bf16[6,768]{1,0:T(8,128)(2,1)} %bitcast.99, bf16[6,768]{1,0:T(8,128)(2,1)} %bitcast.100, bf16[18,768]{1,0:T(8,128)(2,1)} %bitcast.97, bf16[32]{0:T(256)(128)(2,1)S(1)} %pad.8.clone), kind=kLoop, calls=%fused_computation.23 | loop fusion | flops 196608 | bytes 95296 | tf_op jit(solution)/shard_map/concatenate | solution.py:213
  8.8 0.0 all-gather.8.cloned.1.call-update
  8.8 0.9 reshape.79
  9.7 0.1 copy.35
  9.8 0.1 reshape.80
  10.0 1.1 reshape_reshape.3
  11.1 0.0 copy-done
  11.1 0.9 convolution_convert_fusion
  12.1 0.1 broadcast_in_dim.33
  12.2 1.0 pad_maximum_fusion
  13.2 17.1 %all-to-all-start = ((bf16[64,32,128]{2,1,0:T(8,128)(2,1)}), bf16[64,32,128]{2,1,0:T(8,128)(2,1)S(1)}, u32[]{:S(2)}, u32[]{:S(2)}) async-start(bf16[64,32,128]{2,1,0:T(8,128)(2,1)} %pad_maximum_fusion), calls=%async_computation | async-start | bytes 1048576 | tf_op jit(solution)/shard_map/all_to_all | solution.py:232
  30.3 0.0 copy-done.3
  30.3 0.1 convert_reduce_fusion
  30.5 0.2 fusion.6
  30.7 0.1 fusion.9
  30.8 2.7 %all_gather.44 = bf16[2,128,768]{2,1,0:T(8,128)(2,1)S(1)} all-gather(bf16[1,128,768]{2,1,0:T(8,128)(2,1)S(1)} %fusion.9), channel_id=1, replica_groups=mesh['a'=4,'z'=8,'y'=8,'c'=2] {'c'}, dimensions={0}, use_global_device_ids=true | all-gather | bytes 589824 | tf_op jit(solution)/shard_map/all_gather | solution.py:217
  33.5 4.4 %collective-permute-start = (bf16[2,128,768]{2,1,0:T(8,128)(2,1)S(1)}, bf16[2,128,768]{2,1,0:T(8,128)(2,1)S(1)}, u32[]{:S(2)}, u32[]{:S(2)}) collective-permute-start(bf16[2,128,768]{2,1,0:T(8,128)(2,1)S(1)} %all_gather.44), channel_id=1, source_target_pairs={{0,2},{1,15},{2,4},{3,1},{4,6},{5,3},{6,8},{7,5},{8,10},{9,7},{10,... | collective-permute-start | bytes 1179656 | tf_op jit(solution)/shard_map/ppermute | solution.py:203
  38.0 2.6 %fusion.2 = bf16[2048,384]{1,0:T(8,128)(2,1)S(1)} fusion(s32[384]{0:T(512)S(1)} %get-tuple-element.29, s32[384]{0:T(512)S(1)} %get-tuple-element.30, s32[]{:T(128)S(6)} %mul.39, s32[384]{0:T(512)S(1)} %get-tuple-element.28, s32[384]{0:T(512)S(1)} %get-tuple-element.31, s32[2048]{0:T(1024)S(1)} %get-tuple-element.23, s32[2048]{0:T(1024)S(1)} %get-tuple-element.24, ...), kind=kLoop, calls=%fused_computation.4 | loop fusion | flops 11796480 | bytes 1616648 | tf_op jit(solution)/shard_map/convert_element_type | solution.py:237
  40.6 8.2 %collective-permute-done.one_ref = bf16[2,128,768]{2,1,0:T(8,128)(2,1)S(1)} collective-permute-done((bf16[2,128,768]{2,1,0:T(8,128)(2,1)S(1)}, bf16[2,128,768]{2,1,0:T(8,128)(2,1)S(1)}, u32[]{:S(2)}, u32[]{:S(2)}) %collective-permute-start) | collective-permute-done | bytes 393248 | tf_op jit(solution)/shard_map/ppermute | solution.py:203
  48.8 3.2 %collective-permute-start.1 = (bf16[2,128,768]{2,1,0:T(8,128)(2,1)S(1)}, bf16[2,128,768]{2,1,0:T(8,128)(2,1)S(1)}, u32[]{:S(2)}, u32[]{:S(2)}) collective-permute-start(bf16[2,128,768]{2,1,0:T(8,128)(2,1)S(1)} %collective-permute-done.one_ref), channel_id=1, source_target_pairs={{0,2},{1,15},{2,4},{3,1},{4,6},{5,3},{6,8},{7,5},{8,10},{9,7},{10,... | collective-permute-start | bytes 1179656 | tf_op jit(solution)/shard_map/ppermute | solution.py:203
  52.0 0.0 all-to-all-done
  52.0 0.5 fusion.27
  52.5 1.9 %all-gather = bf16[192,384]{1,0:T(8,128)(2,1)S(1)} all-gather(bf16[96,384]{1,0:T(8,128)(2,1)S(1)} %slice.113), channel_id=2, replica_groups=mesh['a'=4,'z'=8,'y'=8,'c'=2] {'c'}, dimensions={0}, use_global_device_ids=true | all-gather | bytes 221184 | tf_op jit(solution)/shard_map/all_gather | solution.py:240
  54.4 3.6 %collective-permute-done.1.two_ref = bf16[2,128,768]{2,1,0:T(8,128)(2,1)S(1)} collective-permute-done((bf16[2,128,768]{2,1,0:T(8,128)(2,1)S(1)}, bf16[2,128,768]{2,1,0:T(8,128)(2,1)S(1)}, u32[]{:S(2)}, u32[]{:S(2)}) %collective-permute-start.1) | collective-permute-done | bytes 393248 | tf_op jit(solution)/shard_map/ppermute | solution.py:203
  58.0 4.0 %collective-permute-start.2 = (bf16[2,128,768]{2,1,0:T(8,128)(2,1)S(1)}, bf16[2,128,768]{2,1,0:T(8,128)(2,1)S(1)}, u32[]{:S(2)}, u32[]{:S(2)}) collective-permute-start(bf16[2,128,768]{2,1,0:T(8,128)(2,1)S(1)} %collective-permute-done.1.two_ref), channel_id=1, source_target_pairs={{0,2},{1,15},{2,4},{3,1},{4,6},{5,3},{6,8},{7,5},{8,10},{9,7},{10,... | collective-permute-start | bytes 1179656 | tf_op jit(solution)/shard_map/ppermute | solution.py:203
  62.0 0.8 broadcast_in_dim.35
  62.7 6.6 %all-to-all-start.1 = ((bf16[8,48,384]{2,1,0:T(8,128)(2,1)}), bf16[8,48,384]{2,1,0:T(8,128)(2,1)S(1)}, u32[]{:S(2)}, u32[]{:S(2)}) async-start(bf16[8,48,384]{2,1,0:T(8,128)(2,1)} %broadcast_in_dim.35), calls=%async_computation.1 | async-start | bytes 589824 | tf_op jit(solution)/shard_map/all_to_all | solution.py:245
  69.3 0.1 fusion.7.own_ref
  69.4 0.0 collective-permute-done.2.three_ref
  69.5 2.7 %collective-permute-start.3 = (bf16[128,768]{1,0:T(8,128)(2,1)S(1)}, bf16[128,768]{1,0:T(8,128)(2,1)S(1)}, u32[]{:S(2)}, u32[]{:S(2)}) collective-permute-start(bf16[128,768]{1,0:T(8,128)(2,1)S(1)} %fusion.10), channel_id=1, source_target_pairs={{0,2},{1,15},{2,4},{3,1},{4,6},{5,3},{6,8},{7,5},{8,10},{9,7},{10,... | collective-permute-start | bytes 589832 | tf_op jit(solution)/shard_map/ppermute | solution.py:203
  72.2 0.1 pad_add_fusion.at_ref
  72.3 7.4 %all-to-all-done.1 = bf16[8,48,384]{2,1,0:T(8,128)(2,1)S(1)} async-done(((bf16[8,48,384]{2,1,0:T(8,128)(2,1)}), bf16[8,48,384]{2,1,0:T(8,128)(2,1)S(1)}, u32[]{:S(2)}, u32[]{:S(2)}) %all-to-all-start.1) | async-done | bytes 294944 | tf_op jit(solution)/shard_map/all_to_all | solution.py:245
  79.7 5.3 %all-gather.1 = bf16[16,48,384]{2,1,0:T(8,128)(2,1)S(1)} all-gather(bf16[8,48,384]{2,1,0:T(8,128)(2,1)S(1)} %all-to-all-done.1), channel_id=3, replica_groups=mesh['a'=4,'z'=8,'y'=8,'c'=2] {'c'}, dimensions={0}, use_global_device_ids=true | all-gather | bytes 884736 | tf_op jit(solution)/shard_map/all_gather | solution.py:246
  85.0 0.0 collective-permute-done.3.four_ref
  85.0 2.7 %shard_map.104 = (f32[2,2,64,128]{3,2,1,0:T(8,128)S(1)}, bf16[8,128,128]{2,1,0:T(8,128)(2,1)S(1)}) custom-call(s32[2]{0:T(128)S(1)} %pad_add_fusion.at_ref, bf16[768,384]{1,0:T(8,128)(2,1)S(1)} %bitcast.85, bf16[128,768]{1,0:T(8,128)(2,1)S(1)} %fusion.7.own_ref, bf16[2,128,768]{2,1,0:T(8,128)(2,1)S(1)} %collective-permute-done.one_ref, ...), custom_call_target="tpu_custom_call" | custom-call | tf_op jit(solution)/shard_map/pallas_call | solution.py:253
  87.7 2.0 %all-gather.2 = f32[4,2,64,128]{3,2,1,0:T(8,128)S(1)} all-gather(f32[2,2,64,128]{3,2,1,0:T(8,128)S(1)} %get-tuple-element.14), channel_id=4, replica_groups=mesh['a'=4,'z'=8,'y'=8,'c'=2] {'c'}, dimensions={0}, use_global_device_ids=true | all-gather | bytes 393216 | tf_op jit(solution)/shard_map/all_gather | solution.py:265
  89.7 0.8 broadcast_in_dim.36
  90.5 5.2 %all-to-all-start.2 = ((bf16[8,2,64,128]{3,2,1,0:T(8,128)(2,1)}), bf16[8,2,64,128]{3,2,1,0:T(8,128)(2,1)S(1)}, u32[]{:S(2)}, u32[]{:S(2)}) async-start(bf16[8,2,64,128]{3,2,1,0:T(8,128)(2,1)} %broadcast_in_dim.36), calls=%async_computation.2 | async-start | bytes 524288 | tf_op jit(solution)/shard_map/all_to_all | solution.py:268
  96.4 0.2 copy.28
  96.6 2.5 %all-gather.3 = bf16[16,128,128]{2,1,0:T(8,128)(2,1)S(1)} all-gather(bf16[8,128,128]{2,1,0:T(8,128)(2,1)S(1)} %get-tuple-element.15), channel_id=5, replica_groups=mesh['a'=4,'z'=8,'y'=8,'c'=2] {'c'}, dimensions={0}, use_global_device_ids=true | all-gather | bytes 786432 | tf_op jit(solution)/shard_map/all_gather | solution.py:276
  99.1 10.4 %all-to-all-done.2.part_ref = bf16[8,2,64,128]{3,2,1,0:T(8,128)(2,1)S(1)} async-done(((bf16[8,2,64,128]{3,2,1,0:T(8,128)(2,1)}), bf16[8,2,64,128]{3,2,1,0:T(8,128)(2,1)S(1)}, u32[]{:S(2)}, u32[]{:S(2)}) %all-to-all-start.2) | async-done | bytes 262176 | tf_op jit(solution)/shard_map/all_to_all | solution.py:268
  109.5 1.9 %shard_map.105 = bf16[64,16,128]{2,1,0:T(8,128)(2,1)} custom-call(s32[2]{0:T(128)S(1)} %pad_add_fusion.at_ref, s32[1]{0:T(128)S(6)} %copy.43.span_ref, bf16[8,2,64,128]{3,2,1,0:T(8,128)(2,1)S(1)} %all-to-all-done.2.part_ref, bf16[2,64,128]{2,1,0:T(8,128)(2,1)S(1)} %slice_bitcast_fusion.bias_ref, bf16[2,8,128,128]{3,2,1,0:T(8,128)(2,1)S(1)} %bitcast.86), custom_call_target="tpu_custom_call" | custom-call | tf_op jit(solution)/shard_map/pallas_call | solution.py:269
  111.4 6.1 %all-to-all-start.3 = ((bf16[64,16,128]{2,1,0:T(8,128)(2,1)}), bf16[64,16,128]{2,1,0:T(8,128)(2,1)S(1)}, u32[]{:S(2)}, u32[]{:S(2)}) async-start(bf16[64,16,128]{2,1,0:T(8,128)(2,1)} %shard_map.105), calls=%async_computation.3 | async-start | bytes 524288 | tf_op jit(solution)/shard_map/all_to_all | solution.py:277
  117.6 0.1 slice.70
  117.7 0.1 copy.29
  117.7 3.1 %all-gather.5 = bf16[128,12,128]{2,0,1:T(8,128)(2,1)S(1)} all-gather(bf16[64,12,128]{2,0,1:T(8,128)(2,1)S(1)} %copy.29), channel_id=7, replica_groups=mesh['a'=4,'z'=8,'y'=8,'c'=2] {'c'}, dimensions={0}, use_global_device_ids=true | all-gather | bytes 589824 | tf_op jit(solution)/shard_map/all_gather | solution.py:248
  120.8 0.3 copy.30
  121.1 0.2 reshape.86
  121.3 0.4 constant_dynamic-slice_fusion
  121.8 0.3 copy.31
  122.1 0.1 copy.32
  122.2 0.1 reshape.88
  122.3 0.2 copy.33
  122.5 0.0 all-gather.8.cloned.1.call-done
  122.5 0.0 copy-start.1
  122.5 0.0 copy-start.2
  122.5 5.6 %shard_map.106.far_ref = bf16[3840,768]{1,0:T(8,128)(2,1)} custom-call(bf16[128,32,768]{2,1,0:T(8,128)(2,1)} %bitcast.90), custom_call_target="tpu_custom_call" | custom-call | tf_op jit(solution)/shard_map/pallas_call | solution.py:278
  128.2 1.9 %all-to-all-done.3.bl_ref = bf16[64,16,128]{2,1,0:T(8,128)(2,1)S(1)} async-done(((bf16[64,16,128]{2,1,0:T(8,128)(2,1)}), bf16[64,16,128]{2,1,0:T(8,128)(2,1)S(1)}, u32[]{:S(2)}, u32[]{:S(2)}) %all-to-all-start.3) | async-done | bytes 262176 | tf_op jit(solution)/shard_map/all_to_all | solution.py:277
  130.1 0.0 copy-done.1
  130.1 8.1 %shard_map.107 = (bf16[128,768]{1,0:T(8,128)(2,1)}, bf16[128,128]{1,0:T(8,128)(2,1)}) custom-call(bf16[64,16,128]{2,1,0:T(8,128)(2,1)S(1)} %all-to-all-done.3.bl_ref, bf16[768,128]{1,0:T(8,128)(2,1)S(1)} %bitcast.87, bf16[3840,768]{1,0:T(8,128)(2,1)} %shard_map.106.far_ref, bf16[128,128]{1,0:T(8,128)(2,1)S(1)} %bitcast.88, bf16[12,128]{1,0:T(8,128)(2,1)S(1)} %copy-done.2), custom_call_target="tpu_custom_call" | custom-call | tf_op jit(solution)/shard_map/pallas_call | solution.py:293
  (26 shorter events, 0.3 us)
Async XLA Ops:
  7.2 3.9 %copy-start = (bf16[128,12]{0,1:T(8,128)(2,1)S(1)}, bf16[128,12]{0,1:T(8,128)(2,1)}, u32[]{:S(2)}) copy-start(bf16[128,12]{0,1:T(8,128)(2,1)} %param.16) | copy-start | bytes 9220
  7.2 23.1 %copy-start.3 = (bf16[1,128,768]{2,1,0:T(8,128)(2,1)S(1)}, bf16[1,128,768]{2,1,0:T(8,128)(2,1)}, u32[]{:S(2)}) copy-start(bf16[1,128,768]{2,1,0:T(8,128)(2,1)} %param.9) | copy-start | bytes 589828
  7.2 115.3 %all-gather.8.cloned.1.call-start = ((), (), s32[]{:S(2)}) async-start(), calls=%async_computation.4 | async-start | bytes 6340608 | tf_op jit(solution)/shard_map/all_gather | solution.py:214
  13.2 38.8 %all-to-all-start = ((bf16[64,32,128]{2,1,0:T(8,128)(2,1)}), bf16[64,32,128]{2,1,0:T(8,128)(2,1)S(1)}, u32[]{:S(2)}, u32[]{:S(2)}) async-start(bf16[64,32,128]{2,1,0:T(8,128)(2,1)} %pad_maximum_fusion), calls=%async_computation | async-start | bytes 1048576 | tf_op jit(solution)/shard_map/all_to_all | solution.py:232
  33.5 15.3 %collective-permute-start = (bf16[2,128,768]{2,1,0:T(8,128)(2,1)S(1)}, bf16[2,128,768]{2,1,0:T(8,128)(2,1)S(1)}, u32[]{:S(2)}, u32[]{:S(2)}) collective-permute-start(bf16[2,128,768]{2,1,0:T(8,128)(2,1)S(1)} %all_gather.44), channel_id=1, source_target_pairs={{0,2},{1,15},{2,4},{3,1},{4,6},{5,3},{6,8},{7,5},{8,10},{9,7},{10,... | collective-permute-start | bytes 1179656 | tf_op jit(solution)/shard_map/ppermute | solution.py:203
  48.8 9.2 %collective-permute-start.1 = (bf16[2,128,768]{2,1,0:T(8,128)(2,1)S(1)}, bf16[2,128,768]{2,1,0:T(8,128)(2,1)S(1)}, u32[]{:S(2)}, u32[]{:S(2)}) collective-permute-start(bf16[2,128,768]{2,1,0:T(8,128)(2,1)S(1)} %collective-permute-done.one_ref), channel_id=1, source_target_pairs={{0,2},{1,15},{2,4},{3,1},{4,6},{5,3},{6,8},{7,5},{8,10},{9,7},{10,... | collective-permute-start | bytes 1179656 | tf_op jit(solution)/shard_map/ppermute | solution.py:203
  58.0 11.5 %collective-permute-start.2 = (bf16[2,128,768]{2,1,0:T(8,128)(2,1)S(1)}, bf16[2,128,768]{2,1,0:T(8,128)(2,1)S(1)}, u32[]{:S(2)}, u32[]{:S(2)}) collective-permute-start(bf16[2,128,768]{2,1,0:T(8,128)(2,1)S(1)} %collective-permute-done.1.two_ref), channel_id=1, source_target_pairs={{0,2},{1,15},{2,4},{3,1},{4,6},{5,3},{6,8},{7,5},{8,10},{9,7},{10,... | collective-permute-start | bytes 1179656 | tf_op jit(solution)/shard_map/ppermute | solution.py:203
  62.7 16.9 %all-to-all-start.1 = ((bf16[8,48,384]{2,1,0:T(8,128)(2,1)}), bf16[8,48,384]{2,1,0:T(8,128)(2,1)S(1)}, u32[]{:S(2)}, u32[]{:S(2)}) async-start(bf16[8,48,384]{2,1,0:T(8,128)(2,1)} %broadcast_in_dim.35), calls=%async_computation.1 | async-start | bytes 589824 | tf_op jit(solution)/shard_map/all_to_all | solution.py:245
  69.5 15.5 %collective-permute-start.3 = (bf16[128,768]{1,0:T(8,128)(2,1)S(1)}, bf16[128,768]{1,0:T(8,128)(2,1)S(1)}, u32[]{:S(2)}, u32[]{:S(2)}) collective-permute-start(bf16[128,768]{1,0:T(8,128)(2,1)S(1)} %fusion.10), channel_id=1, source_target_pairs={{0,2},{1,15},{2,4},{3,1},{4,6},{5,3},{6,8},{7,5},{8,10},{9,7},{10,... | collective-permute-start | bytes 589832 | tf_op jit(solution)/shard_map/ppermute | solution.py:203
  90.5 19.0 %all-to-all-start.2 = ((bf16[8,2,64,128]{3,2,1,0:T(8,128)(2,1)}), bf16[8,2,64,128]{3,2,1,0:T(8,128)(2,1)S(1)}, u32[]{:S(2)}, u32[]{:S(2)}) async-start(bf16[8,2,64,128]{3,2,1,0:T(8,128)(2,1)} %broadcast_in_dim.36), calls=%async_computation.2 | async-start | bytes 524288 | tf_op jit(solution)/shard_map/all_to_all | solution.py:268
  111.4 18.7 %all-to-all-start.3 = ((bf16[64,16,128]{2,1,0:T(8,128)(2,1)}), bf16[64,16,128]{2,1,0:T(8,128)(2,1)S(1)}, u32[]{:S(2)}, u32[]{:S(2)}) async-start(bf16[64,16,128]{2,1,0:T(8,128)(2,1)} %shard_map.105), calls=%async_computation.3 | async-start | bytes 524288 | tf_op jit(solution)/shard_map/all_to_all | solution.py:277
  122.5 7.6 %copy-start.1 = (bf16[1,128,128]{2,1,0:T(8,128)(2,1)S(1)}, bf16[1,128,128]{2,1,0:T(8,128)(2,1)}, u32[]{:S(2)}) copy-start(bf16[1,128,128]{2,1,0:T(8,128)(2,1)} %param.11) | copy-start | bytes 98308
  122.5 7.6 %copy-start.2 = (bf16[12,128]{1,0:T(8,128)(2,1)S(1)}, bf16[12,128]{1,0:T(8,128)(2,1)}, u32[]{:S(2)}) copy-start(bf16[12,128]{1,0:T(8,128)(2,1)} %cw_ref.1) | copy-start | bytes 9220
Sparse Core Ops, SparseCore 0:
  11.7 99.1 all-gather.7
